TPU v7x, 256 devices: a whole 4x4x8 slice. The times are simulated.
256 devices in a mesh: gx: 16 (over y, z_hi, core), gy: 16 (over x, z_lo).
Axes of the slice: x: 4, y: 4, z: 8 (z_hi: 2, z_lo: 4; z = z_hi * 4 + z_lo), core: 2. Of those that a mesh axis runs over, the one named last changes fastest.
Arguments:
- right_side: float32 [2, 16, 256, 2048], P(None, None, 'gx', 'gy'), may hold values from -12 to 12
- classes: int32 [16, 256, 2048], P(None, 'gx', 'gy'), may hold values from 0 to 15
- sea_mask: int32 [16, 256, 2048], P(None, 'gx', 'gy'), may hold values from 0 to 1, as said below
- kappa_table: float32 [16], replicated, may hold values from 0.002 to 0.2
- cross_table: float32 [16], replicated, may hold values from 0.5 to 4
- vertical_table: float32 [16], replicated, may hold values from 0.05 to 0.5
Outputs:
- solution_field: float32 [2, 16, 256, 2048], P(None, None, 'gx', 'gy')
- residual: float32 [2, 16, 256, 2048], P(None, None, 'gx', 'gy')
Inputs may be any that keep to these rules, and one draw needn't show every extreme that they name: `sea_mask`: land cells (value 0) occur only where both horizontal indices of the cell are even.
All inputs are finite; a program needn't handle non-finite values.
Results may differ from a plain program's by a relative error of at most 0.0055.
Values sent between devices are 32-bit elements; how exact they have to be, the bound alone decides.
No kernel may reach another device: no remote copies, remote signals or barrier semaphores. Data moves between devices by JAX's collectives and lax.ppermute only.
A program may use at most 128 MiB of HBM per device.

v0:
```python
import math

import jax
import jax.numpy as jnp
from jax import lax
from jax.sharding import PartitionSpec as P

LEVELS = 3


def with_halo(block, sides, width):
    for axis, dim in sides:
        count = lax.axis_size(axis)
        forward = [(i, i + 1) for i in range(count - 1)]
        backward = [(target, source) for source, target in forward]
        low = lax.ppermute(
            lax.slice_in_dim(block, block.shape[dim] - width, None, axis=dim), axis, forward
        )
        high = lax.ppermute(lax.slice_in_dim(block, 0, width, axis=dim), axis, backward)
        block = jnp.concatenate([low, block, high], axis=dim)
    return block


def cheb_weights(degree, lower_end, upper_end):
    middle = 0.5 * (upper_end + lower_end)
    radius = 0.5 * (upper_end - lower_end)
    return [
        1.0 / (middle + radius * math.cos(math.pi * (2 * index_k + 1) / (2 * degree)))
        for index_k in range(degree)
    ]


def look_up(classes, values_table):
    result = jnp.zeros(classes.shape, jnp.float32)
    for entry in range(values_table.shape[0]):
        result = jnp.where(classes == entry, values_table[entry], result)
    return result


def coarsen_sum(vector):
    shape = vector.shape
    blocks = vector.reshape(shape[:-3] + (shape[-3] // 2, 2, shape[-2] // 2, 2, shape[-1] // 2, 2))
    return jnp.sum(blocks, axis=(-5, -3, -1))


def coarsen_mean(vector):
    return 0.125 * coarsen_sum(vector)


def spread_up(vector):
    return jnp.repeat(jnp.repeat(jnp.repeat(vector, 2, axis=-3), 2, axis=-2), 2, axis=-1)


def build_coeffs(padded_w, vertical, mass_term, factor):
    face_x = factor * jnp.sqrt(padded_w[:, :-1, 1:-1] * padded_w[:, 1:, 1:-1])
    face_y = factor * jnp.sqrt(padded_w[:, 1:-1, :-1] * padded_w[:, 1:-1, 1:])
    face_z = jnp.pad(factor * jnp.sqrt(vertical[:-1] * vertical[1:]), ((1, 1), (0, 0), (0, 0)))
    diagonal = (
        mass_term
        + face_x[:, :-1]
        + face_x[:, 1:]
        + face_y[:, :, :-1]
        + face_y[:, :, 1:]
        + face_z[:-1]
        + face_z[1:]
    )
    return (face_x, face_y, face_z, diagonal)


def apply_operator(vector, coeffs, padded):
    face_x, face_y, face_z, diagonal = coeffs
    padded_z = jnp.pad(vector, ((0, 0), (1, 1), (0, 0), (0, 0)))
    neighbours = face_x[:, :-1] * padded[:, :, :-2, 1:-1] + face_x[:, 1:] * padded[:, :, 2:, 1:-1]
    neighbours = (
        neighbours
        + face_y[:, :, :-1] * padded[:, :, 1:-1, :-2]
        + face_y[:, :, 1:] * padded[:, :, 1:-1, 2:]
    )
    neighbours = neighbours + face_z[:-1] * padded_z[:, :-2] + face_z[1:] * padded_z[:, 2:]
    return diagonal * vector - neighbours


def smooth_pass(approx, source, coeffs, weights, operator):
    for step_index, weight in enumerate(weights):
        if approx is None:
            approx = weight * source / coeffs[3]
        else:
            approx = approx + weight * (source - operator(approx)) / coeffs[3]
    return approx


def pad_sides(vector):
    return with_halo(vector, (("gx", 2), ("gy", 3)), 1)


def pad_material(crosswise):
    return with_halo(crosswise, (("gx", 1), ("gy", 2)), 1)


def cycle_down(source, coeff_list, tier_index):
    coeffs = coeff_list[tier_index]

    def operator(vector):
        return apply_operator(vector, coeffs, pad_sides(vector))

    if tier_index == len(coeff_list) - 1:
        coarse_weights = cheb_weights(4, 0.1, 2.0)
        return smooth_pass(None, source, coeffs, coarse_weights, operator)
    smooth_weights = cheb_weights(2, 0.3, 2.0)
    approx = smooth_pass(None, source, coeffs, smooth_weights, operator)
    defect = source - operator(approx)
    approx = approx + spread_up(cycle_down(coarsen_sum(defect), coeff_list, tier_index + 1))
    return smooth_pass(approx, source, coeffs, smooth_weights, operator)


def shards(right_side, classes, sea_mask, kappa_table, cross_table, vertical_table):
    sea = sea_mask.astype(jnp.float32)
    crosswise = look_up(classes, cross_table) * sea
    vertical = look_up(classes, vertical_table) * sea
    mass_term = look_up(classes, kappa_table) * sea + (1.0 - sea)
    coeff_list = []
    factor = 1.0
    for tier_index in range(LEVELS - 1):
        coeff_list.append(build_coeffs(pad_material(crosswise), vertical, mass_term, factor))
        crosswise = coarsen_mean(crosswise)
        vertical = coarsen_mean(vertical)
        mass_term = coarsen_sum(mass_term)
        factor = 4.0
    coeff_list.append(build_coeffs(pad_material(crosswise), vertical, mass_term, factor))
    direction = cycle_down(cycle_down(right_side, coeff_list, 0), coeff_list, 0)
    local_rz = jnp.sum(right_side * direction, axis=(1, 2, 3))
    first_image = apply_operator(direction, coeff_list[0], pad_sides(direction))
    image = apply_operator(first_image, coeff_list[0], pad_sides(first_image))
    total_rz, total_curve = lax.psum(
        (local_rz, jnp.sum(direction * image, axis=(1, 2, 3))), ("gx", "gy")
    )
    step_length = (total_rz / total_curve)[:, None, None, None]
    return (step_length * direction, right_side - step_length * image)


def solution(mesh):
    return jax.shard_map(
        shards,
        mesh=mesh,
        in_specs=(
            P(None, None, "gx", "gy"),
            P(None, "gx", "gy"),
            P(None, "gx", "gy"),
            P(),
            P(),
            P(),
        ),
        out_specs=(P(None, None, "gx", "gy"), P(None, None, "gx", "gy")),
        check_vma=False,
    )
```

profile of v0, /device:TPU:1, one launch (start us, length us, event | category | flops | bytes accessed | tf_op | source)
XLA Modules:
  0.0 907.2 jit_solution(8956377389170854305)
XLA Ops:
  4.6 11.4 %select_multiply_fusion = (f32[16,16,128]{2,1,0:T(8,128)S(1)}, pred[16,16,128]{2,1,0:T(8,128)(4,1)S(1)}, pred[16,16,128]{2,1,0:T(8,128)(4,1)S(1)}, pred[16,16,12...) fusion(s32[16,16,128]{2,1,0:T(8,128)} %param.8, ...), kind=kLoop, calls=%fused_computation.236 | loop fusion | flops 1114112 | bytes 917568 | tf_op jit(solution)/shard_map/mul | solution.py:119
  15.9 11.1 %select_multiply_fusion.1 = f32[16,16,128]{2,1,0:T(8,128)S(1)} fusion(pred[16,16,128]{2,1,0:T(8,128)(4,1)S(1)} %get-tuple-element.35, pred[16,16,128]{2,1,0:T(8,128)(4,1)S(1)} %get-tuple-element.34, pred[16,16,128]{2,1,0:T(8,128)(4,1)S(1)} %get-tuple-element.33, pred[16,16,128]{2,1,0:T(8,128)(4,1)S(1)} %get-tuple-element.32, ...), kind=kLoop, calls=%fused_computation.237 | loop fusion | flops 589824 | bytes 786496 | tf_op jit(solution)/shard_map/mul | solution.py:118
  27.1 10.2 %collective-permute-start = (f32[16,1,128]{2,1,0:T(1,128)S(1)}, f32[16,1,128]{2,1,0:T(1,128)S(1)}, u32[]{:S(2)}, u32[]{:S(2)}) collective-permute-start(f32[16,1,128]{2,1,0:T(1,128)S(1)} %get-tuple-element.102), channel_id=1, source_target_pairs={{0,16},{16,32},{32,48},{48,64},{64,80},{80,96},{96,112},{112,128},... | collective-permute-start | bytes 24584 | tf_op jit(solution)/shard_map/ppermute | solution.py:16
  39.2 9.7 %reshape.96 = f32[8,2,8,2,64,2]{5,4,3,2,1,0:T(8,128)} reshape(f32[16,16,128]{2,1,0:T(8,128)S(1)} %select_multiply_fusion.1) | data formatting | bytes 262144 | tf_op jit(solution)/shard_map/reshape | solution.py:42
  53.0 7.5 collective-permute-start.12
  66.3 9.7 %reshape.97 = f32[8,2,8,2,64,2]{5,4,3,2,1,0:T(8,128)} reshape(f32[16,16,128]{2,1,0:T(8,128)S(1)} %get-tuple-element.19) | data formatting | bytes 262144 | tf_op jit(solution)/shard_map/reshape | solution.py:42
  85.3 6.3 collective-permute-done.13
  106.6 10.4 %add_add_fusion = (f32[16,16,128]{2,1,0:T(8,128)S(1)}, f32[16,16,128]{2,1,0:T(8,128)S(1)}) fusion(f32[16,16,129]{2,1,0:T(8,128)S(1)} %fusion.127, f32[16,17,128]{2,1,0:T(8,128)S(1)} %fusion.128, f32[15,16,128]{2,1,0:T(8,128)S(1)} %fusion.129, s32[16,16,128]{2,1,0:T(8,128)S(1)} %copy-done.20, pred[16,16,128]{2,1,0:T(8,128)(4,1)S(1)} %get-tuple-element.35, ...), kind=kLoop, calls=%fused_computation.235 | loop fusion | flops 851968 | bytes 1564736 | tf_op jit(solution)/shard_map/add | solution.py:59
  117.1 9.0 collective-permute-start.4
  128.1 6.9 collective-permute-done.5
  140.7 10.4 %collective-permute-done.7 = f32[2,16,18,1]{3,1,2,0:T(8,128)S(1)} collective-permute-done((f32[2,16,18,1]{3,1,2,0:T(8,128)S(1)}, f32[2,16,18,1]{3,1,2,0:T(8,128)S(1)}, u32[]{:S(2)}, u32[]{:S(2)}) %collective-permute-start.7) | collective-permute-done | bytes 2336 | tf_op jit(solution)/shard_map/ppermute | solution.py:19
  151.7 7.5 collective-permute-start.8
  159.3 9.7 %reshape.95 = f32[8,2,8,2,64,2]{5,4,3,2,1,0:T(8,128)} reshape(f32[16,16,128]{2,1,0:T(8,128)S(1)} %get-tuple-element.18) | data formatting | bytes 262144 | tf_op jit(solution)/shard_map/reshape | solution.py:42
  175.2 6.9 collective-permute-done.9
  190.0 6.6 collective-permute-done.11
  197.2 18.1 %reshape.94 = f32[2,8,2,8,2,64,2]{6,5,4,3,2,1,0:T(8,128)} reshape(f32[2,16,16,128]{3,2,1,0:T(8,128)S(1)} %fusion.13) | data formatting | bytes 524288 | tf_op jit(solution)/shard_map/reshape | solution.py:42
  215.3 7.0 reduce_sum.108
  222.4 8.5 collective-permute-start.16
  247.7 7.8 collective-permute-start.20
  258.9 5.5 collective-permute-done.21
  269.2 6.2 collective-permute-done.23
  286.1 6.9 collective-permute-done.29
  293.1 6.4 collective-permute-start.30
  310.8 6.9 collective-permute-done.33
  332.7 6.9 collective-permute-done.37
  339.7 4.3 collective-permute-start.38
  356.3 6.9 collective-permute-done.41
  363.3 4.3 collective-permute-start.42
  369.1 4.8 collective-permute-done.43
  379.9 6.9 collective-permute-done.45
  392.1 4.8 collective-permute-done.47
  408.4 7.0 collective-permute-done.49
  422.9 7.8 collective-permute-done.51
  436.3 7.7 collective-permute-done.53
  450.5 7.0 collective-permute-done.55
  458.1 5.3 collective-permute-start.56
  465.5 7.4 collective-permute-done.57
  478.9 7.7 collective-permute-done.59
  487.2 4.6 collective-permute-start.60
  493.9 7.5 collective-permute-done.61
  507.5 7.6 collective-permute-done.63
  515.7 18.1 %reshape.106 = f32[2,8,2,8,2,64,2]{6,5,4,3,2,1,0:T(8,128)} reshape(f32[2,16,16,128]{3,2,1,0:T(8,128)S(1)} %fusion.46) | data formatting | bytes 524288 | tf_op jit(solution)/shard_map/reshape | solution.py:42
  533.8 7.1 reduce_sum.116
  540.9 8.1 collective-permute-start.64
  551.0 7.0 collective-permute-done.65
  565.9 5.1 collective-permute-start.68
  573.0 7.1 collective-permute-done.69
  599.0 7.0 collective-permute-done.73
  620.8 7.6 collective-permute-done.77
  644.0 7.6 collective-permute-done.81
  668.5 7.6 collective-permute-done.85
  681.7 4.6 collective-permute-done.87
  692.9 7.6 collective-permute-done.89
  705.7 4.5 collective-permute-done.91
  722.4 7.6 collective-permute-done.93
  737.4 7.8 collective-permute-done.95
  750.5 7.8 collective-permute-done.97
  764.7 7.3 collective-permute-done.99
  772.6 4.2 collective-permute-start.100
  778.8 7.7 collective-permute-done.101
  792.4 7.6 collective-permute-done.103
  806.8 7.2 collective-permute-done.105
  820.1 7.9 collective-permute-done.107
  828.9 77.2 %all-reduce.27 = (f32[2]{0:T(128)S(1)}, f32[2]{0:T(128)S(1)}) all-reduce(f32[2]{0:T(128)S(1)} %get-tuple-element.11, f32[2]{0:T(128)S(1)} %get-tuple-element.10), channel_id=1, replica_groups=mesh['gx'=16,'gy'=16] {'gx','gy'}, use_global_device_ids=true, to_apply=%region_11.12 | all-reduce | flops 4 | bytes 32 | tf_op jit(solution)/shard_map/psum | solution.py:134
  (439 shorter events, 347.1 us)
Async XLA Ops:
  27.1 68.6 %collective-permute-start = (f32[16,1,128]{2,1,0:T(1,128)S(1)}, f32[16,1,128]{2,1,0:T(1,128)S(1)}, u32[]{:S(2)}, u32[]{:S(2)}) collective-permute-start(f32[16,1,128]{2,1,0:T(1,128)S(1)} %get-tuple-element.102), channel_id=1, source_target_pairs={{0,16},{16,32},{32,48},{48,64},{64,80},{80,96},{96,112},{112,128},... | collective-permute-start | bytes 24584 | tf_op jit(solution)/shard_map/ppermute | solution.py:16
  37.3 58.3 %collective-permute-start.1 = (f32[16,1,128]{2,1,0:T(1,128)S(1)}, f32[16,1,128]{2,1,0:T(1,128)S(1)}, u32[]{:S(2)}, u32[]{:S(2)}) collective-permute-start(f32[16,1,128]{2,1,0:T(1,128)S(1)} %get-tuple-element.103), channel_id=1, source_target_pairs={{16,0},{32,16},{48,32},{64,48},{80,64},{96,80},{112,96},{128,112},... | collective-permute-start | bytes 24584 | tf_op jit(solution)/shard_map/ppermute | solution.py:19
  53.0 32.2 %collective-permute-start.12 = (f32[8,1,64]{2,1,0:T(1,128)S(1)}, f32[8,1,64]{2,1,0:T(1,128)S(1)}, u32[]{:S(2)}, u32[]{:S(2)}) collective-permute-start(f32[8,1,64]{2,1,0:T(1,128)S(1)} %get-tuple-element.173), channel_id=1, source_target_pairs={{0,16},{16,32},{32,48},{48,64},{64,80},{80,96},{96,112},{112,128},... | collective-permute-start | bytes 6152 | tf_op jit(solution)/shard_map/ppermute | solution.py:16
  61.9 20.8 %collective-permute-start.24 = (f32[4,1,32]{2,1,0:T(1,128)S(1)}, f32[4,1,32]{2,1,0:T(1,128)S(1)}, u32[]{:S(2)}, u32[]{:S(2)}) collective-permute-start(f32[4,1,32]{2,1,0:T(1,128)S(1)} %get-tuple-element.196), channel_id=1, source_target_pairs={{0,16},{16,32},{32,48},{48,64},{64,80},{80,96},{96,112},{112,128},... | collective-permute-start | bytes 1544 | tf_op jit(solution)/shard_map/ppermute | solution.py:16
  63.8 20.8 %collective-permute-start.25 = (f32[4,1,32]{2,1,0:T(1,128)S(1)}, f32[4,1,32]{2,1,0:T(1,128)S(1)}, u32[]{:S(2)}, u32[]{:S(2)}) collective-permute-start(f32[4,1,32]{2,1,0:T(1,128)S(1)} %get-tuple-element.197), channel_id=1, source_target_pairs={{16,0},{32,16},{48,32},{64,48},{80,64},{96,80},{112,96},{128,112},... | collective-permute-start | bytes 1544 | tf_op jit(solution)/shard_map/ppermute | solution.py:19
  82.7 8.8 collective-permute-start.13
  91.6 67.6 %collective-permute-start.14 = (f32[8,10,1]{2,1,0:T(8,128)S(1)}, f32[8,10,1]{2,1,0:T(8,128)S(1)}, u32[]{:S(2)}, u32[]{:S(2)}) collective-permute-start(f32[8,10,1]{2,1,0:T(8,128)S(1)} %get-tuple-element.157), channel_id=1, source_target_pairs={{0,1},{1,2},{2,3},{3,4},{4,5},{5,6},{6,7},{7,8},{8,9},{9,10},{10,1... | collective-permute-start | bytes 968 | tf_op jit(solution)/shard_map/ppermute | solution.py:16
  94.3 64.9 %collective-permute-start.15 = (f32[8,10,1]{2,1,0:T(8,128)S(1)}, f32[8,10,1]{2,1,0:T(8,128)S(1)}, u32[]{:S(2)}, u32[]{:S(2)}) collective-permute-start(f32[8,10,1]{2,1,0:T(8,128)S(1)} %get-tuple-element.158), channel_id=1, source_target_pairs={{1,0},{2,1},{3,2},{4,3},{5,4},{6,5},{7,6},{8,7},{9,8},{10,9},{11,1... | collective-permute-start | bytes 968 | tf_op jit(solution)/shard_map/ppermute | solution.py:19
  95.8 6.6 collective-permute-start.2
  99.8 6.6 collective-permute-start.3
  117.1 10.9 %collective-permute-start.4 = (f32[2,16,1,128]{3,1,2,0:T(8,128)S(1)}, f32[2,16,1,128]{3,1,2,0:T(8,128)S(1)}, u32[]{:S(2)}, u32[]{:S(2)}) collective-permute-start(f32[2,16,1,128]{3,1,2,0:T(8,128)S(1)} %bitcast.199), channel_id=1, source_target_pairs={{0,16},{16,32},{32,48},{48,64},{64,80},{80,96},{96,112},{112,128},... | collective-permute-start | bytes 49160 | tf_op jit(solution)/shard_map/ppermute | solution.py:16
  126.1 9.0 collective-permute-start.5
  137.1 14.0 %collective-permute-start.7 = (f32[2,16,18,1]{3,1,2,0:T(8,128)S(1)}, f32[2,16,18,1]{3,1,2,0:T(8,128)S(1)}, u32[]{:S(2)}, u32[]{:S(2)}) collective-permute-start(f32[2,16,18,1]{3,1,2,0:T(8,128)S(1)} %get-tuple-element.75), channel_id=1, source_target_pairs={{1,0},{2,1},{3,2},{4,3},{5,4},{6,5},{7,6},{8,7},{9,8},{10,9},{11,1... | collective-permute-start | bytes 6920 | tf_op jit(solution)/shard_map/ppermute | solution.py:19
  151.7 23.3 %collective-permute-start.8 = (f32[2,16,1,128]{3,1,2,0:T(8,128)S(1)}, f32[2,16,1,128]{3,1,2,0:T(8,128)S(1)}, u32[]{:S(2)}, u32[]{:S(2)}) collective-permute-start(f32[2,16,1,128]{3,1,2,0:T(8,128)S(1)} %bitcast.189), channel_id=1, source_target_pairs={{0,16},{16,32},{32,48},{48,64},{64,80},{80,96},{96,112},{112,128},... | collective-permute-start | bytes 49160 | tf_op jit(solution)/shard_map/ppermute | solution.py:16
  173.1 9.0 collective-permute-start.9
  182.3 7.8 collective-permute-start.10
  186.4 10.3 %collective-permute-start.11 = (f32[2,16,18,1]{3,1,2,0:T(8,128)S(1)}, f32[2,16,18,1]{3,1,2,0:T(8,128)S(1)}, u32[]{:S(2)}, u32[]{:S(2)}) collective-permute-start(f32[2,16,18,1]{3,1,2,0:T(8,128)S(1)} %get-tuple-element.71), channel_id=1, source_target_pairs={{1,0},{2,1},{3,2},{4,3},{5,4},{6,5},{7,6},{8,7},{9,8},{10,9},{11,1... | collective-permute-start | bytes 6920 | tf_op jit(solution)/shard_map/ppermute | solution.py:19
  222.4 14.0 %collective-permute-start.16 = (f32[2,8,1,64]{3,2,1,0:T(1,128)S(1)}, f32[2,8,1,64]{3,2,1,0:T(1,128)S(1)}, u32[]{:S(2)}, u32[]{:S(2)}) collective-permute-start(f32[2,8,1,64]{3,2,1,0:T(1,128)S(1)} %get-tuple-element.155), channel_id=1, source_target_pairs={{0,16},{16,32},{32,48},{48,64},{64,80},{80,96},{96,112},{112,128},... | collective-permute-start | bytes 12296 | tf_op jit(solution)/shard_map/ppermute | solution.py:16
  230.9 8.9 collective-permute-start.17
  232.9 24.5 %collective-permute-start.26 = (f32[4,6,1]{2,1,0:T(8,128)S(1)}, f32[4,6,1]{2,1,0:T(8,128)S(1)}, u32[]{:S(2)}, u32[]{:S(2)}) collective-permute-start(f32[4,6,1]{2,1,0:T(8,128)S(1)} %get-tuple-element.192), channel_id=1, source_target_pairs={{0,1},{1,2},{2,3},{3,4},{4,5},{5,6},{6,7},{7,8},{8,9},{9,10},{10,1... | collective-permute-start | bytes 296 | tf_op jit(solution)/shard_map/ppermute | solution.py:16
  235.1 22.4 %collective-permute-start.27 = (f32[4,6,1]{2,1,0:T(8,128)S(1)}, f32[4,6,1]{2,1,0:T(8,128)S(1)}, u32[]{:S(2)}, u32[]{:S(2)}) collective-permute-start(f32[4,6,1]{2,1,0:T(8,128)S(1)} %get-tuple-element.193), channel_id=1, source_target_pairs={{1,0},{2,1},{3,2},{4,3},{5,4},{6,5},{7,6},{8,7},{9,8},{10,9},{11,1... | collective-permute-start | bytes 296 | tf_op jit(solution)/shard_map/ppermute | solution.py:19
  247.7 11.1 %collective-permute-start.20 = (f32[2,8,1,64]{3,2,1,0:T(1,128)S(1)}, f32[2,8,1,64]{3,2,1,0:T(1,128)S(1)}, u32[]{:S(2)}, u32[]{:S(2)}) collective-permute-start(f32[2,8,1,64]{3,2,1,0:T(1,128)S(1)} %get-tuple-element.150), channel_id=1, source_target_pairs={{0,16},{16,32},{32,48},{48,64},{64,80},{80,96},{96,112},{112,128},... | collective-permute-start | bytes 12296 | tf_op jit(solution)/shard_map/ppermute | solution.py:16
  255.5 8.9 collective-permute-start.21
  267.2 8.2 collective-permute-start.23
  284.2 8.8 collective-permute-start.29
  293.1 7.7 collective-permute-start.30
  308.8 8.8 collective-permute-start.33
  330.8 8.8 collective-permute-start.37
  354.3 8.9 collective-permute-start.41
  367.6 6.3 collective-permute-start.43
  377.9 8.9 collective-permute-start.45
  390.7 6.3 collective-permute-start.47
  406.3 9.0 collective-permute-start.49
  415.5 7.4 collective-permute-start.50
  419.3 11.5 %collective-permute-start.51 = (f32[2,16,18,1]{3,1,2,0:T(8,128)S(1)}, f32[2,16,18,1]{3,1,2,0:T(8,128)S(1)}, u32[]{:S(2)}, u32[]{:S(2)}) collective-permute-start(f32[2,16,18,1]{3,1,2,0:T(8,128)S(1)} %get-tuple-element.67), channel_id=1, source_target_pairs={{1,0},{2,1},{3,2},{4,3},{5,4},{6,5},{7,6},{8,7},{9,8},{10,9},{11,1... | collective-permute-start | bytes 6920 | tf_op jit(solution)/shard_map/ppermute | solution.py:19
  434.2 9.7 %collective-permute-start.53 = (f32[2,16,1,128]{3,1,2,0:T(8,128)S(1)}, f32[2,16,1,128]{3,1,2,0:T(8,128)S(1)}, u32[]{:S(2)}, u32[]{:S(2)}) collective-permute-start(f32[2,16,1,128]{3,1,2,0:T(8,128)S(1)} %bitcast.192), channel_id=1, source_target_pairs={{16,0},{32,16},{48,32},{64,48},{80,64},{96,80},{112,96},{128,112},... | collective-permute-start | bytes 49160 | tf_op jit(solution)/shard_map/ppermute | solution.py:19
  444.1 6.4 collective-permute-start.54
  446.9 10.6 %collective-permute-start.55 = (f32[2,16,18,1]{3,1,2,0:T(8,128)S(1)}, f32[2,16,18,1]{3,1,2,0:T(8,128)S(1)}, u32[]{:S(2)}, u32[]{:S(2)}) collective-permute-start(f32[2,16,18,1]{3,1,2,0:T(8,128)S(1)} %get-tuple-element.63), channel_id=1, source_target_pairs={{1,0},{2,1},{3,2},{4,3},{5,4},{6,5},{7,6},{8,7},{9,8},{10,9},{11,1... | collective-permute-start | bytes 6920 | tf_op jit(solution)/shard_map/ppermute | solution.py:19
  458.1 7.3 collective-permute-start.56
  463.5 9.5 %collective-permute-start.57 = (f32[2,16,1,128]{3,1,2,0:T(8,128)S(1)}, f32[2,16,1,128]{3,1,2,0:T(8,128)S(1)}, u32[]{:S(2)}, u32[]{:S(2)}) collective-permute-start(f32[2,16,1,128]{3,1,2,0:T(8,128)S(1)} %bitcast.193), channel_id=1, source_target_pairs={{16,0},{32,16},{48,32},{64,48},{80,64},{96,80},{112,96},{128,112},... | collective-permute-start | bytes 49160 | tf_op jit(solution)/shard_map/ppermute | solution.py:19
  475.3 11.3 %collective-permute-start.59 = (f32[2,16,18,1]{3,1,2,0:T(8,128)S(1)}, f32[2,16,18,1]{3,1,2,0:T(8,128)S(1)}, u32[]{:S(2)}, u32[]{:S(2)}) collective-permute-start(f32[2,16,18,1]{3,1,2,0:T(8,128)S(1)} %get-tuple-element.59), channel_id=1, source_target_pairs={{1,0},{2,1},{3,2},{4,3},{5,4},{6,5},{7,6},{8,7},{9,8},{10,9},{11,1... | collective-permute-start | bytes 6920 | tf_op jit(solution)/shard_map/ppermute | solution.py:19
  487.2 6.6 collective-permute-start.60
  491.9 9.6 %collective-permute-start.61 = (f32[2,16,1,128]{3,1,2,0:T(8,128)S(1)}, f32[2,16,1,128]{3,1,2,0:T(8,128)S(1)}, u32[]{:S(2)}, u32[]{:S(2)}) collective-permute-start(f32[2,16,1,128]{3,1,2,0:T(8,128)S(1)} %bitcast.194), channel_id=1, source_target_pairs={{16,0},{32,16},{48,32},{64,48},{80,64},{96,80},{112,96},{128,112},... | collective-permute-start | bytes 49160 | tf_op jit(solution)/shard_map/ppermute | solution.py:19
  503.8 11.3 %collective-permute-start.63 = (f32[2,16,18,1]{3,1,2,0:T(8,128)S(1)}, f32[2,16,18,1]{3,1,2,0:T(8,128)S(1)}, u32[]{:S(2)}, u32[]{:S(2)}) collective-permute-start(f32[2,16,18,1]{3,1,2,0:T(8,128)S(1)} %get-tuple-element.55), channel_id=1, source_target_pairs={{1,0},{2,1},{3,2},{4,3},{5,4},{6,5},{7,6},{8,7},{9,8},{10,9},{11,1... | collective-permute-start | bytes 6920 | tf_op jit(solution)/shard_map/ppermute | solution.py:19
  540.9 10.0 %collective-permute-start.64 = (f32[2,8,1,64]{3,2,1,0:T(1,128)S(1)}, f32[2,8,1,64]{3,2,1,0:T(1,128)S(1)}, u32[]{:S(2)}, u32[]{:S(2)}) collective-permute-start(f32[2,8,1,64]{3,2,1,0:T(1,128)S(1)} %get-tuple-element.144), channel_id=1, source_target_pairs={{0,16},{16,32},{32,48},{48,64},{64,80},{80,96},{96,112},{112,128},... | collective-permute-start | bytes 12296 | tf_op jit(solution)/shard_map/ppermute | solution.py:16
  549.0 8.9 collective-permute-start.65
  565.9 7.1 collective-permute-start.68
  571.0 9.0 collective-permute-start.69
  597.1 9.0 collective-permute-start.73
  618.9 9.5 %collective-permute-start.77 = (f32[2,4,1,32]{3,2,1,0:T(1,128)S(1)}, f32[2,4,1,32]{3,2,1,0:T(1,128)S(1)}, u32[]{:S(2)}, u32[]{:S(2)}) collective-permute-start(f32[2,4,1,32]{3,2,1,0:T(1,128)S(1)} %get-tuple-element.180), channel_id=1, source_target_pairs={{16,0},{32,16},{48,32},{64,48},{80,64},{96,80},{112,96},{128,112},... | collective-permute-start | bytes 3080 | tf_op jit(solution)/shard_map/ppermute | solution.py:19
  642.1 9.5 %collective-permute-start.81 = (f32[2,4,1,32]{3,2,1,0:T(1,128)S(1)}, f32[2,4,1,32]{3,2,1,0:T(1,128)S(1)}, u32[]{:S(2)}, u32[]{:S(2)}) collective-permute-start(f32[2,4,1,32]{3,2,1,0:T(1,128)S(1)} %get-tuple-element.178), channel_id=1, source_target_pairs={{16,0},{32,16},{48,32},{64,48},{80,64},{96,80},{112,96},{128,112},... | collective-permute-start | bytes 3080 | tf_op jit(solution)/shard_map/ppermute | solution.py:19
  666.5 9.5 %collective-permute-start.85 = (f32[2,8,1,64]{3,2,1,0:T(1,128)S(1)}, f32[2,8,1,64]{3,2,1,0:T(1,128)S(1)}, u32[]{:S(2)}, u32[]{:S(2)}) collective-permute-start(f32[2,8,1,64]{3,2,1,0:T(1,128)S(1)} %get-tuple-element.141), channel_id=1, source_target_pairs={{16,0},{32,16},{48,32},{64,48},{80,64},{96,80},{112,96},{128,112},... | collective-permute-start | bytes 12296 | tf_op jit(solution)/shard_map/ppermute | solution.py:19
  691.0 9.6 %collective-permute-start.89 = (f32[2,8,1,64]{3,2,1,0:T(1,128)S(1)}, f32[2,8,1,64]{3,2,1,0:T(1,128)S(1)}, u32[]{:S(2)}, u32[]{:S(2)}) collective-permute-start(f32[2,8,1,64]{3,2,1,0:T(1,128)S(1)} %get-tuple-element.139), channel_id=1, source_target_pairs={{16,0},{32,16},{48,32},{64,48},{80,64},{96,80},{112,96},{128,112},... | collective-permute-start | bytes 12296 | tf_op jit(solution)/shard_map/ppermute | solution.py:19
  720.4 9.7 %collective-permute-start.93 = (f32[2,16,1,128]{3,1,2,0:T(8,128)S(1)}, f32[2,16,1,128]{3,1,2,0:T(8,128)S(1)}, u32[]{:S(2)}, u32[]{:S(2)}) collective-permute-start(f32[2,16,1,128]{3,1,2,0:T(8,128)S(1)} %bitcast.195), channel_id=1, source_target_pairs={{16,0},{32,16},{48,32},{64,48},{80,64},{96,80},{112,96},{128,112},... | collective-permute-start | bytes 49160 | tf_op jit(solution)/shard_map/ppermute | solution.py:19
  730.2 7.2 collective-permute-start.94
  733.7 11.4 %collective-permute-start.95 = (f32[2,16,18,1]{3,1,2,0:T(8,128)S(1)}, f32[2,16,18,1]{3,1,2,0:T(8,128)S(1)}, u32[]{:S(2)}, u32[]{:S(2)}) collective-permute-start(f32[2,16,18,1]{3,1,2,0:T(8,128)S(1)} %get-tuple-element.51), channel_id=1, source_target_pairs={{1,0},{2,1},{3,2},{4,3},{5,4},{6,5},{7,6},{8,7},{9,8},{10,9},{11,1... | collective-permute-start | bytes 6920 | tf_op jit(solution)/shard_map/ppermute | solution.py:19
  748.4 9.9 %collective-permute-start.97 = (f32[2,16,1,128]{3,1,2,0:T(8,128)S(1)}, f32[2,16,1,128]{3,1,2,0:T(8,128)S(1)}, u32[]{:S(2)}, u32[]{:S(2)}) collective-permute-start(f32[2,16,1,128]{3,1,2,0:T(8,128)S(1)} %bitcast.196), channel_id=1, source_target_pairs={{16,0},{32,16},{48,32},{64,48},{80,64},{96,80},{112,96},{128,112},... | collective-permute-start | bytes 49160 | tf_op jit(solution)/shard_map/ppermute | solution.py:19
  758.4 6.3 collective-permute-start.98
  761.1 10.9 %collective-permute-start.99 = (f32[2,16,18,1]{3,1,2,0:T(8,128)S(1)}, f32[2,16,18,1]{3,1,2,0:T(8,128)S(1)}, u32[]{:S(2)}, u32[]{:S(2)}) collective-permute-start(f32[2,16,18,1]{3,1,2,0:T(8,128)S(1)} %get-tuple-element.47), channel_id=1, source_target_pairs={{1,0},{2,1},{3,2},{4,3},{5,4},{6,5},{7,6},{8,7},{9,8},{10,9},{11,1... | collective-permute-start | bytes 6920 | tf_op jit(solution)/shard_map/ppermute | solution.py:19
  772.6 6.1 collective-permute-start.100
  776.7 9.7 %collective-permute-start.101 = (f32[2,16,1,128]{3,1,2,0:T(8,128)S(1)}, f32[2,16,1,128]{3,1,2,0:T(8,128)S(1)}, u32[]{:S(2)}, u32[]{:S(2)}) collective-permute-start(f32[2,16,1,128]{3,1,2,0:T(8,128)S(1)} %bitcast.197), channel_id=1, source_target_pairs={{16,0},{32,16},{48,32},{64,48},{80,64},{96,80},{112,96},{128,112},... | collective-permute-start | bytes 49160 | tf_op jit(solution)/shard_map/ppermute | solution.py:19
  788.8 11.3 %collective-permute-start.103 = (f32[2,16,18,1]{3,1,2,0:T(8,128)S(1)}, f32[2,16,18,1]{3,1,2,0:T(8,128)S(1)}, u32[]{:S(2)}, u32[]{:S(2)}) collective-permute-start(f32[2,16,18,1]{3,1,2,0:T(8,128)S(1)} %get-tuple-element.43), channel_id=1, source_target_pairs={{1,0},{2,1},{3,2},{4,3},{5,4},{6,5},{7,6},{8,7},{9,8},{10,9},{11,1... | collective-permute-start | bytes 6920 | tf_op jit(solution)/shard_map/ppermute | solution.py:19
  804.8 9.3 %collective-permute-start.105 = (f32[2,16,1,128]{3,1,2,0:T(8,128)S(1)}, f32[2,16,1,128]{3,1,2,0:T(8,128)S(1)}, u32[]{:S(2)}, u32[]{:S(2)}) collective-permute-start(f32[2,16,1,128]{3,1,2,0:T(8,128)S(1)} %bitcast.198), channel_id=1, source_target_pairs={{16,0},{32,16},{48,32},{64,48},{80,64},{96,80},{112,96},{128,112},... | collective-permute-start | bytes 49160 | tf_op jit(solution)/shard_map/ppermute | solution.py:19
  816.5 11.6 %collective-permute-start.107 = (f32[2,16,18,1]{3,1,2,0:T(8,128)S(1)}, f32[2,16,18,1]{3,1,2,0:T(8,128)S(1)}, u32[]{:S(2)}, u32[]{:S(2)}) collective-permute-start(f32[2,16,18,1]{3,1,2,0:T(8,128)S(1)} %get-tuple-element.39), channel_id=1, source_target_pairs={{1,0},{2,1},{3,2},{4,3},{5,4},{6,5},{7,6},{8,7},{9,8},{10,9},{11,1... | collective-permute-start | bytes 6920 | tf_op jit(solution)/shard_map/ppermute | solution.py:19
  (72 other events, 1491.6 us)
where the time goes:
time: 920 us; the launch traced here: 907 us
  waiting for transfers between devices  341 us (37%)
  starting transfers between devices  304 us (33%)
  local copies, waits for them, and re-layouts  93.2 us (10%)
  other arithmetic  88.4 us (10%)
  blocking collectives  77.2 us (8%)
    ppermute x54, waiting for transfers between devices, with_halo(): lax.ppermute(lax.slice_in_dim(block, 0, width, axis=dim), axis, backward)  316 us
    ppermute x54, starting transfers between devices, with_halo(): lax.ppermute(lax.slice_in_dim(block, block.shape[dim] - width, None, axis...  216 us
    ppermute x54, starting transfers between devices, with_halo(): lax.ppermute(lax.slice_in_dim(block, 0, width, axis=dim), axis, backward)  87.9 us
    psum x1, blocking collectives, shards(): lax.psum((local_rz, jnp.sum(direction * image, axis=(1, 2, 3))), ('gx', '...  77.2 us
    reshape x8, local copies, waits for them, and re-layouts, coarsen_sum(): vector.reshape(shape[:-3] + (shape[-3] // 2, 2, shape[-2] // 2, 2, shape[...  72.4 us
    reduce_sum x10, other arithmetic, coarsen_sum(): return jnp.sum(blocks, axis=(-5, -3, -1))  28.4 us
    ppermute x54, waiting for transfers between devices, with_halo(): lax.ppermute(lax.slice_in_dim(block, block.shape[dim] - width, None, axis...  24.8 us
  transfers between devices with their start and end apart: 108, of which 67 were waited for; matrix products, arithmetic and copies ran while one was open for 7% of the time, Pallas kernels for 0%

commit v1 on v0

v1 whole, which is shorter than its diff:
```python
import functools
import math

import jax
import jax.numpy as jnp
from jax import lax
from jax.experimental import pallas as pl
from jax.experimental.pallas import tpu as pltpu
from jax.sharding import PartitionSpec as P

F32 = jnp.float32
NZ = 16
ROWS = 16
COLS = 128
WIDE = 256
HALF = 64
EXT0 = 32
EXT1 = 40
EXT2 = 24


def cheb_weights(degree, lower_end, upper_end):
    middle = 0.5 * (upper_end + lower_end)
    radius = 0.5 * (upper_end - lower_end)
    return [
        1.0 / (middle + radius * math.cos(math.pi * (2 * index_k + 1) / (2 * degree)))
        for index_k in range(degree)
    ]


FINE = cheb_weights(2, 0.3, 2.0)
COARSE = cheb_weights(4, 0.1, 2.0)


def loop(count, body):
    def step(index, carry):
        body(index)
        return carry

    lax.fori_loop(0, count, step, 0)


def lanes(rows, width):
    return lax.broadcasted_iota(jnp.int32, (rows, width), 1)


def sublanes(rows, width):
    return lax.broadcasted_iota(jnp.int32, (rows, width), 0)


def lane_sum(value, step):
    width = value.shape[1]
    first = (lanes(*value.shape) // step) % 2 == 0
    return value + jnp.where(first, pltpu.roll(value, width - step, 1), pltpu.roll(value, step, 1))


def across(value, step):
    rows, width = value.shape
    return (
        pltpu.roll(value, 1, 0)
        + pltpu.roll(value, rows - 1, 0)
        + pltpu.roll(value, step, 1)
        + pltpu.roll(value, width - step, 1)
    )


def row_pairs(buffer, value):
    rows = value.shape[0]
    parts = []
    for half in range(2):
        buffer[half, 0:rows, :] = value[:, half * COLS : (half + 1) * COLS]
        parts.append(
            buffer[half, pl.ds(0, rows // 2, stride=2), :] + buffer[half, pl.ds(1, rows // 2, stride=2), :]
        )
    return jnp.concatenate(parts, axis=1)


def row_repeat(buffer, value):
    rows = value.shape[0]
    parts = []
    for half in range(2):
        part = value[:, half * COLS : (half + 1) * COLS]
        buffer[half, pl.ds(0, rows, stride=2), :] = part
        buffer[half, pl.ds(1, rows, stride=2), :] = part
        parts.append(buffer[half, 0 : 2 * rows, :])
    return jnp.concatenate(parts, axis=1)


def pick(table_row, index):
    rows, width = index.shape
    table = jnp.broadcast_to(table_row, (rows, COLS))
    parts = [
        jnp.take_along_axis(table, index[:, start : start + COLS], axis=1)
        for start in range(0, width, COLS)
    ]
    return parts[0] if len(parts) == 1 else jnp.concatenate(parts, axis=1)


def pack_halves(first, second):
    left = lanes(*first.shape) < HALF
    low = jnp.where(left, first, pltpu.roll(second, HALF, 1))
    high = jnp.where(left, pltpu.roll(first, HALF, 1), second)
    return low, high


def unpack_halves(from_right, from_left):
    left = lanes(*from_right.shape) < HALF
    first = jnp.where(left, from_right, pltpu.roll(from_left, HALF, 1))
    second = jnp.where(left, pltpu.roll(from_right, HALF, 1), from_left)
    return first, second


def pack_sea(fields):
    rows, width = fields[0].shape
    even_lane = lanes(rows, width) % 2 == 0
    even_row = sublanes(rows, width) % 2 == 0
    pairs = [
        jnp.where(even_lane, fields[i], pltpu.roll(fields[i + 1], 1, 1)) for i in (0, 2)
    ]
    return jnp.where(even_row, pairs[0], pltpu.roll(pairs[1], 1, 0))


def unpack_sea(packed):
    rows, width = packed.shape
    spot = (lanes(rows, width) % 2 == 0) & (sublanes(rows, width) % 2 == 0)
    fields = []
    for pair in (packed, pltpu.roll(packed, rows - 1, 0)):
        for field in (pair, pltpu.roll(pair, width - 1, 1)):
            fields.append(jnp.where(spot, field, 1.0))
    return fields


def columns_kernel(rhs, classes, sea, to_left, to_right):
    def pair(z):
        low, high = pack_halves(rhs[0, z], rhs[1, z])
        to_left[z] = low
        to_right[z] = high

    loop(NZ, pair)

    def class_pair(z):
        low, high = pack_halves(classes[z].astype(F32), classes[z + 8].astype(F32))
        to_left[16 + z] = low
        to_right[16 + z] = high

    loop(8, class_pair)
    for j in range(2):
        quads = [
            pack_sea([sea[8 * j + 4 * q + i].astype(F32) for i in range(4)]) for q in range(2)
        ]
        low, high = pack_halves(quads[0], quads[1])
        to_left[24 + j] = low
        to_right[24 + j] = high


MSG_Y = 26
MSG_X = 54


def rows_kernel(place, rhs, classes, sea, from_left, from_right, table, r_out, c_out, s_out, msg_x, msg_o, row_c, row_s):
    core = place[0]
    gy = place[2]
    left = lanes(ROWS, COLS) < HALF
    inside = jnp.where(
        left,
        jnp.where(gy < place[4] - 1, 1.0, 0.0),
        jnp.where(gy > 0, 1.0, 0.0),
    )

    def rhs_step(z):
        halo = unpack_halves(from_right[z], from_left[z])
        for i in range(2):
            r_out[z, i] = jnp.concatenate([rhs[i, z], halo[i]], axis=1)

    loop(NZ, rhs_step)

    def class_step(z):
        first, second = unpack_halves(from_right[16 + z], from_left[16 + z])
        c_out[z] = jnp.concatenate([classes[z].astype(F32), first], axis=1)
        c_out[z + 8] = jnp.concatenate([classes[z + 8].astype(F32), second], axis=1)

    loop(8, class_step)
    for j in range(2):
        quads = unpack_halves(from_right[24 + j], from_left[24 + j])
        for q in range(2):
            for i, field in enumerate(unpack_sea(quads[q])):
                z = 8 * j + 4 * q + i
                s_out[z] = jnp.concatenate([sea[z].astype(F32), field * inside], axis=1)

    for message, start, edge in (
        (msg_x, 8 * (1 - core), 8 - (1 - core)),
        (msg_o, 8 * core, 8 - core),
    ):
        start = pl.multiple_of(start, 8)

        def copy(z, message=message, start=start, edge=edge):
            for i in range(2):
                message[2 * z + i] = r_out[z, i, pl.ds(start, 8), :]
            message[32 + z] = c_out[z, pl.ds(start, 8), :]
            row_c[pl.ds(z, 1), :] = c_out[z, pl.ds(edge, 1), :]
            row_s[pl.ds(z, 1), :] = s_out[z, pl.ds(edge, 1), :]

        loop(NZ, copy)

        def copy_sea(j, message=message, start=start):
            message[48 + j] = pack_sea([s_out[4 * j + i, pl.ds(start, 8), :] for i in range(4)])

        loop(4, copy_sea)
        edge_g = pick(table[0:1], row_c[...].astype(jnp.int32)) * row_s[...]
        message[52] = edge_g[0:8]
        message[53] = edge_g[8:16]


def material_kernel(c_in, s_in, table, g_out, h_out, k_out, packed, buffer):
    def fields(z):
        index = c_in[z].astype(jnp.int32)
        sea = s_in[z]
        g = pick(table[0:1], index) * sea
        h = pick(table[1:2], index) * sea
        k = pick(table[2:3], index) * sea + (1.0 - sea)
        g_out[z] = g
        h_out[z] = h
        k_out[z] = k
        return g * g, h * h, k

    even = lanes(8, WIDE) % 2 == 0

    def coarse(pair):
        first = fields(2 * pair)
        second = fields(2 * pair + 1)
        return [
            lane_sum(row_pairs(buffer.at[i], first[i] + second[i]), 1) for i in range(3)
        ]

    def step(j):
        near = coarse(j)
        far = coarse(j + 4)
        packed[j] = jnp.where(even, 0.125 * near[0], 0.125 * near[1])
        packed[j + 4] = jnp.where(even, 0.125 * far[0], 0.125 * far[1])
        packed[j + 8] = jnp.where(even, near[2], far[2])

    loop(4, step)


def unpack_lanes(packed):
    even = lanes(*packed.shape) % 2 == 0
    width = packed.shape[1]
    return (
        jnp.where(even, packed, pltpu.roll(packed, 1, 1)),
        jnp.where(even, pltpu.roll(packed, width - 1, 1), packed),
    )


class Level:
    def __init__(self, depth, step, g, h, inverse, diagonal=None):
        self.depth, self.step = depth, step
        self.g, self.h, self.inverse, self.diagonal = g, h, inverse, diagonal

    def couple(self, x, z, i):
        horizontal = self.g[z] * across(self.g[z] * x[z + 1, i], self.step)
        vertical = self.h[z + 1] * (self.h[z] * x[z, i] + self.h[z + 2] * x[z + 2, i])
        return horizontal + vertical

    def first(self, x, r, weight):
        def body(z):
            scaled = weight * self.inverse[z]
            for i in range(2):
                x[z + 1, i] = scaled * r[z, i]

        loop(self.depth, body)

    def update(self, new, x, r, weight):
        def body(z):
            scaled = weight * self.inverse[z]
            for i in range(2):
                new[z + 1, i] = (1.0 - weight) * x[z + 1, i] + scaled * (r[z, i] + self.couple(x, z, i))

        loop(self.depth, body)

    def defect(self, x, r, z, i):
        return r[z, i] - self.diagonal[z] * x[z + 1, i] + self.couple(x, z, i)

    def diagonal_of(self, k, z):
        horizontal = self.g[z] * across(self.g[z], self.step)
        vertical = self.h[z + 1] * (self.h[z] + self.h[z + 2])
        return k + horizontal + vertical


def clear_ends(*refs):
    for ref in refs:
        ref[0] = jnp.zeros(ref.shape[1:], ref.dtype)
        ref[ref.shape[0] - 1] = jnp.zeros(ref.shape[1:], ref.dtype)


def fine_restrict(level, x, r, buffer, out):
    even = lanes(8, WIDE) % 2 == 0

    def body(pair):
        sums = []
        for i in range(2):
            total = level.defect(x, r, 2 * pair, i) + level.defect(x, r, 2 * pair + 1, i)
            sums.append(lane_sum(row_pairs(buffer.at[i], total[8:24]), 1))
        out[pair] = jnp.where(even, sums[0], sums[1])

    loop(NZ // 2, body)


def down_kernel(place, r_own, g_own, h_own, k_own, from_x, from_o, table, r, g, h, d, inverse, xp, r1, xa, ka, edges, buffer):
    core = place[0]
    gx = place[1]
    gy = place[2]
    open_side = jnp.where((gx > 0) & (gx < place[3] - 1), 1.0, 0.0)
    lane = lanes(8, WIDE)
    ends = jnp.where(
        lane < COLS,
        1.0,
        jnp.where(lane < COLS + HALF, jnp.where(gy < place[4] - 1, 1.0, 0.0), jnp.where(gy > 0, 1.0, 0.0)),
    )
    clear_ends(h, xp, xa)

    def own(z):
        for i in range(2):
            r[z, i, 8:24, :] = r_own[z, i]
        g[z, 8:24, :] = g_own[z]
        h[z + 1, 8:24, :] = h_own[z]
        ka[z, 8:24, :] = k_own[z]

    loop(NZ, own)
    for message, start, scale, slot in ((from_x, 24 * (1 - core), 1.0, 1 - core), (from_o, 24 * core, open_side, core)):
        start = pl.multiple_of(start, 8)

        def halo(j, message=message, start=start, scale=scale):
            for q, sea in enumerate(unpack_sea(message[48 + j])):
                z = 4 * j + q
                sea = sea * (scale * ends)
                index = message[32 + z].astype(jnp.int32)
                g[z, pl.ds(start, 8), :] = pick(table[0:1], index) * sea
                h[z + 1, pl.ds(start, 8), :] = pick(table[1:2], index) * sea
                ka[z, pl.ds(start, 8), :] = pick(table[2:3], index) * sea + (1.0 - sea)
                for i in range(2):
                    r[z, i, pl.ds(start, 8), :] = message[2 * z + i]

        loop(4, halo)
        edges[slot, 0:8, :] = message[52] * scale
        edges[slot, 8:16, :] = message[53] * scale

    level = Level(NZ, 1, g, h, inverse, d)
    row = sublanes(EXT0, WIDE)

    def diagonals(z):
        here = g[z]
        below = jnp.where(row == 0, edges[0, pl.ds(z, 1), :], pltpu.roll(here, 1, 0))
        above = jnp.where(row == EXT0 - 1, edges[1, pl.ds(z, 1), :], pltpu.roll(here, EXT0 - 1, 0))
        beside = pltpu.roll(here, 1, 1) + pltpu.roll(here, WIDE - 1, 1)
        total = ka[z] + here * (below + above + beside) + h[z + 1] * (h[z] + h[z + 2])
        d[z] = total
        inverse[z] = 1.0 / total

    loop(NZ, diagonals)
    level.first(xa, r, FINE[0])
    level.update(xp, xa, r, FINE[1])
    fine_restrict(level, xp, r, buffer, r1)


def gather_rows(core, out_store, own, partner, odd, second, count):
    starts = (16, 24 - 16 * core, 8 + 16 * core, 32 * core, 32 - 32 * core)

    def body(j):
        tiles = (own[j], partner[j], odd[j], odd[count + j], second[j])
        for start, tile in zip(starts, tiles):
            start = start if isinstance(start, int) else pl.multiple_of(start, 8)
            out_store(j, start, tile)

    return body


def coarse_coefficients(core, pieces, g1, h1, d1, i1, g2, h2, i2, w1, k1, u1, k2, buffer):
    clear_ends(h1, h2)

    def store(j, start, tile):
        first, second = unpack_lanes(tile)
        w1[j, pl.ds(start, 8), :] = first
        u1[j, pl.ds(start, 8), :] = second

    def store_k(j, start, tile):
        first, second = unpack_lanes(tile)
        k1[j, pl.ds(start, 8), :] = jnp.where(first == 0.0, 1.0, first)
        k1[j + 4, pl.ds(start, 8), :] = jnp.where(second == 0.0, 1.0, second)

    own, partner, odd, far = pieces
    starts = (16, 24 - 16 * core, 8 + 16 * core, 32 * core, 32 - 32 * core)
    starts = [s if isinstance(s, int) else pl.multiple_of(s, 8) for s in starts]

    def crosswise(j):
        for start, tile in zip(starts, (own[j], partner[j], odd[j], odd[12 + j], far[j])):
            store(j, start, tile)

    loop(8, crosswise)

    def masses(j):
        tiles = (own[8 + j], partner[8 + j], odd[8 + j], odd[20 + j], far[8 + j])
        for start, tile in zip(starts, tiles):
            store_k(j, start, tile)

    loop(4, masses)

    def roots(z):
        g1[z] = 2.0 * jnp.sqrt(w1[z])
        h1[z + 1] = 2.0 * jnp.sqrt(u1[z])

    loop(8, roots)
    one = Level(8, 2, g1, h1, i1, d1)

    def diagonals(z):
        total = one.diagonal_of(k1[z], z)
        d1[z] = total
        i1[z] = 1.0 / total

    loop(8, diagonals)

    def coarser(z):
        sums = [
            lane_sum(row_pairs(buffer.at[i], field[2 * z] + field[2 * z + 1]), 2)
            for i, field in enumerate((w1, u1, k1))
        ]
        blank = jnp.zeros((4, WIDE), F32)
        g2[z] = jnp.concatenate([2.0 * jnp.sqrt(0.125 * sums[0]), blank], axis=0)
        h2[z + 1] = jnp.concatenate([2.0 * jnp.sqrt(0.125 * sums[1]), blank], axis=0)
        k2[z] = jnp.concatenate([sums[2], blank + 1.0], axis=0)

    loop(4, coarser)
    two = Level(4, 4, g2, h2, i2)

    def diagonals_two(z):
        i2[z] = 1.0 / two.diagonal_of(k2[z], z)

    loop(4, diagonals_two)


def coarse_solve(core, one, two, pieces, r1, xa1, xb1, r2, xa2, xb2, buffer):
    own, partner, odd, far = pieces
    clear_ends(xa1, xb1, xa2, xb2)
    starts = (16, 24 - 16 * core, 8 + 16 * core, 32 * core, 32 - 32 * core)
    starts = [s if isinstance(s, int) else pl.multiple_of(s, 8) for s in starts]

    def assemble(z):
        tiles = (own[z], partner[z], odd[z], odd[8 + z], far[z])
        for start, tile in zip(starts, tiles):
            for i, field in enumerate(unpack_lanes(tile)):
                r1[z, i, pl.ds(start, 8), :] = field

    loop(8, assemble)
    one.first(xa1, r1, FINE[0])
    one.update(xb1, xa1, r1, FINE[1])

    def restrict(z):
        for i in range(2):
            total = one.defect(xb1, r1, 2 * z, i) + one.defect(xb1, r1, 2 * z + 1, i)
            sums = lane_sum(row_pairs(buffer.at[i], total), 2)
            r2[z, i] = jnp.concatenate([sums, jnp.zeros((4, WIDE), F32)], axis=0)

    loop(4, restrict)
    two.first(xa2, r2, COARSE[0])
    two.update(xb2, xa2, r2, COARSE[1])
    two.update(xa2, xb2, r2, COARSE[2])
    two.update(xb2, xa2, r2, COARSE[3])

    def prolong(z):
        for i in range(2):
            fine = row_repeat(buffer.at[i], xb2[z + 1, i, 0:20, :])
            for half in range(2):
                xa1[2 * z + half + 1, i] = xb1[2 * z + half + 1, i] + fine

    loop(4, prolong)
    one.update(xb1, xa1, r1, FINE[0])
    one.update(xa1, xb1, r1, FINE[1])


def fine_correct(level, out, xp, c1, buffer):
    def body(pair):
        for i in range(2):
            fine = row_repeat(buffer.at[i], c1[pair + 1, i, 12:28, :])
            for half in range(2):
                out[2 * pair + half + 1, i] = xp[2 * pair + half + 1, i] + fine

    loop(NZ // 2, body)


def middle_kernel(
    place, r, g, h, d, inverse, xp, own, partner, odd, far, m_own, m_partner, m_odd, m_far,
    z_out, xp_out, r1_out, g1, h1, d1, i1, g2, h2, i2,
    xa, xb, r1, xa1, xb1, r2, xa2, xb2, w1, k1, u1, k2, buffer,
):
    core = place[0]
    coarse_coefficients(
        core, (m_own, m_partner, m_odd, m_far), g1, h1, d1, i1, g2, h2, i2, w1, k1, u1, k2, buffer
    )
    zero = Level(NZ, 1, g, h, inverse, d)
    one = Level(8, 2, g1, h1, i1, d1)
    two = Level(4, 4, g2, h2, i2)
    coarse_solve(core, one, two, (own, partner, odd, far), r1, xa1, xb1, r2, xa2, xb2, buffer)
    clear_ends(xa, xb, xp_out)
    fine_correct(zero, xa, xp, xa1, buffer)
    zero.update(xb, xa, r, FINE[0])

    def last(z):
        scaled = FINE[1] * inverse[z]
        for i in range(2):
            z_out[z, i] = (1.0 - FINE[1]) * xb[z + 1, i] + scaled * (r[z, i] + zero.couple(xb, z, i))

    loop(NZ, last)
    zero.first(xa, z_out, FINE[0])
    zero.update(xp_out, xa, z_out, FINE[1])
    fine_restrict(zero, xp_out, z_out, buffer, r1_out)


def last_kernel(
    place, rhs, r, g, h, d, inverse, xp, own, partner, odd, far, g1, h1, d1, i1, g2, h2, i2,
    direction, image, sums,
    xa, xb, r1, xa1, xb1, r2, xa2, xb2, totals, buffer,
):
    core = place[0]
    zero = Level(NZ, 1, g, h, inverse, d)
    one = Level(8, 2, g1, h1, i1, d1)
    two = Level(4, 4, g2, h2, i2)
    coarse_solve(core, one, two, (own, partner, odd, far), r1, xa1, xb1, r2, xa2, xb2, buffer)
    clear_ends(xa, xb)
    fine_correct(zero, xa, xp, xa1, buffer)
    zero.update(xb, xa, r, FINE[0])
    zero.update(xa, xb, r, FINE[1])

    def first_image(z):
        for i in range(2):
            xb[z + 1, i] = d[z] * xa[z + 1, i] - zero.couple(xa, z, i)

    loop(NZ, first_image)
    totals[...] = jnp.zeros(totals.shape, F32)

    def second_image(z):
        for i in range(2):
            field = xa[z + 1, i, 8:24, 0:COLS]
            value = (d[z] * xb[z + 1, i] - zero.couple(xb, z, i))[8:24, 0:COLS]
            direction[i, z] = field
            image[i, z] = value
            totals[i] += rhs[i, z] * field
            totals[2 + i] += field * value

    loop(NZ, second_image)
    row = sublanes(8, COLS)
    lane = lanes(8, COLS)
    line = jnp.zeros((8, COLS), F32)
    for i in range(4):
        line = jnp.where(lane == i, jnp.sum(totals[i]), line)

    def spread(j):
        sums[pl.ds(pl.multiple_of(8 * j, 8), 8), :] = line

    loop(sums.shape[0] // 8, spread)


def scale_kernel(rhs, direction, image, sums, solution_field, residual):
    total = jnp.sum(sums[...], axis=0, keepdims=True)
    lane = lanes(1, COLS)
    parts = [jnp.sum(jnp.where(lane == i, total, 0.0), axis=1, keepdims=True) for i in range(4)]
    for i in range(2):
        alpha = parts[i] / parts[2 + i]

        def body(z, i=i, alpha=alpha):
            solution_field[i, z] = alpha * direction[i, z]
            residual[i, z] = rhs[i, z] - alpha * image[i, z]

        loop(NZ, body)


def call(kernel, operands, outs, scratch=(), place=True):
    vmem = pl.BlockSpec(memory_space=pltpu.VMEM)
    specs = [vmem] * len(operands)
    if place:
        specs[0] = pl.BlockSpec(memory_space=pltpu.SMEM)
    return pl.pallas_call(
        kernel,
        out_shape=[jax.ShapeDtypeStruct(shape, F32) for shape in outs],
        in_specs=specs,
        out_specs=[vmem] * len(outs),
        scratch_shapes=[pltpu.VMEM(shape, F32) for shape in scratch],
        compiler_params=pltpu.CompilerParams(vmem_limit_bytes=48 * 1024 * 1024),
    )(*operands)


FIELD0 = (NZ, 2, EXT0, WIDE)
PADDED0 = (NZ + 2, 2, EXT0, WIDE)
PADDED1 = (10, 2, EXT1, WIDE)
PADDED2 = (6, 2, EXT2, WIDE)
BUFFER = (3, 2, EXT1, COLS)
COARSE_SCRATCH = [(8, 2, EXT1, WIDE), PADDED1, PADDED1, (4, 2, EXT2, WIDE), PADDED2, PADDED2]


def shards(count_x, count_y, right_side, classes, sea_mask, kappa_table, cross_table, vertical_table):
    gx = lax.axis_index("gx")
    gy = lax.axis_index("gy")
    place = jnp.stack([gx % 2, gx, gy, jnp.int32(count_x), jnp.int32(count_y)]).astype(jnp.int32)
    table = jnp.stack([jnp.sqrt(cross_table), jnp.sqrt(vertical_table), kappa_table])
    table = jnp.pad(table, ((0, 5), (0, COLS - table.shape[1])))

    pairs_on_chip = [(i, i ^ 1) for i in range(count_x)]
    pairs_across = [(i, i + 1 if i % 2 else i - 1) for i in range(1, count_x - 1)]

    def on_chip(value):
        return lax.ppermute(value, "gx", pairs_on_chip)

    def across_chips(value):
        return lax.ppermute(value, "gx", pairs_across)

    def three_steps(own):
        partner = on_chip(own)
        odd = across_chips(jnp.concatenate([own, partner], axis=0))
        far = on_chip(odd[: own.shape[0]])
        return own, partner, odd, far

    to_left, to_right = call(
        columns_kernel, (right_side, classes, sea_mask), [(MSG_Y, ROWS, COLS)] * 2, place=False
    )
    forward = [(i, i + 1) for i in range(count_y - 1)]
    backward = [(i + 1, i) for i in range(count_y - 1)]
    from_left = lax.ppermute(to_right, "gy", forward)
    from_right = lax.ppermute(to_left, "gy", backward)

    r_own, c_own, s_own, msg_x, msg_o = call(
        rows_kernel,
        (place, right_side, classes, sea_mask, from_left, from_right, table),
        [(NZ, 2, ROWS, WIDE), (NZ, ROWS, WIDE), (NZ, ROWS, WIDE), (MSG_X, 8, WIDE), (MSG_X, 8, WIDE)],
        [(NZ, WIDE), (NZ, WIDE)],
    )
    from_o = across_chips(msg_o)
    from_x = on_chip(msg_x)
    g_own, h_own, k_own, packed = call(
        material_kernel,
        (c_own, s_own, table),
        [(NZ, ROWS, WIDE)] * 3 + [(12, 8, WIDE)],
        [BUFFER],
        place=False,
    )
    material = three_steps(packed)
    r, g, h, d, inverse, xp, r1 = call(
        down_kernel,
        (place, r_own, g_own, h_own, k_own, from_x, from_o, table),
        [FIELD0, (NZ, EXT0, WIDE), (NZ + 2, EXT0, WIDE), (NZ, EXT0, WIDE), (NZ, EXT0, WIDE), PADDED0, (8, 8, WIDE)],
        [PADDED0, (NZ, EXT0, WIDE), (2, NZ, WIDE), BUFFER],
    )
    one = [(8, EXT1, WIDE), (10, EXT1, WIDE), (8, EXT1, WIDE), (8, EXT1, WIDE)]
    two = [(4, EXT2, WIDE), (6, EXT2, WIDE), (4, EXT2, WIDE)]
    r, xp, r1, *coarse = call(
        middle_kernel,
        (place, r, g, h, d, inverse, xp, *three_steps(r1), *material),
        [FIELD0, PADDED0, (8, 8, WIDE), *one, *two],
        [PADDED0, PADDED0, *COARSE_SCRATCH, one[0], one[0], one[0], two[0], BUFFER],
    )
    count = count_x * count_y
    direction, image, sums = call(
        last_kernel,
        (place, right_side, r, g, h, d, inverse, xp, *three_steps(r1), *coarse),
        [(2, NZ, ROWS, COLS)] * 2 + [(count, COLS)],
        [PADDED0, PADDED0, *COARSE_SCRATCH, (4, ROWS, COLS), BUFFER],
    )
    sums = lax.all_to_all(sums.reshape(count, 1, COLS), ("gx", "gy"), 0, 0).reshape(count, COLS)
    return tuple(
        call(
            scale_kernel,
            (right_side, direction, image, sums),
            [(2, NZ, ROWS, COLS)] * 2,
            place=False,
        )
    )


def solution(mesh):
    return jax.shard_map(
        functools.partial(shards, mesh.shape["gx"], mesh.shape["gy"]),
        mesh=mesh,
        in_specs=(
            P(None, None, "gx", "gy"),
            P(None, "gx", "gy"),
            P(None, "gx", "gy"),
            P(),
            P(),
            P(),
        ),
        out_specs=(P(None, None, "gx", "gy"), P(None, None, "gx", "gy")),
        check_vma=False,
    )
```

time: 920 us -> 166 us (0.18); the launches traced: 907 us -> 166 us
  waiting for transfers between devices: 341 us -> 43.4 us
  starting transfers between devices: 304 us -> 37 us
  other arithmetic: 88.4 us -> 0.78 us
  local copies, waits for them, and re-layouts: 93.2 us -> 7.21 us
  blocking collectives: 77.2 us -> 26.5 us
  Pallas kernels: 0 us -> 50.1 us
    ppermute x108 -> x13, waiting for transfers between devices: 341 us -> 43.4 us  [the longest x4 29.6 us: across_chips(): return lax.ppermute(value, 'gx', pairs_across)]
    ppermute x108 -> x13, starting transfers between devices: 304 us -> 37 us  [the longest x4 30.4 us: across_chips(): return lax.ppermute(value, 'gx', pairs_across)]
    reshape x16 -> x0, local copies, waits for them, and re-layouts: 78.9 us -> none  [the longest x8 72.4 us: coarsen_sum(): vector.reshape(shape[:-3] + (shape[-3] // 2, 2, shape[-2] // 2, 2, shape[...]
    psum x1 -> x0, blocking collectives: 77.2 us -> none  [shards(): lax.psum((local_rz, jnp.sum(direction * image, axis=(1, 2, 3))), ('gx', '...]
    pallas_call x0 -> x7, Pallas kernels: none -> 50.1 us  [call(): pl.pallas_call(kernel, out_shape=[jax.ShapeDtypeStruct(shape, F32) for sh...]
    reduce_sum x11 -> x0, other arithmetic: 29 us -> none  [the longest x10 28.4 us: coarsen_sum(): return jnp.sum(blocks, axis=(-5, -3, -1))]
    all_to_all x0 -> x1, blocking collectives: none -> 26.5 us  [shards(): lax.all_to_all(sums.reshape(count, 1, COLS), ('gx', 'gy'), 0, 0)]
    add x22 -> x0, other arithmetic: 25.4 us -> none  [the longest x17 11.2 us: smooth_pass(): approx = approx + weight * (source - operator(approx)) / coeffs[3]]
  transfers between devices with their start and end apart: 108 -> 13, of which waited for: 67 -> 9; matrix products, arithmetic and copies ran while one was open for 7% -> 1% of each run, Pallas kernels for 0% -> 5%
where the time goes in v1:
time: 166 us
  Pallas kernels  50.1 us (30%)
  waiting for transfers between devices  43.4 us (26%)
  starting transfers between devices  37 us (22%)
  blocking collectives  26.5 us (16%)
  local copies, waits for them, and re-layouts  7.21 us (4%)
    pallas_call x7, Pallas kernels, call(): pl.pallas_call(kernel, out_shape=[jax.ShapeDtypeStruct(shape, F32) for sh...  50.1 us
    ppermute x4, starting transfers between devices, across_chips(): return lax.ppermute(value, 'gx', pairs_across)  30.4 us
    ppermute x4, waiting for transfers between devices, across_chips(): return lax.ppermute(value, 'gx', pairs_across)  29.6 us
    all_to_all x1, blocking collectives, shards(): lax.all_to_all(sums.reshape(count, 1, COLS), ('gx', 'gy'), 0, 0)  26.5 us
    ppermute x1, waiting for transfers between devices, shards(): from_right = lax.ppermute(to_left, 'gy', backward)  9.07 us
    unnamed x16, local copies, waits for them, and re-layouts  6.51 us
    ppermute x1, starting transfers between devices, shards(): from_left = lax.ppermute(to_right, 'gy', forward)  4.38 us
    ppermute x7, waiting for transfers between devices, on_chip(): return lax.ppermute(value, 'gx', pairs_on_chip)  3.59 us
  transfers between devices with their start and end apart: 13, of which 9 were waited for; matrix products, arithmetic and copies ran while one was open for 1% of the time, Pallas kernels for 5%

profile of v1, /device:TPU:1, one launch (start us, length us, event | category | flops | bytes accessed | tf_op | source)
XLA Modules:
  0.0 165.8 jit_solution(8164720937880710635)
XLA Ops:
  0.6 0.0 copy-start
  0.6 0.9 copy-done
  1.6 0.0 copy-start.4
  1.6 0.9 copy-done.4
  2.5 0.0 copy-start.6
  2.5 0.9 copy-done.6
  3.4 1.8 %shard_map.77 = (f32[26,16,128]{2,1,0:T(8,128)S(1)}, f32[26,16,128]{2,1,0:T(8,128)S(1)}) custom-call(f32[2,16,16,128]{3,2,1,0:T(8,128)S(1)} %copy-done, s32[16,16,128]{2,1,0:T(8,128)S(1)} %copy-done.4, s32[16,16,128]{2,1,0:T(8,128)S(1)} %copy-done.6), custom_call_target="tpu_custom_call" | custom-call | tf_op jit(solution)/shard_map/pallas_call | solution.py:580
  5.2 4.4 %collective-permute-start = (f32[26,16,128]{2,1,0:T(8,128)S(1)}, f32[26,16,128]{2,1,0:T(8,128)S(1)}, u32[]{:S(2)}, u32[]{:S(2)}) collective-permute-start(f32[26,16,128]{2,1,0:T(8,128)S(1)} %get-tuple-element.33), channel_id=1, source_target_pairs={{0,1},{1,2},{2,3},{3,4},{4,5},{5,6},{6,7},{7,8},{8,9},{9,10},{10,1... | collective-permute-start | bytes 638984 | tf_op jit(solution)/shard_map/ppermute | solution.py:625
  9.6 1.3 collective-permute-start.1
  10.9 0.7 sqrt_bitcast_fusion
  11.6 0.1 pad_add_fusion.place
  11.7 0.7 select_maximum_fusion.table
  12.3 1.1 collective-permute-done.from_left
  13.5 9.1 %collective-permute-done.1.from_right = f32[26,16,128]{2,1,0:T(8,128)S(1)} collective-permute-done((f32[26,16,128]{2,1,0:T(8,128)S(1)}, f32[26,16,128]{2,1,0:T(8,128)S(1)}, u32[]{:S(2)}, u32[]{:S(2)}) %collective-permute-start.1) | collective-permute-done | bytes 213024 | tf_op jit(solution)/shard_map/ppermute | solution.py:626
  22.6 0.0 copy-start.1
  22.6 0.9 copy-done.1
  23.5 0.0 copy-start.5
  23.5 0.9 copy-done.5
  24.4 0.0 copy-start.7
  24.4 0.9 copy-done.7
  25.3 3.4 %shard_map.78 = (f32[16,2,16,256]{3,2,1,0:T(8,128)S(1)}, f32[16,16,256]{2,1,0:T(8,128)S(1)}, f32[16,16,256]{2,1,0:T(8,128)S(1)}, f32[54,8,256]{2,1,0:T(8,128)S(1)}, f32[54,8,256]{2,1,0:T(8,128)S(1)}) custom-call(s32[5]{0:T(128)S(1)} %pad_add_fusion.place, f32[2,16,16,128]{3,2,1,0:T(8,128)S(1)} %copy-done.1, s32[16,16,128]{2,1,0:T(8,128)S(1)} %copy-done.5, ...), custom_call_target="tpu_custom_call" | custom-call | tf_op jit(solution)/shard_map/pallas_call | solution.py:580
  28.8 0.5 collective-permute-start.2
  29.3 8.5 %collective-permute-start.3 = (f32[54,8,256]{2,1,0:T(8,128)S(1)}, f32[54,8,256]{2,1,0:T(8,128)S(1)}, u32[]{:S(2)}, u32[]{:S(2)}) collective-permute-start(f32[54,8,256]{2,1,0:T(8,128)S(1)} %get-tuple-element.42), channel_id=1, source_target_pairs={{16,32},{32,16},{48,64},{64,48},{80,96},{96,80},{112,128},{128,112... | collective-permute-start | bytes 1327112 | tf_op jit(solution)/shard_map/ppermute | solution.py:612
  37.8 1.2 shard_map.79
  39.0 0.1 collective-permute-start.7
  39.1 0.0 collective-permute-done.2.from_x
  39.1 14.2 %collective-permute-done.3.from_o = f32[54,8,256]{2,1,0:T(8,128)S(1)} collective-permute-done((f32[54,8,256]{2,1,0:T(8,128)S(1)}, f32[54,8,256]{2,1,0:T(8,128)S(1)}, u32[]{:S(2)}, u32[]{:S(2)}) %collective-permute-start.3) | collective-permute-done | bytes 442400 | tf_op jit(solution)/shard_map/ppermute | solution.py:612
  53.3 7.9 %shard_map.80 = (f32[16,2,32,256]{3,2,1,0:T(8,128)S(1)}, f32[16,32,256]{2,1,0:T(8,128)S(1)}, f32[18,32,256]{2,1,0:T(8,128)S(1)}, f32[16,32,256]{2,1,0:T(8,128)S(...) custom-call(s32[5]{0:T(128)S(1)} %pad_add_fusion.place, ...), custom_call_target="tpu_custom_call" | custom-call | tf_op jit(solution)/shard_map/pallas_call | solution.py:580
  61.1 0.0 copy-start.3
  61.1 1.0 copy-done.3
  62.1 0.0 collective-permute-start.4
  62.1 0.0 collective-permute-done.7.m_partner
  62.2 11.4 %collective-permute-start.8 = (f32[24,8,256]{2,1,0:T(8,128)S(1)}, f32[24,8,256]{2,1,0:T(8,128)S(1)}, u32[]{:S(2)}, u32[]{:S(2)}) collective-permute-start(f32[24,8,256]{2,1,0:T(8,128)S(1)} %pad_maximum_fusion), channel_id=1, source_target_pairs={{16,32},{32,16},{48,64},{64,48},{80,96},{96,80},{112,128},{128,112... | collective-permute-start | bytes 589832 | tf_op jit(solution)/shard_map/ppermute | solution.py:612
  73.6 0.0 collective-permute-done.4.partner
  73.6 1.9 %collective-permute-start.5 = (f32[16,8,256]{2,1,0:T(8,128)S(1)}, f32[16,8,256]{2,1,0:T(8,128)S(1)}, u32[]{:S(2)}, u32[]{:S(2)}) collective-permute-start(f32[16,8,256]{2,1,0:T(8,128)S(1)} %pad_maximum_fusion.1), channel_id=1, source_target_pairs={{16,32},{32,16},{48,64},{64,48},{80,96},{96,80},{112,128},{128,112... | collective-permute-start | bytes 393224 | tf_op jit(solution)/shard_map/ppermute | solution.py:612
  75.5 2.9 %collective-permute-done.8.m_odd = f32[24,8,256]{2,1,0:T(8,128)S(1)} collective-permute-done((f32[24,8,256]{2,1,0:T(8,128)S(1)}, f32[24,8,256]{2,1,0:T(8,128)S(1)}, u32[]{:S(2)}, u32[]{:S(2)}) %collective-permute-start.8) | collective-permute-done | bytes 196640 | tf_op jit(solution)/shard_map/ppermute | solution.py:612
  78.5 0.1 collective-permute-start.9
  78.6 9.8 %collective-permute-done.5.odd = f32[16,8,256]{2,1,0:T(8,128)S(1)} collective-permute-done((f32[16,8,256]{2,1,0:T(8,128)S(1)}, f32[16,8,256]{2,1,0:T(8,128)S(1)}, u32[]{:S(2)}, u32[]{:S(2)}) %collective-permute-start.5) | collective-permute-done | bytes 131104 | tf_op jit(solution)/shard_map/ppermute | solution.py:612
  88.3 0.0 collective-permute-start.6
  88.3 0.0 collective-permute-done.9.m_far
  88.4 1.2 collective-permute-done.6.far
  89.6 0.0 copy-start.2
  89.6 19.5 %shard_map.81 = (f32[16,2,32,256]{3,2,1,0:T(8,128)S(1)}, f32[18,2,32,256]{3,2,1,0:T(8,128)}, f32[8,8,256]{2,1,0:T(8,128)S(1)}, f32[8,40,256]{2,1,0:T(8,128)S(1)}...) custom-call(s32[5]{0:T(128)S(1)} %pad_add_fusion.place, ...), custom_call_target="tpu_custom_call" | custom-call | tf_op jit(solution)/shard_map/pallas_call | solution.py:580
  109.1 0.2 collective-permute-start.10
  109.3 1.1 collective-permute-done.10.partner
  110.4 8.6 %collective-permute-start.11 = (f32[16,8,256]{2,1,0:T(8,128)S(1)}, f32[16,8,256]{2,1,0:T(8,128)S(1)}, u32[]{:S(2)}, u32[]{:S(2)}) collective-permute-start(f32[16,8,256]{2,1,0:T(8,128)S(1)} %pad_maximum_fusion.2), channel_id=1, source_target_pairs={{16,32},{32,16},{48,64},{64,48},{80,96},{96,80},{112,128},{128,112... | collective-permute-start | bytes 393224 | tf_op jit(solution)/shard_map/ppermute | solution.py:612
  119.0 2.7 %collective-permute-done.11.odd = f32[16,8,256]{2,1,0:T(8,128)S(1)} collective-permute-done((f32[16,8,256]{2,1,0:T(8,128)S(1)}, f32[16,8,256]{2,1,0:T(8,128)S(1)}, u32[]{:S(2)}, u32[]{:S(2)}) %collective-permute-start.11) | collective-permute-done | bytes 131104 | tf_op jit(solution)/shard_map/ppermute | solution.py:612
  121.8 0.0 collective-permute-start.12
  121.8 1.2 collective-permute-done.12.far
  123.0 0.0 copy-done.2
  123.0 15.1 %shard_map.82 = (f32[2,16,16,128]{3,2,1,0:T(8,128)S(1)}, f32[2,16,16,128]{3,2,1,0:T(8,128)S(1)}, f32[256,128]{1,0:T(8,128)S(1)}) custom-call(s32[5]{0:T(128)S(1)} %pad_add_fusion.place, f32[2,16,16,128]{3,2,1,0:T(8,128)S(1)} %copy-done.2, f32[16,2,32,256]{3,2,1,0:T(8,128)S(1)} %get-tuple-element.51.r, f32[16,32,256]{2,1,0:T(8,128)S(1)} %get-tuple-element.44.g, ...), custom_call_target="tpu_custom_call" | custom-call | tf_op jit(solution)/shard_map/pallas_call | solution.py:580
  138.2 26.5 %all_to_all.5 = f32[256,1,128]{2,1,0:T(1,128)S(1)} all-to-all(f32[256,1,128]{2,1,0:T(1,128)S(1)} %bitcast.13), channel_id=1, replica_groups=mesh['gx'=16,'gy'=16] {'gx','gy'}, dimensions={0} | all-to-all | bytes 262144 | tf_op jit(solution)/shard_map/all_to_all | solution.py:665
  164.7 1.1 shard_map.83
  (7 shorter events, 0.1 us)
Async XLA Ops:
  0.6 1.0 copy-start
  1.6 0.9 copy-start.4
  2.5 0.9 copy-start.6
  5.2 8.3 %collective-permute-start = (f32[26,16,128]{2,1,0:T(8,128)S(1)}, f32[26,16,128]{2,1,0:T(8,128)S(1)}, u32[]{:S(2)}, u32[]{:S(2)}) collective-permute-start(f32[26,16,128]{2,1,0:T(8,128)S(1)} %get-tuple-element.33), channel_id=1, source_target_pairs={{0,1},{1,2},{2,3},{3,4},{4,5},{5,6},{6,7},{7,8},{8,9},{9,10},{10,1... | collective-permute-start | bytes 638984 | tf_op jit(solution)/shard_map/ppermute | solution.py:625
  9.6 13.0 %collective-permute-start.1 = (f32[26,16,128]{2,1,0:T(8,128)S(1)}, f32[26,16,128]{2,1,0:T(8,128)S(1)}, u32[]{:S(2)}, u32[]{:S(2)}) collective-permute-start(f32[26,16,128]{2,1,0:T(8,128)S(1)} %get-tuple-element.34), channel_id=1, source_target_pairs={{1,0},{2,1},{3,2},{4,3},{5,4},{6,5},{7,6},{8,7},{9,8},{10,9},{11,1... | collective-permute-start | bytes 638984 | tf_op jit(solution)/shard_map/ppermute | solution.py:626
  22.6 1.0 copy-start.1
  23.5 0.9 copy-start.5
  24.4 0.9 copy-start.7
  28.8 10.3 %collective-permute-start.2 = (f32[54,8,256]{2,1,0:T(8,128)S(1)}, f32[54,8,256]{2,1,0:T(8,128)S(1)}, u32[]{:S(2)}, u32[]{:S(2)}) collective-permute-start(f32[54,8,256]{2,1,0:T(8,128)S(1)} %get-tuple-element.41), channel_id=1, source_target_pairs={{0,16},{16,0},{32,48},{48,32},{64,80},{80,64},{96,112},{112,96},{1... | collective-permute-start | bytes 1327112 | tf_op jit(solution)/shard_map/ppermute | solution.py:609
  29.3 24.0 %collective-permute-start.3 = (f32[54,8,256]{2,1,0:T(8,128)S(1)}, f32[54,8,256]{2,1,0:T(8,128)S(1)}, u32[]{:S(2)}, u32[]{:S(2)}) collective-permute-start(f32[54,8,256]{2,1,0:T(8,128)S(1)} %get-tuple-element.42), channel_id=1, source_target_pairs={{16,32},{32,16},{48,64},{64,48},{80,96},{96,80},{112,128},{128,112... | collective-permute-start | bytes 1327112 | tf_op jit(solution)/shard_map/ppermute | solution.py:612
  39.0 23.2 %collective-permute-start.7 = (f32[12,8,256]{2,1,0:T(8,128)S(1)}, f32[12,8,256]{2,1,0:T(8,128)S(1)}, u32[]{:S(2)}, u32[]{:S(2)}) collective-permute-start(f32[12,8,256]{2,1,0:T(8,128)S(1)} %get-tuple-element.50.m_own), channel_id=1, source_target_pairs={{0,16},{16,0},{32,48},{48,32},{64,80},{80,64},{96,112},{112,96},{1... | collective-permute-start | bytes 294920 | tf_op jit(solution)/shard_map/ppermute | solution.py:609
  61.1 1.0 copy-start.3
  62.1 11.5 %collective-permute-start.4 = (f32[8,8,256]{2,1,0:T(8,128)S(1)}, f32[8,8,256]{2,1,0:T(8,128)S(1)}, u32[]{:S(2)}, u32[]{:S(2)}) collective-permute-start(f32[8,8,256]{2,1,0:T(8,128)S(1)} %get-tuple-element.49.own), channel_id=1, source_target_pairs={{0,16},{16,0},{32,48},{48,32},{64,80},{80,64},{96,112},{112,96},{1... | collective-permute-start | bytes 196616 | tf_op jit(solution)/shard_map/ppermute | solution.py:609
  62.2 16.3 %collective-permute-start.8 = (f32[24,8,256]{2,1,0:T(8,128)S(1)}, f32[24,8,256]{2,1,0:T(8,128)S(1)}, u32[]{:S(2)}, u32[]{:S(2)}) collective-permute-start(f32[24,8,256]{2,1,0:T(8,128)S(1)} %pad_maximum_fusion), channel_id=1, source_target_pairs={{16,32},{32,16},{48,64},{64,48},{80,96},{96,80},{112,128},{128,112... | collective-permute-start | bytes 589832 | tf_op jit(solution)/shard_map/ppermute | solution.py:612
  73.6 14.7 %collective-permute-start.5 = (f32[16,8,256]{2,1,0:T(8,128)S(1)}, f32[16,8,256]{2,1,0:T(8,128)S(1)}, u32[]{:S(2)}, u32[]{:S(2)}) collective-permute-start(f32[16,8,256]{2,1,0:T(8,128)S(1)} %pad_maximum_fusion.1), channel_id=1, source_target_pairs={{16,32},{32,16},{48,64},{64,48},{80,96},{96,80},{112,128},{128,112... | collective-permute-start | bytes 393224 | tf_op jit(solution)/shard_map/ppermute | solution.py:612
  78.5 9.9 %collective-permute-start.9 = (f32[12,8,256]{2,1,0:T(8,128)S(1)}, f32[12,8,256]{2,1,0:T(8,128)S(1)}, u32[]{:S(2)}, u32[]{:S(2)}) collective-permute-start(f32[12,8,256]{2,1,0:T(8,128)S(1)} %slice.13), channel_id=1, source_target_pairs={{0,16},{16,0},{32,48},{48,32},{64,80},{80,64},{96,112},{112,96},{1... | collective-permute-start | bytes 294920 | tf_op jit(solution)/shard_map/ppermute | solution.py:609
  88.3 1.3 collective-permute-start.6
  89.6 33.4 %copy-start.2 = (f32[2,16,16,128]{3,2,1,0:T(8,128)S(1)}, f32[2,16,16,128]{3,2,1,0:T(8,128)}, u32[]{:S(2)}) copy-start(f32[2,16,16,128]{3,2,1,0:T(8,128)} %rhs.7) | copy-start | bytes 786436
  109.1 1.3 collective-permute-start.10
  110.4 11.4 %collective-permute-start.11 = (f32[16,8,256]{2,1,0:T(8,128)S(1)}, f32[16,8,256]{2,1,0:T(8,128)S(1)}, u32[]{:S(2)}, u32[]{:S(2)}) collective-permute-start(f32[16,8,256]{2,1,0:T(8,128)S(1)} %pad_maximum_fusion.2), channel_id=1, source_target_pairs={{16,32},{32,16},{48,64},{64,48},{80,96},{96,80},{112,128},{128,112... | collective-permute-start | bytes 393224 | tf_op jit(solution)/shard_map/ppermute | solution.py:612
  121.8 1.3 collective-permute-start.12

commit v2 on v1

--- a/solution.py
+++ b/solution.py
@@ -14,6 +14,7 @@
 COLS = 128
 WIDE = 256
 HALF = 64
+UNROLL = 8
 EXT0 = 32
 EXT1 = 40
 EXT2 = 24
@@ -37,7 +38,7 @@
         body(index)
         return carry
 
-    lax.fori_loop(0, count, step, 0)
+    lax.fori_loop(0, count, step, 0, unroll=min(count, UNROLL))
 
 
 def lanes(rows, width):
@@ -130,34 +131,65 @@
     return fields
 
 
-def columns_kernel(rhs, classes, sea, to_left, to_right):
+def fill_message(message, rhs, classes, sea, start, edge):
+    def fields(z):
+        for i in range(2):
+            message[2 * z + i] = rhs(z, i)[pl.ds(start, 8), :]
+        message[32 + z] = classes.at[z][pl.ds(start, 8), :]
+        message.at[52 + z // 8][pl.ds(z % 8, 1), :] = classes.at[z][pl.ds(edge, 1), :]
+        message.at[54 + z // 8][pl.ds(z % 8, 1), :] = sea.at[z][pl.ds(edge, 1), :]
+
+    loop(NZ, fields)
+
+    def quads(j):
+        message[48 + j] = pack_sea([sea[4 * j + i, pl.ds(start, 8), :] for i in range(4)])
+
+    loop(4, quads)
+
+
+MSG_Y = 26
+MSG_X = 56
+
+
+def start_kernel(place, rhs_in, classes_in, sea_in, rhs, classes, sea, to_left, to_right, message, classes_int, sea_int, sems):
+    core = place[0]
+    copies = [
+        pltpu.make_async_copy(source, target, sems.at[i])
+        for i, (source, target) in enumerate(((classes_in, classes_int), (sea_in, sea_int), (rhs_in, rhs)))
+    ]
+    for copy in copies:
+        copy.start()
+    copies[0].wait()
+    copies[1].wait()
+
+    def convert(pair):
+        for z in (2 * pair, 2 * pair + 1):
+            classes[z] = classes_int[z].astype(F32)
+            sea[z] = sea_int[z].astype(F32)
+        to_left[16 + pair], to_right[16 + pair] = pack_halves(classes[2 * pair], classes[2 * pair + 1])
+
+    loop(8, convert)
+    for j in range(2):
+        quads = [pack_sea([sea[8 * j + 4 * q + i] for i in range(4)]) for q in range(2)]
+        to_left[24 + j], to_right[24 + j] = pack_halves(quads[0], quads[1])
+    copies[2].wait()
+
     def pair(z):
-        low, high = pack_halves(rhs[0, z], rhs[1, z])
-        to_left[z] = low
-        to_right[z] = high
+        to_left[z], to_right[z] = pack_halves(rhs[0, z], rhs[1, z])
 
     loop(NZ, pair)
-
-    def class_pair(z):
-        low, high = pack_halves(classes[z].astype(F32), classes[z + 8].astype(F32))
-        to_left[16 + z] = low
-        to_right[16 + z] = high
-
-    loop(8, class_pair)
-    for j in range(2):
-        quads = [
-            pack_sea([sea[8 * j + 4 * q + i].astype(F32) for i in range(4)]) for q in range(2)
-        ]
-        low, high = pack_halves(quads[0], quads[1])
-        to_left[24 + j] = low
-        to_right[24 + j] = high
-
-
-MSG_Y = 26
-MSG_X = 54
-
-
-def rows_kernel(place, rhs, classes, sea, from_left, from_right, table, r_out, c_out, s_out, msg_x, msg_o, row_c, row_s):
+    start = pl.multiple_of(8 * core, 8)
+    fill_message(message, lambda z, i: rhs.at[i, z], classes, sea, start, 8 - core)
+
+
+def corner_kernel(message, to_left, to_right):
+    def pair(p):
+        to_left[p], to_right[p] = pack_halves(message[2 * p], message[2 * p + 1])
+
+    loop(MSG_X // 2, pair)
+
+
+def rows_kernel(place, rhs, classes, sea, from_left, from_right, after, r_out, c_out, s_out, message):
     core = place[0]
     gy = place[2]
     left = lanes(ROWS, COLS) < HALF
@@ -174,10 +206,9 @@
 
     loop(NZ, rhs_step)
 
-    def class_step(z):
-        first, second = unpack_halves(from_right[16 + z], from_left[16 + z])
-        c_out[z] = jnp.concatenate([classes[z].astype(F32), first], axis=1)
-        c_out[z + 8] = jnp.concatenate([classes[z + 8].astype(F32), second], axis=1)
+    def class_step(pair):
+        for i, halo in enumerate(unpack_halves(from_right[16 + pair], from_left[16 + pair])):
+            c_out[2 * pair + i] = jnp.concatenate([classes[2 * pair + i], halo], axis=1)
 
     loop(8, class_step)
     for j in range(2):
@@ -185,30 +216,9 @@
         for q in range(2):
             for i, field in enumerate(unpack_sea(quads[q])):
                 z = 8 * j + 4 * q + i
-                s_out[z] = jnp.concatenate([sea[z].astype(F32), field * inside], axis=1)
-
-    for message, start, edge in (
-        (msg_x, 8 * (1 - core), 8 - (1 - core)),
-        (msg_o, 8 * core, 8 - core),
-    ):
-        start = pl.multiple_of(start, 8)
-
-        def copy(z, message=message, start=start, edge=edge):
-            for i in range(2):
-                message[2 * z + i] = r_out[z, i, pl.ds(start, 8), :]
-            message[32 + z] = c_out[z, pl.ds(start, 8), :]
-            row_c[pl.ds(z, 1), :] = c_out[z, pl.ds(edge, 1), :]
-            row_s[pl.ds(z, 1), :] = s_out[z, pl.ds(edge, 1), :]
-
-        loop(NZ, copy)
-
-        def copy_sea(j, message=message, start=start):
-            message[48 + j] = pack_sea([s_out[4 * j + i, pl.ds(start, 8), :] for i in range(4)])
-
-        loop(4, copy_sea)
-        edge_g = pick(table[0:1], row_c[...].astype(jnp.int32)) * row_s[...]
-        message[52] = edge_g[0:8]
-        message[53] = edge_g[8:16]
+                s_out[z] = jnp.concatenate([sea[z], field * inside], axis=1)
+    start = pl.multiple_of(8 * (1 - core), 8)
+    fill_message(message, lambda z, i: r_out.at[z, i], c_out, s_out, start, 7 + core)
 
 
 def material_kernel(c_in, s_in, table, g_out, h_out, k_out, packed, buffer):
@@ -305,7 +315,10 @@
     loop(NZ // 2, body)
 
 
-def down_kernel(place, r_own, g_own, h_own, k_own, from_x, from_o, table, r, g, h, d, inverse, xp, r1, xa, ka, edges, buffer):
+def down_kernel(
+    place, r_own, g_own, h_own, k_own, from_x, from_o, corner_left, corner_right, table, after,
+    r, g, h, d, inverse, xp, r1, xa, ka, wide, edges, buffer,
+):
     core = place[0]
     gx = place[1]
     gy = place[2]
@@ -326,13 +339,20 @@
         ka[z, 8:24, :] = k_own[z]
 
     loop(NZ, own)
-    for message, start, scale, slot in ((from_x, 24 * (1 - core), 1.0, 1 - core), (from_o, 24 * core, open_side, core)):
+
+    def widen(p):
+        for i, halo in enumerate(unpack_halves(corner_right[p], corner_left[p])):
+            wide[2 * p + i] = jnp.concatenate([from_o[2 * p + i], halo], axis=1)
+
+    loop(MSG_X // 2, widen)
+    for message, start, scale, slot in ((from_x, 24 * (1 - core), 1.0, 1 - core), (wide, 24 * core, open_side, core)):
         start = pl.multiple_of(start, 8)
-
-        def halo(j, message=message, start=start, scale=scale):
+        valid = scale * ends
+
+        def halo(j, message=message, start=start, valid=valid):
             for q, sea in enumerate(unpack_sea(message[48 + j])):
                 z = 4 * j + q
-                sea = sea * (scale * ends)
+                sea = sea * valid
                 index = message[32 + z].astype(jnp.int32)
                 g[z, pl.ds(start, 8), :] = pick(table[0:1], index) * sea
                 h[z + 1, pl.ds(start, 8), :] = pick(table[1:2], index) * sea
@@ -341,8 +361,9 @@
                     r[z, i, pl.ds(start, 8), :] = message[2 * z + i]
 
         loop(4, halo)
-        edges[slot, 0:8, :] = message[52] * scale
-        edges[slot, 8:16, :] = message[53] * scale
+        for j in range(2):
+            index = message[52 + j].astype(jnp.int32)
+            edges[slot, 8 * j : 8 * j + 8, :] = pick(table[0:1], index) * (message[54 + j] * valid)
 
     level = Level(NZ, 1, g, h, inverse, d)
     row = sublanes(EXT0, WIDE)
@@ -360,18 +381,6 @@
     level.first(xa, r, FINE[0])
     level.update(xp, xa, r, FINE[1])
     fine_restrict(level, xp, r, buffer, r1)
-
-
-def gather_rows(core, out_store, own, partner, odd, second, count):
-    starts = (16, 24 - 16 * core, 8 + 16 * core, 32 * core, 32 - 32 * core)
-
-    def body(j):
-        tiles = (own[j], partner[j], odd[j], odd[count + j], second[j])
-        for start, tile in zip(starts, tiles):
-            start = start if isinstance(start, int) else pl.multiple_of(start, 8)
-            out_store(j, start, tile)
-
-    return body
 
 
 def coarse_coefficients(core, pieces, g1, h1, d1, i1, g2, h2, i2, w1, k1, u1, k2, buffer):
@@ -486,15 +495,20 @@
     loop(NZ // 2, body)
 
 
+def coarse_kernel(
+    place, own, partner, odd, far, g1, h1, d1, i1, g2, h2, i2, w1, k1, u1, k2, buffer
+):
+    coarse_coefficients(
+        place[0], (own, partner, odd, far), g1, h1, d1, i1, g2, h2, i2, w1, k1, u1, k2, buffer
+    )
+
+
 def middle_kernel(
-    place, r, g, h, d, inverse, xp, own, partner, odd, far, m_own, m_partner, m_odd, m_far,
-    z_out, xp_out, r1_out, g1, h1, d1, i1, g2, h2, i2,
-    xa, xb, r1, xa1, xb1, r2, xa2, xb2, w1, k1, u1, k2, buffer,
+    place, r, g, h, d, inverse, xp, own, partner, odd, far, g1, h1, d1, i1, g2, h2, i2,
+    z_out, xp_out, r1_out,
+    xa, xb, r1, xa1, xb1, r2, xa2, xb2, buffer,
 ):
     core = place[0]
-    coarse_coefficients(
-        core, (m_own, m_partner, m_odd, m_far), g1, h1, d1, i1, g2, h2, i2, w1, k1, u1, k2, buffer
-    )
     zero = Level(NZ, 1, g, h, inverse, d)
     one = Level(8, 2, g1, h1, i1, d1)
     two = Level(4, 4, g2, h2, i2)
@@ -572,9 +586,23 @@
         loop(NZ, body)
 
 
-def call(kernel, operands, outs, scratch=(), place=True):
+COSTS = {
+    "start_kernel": 3,
+    "corner_kernel": 1,
+    "rows_kernel": 3,
+    "material_kernel": 2,
+    "down_kernel": 5,
+    "coarse_kernel": 3,
+    "middle_kernel": 9,
+    "last_kernel": 9,
+    "scale_kernel": 1,
+}
+
+
+def call(kernel, operands, outs, scratch=(), place=True, far=None):
+    far = far or {}
     vmem = pl.BlockSpec(memory_space=pltpu.VMEM)
-    specs = [vmem] * len(operands)
+    specs = [pl.BlockSpec(memory_space=far[i]) if i in far else vmem for i in range(len(operands))]
     if place:
         specs[0] = pl.BlockSpec(memory_space=pltpu.SMEM)
     return pl.pallas_call(
@@ -582,8 +610,11 @@
         out_shape=[jax.ShapeDtypeStruct(shape, F32) for shape in outs],
         in_specs=specs,
         out_specs=[vmem] * len(outs),
-        scratch_shapes=[pltpu.VMEM(shape, F32) for shape in scratch],
-        compiler_params=pltpu.CompilerParams(vmem_limit_bytes=48 * 1024 * 1024),
+        scratch_shapes=[pltpu.VMEM(shape, F32) if isinstance(shape, tuple) else shape for shape in scratch],
+        cost_estimate=pl.CostEstimate(
+            flops=COSTS[kernel.__name__] * 1_000_000_000, bytes_accessed=COSTS[kernel.__name__] * 3_000_000, transcendentals=0
+        ),
+        compiler_params=pltpu.CompilerParams(vmem_limit_bytes=16 * 1024 * 1024),
     )(*operands)
 
 
@@ -611,27 +642,41 @@
     def across_chips(value):
         return lax.ppermute(value, "gx", pairs_across)
 
+    def with_partner(own):
+        partner = on_chip(own)
+        return own, partner, jnp.concatenate([own, partner], axis=0)
+
+    def with_neighbours(own, partner, both):
+        odd = across_chips(both)
+        return own, partner, odd, on_chip(odd[: own.shape[0]])
+
     def three_steps(own):
-        partner = on_chip(own)
-        odd = across_chips(jnp.concatenate([own, partner], axis=0))
-        far = on_chip(odd[: own.shape[0]])
-        return own, partner, odd, far
-
-    to_left, to_right = call(
-        columns_kernel, (right_side, classes, sea_mask), [(MSG_Y, ROWS, COLS)] * 2, place=False
-    )
+        return with_neighbours(*with_partner(own))
+
     forward = [(i, i + 1) for i in range(count_y - 1)]
     backward = [(i + 1, i) for i in range(count_y - 1)]
-    from_left = lax.ppermute(to_right, "gy", forward)
-    from_right = lax.ppermute(to_left, "gy", backward)
-
-    r_own, c_own, s_own, msg_x, msg_o = call(
+
+    def both_sides(to_left, to_right):
+        return lax.ppermute(to_right, "gy", forward), lax.ppermute(to_left, "gy", backward)
+
+    block = (NZ, ROWS, COLS)
+    rhs, classes, sea, to_left, to_right, msg_o = call(
+        start_kernel,
+        (place, right_side, classes, sea_mask),
+        [(2, *block), block, block, (MSG_Y, ROWS, COLS), (MSG_Y, ROWS, COLS), (MSG_X, 8, COLS)],
+        [pltpu.VMEM(block, jnp.int32), pltpu.VMEM(block, jnp.int32), pltpu.SemaphoreType.DMA((3,))],
+        far={1: pltpu.HBM, 2: pltpu.HBM, 3: pltpu.HBM},
+    )
+    from_o = across_chips(msg_o)
+    from_left, from_right = both_sides(to_left, to_right)
+    corner_tiles = call(corner_kernel, (from_o,), [(MSG_X // 2, 8, COLS)] * 2, place=False)
+    corners = both_sides(*corner_tiles)
+    r_own, c_own, s_own, msg_x = call(
         rows_kernel,
-        (place, right_side, classes, sea_mask, from_left, from_right, table),
-        [(NZ, 2, ROWS, WIDE), (NZ, ROWS, WIDE), (NZ, ROWS, WIDE), (MSG_X, 8, WIDE), (MSG_X, 8, WIDE)],
-        [(NZ, WIDE), (NZ, WIDE)],
-    )
-    from_o = across_chips(msg_o)
+        (place, rhs, classes, sea, from_left, from_right, corner_tiles[0]),
+        [(NZ, 2, ROWS, WIDE), (NZ, ROWS, WIDE), (NZ, ROWS, WIDE), (MSG_X, 8, WIDE)],
+        far={6: pl.ANY},
+    )
     from_x = on_chip(msg_x)
     g_own, h_own, k_own, packed = call(
         material_kernel,
@@ -640,25 +685,30 @@
         [BUFFER],
         place=False,
     )
-    material = three_steps(packed)
+    material = with_partner(packed)
     r, g, h, d, inverse, xp, r1 = call(
         down_kernel,
-        (place, r_own, g_own, h_own, k_own, from_x, from_o, table),
+        (place, r_own, g_own, h_own, k_own, from_x, from_o, *corners, table, material[2]),
         [FIELD0, (NZ, EXT0, WIDE), (NZ + 2, EXT0, WIDE), (NZ, EXT0, WIDE), (NZ, EXT0, WIDE), PADDED0, (8, 8, WIDE)],
-        [PADDED0, (NZ, EXT0, WIDE), (2, NZ, WIDE), BUFFER],
-    )
+        [PADDED0, (NZ, EXT0, WIDE), (MSG_X, 8, WIDE), (2, NZ, WIDE), BUFFER],
+        far={10: pl.ANY},
+    )
+    material = with_neighbours(*material)
     one = [(8, EXT1, WIDE), (10, EXT1, WIDE), (8, EXT1, WIDE), (8, EXT1, WIDE)]
     two = [(4, EXT2, WIDE), (6, EXT2, WIDE), (4, EXT2, WIDE)]
-    r, xp, r1, *coarse = call(
+    coarse = call(
+        coarse_kernel, (place, *material), [*one, *two], [one[0], one[0], one[0], two[0], BUFFER]
+    )
+    r, xp, r1 = call(
         middle_kernel,
-        (place, r, g, h, d, inverse, xp, *three_steps(r1), *material),
-        [FIELD0, PADDED0, (8, 8, WIDE), *one, *two],
-        [PADDED0, PADDED0, *COARSE_SCRATCH, one[0], one[0], one[0], two[0], BUFFER],
+        (place, r, g, h, d, inverse, xp, *three_steps(r1), *coarse),
+        [FIELD0, PADDED0, (8, 8, WIDE)],
+        [PADDED0, PADDED0, *COARSE_SCRATCH, BUFFER],
     )
     count = count_x * count_y
     direction, image, sums = call(
         last_kernel,
-        (place, right_side, r, g, h, d, inverse, xp, *three_steps(r1), *coarse),
+        (place, rhs, r, g, h, d, inverse, xp, *three_steps(r1), *coarse),
         [(2, NZ, ROWS, COLS)] * 2 + [(count, COLS)],
         [PADDED0, PADDED0, *COARSE_SCRATCH, (4, ROWS, COLS), BUFFER],
     )
@@ -666,7 +716,7 @@
     return tuple(
         call(
             scale_kernel,
-            (right_side, direction, image, sums),
+            (rhs, direction, image, sums),
             [(2, NZ, ROWS, COLS)] * 2,
             place=False,
         )

time: 166 us -> 136 us (0.82)
  Pallas kernels: 50.1 us -> 27.6 us
  waiting for transfers between devices: 43.4 us -> 27.2 us
  blocking collectives: 26.5 us -> 36.4 us
  local copies, waits for them, and re-layouts: 7.21 us -> 2.81 us
  starting transfers between devices: 37 us -> 41 us
    pallas_call x7 -> x9, Pallas kernels: 50.1 us -> 27.6 us  [call(): pl.pallas_call(kernel, out_shape=[jax.ShapeDtypeStruct(shape, F32) for sh...]
    ppermute x4, waiting for transfers between devices: 29.6 us -> 18.2 us  [across_chips(): return lax.ppermute(value, 'gx', pairs_across)]
    all_to_all x1, blocking collectives: 26.5 us -> 36.4 us  [shards(): lax.all_to_all(sums.reshape(count, 1, COLS), ('gx', 'gy'), 0, 0)]
    ppermute x2 -> x4, starting transfers between devices: 5.67 us -> 10.6 us  [the longest x2 8.05 us: both_sides(): lax.ppermute(to_right, 'gy', forward)]
    ppermute x2 -> x4, waiting for transfers between devices: 10.2 us -> 5.94 us  [the longest x2 3.33 us: both_sides(): lax.ppermute(to_left, 'gy', backward)]
    unnamed x16 -> x13, local copies, waits for them, and re-layouts: 6.51 us -> 2.78 us
    ppermute x4, starting transfers between devices: 30.4 us -> 28.2 us  [across_chips(): return lax.ppermute(value, 'gx', pairs_across)]
  transfers between devices with their start and end apart: 13 -> 15, of which waited for: 9 -> 9; matrix products, arithmetic and copies ran while one was open for 1% -> 0% of each run, Pallas kernels for 5% -> 2%
where the time goes in v2:
time: 136 us
  starting transfers between devices  41 us (30%)
  blocking collectives  36.4 us (27%)
  Pallas kernels  27.6 us (20%)
  waiting for transfers between devices  27.2 us (20%)
  local copies, waits for them, and re-layouts  2.81 us (2%)
    all_to_all x1, blocking collectives, shards(): lax.all_to_all(sums.reshape(count, 1, COLS), ('gx', 'gy'), 0, 0)  36.4 us
    ppermute x4, starting transfers between devices, across_chips(): return lax.ppermute(value, 'gx', pairs_across)  28.2 us
    pallas_call x9, Pallas kernels, call(): pl.pallas_call(kernel, out_shape=[jax.ShapeDtypeStruct(shape, F32) for sh...  27.6 us
    ppermute x4, waiting for transfers between devices, across_chips(): return lax.ppermute(value, 'gx', pairs_across)  18.2 us
    ppermute x2, starting transfers between devices, both_sides(): lax.ppermute(to_right, 'gy', forward)  8.05 us
    ppermute x2, waiting for transfers between devices, both_sides(): lax.ppermute(to_left, 'gy', backward)  3.33 us
    ppermute x7, waiting for transfers between devices, on_chip(): return lax.ppermute(value, 'gx', pairs_on_chip)  3.09 us
    unnamed x13, local copies, waits for them, and re-layouts  2.78 us
  transfers between devices with their start and end apart: 15, of which 9 were waited for; matrix products, arithmetic and copies ran while one was open for 0% of the time, Pallas kernels for 2%

profile of v2, /device:TPU:1, one launch (start us, length us, event | category | flops | bytes accessed | tf_op | source)
XLA Modules:
  0.0 136.1 jit_solution(15222474310249167787)
XLA Ops:
  0.7 0.1 pad_add_fusion.place
  0.7 0.0 copy-start
  0.7 0.9 copy-done
  1.7 0.0 copy-start.1
  1.7 0.9 copy-done.1
  2.6 0.0 copy-start.2
  2.6 0.9 copy-done.2
  3.5 0.0 copy-start.3
  3.5 0.0 copy-start.4
  3.5 1.5 %shard_map.77 = (f32[2,16,16,128]{3,2,1,0:T(8,128)S(1)}, f32[16,16,128]{2,1,0:T(8,128)S(1)}, f32[16,16,128]{2,1,0:T(8,128)S(1)}, f32[26,16,128]{2,1,0:T(8,128)S(...) custom-call(s32[5]{0:T(128)S(1)} %pad_add_fusion.place, f32[2,16,16,128]{3,2,1,0:T(8,128)S(1)} %copy-done, ...), custom_call_target="tpu_custom_call" | custom-call | flops 3000000000 | bytes 9000000 | tf_op jit(solution)/shard_map/pallas_call | solution.py:608
  5.0 10.2 %collective-permute-start.2 = (f32[56,8,128]{2,1,0:T(8,128)S(1)}, f32[56,8,128]{2,1,0:T(8,128)S(1)}, u32[]{:S(2)}, u32[]{:S(2)}) collective-permute-start(f32[56,8,128]{2,1,0:T(8,128)S(1)} %get-tuple-element.43), channel_id=1, source_target_pairs={{16,32},{32,16},{48,64},{64,48},{80,96},{96,80},{112,128},{128,112... | collective-permute-start | bytes 688136 | tf_op jit(solution)/shard_map/ppermute | solution.py:643
  15.2 2.7 %collective-permute-start = (f32[26,16,128]{2,1,0:T(8,128)S(1)}, f32[26,16,128]{2,1,0:T(8,128)S(1)}, u32[]{:S(2)}, u32[]{:S(2)}) collective-permute-start(f32[26,16,128]{2,1,0:T(8,128)S(1)} %get-tuple-element.41), channel_id=1, source_target_pairs={{0,1},{1,2},{2,3},{3,4},{4,5},{5,6},{6,7},{7,8},{8,9},{9,10},{10,1... | collective-permute-start | bytes 638984 | tf_op jit(solution)/shard_map/ppermute | solution.py:660
  17.9 1.3 collective-permute-start.1
  19.2 0.0 copy-done.3
  19.2 0.0 copy-done.4
  19.2 3.0 %collective-permute-done.2.message.from_o = f32[56,8,128]{2,1,0:T(8,128)S(1)} collective-permute-done((f32[56,8,128]{2,1,0:T(8,128)S(1)}, f32[56,8,128]{2,1,0:T(8,128)S(1)}, u32[]{:S(2)}, u32[]{:S(2)}) %collective-permute-start.2) | collective-permute-done | bytes 229408 | tf_op jit(solution)/shard_map/ppermute | solution.py:643
  22.2 0.5 shard_map.78
  22.8 2.6 %collective-permute-done.from_left = f32[26,16,128]{2,1,0:T(8,128)S(1)} collective-permute-done((f32[26,16,128]{2,1,0:T(8,128)S(1)}, f32[26,16,128]{2,1,0:T(8,128)S(1)}, u32[]{:S(2)}, u32[]{:S(2)}) %collective-permute-start) | collective-permute-done | bytes 213024 | tf_op jit(solution)/shard_map/ppermute | solution.py:660
  25.4 3.3 %collective-permute-done.1.from_right = f32[26,16,128]{2,1,0:T(8,128)S(1)} collective-permute-done((f32[26,16,128]{2,1,0:T(8,128)S(1)}, f32[26,16,128]{2,1,0:T(8,128)S(1)}, u32[]{:S(2)}, u32[]{:S(2)}) %collective-permute-start.1) | collective-permute-done | bytes 213024 | tf_op jit(solution)/shard_map/ppermute | solution.py:660
  28.7 0.0 copy-start.5
  28.7 1.1 shard_map.79
  29.9 0.1 collective-permute-start.3
  30.0 0.0 copy-done.5
  30.0 1.3 collective-permute-start.5
  31.3 5.4 %collective-permute-start.4 = (f32[28,8,128]{2,1,0:T(8,128)S(1)}, f32[28,8,128]{2,1,0:T(8,128)S(1)}, u32[]{:S(2)}, u32[]{:S(2)}) collective-permute-start(f32[28,8,128]{2,1,0:T(8,128)S(1)} %get-tuple-element.52), channel_id=1, source_target_pairs={{0,1},{1,2},{2,3},{3,4},{4,5},{5,6},{6,7},{7,8},{8,9},{9,10},{10,1... | collective-permute-start | bytes 344072 | tf_op jit(solution)/shard_map/ppermute | solution.py:660
  36.7 1.1 shard_map.80
  37.8 0.9 collective-permute-start.6
  38.6 0.9 collective-permute-done.6.partner
  39.6 0.0 collective-permute-done.4.corner_left
  39.6 0.0 collective-permute-done.5.corner_right
  39.6 0.0 collective-permute-done.3.from_x
  39.6 4.5 %shard_map.81 = (f32[16,2,32,256]{3,2,1,0:T(8,128)S(1)}, f32[16,32,256]{2,1,0:T(8,128)S(1)}, f32[18,32,256]{2,1,0:T(8,128)S(1)}, f32[16,32,256]{2,1,0:T(8,128)S(...) custom-call(s32[5]{0:T(128)S(1)} %pad_add_fusion.place, ...), custom_call_target="tpu_custom_call" | custom-call | flops 5000000000 | bytes 15000000 | tf_op jit(solution)/shard_map/pallas_call | solution.py:608
  44.1 0.5 collective-permute-start.7
  44.6 8.4 %collective-permute-start.10 = (f32[24,8,256]{2,1,0:T(8,128)S(1)}, f32[24,8,256]{2,1,0:T(8,128)S(1)}, u32[]{:S(2)}, u32[]{:S(2)}) collective-permute-start(f32[24,8,256]{2,1,0:T(8,128)S(1)} %constant_dynamic-update-slice_fusion.after), channel_id=1, source_target_pairs={{16,32},{32,16},{48,64},{64,48},{80,96},{96,80},{112,128},{128,112... | collective-permute-start | bytes 589832 | tf_op jit(solution)/shard_map/ppermute | solution.py:643
  53.1 0.0 collective-permute-done.7.partner
  53.1 1.9 %collective-permute-start.8 = (f32[16,8,256]{2,1,0:T(8,128)S(1)}, f32[16,8,256]{2,1,0:T(8,128)S(1)}, u32[]{:S(2)}, u32[]{:S(2)}) collective-permute-start(f32[16,8,256]{2,1,0:T(8,128)S(1)} %pad_maximum_fusion), channel_id=1, source_target_pairs={{16,32},{32,16},{48,64},{64,48},{80,96},{96,80},{112,128},{128,112... | collective-permute-start | bytes 393224 | tf_op jit(solution)/shard_map/ppermute | solution.py:643
  55.0 1.5 %collective-permute-done.10.odd = f32[24,8,256]{2,1,0:T(8,128)S(1)} collective-permute-done((f32[24,8,256]{2,1,0:T(8,128)S(1)}, f32[24,8,256]{2,1,0:T(8,128)S(1)}, u32[]{:S(2)}, u32[]{:S(2)}) %collective-permute-start.10) | collective-permute-done | bytes 196640 | tf_op jit(solution)/shard_map/ppermute | solution.py:643
  56.5 0.1 collective-permute-start.11
  56.6 11.0 %collective-permute-done.8.odd = f32[16,8,256]{2,1,0:T(8,128)S(1)} collective-permute-done((f32[16,8,256]{2,1,0:T(8,128)S(1)}, f32[16,8,256]{2,1,0:T(8,128)S(1)}, u32[]{:S(2)}, u32[]{:S(2)}) %collective-permute-start.8) | collective-permute-done | bytes 131104 | tf_op jit(solution)/shard_map/ppermute | solution.py:643
  67.7 0.0 collective-permute-start.9
  67.7 0.0 collective-permute-done.11.far
  67.7 1.5 %shard_map.82 = (f32[8,40,256]{2,1,0:T(8,128)S(1)}, f32[10,40,256]{2,1,0:T(8,128)S(1)}, f32[8,40,256]{2,1,0:T(8,128)S(1)}, f32[8,40,256]{2,1,0:T(8,128)S(1)}, f3...) custom-call(s32[5]{0:T(128)S(1)} %pad_add_fusion.place, ...), custom_call_target="tpu_custom_call" | custom-call | flops 3000000000 | bytes 9000000 | tf_op jit(solution)/shard_map/pallas_call | solution.py:608
  69.2 0.0 collective-permute-done.9.far
  69.2 8.6 %shard_map.83 = (f32[16,2,32,256]{3,2,1,0:T(8,128)S(1)}, f32[18,2,32,256]{3,2,1,0:T(8,128)S(1)}, f32[8,8,256]{2,1,0:T(8,128)S(1)}) custom-call(s32[5]{0:T(128)S(1)} %pad_add_fusion.place, f32[16,2,32,256]{3,2,1,0:T(8,128)S(1)} %get-tuple-element.54.r, f32[16,32,256]{2,1,0:T(8,128)S(1)} %get-tuple-element.55.g, f32[18,32,256]{2,1,0:T(8,128)S(1)} %get-tuple-element.56.h, ...), custom_call_target="tpu_custom_call" | custom-call | flops 8999999488 | bytes 27000000 | tf_op jit(solution)/shard_map/pallas_call | solution.py:608
  77.8 0.6 collective-permute-start.12
  78.4 0.9 collective-permute-done.12.partner
  79.3 7.7 %collective-permute-start.13 = (f32[16,8,256]{2,1,0:T(8,128)S(1)}, f32[16,8,256]{2,1,0:T(8,128)S(1)}, u32[]{:S(2)}, u32[]{:S(2)}) collective-permute-start(f32[16,8,256]{2,1,0:T(8,128)S(1)} %pad_maximum_fusion.1), channel_id=1, source_target_pairs={{16,32},{32,16},{48,64},{64,48},{80,96},{96,80},{112,128},{128,112... | collective-permute-start | bytes 393224 | tf_op jit(solution)/shard_map/ppermute | solution.py:643
  87.0 2.6 %collective-permute-done.13.odd = f32[16,8,256]{2,1,0:T(8,128)S(1)} collective-permute-done((f32[16,8,256]{2,1,0:T(8,128)S(1)}, f32[16,8,256]{2,1,0:T(8,128)S(1)}, u32[]{:S(2)}, u32[]{:S(2)}) %collective-permute-start.13) | collective-permute-done | bytes 131104 | tf_op jit(solution)/shard_map/ppermute | solution.py:643
  89.6 0.0 collective-permute-start.14
  89.6 1.2 collective-permute-done.14.far
  90.9 7.8 %shard_map.84 = (f32[2,16,16,128]{3,2,1,0:T(8,128)S(1)}, f32[2,16,16,128]{3,2,1,0:T(8,128)S(1)}, f32[256,128]{1,0:T(8,128)S(1)}) custom-call(s32[5]{0:T(128)S(1)} %pad_add_fusion.place, f32[2,16,16,128]{3,2,1,0:T(8,128)S(1)} %get-tuple-element.38.rhs, f32[16,2,32,256]{3,2,1,0:T(8,128)S(1)} %get-tuple-element.68.r, f32[16,32,256]{2,1,0:T(8,128)S(1)} %get-tuple-element.55.g, ...), custom_call_target="tpu_custom_call" | custom-call | flops 8999999488 | bytes 27000000 | tf_op jit(solution)/shard_map/pallas_call | solution.py:608
  98.7 36.4 %all_to_all.5 = f32[256,1,128]{2,1,0:T(1,128)S(1)} all-to-all(f32[256,1,128]{2,1,0:T(1,128)S(1)} %bitcast.12), channel_id=1, replica_groups=mesh['gx'=16,'gy'=16] {'gx','gy'}, dimensions={0} | all-to-all | bytes 262144 | tf_op jit(solution)/shard_map/all_to_all | solution.py:715
  135.1 1.0 shard_map.85
  (10 shorter events, 0.1 us)
Async XLA Ops:
  0.7 1.0 copy-start
  1.7 0.9 copy-start.1
  2.6 0.9 copy-start.2
  3.5 15.7 %copy-start.3 = (f32[16]{0:T(128)S(1)}, f32[16]{0:T(128)}, u32[]{:S(2)}) copy-start(f32[16]{0:T(128)} %param.11) | copy-start | bytes 196
  3.5 15.7 %copy-start.4 = (f32[16]{0:T(128)S(1)}, f32[16]{0:T(128)}, u32[]{:S(2)}) copy-start(f32[16]{0:T(128)} %param.10) | copy-start | bytes 196
  5.0 17.3 %collective-permute-start.2 = (f32[56,8,128]{2,1,0:T(8,128)S(1)}, f32[56,8,128]{2,1,0:T(8,128)S(1)}, u32[]{:S(2)}, u32[]{:S(2)}) collective-permute-start(f32[56,8,128]{2,1,0:T(8,128)S(1)} %get-tuple-element.43), channel_id=1, source_target_pairs={{16,32},{32,16},{48,64},{64,48},{80,96},{96,80},{112,128},{128,112... | collective-permute-start | bytes 688136 | tf_op jit(solution)/shard_map/ppermute | solution.py:643
  15.2 10.2 %collective-permute-start = (f32[26,16,128]{2,1,0:T(8,128)S(1)}, f32[26,16,128]{2,1,0:T(8,128)S(1)}, u32[]{:S(2)}, u32[]{:S(2)}) collective-permute-start(f32[26,16,128]{2,1,0:T(8,128)S(1)} %get-tuple-element.41), channel_id=1, source_target_pairs={{0,1},{1,2},{2,3},{3,4},{4,5},{5,6},{6,7},{7,8},{8,9},{9,10},{10,1... | collective-permute-start | bytes 638984 | tf_op jit(solution)/shard_map/ppermute | solution.py:660
  17.9 10.8 %collective-permute-start.1 = (f32[26,16,128]{2,1,0:T(8,128)S(1)}, f32[26,16,128]{2,1,0:T(8,128)S(1)}, u32[]{:S(2)}, u32[]{:S(2)}) collective-permute-start(f32[26,16,128]{2,1,0:T(8,128)S(1)} %get-tuple-element.42), channel_id=1, source_target_pairs={{1,0},{2,1},{3,2},{4,3},{5,4},{6,5},{7,6},{8,7},{9,8},{10,9},{11,1... | collective-permute-start | bytes 638984 | tf_op jit(solution)/shard_map/ppermute | solution.py:660
  28.7 1.3 copy-start.5
  29.9 9.7 %collective-permute-start.3 = (f32[56,8,256]{2,1,0:T(8,128)S(1)}, f32[56,8,256]{2,1,0:T(8,128)S(1)}, u32[]{:S(2)}, u32[]{:S(2)}) collective-permute-start(f32[56,8,256]{2,1,0:T(8,128)S(1)} %get-tuple-element.51), channel_id=1, source_target_pairs={{0,16},{16,0},{32,48},{48,32},{64,80},{80,64},{96,112},{112,96},{1... | collective-permute-start | bytes 1376264 | tf_op jit(solution)/shard_map/ppermute | solution.py:640
  30.0 9.6 %collective-permute-start.5 = (f32[28,8,128]{2,1,0:T(8,128)S(1)}, f32[28,8,128]{2,1,0:T(8,128)S(1)}, u32[]{:S(2)}, u32[]{:S(2)}) collective-permute-start(f32[28,8,128]{2,1,0:T(8,128)S(1)} %get-tuple-element.44.after), channel_id=1, source_target_pairs={{1,0},{2,1},{3,2},{4,3},{5,4},{6,5},{7,6},{8,7},{9,8},{10,9},{11,1... | collective-permute-start | bytes 344072 | tf_op jit(solution)/shard_map/ppermute | solution.py:660
  31.3 8.3 %collective-permute-start.4 = (f32[28,8,128]{2,1,0:T(8,128)S(1)}, f32[28,8,128]{2,1,0:T(8,128)S(1)}, u32[]{:S(2)}, u32[]{:S(2)}) collective-permute-start(f32[28,8,128]{2,1,0:T(8,128)S(1)} %get-tuple-element.52), channel_id=1, source_target_pairs={{0,1},{1,2},{2,3},{3,4},{4,5},{5,6},{6,7},{7,8},{8,9},{9,10},{10,1... | collective-permute-start | bytes 344072 | tf_op jit(solution)/shard_map/ppermute | solution.py:660
  37.8 1.8 %collective-permute-start.6 = (f32[12,8,256]{2,1,0:T(8,128)S(1)}, f32[12,8,256]{2,1,0:T(8,128)S(1)}, u32[]{:S(2)}, u32[]{:S(2)}) collective-permute-start(f32[12,8,256]{2,1,0:T(8,128)S(1)} %get-tuple-element.53.own), channel_id=1, source_target_pairs={{0,16},{16,0},{32,48},{48,32},{64,80},{80,64},{96,112},{112,96},{1... | collective-permute-start | bytes 294920 | tf_op jit(solution)/shard_map/ppermute | solution.py:640
  44.1 8.9 %collective-permute-start.7 = (f32[8,8,256]{2,1,0:T(8,128)S(1)}, f32[8,8,256]{2,1,0:T(8,128)S(1)}, u32[]{:S(2)}, u32[]{:S(2)}) collective-permute-start(f32[8,8,256]{2,1,0:T(8,128)S(1)} %get-tuple-element.60.own), channel_id=1, source_target_pairs={{0,16},{16,0},{32,48},{48,32},{64,80},{80,64},{96,112},{112,96},{1... | collective-permute-start | bytes 196616 | tf_op jit(solution)/shard_map/ppermute | solution.py:640
  44.6 11.9 %collective-permute-start.10 = (f32[24,8,256]{2,1,0:T(8,128)S(1)}, f32[24,8,256]{2,1,0:T(8,128)S(1)}, u32[]{:S(2)}, u32[]{:S(2)}) collective-permute-start(f32[24,8,256]{2,1,0:T(8,128)S(1)} %constant_dynamic-update-slice_fusion.after), channel_id=1, source_target_pairs={{16,32},{32,16},{48,64},{64,48},{80,96},{96,80},{112,128},{128,112... | collective-permute-start | bytes 589832 | tf_op jit(solution)/shard_map/ppermute | solution.py:643
  53.1 14.5 %collective-permute-start.8 = (f32[16,8,256]{2,1,0:T(8,128)S(1)}, f32[16,8,256]{2,1,0:T(8,128)S(1)}, u32[]{:S(2)}, u32[]{:S(2)}) collective-permute-start(f32[16,8,256]{2,1,0:T(8,128)S(1)} %pad_maximum_fusion), channel_id=1, source_target_pairs={{16,32},{32,16},{48,64},{64,48},{80,96},{96,80},{112,128},{128,112... | collective-permute-start | bytes 393224 | tf_op jit(solution)/shard_map/ppermute | solution.py:643
  56.5 11.1 %collective-permute-start.11 = (f32[12,8,256]{2,1,0:T(8,128)S(1)}, f32[12,8,256]{2,1,0:T(8,128)S(1)}, u32[]{:S(2)}, u32[]{:S(2)}) collective-permute-start(f32[12,8,256]{2,1,0:T(8,128)S(1)} %slice.13), channel_id=1, source_target_pairs={{0,16},{16,0},{32,48},{48,32},{64,80},{80,64},{96,112},{112,96},{1... | collective-permute-start | bytes 294920 | tf_op jit(solution)/shard_map/ppermute | solution.py:640
  67.7 1.5 %collective-permute-start.9 = (f32[8,8,256]{2,1,0:T(8,128)S(1)}, f32[8,8,256]{2,1,0:T(8,128)S(1)}, u32[]{:S(2)}, u32[]{:S(2)}) collective-permute-start(f32[8,8,256]{2,1,0:T(8,128)S(1)} %slice.12), channel_id=1, source_target_pairs={{0,16},{16,0},{32,48},{48,32},{64,80},{80,64},{96,112},{112,96},{1... | collective-permute-start | bytes 196616 | tf_op jit(solution)/shard_map/ppermute | solution.py:640
  77.8 1.5 %collective-permute-start.12 = (f32[8,8,256]{2,1,0:T(8,128)S(1)}, f32[8,8,256]{2,1,0:T(8,128)S(1)}, u32[]{:S(2)}, u32[]{:S(2)}) collective-permute-start(f32[8,8,256]{2,1,0:T(8,128)S(1)} %get-tuple-element.70.own), channel_id=1, source_target_pairs={{0,16},{16,0},{32,48},{48,32},{64,80},{80,64},{96,112},{112,96},{1... | collective-permute-start | bytes 196616 | tf_op jit(solution)/shard_map/ppermute | solution.py:640
  79.3 10.3 %collective-permute-start.13 = (f32[16,8,256]{2,1,0:T(8,128)S(1)}, f32[16,8,256]{2,1,0:T(8,128)S(1)}, u32[]{:S(2)}, u32[]{:S(2)}) collective-permute-start(f32[16,8,256]{2,1,0:T(8,128)S(1)} %pad_maximum_fusion.1), channel_id=1, source_target_pairs={{16,32},{32,16},{48,64},{64,48},{80,96},{96,80},{112,128},{128,112... | collective-permute-start | bytes 393224 | tf_op jit(solution)/shard_map/ppermute | solution.py:643
  89.6 1.3 collective-permute-start.14

commit v3 on v2

--- a/solution.py
+++ b/solution.py
@@ -151,35 +151,24 @@
 MSG_X = 56
 
 
-def start_kernel(place, rhs_in, classes_in, sea_in, rhs, classes, sea, to_left, to_right, message, classes_int, sea_int, sems):
+def start_kernel(place, fields, to_left, to_right, message):
     core = place[0]
-    copies = [
-        pltpu.make_async_copy(source, target, sems.at[i])
-        for i, (source, target) in enumerate(((classes_in, classes_int), (sea_in, sea_int), (rhs_in, rhs)))
-    ]
-    for copy in copies:
-        copy.start()
-    copies[0].wait()
-    copies[1].wait()
+    classes, sea = fields.at[2], fields.at[3]
 
     def convert(pair):
-        for z in (2 * pair, 2 * pair + 1):
-            classes[z] = classes_int[z].astype(F32)
-            sea[z] = sea_int[z].astype(F32)
         to_left[16 + pair], to_right[16 + pair] = pack_halves(classes[2 * pair], classes[2 * pair + 1])
 
     loop(8, convert)
     for j in range(2):
         quads = [pack_sea([sea[8 * j + 4 * q + i] for i in range(4)]) for q in range(2)]
         to_left[24 + j], to_right[24 + j] = pack_halves(quads[0], quads[1])
-    copies[2].wait()
 
     def pair(z):
-        to_left[z], to_right[z] = pack_halves(rhs[0, z], rhs[1, z])
+        to_left[z], to_right[z] = pack_halves(fields[0, z], fields[1, z])
 
     loop(NZ, pair)
     start = pl.multiple_of(8 * core, 8)
-    fill_message(message, lambda z, i: rhs.at[i, z], classes, sea, start, 8 - core)
+    fill_message(message, lambda z, i: fields.at[i, z], classes, sea, start, 8 - core)
 
 
 def corner_kernel(message, to_left, to_right):
@@ -189,7 +178,7 @@
     loop(MSG_X // 2, pair)
 
 
-def rows_kernel(place, rhs, classes, sea, from_left, from_right, after, r_out, c_out, s_out, message):
+def rows_kernel(place, fields, from_left, from_right, after, r_out, c_out, s_out, message):
     core = place[0]
     gy = place[2]
     left = lanes(ROWS, COLS) < HALF
@@ -202,13 +191,13 @@
     def rhs_step(z):
         halo = unpack_halves(from_right[z], from_left[z])
         for i in range(2):
-            r_out[z, i] = jnp.concatenate([rhs[i, z], halo[i]], axis=1)
+            r_out[z, i] = jnp.concatenate([fields[i, z], halo[i]], axis=1)
 
     loop(NZ, rhs_step)
 
     def class_step(pair):
         for i, halo in enumerate(unpack_halves(from_right[16 + pair], from_left[16 + pair])):
-            c_out[2 * pair + i] = jnp.concatenate([classes[2 * pair + i], halo], axis=1)
+            c_out[2 * pair + i] = jnp.concatenate([fields[2, 2 * pair + i], halo], axis=1)
 
     loop(8, class_step)
     for j in range(2):
@@ -216,7 +205,7 @@
         for q in range(2):
             for i, field in enumerate(unpack_sea(quads[q])):
                 z = 8 * j + 4 * q + i
-                s_out[z] = jnp.concatenate([sea[z], field * inside], axis=1)
+                s_out[z] = jnp.concatenate([fields[3, z], field * inside], axis=1)
     start = pl.multiple_of(8 * (1 - core), 8)
     fill_message(message, lambda z, i: r_out.at[z, i], c_out, s_out, start, 7 + core)
 
@@ -316,7 +305,7 @@
 
 
 def down_kernel(
-    place, r_own, g_own, h_own, k_own, from_x, from_o, corner_left, corner_right, table, after,
+    place, r_own, g_own, h_own, k_own, from_x, from_o, corner_left, corner_right, table,
     r, g, h, d, inverse, xp, r1, xa, ka, wide, edges, buffer,
 ):
     core = place[0]
@@ -383,33 +372,31 @@
     fine_restrict(level, xp, r, buffer, r1)
 
 
-def coarse_coefficients(core, pieces, g1, h1, d1, i1, g2, h2, i2, w1, k1, u1, k2, buffer):
+def coarse_coefficients(place, pieces, g1, h1, d1, i1, g2, h2, i2, w1, k1, u1, k2, buffer):
+    core = place[0]
     clear_ends(h1, h2)
-
-    def store(j, start, tile):
-        first, second = unpack_lanes(tile)
-        w1[j, pl.ds(start, 8), :] = first
-        u1[j, pl.ds(start, 8), :] = second
-
-    def store_k(j, start, tile):
-        first, second = unpack_lanes(tile)
-        k1[j, pl.ds(start, 8), :] = jnp.where(first == 0.0, 1.0, first)
-        k1[j + 4, pl.ds(start, 8), :] = jnp.where(second == 0.0, 1.0, second)
-
     own, partner, odd, far = pieces
+    low = jnp.where(place[1] >= 2, 1.0, 0.0)
+    high = jnp.where(place[1] < place[3] - 2, 1.0, 0.0)
+    near_side = jnp.where(core == 0, low, high)
+    far_side = jnp.where(core == 0, high, low)
+    scales = (1.0, 1.0, near_side, near_side, far_side)
     starts = (16, 24 - 16 * core, 8 + 16 * core, 32 * core, 32 - 32 * core)
     starts = [s if isinstance(s, int) else pl.multiple_of(s, 8) for s in starts]
 
     def crosswise(j):
-        for start, tile in zip(starts, (own[j], partner[j], odd[j], odd[12 + j], far[j])):
-            store(j, start, tile)
+        tiles = (own[j], partner[j], odd[j], odd[12 + j], far[j])
+        for start, tile, scale in zip(starts, tiles, scales):
+            first, second = unpack_lanes(tile)
+            w1[j, pl.ds(start, 8), :] = first * scale
+            u1[j, pl.ds(start, 8), :] = second * scale
 
     loop(8, crosswise)
 
     def masses(j):
         tiles = (own[8 + j], partner[8 + j], odd[8 + j], odd[20 + j], far[8 + j])
         for start, tile in zip(starts, tiles):
-            store_k(j, start, tile)
+            k1[j, pl.ds(start, 8), :], k1[j + 4, pl.ds(start, 8), :] = unpack_lanes(tile)
 
     loop(4, masses)
 
@@ -499,7 +486,7 @@
     place, own, partner, odd, far, g1, h1, d1, i1, g2, h2, i2, w1, k1, u1, k2, buffer
 ):
     coarse_coefficients(
-        place[0], (own, partner, odd, far), g1, h1, d1, i1, g2, h2, i2, w1, k1, u1, k2, buffer
+        place, (own, partner, odd, far), g1, h1, d1, i1, g2, h2, i2, w1, k1, u1, k2, buffer
     )
 
 
@@ -634,7 +621,7 @@
     table = jnp.pad(table, ((0, 5), (0, COLS - table.shape[1])))
 
     pairs_on_chip = [(i, i ^ 1) for i in range(count_x)]
-    pairs_across = [(i, i + 1 if i % 2 else i - 1) for i in range(1, count_x - 1)]
+    pairs_across = [(i, (i + 1 if i % 2 else i - 1) % count_x) for i in range(count_x)]
 
     def on_chip(value):
         return lax.ppermute(value, "gx", pairs_on_chip)
@@ -642,30 +629,24 @@
     def across_chips(value):
         return lax.ppermute(value, "gx", pairs_across)
 
-    def with_partner(own):
-        partner = on_chip(own)
-        return own, partner, jnp.concatenate([own, partner], axis=0)
-
-    def with_neighbours(own, partner, both):
-        odd = across_chips(both)
+    def neighbours(own, partner):
+        return across_chips(jnp.concatenate([own, partner], axis=0))
+
+    def rows_of(own, partner):
+        odd = neighbours(own, partner)
         return own, partner, odd, on_chip(odd[: own.shape[0]])
 
-    def three_steps(own):
-        return with_neighbours(*with_partner(own))
-
-    forward = [(i, i + 1) for i in range(count_y - 1)]
-    backward = [(i + 1, i) for i in range(count_y - 1)]
+    forward = [(i, (i + 1) % count_y) for i in range(count_y)]
+    backward = [(target, source) for source, target in forward]
 
     def both_sides(to_left, to_right):
         return lax.ppermute(to_right, "gy", forward), lax.ppermute(to_left, "gy", backward)
 
-    block = (NZ, ROWS, COLS)
-    rhs, classes, sea, to_left, to_right, msg_o = call(
-        start_kernel,
-        (place, right_side, classes, sea_mask),
-        [(2, *block), block, block, (MSG_Y, ROWS, COLS), (MSG_Y, ROWS, COLS), (MSG_X, 8, COLS)],
-        [pltpu.VMEM(block, jnp.int32), pltpu.VMEM(block, jnp.int32), pltpu.SemaphoreType.DMA((3,))],
-        far={1: pltpu.HBM, 2: pltpu.HBM, 3: pltpu.HBM},
+    fields = jnp.concatenate(
+        [right_side, classes.astype(F32)[None], sea_mask.astype(F32)[None]], axis=0
+    )
+    to_left, to_right, msg_o = call(
+        start_kernel, (place, fields), [(MSG_Y, ROWS, COLS), (MSG_Y, ROWS, COLS), (MSG_X, 8, COLS)]
     )
     from_o = across_chips(msg_o)
     from_left, from_right = both_sides(to_left, to_right)
@@ -673,9 +654,9 @@
     corners = both_sides(*corner_tiles)
     r_own, c_own, s_own, msg_x = call(
         rows_kernel,
-        (place, rhs, classes, sea, from_left, from_right, corner_tiles[0]),
+        (place, fields, from_left, from_right, corner_tiles[0]),
         [(NZ, 2, ROWS, WIDE), (NZ, ROWS, WIDE), (NZ, ROWS, WIDE), (MSG_X, 8, WIDE)],
-        far={6: pl.ANY},
+        far={4: pl.ANY},
     )
     from_x = on_chip(msg_x)
     g_own, h_own, k_own, packed = call(
@@ -685,15 +666,16 @@
         [BUFFER],
         place=False,
     )
-    material = with_partner(packed)
+    packed_partner = on_chip(packed)
+    packed_odd = neighbours(packed, packed_partner)
     r, g, h, d, inverse, xp, r1 = call(
         down_kernel,
-        (place, r_own, g_own, h_own, k_own, from_x, from_o, *corners, table, material[2]),
+        (place, r_own, g_own, h_own, k_own, from_x, from_o, *corners, table),
         [FIELD0, (NZ, EXT0, WIDE), (NZ + 2, EXT0, WIDE), (NZ, EXT0, WIDE), (NZ, EXT0, WIDE), PADDED0, (8, 8, WIDE)],
         [PADDED0, (NZ, EXT0, WIDE), (MSG_X, 8, WIDE), (2, NZ, WIDE), BUFFER],
-        far={10: pl.ANY},
-    )
-    material = with_neighbours(*material)
+    )
+    received = on_chip(jnp.concatenate([r1, packed_odd[:12]], axis=0))
+    material = (packed, packed_partner, packed_odd, received[8:])
     one = [(8, EXT1, WIDE), (10, EXT1, WIDE), (8, EXT1, WIDE), (8, EXT1, WIDE)]
     two = [(4, EXT2, WIDE), (6, EXT2, WIDE), (4, EXT2, WIDE)]
     coarse = call(
@@ -701,14 +683,14 @@
     )
     r, xp, r1 = call(
         middle_kernel,
-        (place, r, g, h, d, inverse, xp, *three_steps(r1), *coarse),
+        (place, r, g, h, d, inverse, xp, *rows_of(r1, received[:8]), *coarse),
         [FIELD0, PADDED0, (8, 8, WIDE)],
         [PADDED0, PADDED0, *COARSE_SCRATCH, BUFFER],
     )
     count = count_x * count_y
     direction, image, sums = call(
         last_kernel,
-        (place, rhs, r, g, h, d, inverse, xp, *three_steps(r1), *coarse),
+        (place, fields, r, g, h, d, inverse, xp, *rows_of(r1, on_chip(r1)), *coarse),
         [(2, NZ, ROWS, COLS)] * 2 + [(count, COLS)],
         [PADDED0, PADDED0, *COARSE_SCRATCH, (4, ROWS, COLS), BUFFER],
     )
@@ -716,7 +698,7 @@
     return tuple(
         call(
             scale_kernel,
-            (rhs, direction, image, sums),
+            (fields, direction, image, sums),
             [(2, NZ, ROWS, COLS)] * 2,
             place=False,
         )

time: 136 us -> 129 us (0.949)
  waiting for transfers between devices: 27.2 us -> 44.2 us
  blocking collectives: 36.4 us -> 20 us
  starting transfers between devices: 41 us -> 34.7 us
  local copies, waits for them, and re-layouts: 2.81 us -> 0.05 us
  other arithmetic: 0.11 us -> 2.11 us
    ppermute x4, waiting for transfers between devices: 18.2 us -> 37 us  [across_chips(): return lax.ppermute(value, 'gx', pairs_across)]
    all_to_all x1, blocking collectives: 36.4 us -> 20 us  [shards(): lax.all_to_all(sums.reshape(count, 1, COLS), ('gx', 'gy'), 0, 0)]
    ppermute x4, starting transfers between devices: 28.2 us -> 12.6 us  [across_chips(): return lax.ppermute(value, 'gx', pairs_across)]
    ppermute x2, starting transfers between devices: 2.58 us -> 9.46 us  [both_sides(): lax.ppermute(to_left, 'gy', backward)]
    ppermute x7 -> x6, starting transfers between devices: 2.12 us -> 7.98 us  [on_chip(): return lax.ppermute(value, 'gx', pairs_on_chip)]
    ppermute x2, starting transfers between devices: 8.05 us -> 4.63 us  [both_sides(): lax.ppermute(to_right, 'gy', forward)]
    ppermute x2, waiting for transfers between devices: 3.33 us -> 0.01 us  [both_sides(): lax.ppermute(to_left, 'gy', backward)]
    unnamed x13 -> x6, local copies, waits for them, and re-layouts: 2.78 us -> 0.01 us
  transfers between devices with their start and end apart: 15 -> 14, of which waited for: 9 -> 9; matrix products, arithmetic and copies ran while one was open for 0% -> 0% of each run, Pallas kernels for 2% -> 2%
where the time goes in v3:
time: 129 us
  waiting for transfers between devices  44.2 us (34%)
  starting transfers between devices  34.7 us (27%)
  Pallas kernels  27.2 us (21%)
  blocking collectives  20 us (16%)
  other arithmetic  2.11 us (2%)
    ppermute x4, waiting for transfers between devices, across_chips(): return lax.ppermute(value, 'gx', pairs_across)  37 us
    pallas_call x9, Pallas kernels, call(): pl.pallas_call(kernel, out_shape=[jax.ShapeDtypeStruct(shape, F32) for sh...  27.2 us
    all_to_all x1, blocking collectives, shards(): lax.all_to_all(sums.reshape(count, 1, COLS), ('gx', 'gy'), 0, 0)  20 us
    ppermute x4, starting transfers between devices, across_chips(): return lax.ppermute(value, 'gx', pairs_across)  12.6 us
    ppermute x2, starting transfers between devices, both_sides(): lax.ppermute(to_left, 'gy', backward)  9.46 us
    ppermute x6, starting transfers between devices, on_chip(): return lax.ppermute(value, 'gx', pairs_on_chip)  7.98 us
    ppermute x2, starting transfers between devices, both_sides(): lax.ppermute(to_right, 'gy', forward)  4.63 us
    ppermute x6, waiting for transfers between devices, on_chip(): return lax.ppermute(value, 'gx', pairs_on_chip)  4.12 us
  transfers between devices with their start and end apart: 14, of which 9 were waited for; matrix products, arithmetic and copies ran while one was open for 0% of the time, Pallas kernels for 2%

profile of v3, /device:TPU:1, one launch (start us, length us, event | category | flops | bytes accessed | tf_op | source)
XLA Modules:
  0.0 129.1 jit_solution(4012783743620379929)
XLA Ops:
  0.6 1.0 convert_bitcast_fusion
  1.6 1.0 pad_maximum_fusion.fields.rhs
  2.6 0.1 pad_add_fusion.place
  2.7 0.0 copy-start
  2.7 0.0 copy-start.1
  2.7 0.0 copy-start.2
  2.7 1.1 shard_map.77
  3.8 2.5 %collective-permute-start = (f32[26,16,128]{2,1,0:T(8,128)S(1)}, f32[26,16,128]{2,1,0:T(8,128)S(1)}, u32[]{:S(2)}, u32[]{:S(2)}) collective-permute-start(f32[26,16,128]{2,1,0:T(8,128)S(1)} %get-tuple-element.35), channel_id=1, source_target_pairs={{0,1},{1,2},{2,3},{3,4},{4,5},{5,6},{6,7},{7,8},{8,9},{9,10},{10,1... | collective-permute-start | bytes 638984 | tf_op jit(solution)/shard_map/ppermute | solution.py:643
  6.3 5.0 %collective-permute-start.1 = (f32[26,16,128]{2,1,0:T(8,128)S(1)}, f32[26,16,128]{2,1,0:T(8,128)S(1)}, u32[]{:S(2)}, u32[]{:S(2)}) collective-permute-start(f32[26,16,128]{2,1,0:T(8,128)S(1)} %get-tuple-element.36), channel_id=1, source_target_pairs={{1,0},{2,1},{3,2},{4,3},{5,4},{6,5},{7,6},{8,7},{9,8},{10,9},{11,1... | collective-permute-start | bytes 638984 | tf_op jit(solution)/shard_map/ppermute | solution.py:643
  11.3 6.8 %collective-permute-start.2 = (f32[56,8,128]{2,1,0:T(8,128)S(1)}, f32[56,8,128]{2,1,0:T(8,128)S(1)}, u32[]{:S(2)}, u32[]{:S(2)}) collective-permute-start(f32[56,8,128]{2,1,0:T(8,128)S(1)} %get-tuple-element.37), channel_id=1, source_target_pairs={{0,240},{16,32},{32,16},{48,64},{64,48},{80,96},{96,80},{112,128},... | collective-permute-start | bytes 688136 | tf_op jit(solution)/shard_map/ppermute | solution.py:630
  18.1 0.0 copy-done
  18.1 0.0 copy-done.1
  18.1 0.0 copy-done.2
  18.1 14.3 %collective-permute-done.2.message.from_o = f32[56,8,128]{2,1,0:T(8,128)S(1)} collective-permute-done((f32[56,8,128]{2,1,0:T(8,128)S(1)}, f32[56,8,128]{2,1,0:T(8,128)S(1)}, u32[]{:S(2)}, u32[]{:S(2)}) %collective-permute-start.2) | collective-permute-done | bytes 229408 | tf_op jit(solution)/shard_map/ppermute | solution.py:630
  32.4 0.5 shard_map.78
  33.0 0.0 collective-permute-done.from_left
  33.0 0.0 collective-permute-done.1.from_right
  33.0 1.2 shard_map.79
  34.1 0.1 collective-permute-start.3
  34.2 1.1 shard_map.80
  35.3 0.6 collective-permute-start.6
  35.9 0.9 collective-permute-done.6.partner
  36.9 0.1 collective-permute-start.7
  37.0 2.1 %collective-permute-start.4 = (f32[28,8,128]{2,1,0:T(8,128)S(1)}, f32[28,8,128]{2,1,0:T(8,128)S(1)}, u32[]{:S(2)}, u32[]{:S(2)}) collective-permute-start(f32[28,8,128]{2,1,0:T(8,128)S(1)} %get-tuple-element.46), channel_id=1, source_target_pairs={{0,1},{1,2},{2,3},{3,4},{4,5},{5,6},{6,7},{7,8},{8,9},{9,10},{10,1... | collective-permute-start | bytes 344072 | tf_op jit(solution)/shard_map/ppermute | solution.py:643
  39.0 4.5 %collective-permute-start.5 = (f32[28,8,128]{2,1,0:T(8,128)S(1)}, f32[28,8,128]{2,1,0:T(8,128)S(1)}, u32[]{:S(2)}, u32[]{:S(2)}) collective-permute-start(f32[28,8,128]{2,1,0:T(8,128)S(1)} %get-tuple-element.38.after), channel_id=1, source_target_pairs={{1,0},{2,1},{3,2},{4,3},{5,4},{6,5},{7,6},{8,7},{9,8},{10,9},{11,1... | collective-permute-start | bytes 344072 | tf_op jit(solution)/shard_map/ppermute | solution.py:643
  43.5 7.9 %collective-permute-done.7.odd = f32[24,8,256]{2,1,0:T(8,128)S(1)} collective-permute-done((f32[24,8,256]{2,1,0:T(8,128)S(1)}, f32[24,8,256]{2,1,0:T(8,128)S(1)}, u32[]{:S(2)}, u32[]{:S(2)}) %collective-permute-start.7) | collective-permute-done | bytes 196640 | tf_op jit(solution)/shard_map/ppermute | solution.py:630
  51.4 3.1 %collective-permute-done.4.corner_left = f32[28,8,128]{2,1,0:T(8,128)S(1)} collective-permute-done((f32[28,8,128]{2,1,0:T(8,128)S(1)}, f32[28,8,128]{2,1,0:T(8,128)S(1)}, u32[]{:S(2)}, u32[]{:S(2)}) %collective-permute-start.4) | collective-permute-done | bytes 114720 | tf_op jit(solution)/shard_map/ppermute | solution.py:643
  54.5 0.0 collective-permute-done.5.corner_right
  54.5 0.0 collective-permute-done.3.from_x
  54.5 4.5 %shard_map.81 = (f32[16,2,32,256]{3,2,1,0:T(8,128)S(1)}, f32[16,32,256]{2,1,0:T(8,128)S(1)}, f32[18,32,256]{2,1,0:T(8,128)S(1)}, f32[16,32,256]{2,1,0:T(8,128)S(...) custom-call(s32[5]{0:T(128)S(1)} %pad_add_fusion.place, ...), custom_call_target="tpu_custom_call" | custom-call | flops 5000000000 | bytes 15000000 | tf_op jit(solution)/shard_map/pallas_call | solution.py:595
  59.0 2.4 %collective-permute-start.8 = (f32[20,8,256]{2,1,0:T(8,128)S(1)}, f32[20,8,256]{2,1,0:T(8,128)S(1)}, u32[]{:S(2)}, u32[]{:S(2)}) collective-permute-start(f32[20,8,256]{2,1,0:T(8,128)S(1)} %pad_maximum_fusion.2), channel_id=1, source_target_pairs={{0,16},{16,0},{32,48},{48,32},{64,80},{80,64},{96,112},{112,96},{1... | collective-permute-start | bytes 491528 | tf_op jit(solution)/shard_map/ppermute | solution.py:627
  61.5 1.0 collective-permute-done.8
  62.5 3.2 %collective-permute-start.9 = (f32[16,8,256]{2,1,0:T(8,128)S(1)}, f32[16,8,256]{2,1,0:T(8,128)S(1)}, u32[]{:S(2)}, u32[]{:S(2)}) collective-permute-start(f32[16,8,256]{2,1,0:T(8,128)S(1)} %pad_maximum_fusion.3), channel_id=1, source_target_pairs={{0,240},{16,32},{32,16},{48,64},{64,48},{80,96},{96,80},{112,128},... | collective-permute-start | bytes 393224 | tf_op jit(solution)/shard_map/ppermute | solution.py:630
  65.7 8.2 %collective-permute-done.9.odd = f32[16,8,256]{2,1,0:T(8,128)S(1)} collective-permute-done((f32[16,8,256]{2,1,0:T(8,128)S(1)}, f32[16,8,256]{2,1,0:T(8,128)S(1)}, u32[]{:S(2)}, u32[]{:S(2)}) %collective-permute-start.9) | collective-permute-done | bytes 131104 | tf_op jit(solution)/shard_map/ppermute | solution.py:630
  73.9 2.0 %collective-permute-start.10 = (f32[8,8,256]{2,1,0:T(8,128)S(1)}, f32[8,8,256]{2,1,0:T(8,128)S(1)}, u32[]{:S(2)}, u32[]{:S(2)}) collective-permute-start(f32[8,8,256]{2,1,0:T(8,128)S(1)} %slice.22), channel_id=1, source_target_pairs={{0,16},{16,0},{32,48},{48,32},{64,80},{80,64},{96,112},{112,96},{1... | collective-permute-start | bytes 196616 | tf_op jit(solution)/shard_map/ppermute | solution.py:627
  75.9 1.5 %shard_map.82 = (f32[8,40,256]{2,1,0:T(8,128)S(1)}, f32[10,40,256]{2,1,0:T(8,128)S(1)}, f32[8,40,256]{2,1,0:T(8,128)S(1)}, f32[8,40,256]{2,1,0:T(8,128)S(1)}, f3...) custom-call(s32[5]{0:T(128)S(1)} %pad_add_fusion.place, ...), custom_call_target="tpu_custom_call" | custom-call | flops 3000000000 | bytes 9000000 | tf_op jit(solution)/shard_map/pallas_call | solution.py:595
  77.4 0.0 collective-permute-done.10.far
  77.4 8.6 %shard_map.83 = (f32[16,2,32,256]{3,2,1,0:T(8,128)S(1)}, f32[18,2,32,256]{3,2,1,0:T(8,128)S(1)}, f32[8,8,256]{2,1,0:T(8,128)S(1)}) custom-call(s32[5]{0:T(128)S(1)} %pad_add_fusion.place, f32[16,2,32,256]{3,2,1,0:T(8,128)S(1)} %get-tuple-element.47.r, f32[16,32,256]{2,1,0:T(8,128)S(1)} %get-tuple-element.48.g, f32[18,32,256]{2,1,0:T(8,128)S(1)} %get-tuple-element.49.h, ...), custom_call_target="tpu_custom_call" | custom-call | flops 8999999488 | bytes 27000000 | tf_op jit(solution)/shard_map/pallas_call | solution.py:595
  86.0 0.1 collective-permute-start.11
  86.1 1.2 collective-permute-done.11.partner
  87.4 2.6 %collective-permute-start.12 = (f32[16,8,256]{2,1,0:T(8,128)S(1)}, f32[16,8,256]{2,1,0:T(8,128)S(1)}, u32[]{:S(2)}, u32[]{:S(2)}) collective-permute-start(f32[16,8,256]{2,1,0:T(8,128)S(1)} %pad_maximum_fusion.4), channel_id=1, source_target_pairs={{0,240},{16,32},{32,16},{48,64},{64,48},{80,96},{96,80},{112,128},... | collective-permute-start | bytes 393224 | tf_op jit(solution)/shard_map/ppermute | solution.py:630
  89.9 6.6 %collective-permute-done.12.odd = f32[16,8,256]{2,1,0:T(8,128)S(1)} collective-permute-done((f32[16,8,256]{2,1,0:T(8,128)S(1)}, f32[16,8,256]{2,1,0:T(8,128)S(1)}, u32[]{:S(2)}, u32[]{:S(2)}) %collective-permute-start.12) | collective-permute-done | bytes 131104 | tf_op jit(solution)/shard_map/ppermute | solution.py:630
  96.6 2.8 %collective-permute-start.13 = (f32[8,8,256]{2,1,0:T(8,128)S(1)}, f32[8,8,256]{2,1,0:T(8,128)S(1)}, u32[]{:S(2)}, u32[]{:S(2)}) collective-permute-start(f32[8,8,256]{2,1,0:T(8,128)S(1)} %slice.24), channel_id=1, source_target_pairs={{0,16},{16,0},{32,48},{48,32},{64,80},{80,64},{96,112},{112,96},{1... | collective-permute-start | bytes 196616 | tf_op jit(solution)/shard_map/ppermute | solution.py:627
  99.4 0.9 collective-permute-done.13.far
  100.3 7.8 %shard_map.84 = (f32[2,16,16,128]{3,2,1,0:T(8,128)S(1)}, f32[2,16,16,128]{3,2,1,0:T(8,128)S(1)}, f32[256,128]{1,0:T(8,128)S(1)}) custom-call(s32[5]{0:T(128)S(1)} %pad_add_fusion.place, f32[4,16,16,128]{3,2,1,0:T(8,128)S(1)} %pad_maximum_fusion.fields.rhs, f32[16,2,32,256]{3,2,1,0:T(8,128)S(1)} %get-tuple-element.62.r, ...), custom_call_target="tpu_custom_call" | custom-call | flops 8999999488 | bytes 27000000 | tf_op jit(solution)/shard_map/pallas_call | solution.py:595
  108.1 20.0 %all_to_all.5 = f32[256,1,128]{2,1,0:T(1,128)S(1)} all-to-all(f32[256,1,128]{2,1,0:T(1,128)S(1)} %bitcast.16), channel_id=1, replica_groups=mesh['gx'=16,'gy'=16] {'gx','gy'}, dimensions={0} | all-to-all | bytes 262144 | tf_op jit(solution)/shard_map/all_to_all | solution.py:697
  128.2 1.0 shard_map.85
  (12 shorter events, 0.1 us)
Async XLA Ops:
  2.7 15.4 %copy-start = (f32[16]{0:T(128)S(1)}, f32[16]{0:T(128)}, u32[]{:S(2)}) copy-start(f32[16]{0:T(128)} %param.11) | copy-start | bytes 196
  2.7 15.4 %copy-start.1 = (f32[16]{0:T(128)S(1)}, f32[16]{0:T(128)}, u32[]{:S(2)}) copy-start(f32[16]{0:T(128)} %param.10) | copy-start | bytes 196
  2.7 15.4 %copy-start.2 = (f32[16]{0:T(128)S(1)}, f32[16]{0:T(128)}, u32[]{:S(2)}) copy-start(f32[16]{0:T(128)} %param.9) | copy-start | bytes 196
  3.8 29.2 %collective-permute-start = (f32[26,16,128]{2,1,0:T(8,128)S(1)}, f32[26,16,128]{2,1,0:T(8,128)S(1)}, u32[]{:S(2)}, u32[]{:S(2)}) collective-permute-start(f32[26,16,128]{2,1,0:T(8,128)S(1)} %get-tuple-element.35), channel_id=1, source_target_pairs={{0,1},{1,2},{2,3},{3,4},{4,5},{5,6},{6,7},{7,8},{8,9},{9,10},{10,1... | collective-permute-start | bytes 638984 | tf_op jit(solution)/shard_map/ppermute | solution.py:643
  6.3 26.6 %collective-permute-start.1 = (f32[26,16,128]{2,1,0:T(8,128)S(1)}, f32[26,16,128]{2,1,0:T(8,128)S(1)}, u32[]{:S(2)}, u32[]{:S(2)}) collective-permute-start(f32[26,16,128]{2,1,0:T(8,128)S(1)} %get-tuple-element.36), channel_id=1, source_target_pairs={{1,0},{2,1},{3,2},{4,3},{5,4},{6,5},{7,6},{8,7},{9,8},{10,9},{11,1... | collective-permute-start | bytes 638984 | tf_op jit(solution)/shard_map/ppermute | solution.py:643
  11.3 21.1 %collective-permute-start.2 = (f32[56,8,128]{2,1,0:T(8,128)S(1)}, f32[56,8,128]{2,1,0:T(8,128)S(1)}, u32[]{:S(2)}, u32[]{:S(2)}) collective-permute-start(f32[56,8,128]{2,1,0:T(8,128)S(1)} %get-tuple-element.37), channel_id=1, source_target_pairs={{0,240},{16,32},{32,16},{48,64},{64,48},{80,96},{96,80},{112,128},... | collective-permute-start | bytes 688136 | tf_op jit(solution)/shard_map/ppermute | solution.py:630
  34.1 20.4 %collective-permute-start.3 = (f32[56,8,256]{2,1,0:T(8,128)S(1)}, f32[56,8,256]{2,1,0:T(8,128)S(1)}, u32[]{:S(2)}, u32[]{:S(2)}) collective-permute-start(f32[56,8,256]{2,1,0:T(8,128)S(1)} %get-tuple-element.45), channel_id=1, source_target_pairs={{0,16},{16,0},{32,48},{48,32},{64,80},{80,64},{96,112},{112,96},{1... | collective-permute-start | bytes 1376264 | tf_op jit(solution)/shard_map/ppermute | solution.py:627
  35.3 1.5 %collective-permute-start.6 = (f32[12,8,256]{2,1,0:T(8,128)S(1)}, f32[12,8,256]{2,1,0:T(8,128)S(1)}, u32[]{:S(2)}, u32[]{:S(2)}) collective-permute-start(f32[12,8,256]{2,1,0:T(8,128)S(1)} %get-tuple-element.54.own), channel_id=1, source_target_pairs={{0,16},{16,0},{32,48},{48,32},{64,80},{80,64},{96,112},{112,96},{1... | collective-permute-start | bytes 294920 | tf_op jit(solution)/shard_map/ppermute | solution.py:627
  36.9 14.5 %collective-permute-start.7 = (f32[24,8,256]{2,1,0:T(8,128)S(1)}, f32[24,8,256]{2,1,0:T(8,128)S(1)}, u32[]{:S(2)}, u32[]{:S(2)}) collective-permute-start(f32[24,8,256]{2,1,0:T(8,128)S(1)} %pad_maximum_fusion.1), channel_id=1, source_target_pairs={{0,240},{16,32},{32,16},{48,64},{64,48},{80,96},{96,80},{112,128},... | collective-permute-start | bytes 589832 | tf_op jit(solution)/shard_map/ppermute | solution.py:630
  37.0 17.5 %collective-permute-start.4 = (f32[28,8,128]{2,1,0:T(8,128)S(1)}, f32[28,8,128]{2,1,0:T(8,128)S(1)}, u32[]{:S(2)}, u32[]{:S(2)}) collective-permute-start(f32[28,8,128]{2,1,0:T(8,128)S(1)} %get-tuple-element.46), channel_id=1, source_target_pairs={{0,1},{1,2},{2,3},{3,4},{4,5},{5,6},{6,7},{7,8},{8,9},{9,10},{10,1... | collective-permute-start | bytes 344072 | tf_op jit(solution)/shard_map/ppermute | solution.py:643
  39.0 15.5 %collective-permute-start.5 = (f32[28,8,128]{2,1,0:T(8,128)S(1)}, f32[28,8,128]{2,1,0:T(8,128)S(1)}, u32[]{:S(2)}, u32[]{:S(2)}) collective-permute-start(f32[28,8,128]{2,1,0:T(8,128)S(1)} %get-tuple-element.38.after), channel_id=1, source_target_pairs={{1,0},{2,1},{3,2},{4,3},{5,4},{6,5},{7,6},{8,7},{9,8},{10,9},{11,1... | collective-permute-start | bytes 344072 | tf_op jit(solution)/shard_map/ppermute | solution.py:643
  59.0 3.5 %collective-permute-start.8 = (f32[20,8,256]{2,1,0:T(8,128)S(1)}, f32[20,8,256]{2,1,0:T(8,128)S(1)}, u32[]{:S(2)}, u32[]{:S(2)}) collective-permute-start(f32[20,8,256]{2,1,0:T(8,128)S(1)} %pad_maximum_fusion.2), channel_id=1, source_target_pairs={{0,16},{16,0},{32,48},{48,32},{64,80},{80,64},{96,112},{112,96},{1... | collective-permute-start | bytes 491528 | tf_op jit(solution)/shard_map/ppermute | solution.py:627
  62.5 11.4 %collective-permute-start.9 = (f32[16,8,256]{2,1,0:T(8,128)S(1)}, f32[16,8,256]{2,1,0:T(8,128)S(1)}, u32[]{:S(2)}, u32[]{:S(2)}) collective-permute-start(f32[16,8,256]{2,1,0:T(8,128)S(1)} %pad_maximum_fusion.3), channel_id=1, source_target_pairs={{0,240},{16,32},{32,16},{48,64},{64,48},{80,96},{96,80},{112,128},... | collective-permute-start | bytes 393224 | tf_op jit(solution)/shard_map/ppermute | solution.py:630
  73.9 3.4 %collective-permute-start.10 = (f32[8,8,256]{2,1,0:T(8,128)S(1)}, f32[8,8,256]{2,1,0:T(8,128)S(1)}, u32[]{:S(2)}, u32[]{:S(2)}) collective-permute-start(f32[8,8,256]{2,1,0:T(8,128)S(1)} %slice.22), channel_id=1, source_target_pairs={{0,16},{16,0},{32,48},{48,32},{64,80},{80,64},{96,112},{112,96},{1... | collective-permute-start | bytes 196616 | tf_op jit(solution)/shard_map/ppermute | solution.py:627
  86.0 1.3 %collective-permute-start.11 = (f32[8,8,256]{2,1,0:T(8,128)S(1)}, f32[8,8,256]{2,1,0:T(8,128)S(1)}, u32[]{:S(2)}, u32[]{:S(2)}) collective-permute-start(f32[8,8,256]{2,1,0:T(8,128)S(1)} %get-tuple-element.64.own), channel_id=1, source_target_pairs={{0,16},{16,0},{32,48},{48,32},{64,80},{80,64},{96,112},{112,96},{1... | collective-permute-start | bytes 196616 | tf_op jit(solution)/shard_map/ppermute | solution.py:627
  87.4 9.2 %collective-permute-start.12 = (f32[16,8,256]{2,1,0:T(8,128)S(1)}, f32[16,8,256]{2,1,0:T(8,128)S(1)}, u32[]{:S(2)}, u32[]{:S(2)}) collective-permute-start(f32[16,8,256]{2,1,0:T(8,128)S(1)} %pad_maximum_fusion.4), channel_id=1, source_target_pairs={{0,240},{16,32},{32,16},{48,64},{64,48},{80,96},{96,80},{112,128},... | collective-permute-start | bytes 393224 | tf_op jit(solution)/shard_map/ppermute | solution.py:630
  96.6 3.7 %collective-permute-start.13 = (f32[8,8,256]{2,1,0:T(8,128)S(1)}, f32[8,8,256]{2,1,0:T(8,128)S(1)}, u32[]{:S(2)}, u32[]{:S(2)}) collective-permute-start(f32[8,8,256]{2,1,0:T(8,128)S(1)} %slice.24), channel_id=1, source_target_pairs={{0,16},{16,0},{32,48},{48,32},{64,80},{80,64},{96,112},{112,96},{1... | collective-permute-start | bytes 196616 | tf_op jit(solution)/shard_map/ppermute | solution.py:627

commit v4 on v3

--- a/solution.py
+++ b/solution.py
@@ -66,25 +66,39 @@
 
 
 def row_pairs(buffer, value):
-    rows = value.shape[0]
+    rows, width = value.shape
     parts = []
-    for half in range(2):
+    for half in range(width // COLS):
         buffer[half, 0:rows, :] = value[:, half * COLS : (half + 1) * COLS]
         parts.append(
             buffer[half, pl.ds(0, rows // 2, stride=2), :] + buffer[half, pl.ds(1, rows // 2, stride=2), :]
         )
-    return jnp.concatenate(parts, axis=1)
+    return parts[0] if len(parts) == 1 else jnp.concatenate(parts, axis=1)
 
 
 def row_repeat(buffer, value):
-    rows = value.shape[0]
+    rows, width = value.shape
     parts = []
-    for half in range(2):
+    for half in range(width // COLS):
         part = value[:, half * COLS : (half + 1) * COLS]
         buffer[half, pl.ds(0, rows, stride=2), :] = part
         buffer[half, pl.ds(1, rows, stride=2), :] = part
         parts.append(buffer[half, 0 : 2 * rows, :])
-    return jnp.concatenate(parts, axis=1)
+    return parts[0] if len(parts) == 1 else jnp.concatenate(parts, axis=1)
+
+
+def column_pairs(value):
+    row = lax.broadcasted_iota(jnp.int32, (WIDE, COLS), 0)
+    column = lax.broadcasted_iota(jnp.int32, (WIDE, COLS), 1)
+    matrix = jnp.where(row // 2 == column, 1.0, 0.0)
+    return jnp.dot(value, matrix, precision=lax.Precision.HIGHEST, preferred_element_type=F32)
+
+
+def column_repeat(value):
+    row = lax.broadcasted_iota(jnp.int32, (COLS, WIDE), 0)
+    column = lax.broadcasted_iota(jnp.int32, (COLS, WIDE), 1)
+    matrix = jnp.where(column // 2 == row, 1.0, 0.0)
+    return jnp.dot(value, matrix, precision=lax.Precision.HIGHEST, preferred_element_type=F32)
 
 
 def pick(table_row, index):
@@ -149,6 +163,8 @@
 
 MSG_Y = 26
 MSG_X = 56
+R_TILES = 16
+M_TILES = 24
 
 
 def start_kernel(place, fields, to_left, to_right, message):
@@ -210,7 +226,7 @@
     fill_message(message, lambda z, i: r_out.at[z, i], c_out, s_out, start, 7 + core)
 
 
-def material_kernel(c_in, s_in, table, g_out, h_out, k_out, packed, buffer):
+def material_kernel(c_in, s_in, table, g_out, h_out, k_out, coarse, sums, buffer):
     def fields(z):
         index = c_in[z].astype(jnp.int32)
         sea = s_in[z]
@@ -220,34 +236,16 @@
         g_out[z] = g
         h_out[z] = h
         k_out[z] = k
-        return g * g, h * h, k
-
-    even = lanes(8, WIDE) % 2 == 0
-
-    def coarse(pair):
+        return 0.125 * g * g, 0.125 * h * h, k
+
+    def step(pair):
         first = fields(2 * pair)
         second = fields(2 * pair + 1)
-        return [
-            lane_sum(row_pairs(buffer.at[i], first[i] + second[i]), 1) for i in range(3)
-        ]
-
-    def step(j):
-        near = coarse(j)
-        far = coarse(j + 4)
-        packed[j] = jnp.where(even, 0.125 * near[0], 0.125 * near[1])
-        packed[j + 4] = jnp.where(even, 0.125 * far[0], 0.125 * far[1])
-        packed[j + 8] = jnp.where(even, near[2], far[2])
-
-    loop(4, step)
-
-
-def unpack_lanes(packed):
-    even = lanes(*packed.shape) % 2 == 0
-    width = packed.shape[1]
-    return (
-        jnp.where(even, packed, pltpu.roll(packed, 1, 1)),
-        jnp.where(even, pltpu.roll(packed, width - 1, 1), packed),
-    )
+        for i in range(3):
+            sums[8 * i + pair] = row_pairs(buffer.at[i], first[i] + second[i])
+
+    loop(8, step)
+    coarse[...] = column_pairs(sums[...].reshape(M_TILES * 8, WIDE)).reshape(M_TILES, 8, COLS)
 
 
 class Level:
@@ -291,22 +289,19 @@
         ref[ref.shape[0] - 1] = jnp.zeros(ref.shape[1:], ref.dtype)
 
 
-def fine_restrict(level, x, r, buffer, out):
-    even = lanes(8, WIDE) % 2 == 0
-
+def fine_restrict(level, x, r, sums, buffer, out):
     def body(pair):
-        sums = []
         for i in range(2):
             total = level.defect(x, r, 2 * pair, i) + level.defect(x, r, 2 * pair + 1, i)
-            sums.append(lane_sum(row_pairs(buffer.at[i], total[8:24]), 1))
-        out[pair] = jnp.where(even, sums[0], sums[1])
+            sums[2 * pair + i] = row_pairs(buffer.at[i], total[8:24])
 
     loop(NZ // 2, body)
+    out[...] = column_pairs(sums[...].reshape(R_TILES * 8, WIDE)).reshape(R_TILES, 8, COLS)
 
 
 def down_kernel(
     place, r_own, g_own, h_own, k_own, from_x, from_o, corner_left, corner_right, table,
-    r, g, h, d, inverse, xp, r1, xa, ka, wide, edges, buffer,
+    r, g, h, d, inverse, xp, r1, xa, ka, wide, edges, sums, buffer,
 ):
     core = place[0]
     gx = place[1]
@@ -369,7 +364,7 @@
     loop(NZ, diagonals)
     level.first(xa, r, FINE[0])
     level.update(xp, xa, r, FINE[1])
-    fine_restrict(level, xp, r, buffer, r1)
+    fine_restrict(level, xp, r, sums, buffer, r1)
 
 
 def coarse_coefficients(place, pieces, g1, h1, d1, i1, g2, h2, i2, w1, k1, u1, k2, buffer):
@@ -384,28 +379,21 @@
     starts = (16, 24 - 16 * core, 8 + 16 * core, 32 * core, 32 - 32 * core)
     starts = [s if isinstance(s, int) else pl.multiple_of(s, 8) for s in starts]
 
-    def crosswise(j):
-        tiles = (own[j], partner[j], odd[j], odd[12 + j], far[j])
-        for start, tile, scale in zip(starts, tiles, scales):
-            first, second = unpack_lanes(tile)
-            w1[j, pl.ds(start, 8), :] = first * scale
-            u1[j, pl.ds(start, 8), :] = second * scale
-
-    loop(8, crosswise)
-
-    def masses(j):
-        tiles = (own[8 + j], partner[8 + j], odd[8 + j], odd[20 + j], far[8 + j])
-        for start, tile in zip(starts, tiles):
-            k1[j, pl.ds(start, 8), :], k1[j + 4, pl.ds(start, 8), :] = unpack_lanes(tile)
-
-    loop(4, masses)
+    def assemble(z):
+        for i, field in enumerate((w1, u1, k1)):
+            j = 8 * i + z
+            tiles = (own[j], partner[j], odd[j], odd[M_TILES + j], far[j])
+            for start, tile, scale in zip(starts, tiles, scales):
+                field[z, pl.ds(start, 8), :] = tile * scale if i < 2 else tile
+
+    loop(8, assemble)
 
     def roots(z):
         g1[z] = 2.0 * jnp.sqrt(w1[z])
         h1[z + 1] = 2.0 * jnp.sqrt(u1[z])
 
     loop(8, roots)
-    one = Level(8, 2, g1, h1, i1, d1)
+    one = Level(8, 1, g1, h1, i1, d1)
 
     def diagonals(z):
         total = one.diagonal_of(k1[z], z)
@@ -416,16 +404,16 @@
 
     def coarser(z):
         sums = [
-            lane_sum(row_pairs(buffer.at[i], field[2 * z] + field[2 * z + 1]), 2)
+            lane_sum(row_pairs(buffer.at[i], field[2 * z] + field[2 * z + 1]), 1)
             for i, field in enumerate((w1, u1, k1))
         ]
-        blank = jnp.zeros((4, WIDE), F32)
+        blank = jnp.zeros((4, COLS), F32)
         g2[z] = jnp.concatenate([2.0 * jnp.sqrt(0.125 * sums[0]), blank], axis=0)
         h2[z + 1] = jnp.concatenate([2.0 * jnp.sqrt(0.125 * sums[1]), blank], axis=0)
         k2[z] = jnp.concatenate([sums[2], blank + 1.0], axis=0)
 
     loop(4, coarser)
-    two = Level(4, 4, g2, h2, i2)
+    two = Level(4, 2, g2, h2, i2)
 
     def diagonals_two(z):
         i2[z] = 1.0 / two.diagonal_of(k2[z], z)
@@ -440,10 +428,11 @@
     starts = [s if isinstance(s, int) else pl.multiple_of(s, 8) for s in starts]
 
     def assemble(z):
-        tiles = (own[z], partner[z], odd[z], odd[8 + z], far[z])
-        for start, tile in zip(starts, tiles):
-            for i, field in enumerate(unpack_lanes(tile)):
-                r1[z, i, pl.ds(start, 8), :] = field
+        for i in range(2):
+            j = 2 * z + i
+            tiles = (own[j], partner[j], odd[j], odd[R_TILES + j], far[j])
+            for start, tile in zip(starts, tiles):
+                r1[z, i, pl.ds(start, 8), :] = tile
 
     loop(8, assemble)
     one.first(xa1, r1, FINE[0])
@@ -452,8 +441,8 @@
     def restrict(z):
         for i in range(2):
             total = one.defect(xb1, r1, 2 * z, i) + one.defect(xb1, r1, 2 * z + 1, i)
-            sums = lane_sum(row_pairs(buffer.at[i], total), 2)
-            r2[z, i] = jnp.concatenate([sums, jnp.zeros((4, WIDE), F32)], axis=0)
+            sums = lane_sum(row_pairs(buffer.at[i], total), 1)
+            r2[z, i] = jnp.concatenate([sums, jnp.zeros((4, COLS), F32)], axis=0)
 
     loop(4, restrict)
     two.first(xa2, r2, COARSE[0])
@@ -461,25 +450,40 @@
     two.update(xa2, xb2, r2, COARSE[2])
     two.update(xb2, xa2, r2, COARSE[3])
 
+    inner = [ref.at[:, :, 8:32, :] for ref in (xa1, xb1, r1)]
+    inner_one = Level(8, 1, *(ref.at[:, 8:32, :] for ref in (one.g, one.h, one.inverse)))
+
     def prolong(z):
         for i in range(2):
-            fine = row_repeat(buffer.at[i], xb2[z + 1, i, 0:20, :])
+            fine = row_repeat(buffer.at[i], xb2[z + 1, i, 4:16, :])
             for half in range(2):
-                xa1[2 * z + half + 1, i] = xb1[2 * z + half + 1, i] + fine
+                inner[0][2 * z + half + 1, i] = inner[1][2 * z + half + 1, i] + fine
 
     loop(4, prolong)
-    one.update(xb1, xa1, r1, FINE[0])
-    one.update(xa1, xb1, r1, FINE[1])
-
-
-def fine_correct(level, out, xp, c1, buffer):
+    inner_one.update(inner[1], inner[0], inner[2], FINE[0])
+    inner_one.update(inner[0], inner[1], inner[2], FINE[1])
+
+
+def fine_correct(level, out, xp, c1, wide, buffer):
+    rows = c1[1:9, :, 12:28, :].reshape(R_TILES * 16, COLS)
+    wide[...] = column_repeat(rows).reshape(R_TILES, 16, WIDE)
+
     def body(pair):
         for i in range(2):
-            fine = row_repeat(buffer.at[i], c1[pair + 1, i, 12:28, :])
+            fine = row_repeat(buffer.at[i], wide[2 * pair + i])
             for half in range(2):
                 out[2 * pair + half + 1, i] = xp[2 * pair + half + 1, i] + fine
 
     loop(NZ // 2, body)
+
+
+def join_kernel(r1, odd, message):
+    message[0:R_TILES] = r1[...]
+    message[R_TILES:] = odd[0:M_TILES]
+
+
+def near_kernel(odd, after, near):
+    near[...] = odd[0:R_TILES]
 
 
 def coarse_kernel(
@@ -493,15 +497,15 @@
 def middle_kernel(
     place, r, g, h, d, inverse, xp, own, partner, odd, far, g1, h1, d1, i1, g2, h2, i2,
     z_out, xp_out, r1_out,
-    xa, xb, r1, xa1, xb1, r2, xa2, xb2, buffer,
+    xa, xb, r1, xa1, xb1, r2, xa2, xb2, wide, sums, buffer,
 ):
     core = place[0]
     zero = Level(NZ, 1, g, h, inverse, d)
-    one = Level(8, 2, g1, h1, i1, d1)
-    two = Level(4, 4, g2, h2, i2)
+    one = Level(8, 1, g1, h1, i1, d1)
+    two = Level(4, 2, g2, h2, i2)
     coarse_solve(core, one, two, (own, partner, odd, far), r1, xa1, xb1, r2, xa2, xb2, buffer)
     clear_ends(xa, xb, xp_out)
-    fine_correct(zero, xa, xp, xa1, buffer)
+    fine_correct(zero, xa, xp, xa1, wide, buffer)
     zero.update(xb, xa, r, FINE[0])
 
     def last(z):
@@ -512,21 +516,21 @@
     loop(NZ, last)
     zero.first(xa, z_out, FINE[0])
     zero.update(xp_out, xa, z_out, FINE[1])
-    fine_restrict(zero, xp_out, z_out, buffer, r1_out)
+    fine_restrict(zero, xp_out, z_out, sums, buffer, r1_out)
 
 
 def last_kernel(
     place, rhs, r, g, h, d, inverse, xp, own, partner, odd, far, g1, h1, d1, i1, g2, h2, i2,
     direction, image, sums,
-    xa, xb, r1, xa1, xb1, r2, xa2, xb2, totals, buffer,
+    xa, xb, r1, xa1, xb1, r2, xa2, xb2, wide, totals, buffer,
 ):
     core = place[0]
     zero = Level(NZ, 1, g, h, inverse, d)
-    one = Level(8, 2, g1, h1, i1, d1)
-    two = Level(4, 4, g2, h2, i2)
+    one = Level(8, 1, g1, h1, i1, d1)
+    two = Level(4, 2, g2, h2, i2)
     coarse_solve(core, one, two, (own, partner, odd, far), r1, xa1, xb1, r2, xa2, xb2, buffer)
     clear_ends(xa, xb)
-    fine_correct(zero, xa, xp, xa1, buffer)
+    fine_correct(zero, xa, xp, xa1, wide, buffer)
     zero.update(xb, xa, r, FINE[0])
     zero.update(xa, xb, r, FINE[1])
 
@@ -579,6 +583,8 @@
     "rows_kernel": 3,
     "material_kernel": 2,
     "down_kernel": 5,
+    "join_kernel": 1,
+    "near_kernel": 1,
     "coarse_kernel": 3,
     "middle_kernel": 9,
     "last_kernel": 9,
@@ -607,10 +613,12 @@
 
 FIELD0 = (NZ, 2, EXT0, WIDE)
 PADDED0 = (NZ + 2, 2, EXT0, WIDE)
-PADDED1 = (10, 2, EXT1, WIDE)
-PADDED2 = (6, 2, EXT2, WIDE)
+PADDED1 = (10, 2, EXT1, COLS)
+PADDED2 = (6, 2, EXT2, COLS)
 BUFFER = (3, 2, EXT1, COLS)
-COARSE_SCRATCH = [(8, 2, EXT1, WIDE), PADDED1, PADDED1, (4, 2, EXT2, WIDE), PADDED2, PADDED2]
+SUMS = (R_TILES, 8, WIDE)
+SPREAD = (R_TILES, 16, WIDE)
+COARSE_SCRATCH = [(8, 2, EXT1, COLS), PADDED1, PADDED1, (4, 2, EXT2, COLS), PADDED2, PADDED2, SPREAD]
 
 
 def shards(count_x, count_y, right_side, classes, sea_mask, kappa_table, cross_table, vertical_table):
@@ -642,9 +650,9 @@
     def both_sides(to_left, to_right):
         return lax.ppermute(to_right, "gy", forward), lax.ppermute(to_left, "gy", backward)
 
-    fields = jnp.concatenate(
-        [right_side, classes.astype(F32)[None], sea_mask.astype(F32)[None]], axis=0
-    )
+    part = lax.broadcasted_iota(jnp.int32, (4, *classes.shape), 0)
+    materials = jnp.where(part == 2, classes[None], sea_mask[None]).astype(F32)
+    fields = jnp.where(part == 0, right_side[0:1], jnp.where(part == 1, right_side[1:2], materials))
     to_left, to_right, msg_o = call(
         start_kernel, (place, fields), [(MSG_Y, ROWS, COLS), (MSG_Y, ROWS, COLS), (MSG_X, 8, COLS)]
     )
@@ -662,8 +670,8 @@
     g_own, h_own, k_own, packed = call(
         material_kernel,
         (c_own, s_own, table),
-        [(NZ, ROWS, WIDE)] * 3 + [(12, 8, WIDE)],
-        [BUFFER],
+        [(NZ, ROWS, WIDE)] * 3 + [(M_TILES, 8, COLS)],
+        [(M_TILES, 8, WIDE), BUFFER],
         place=False,
     )
     packed_partner = on_chip(packed)
@@ -671,21 +679,24 @@
     r, g, h, d, inverse, xp, r1 = call(
         down_kernel,
         (place, r_own, g_own, h_own, k_own, from_x, from_o, *corners, table),
-        [FIELD0, (NZ, EXT0, WIDE), (NZ + 2, EXT0, WIDE), (NZ, EXT0, WIDE), (NZ, EXT0, WIDE), PADDED0, (8, 8, WIDE)],
-        [PADDED0, (NZ, EXT0, WIDE), (MSG_X, 8, WIDE), (2, NZ, WIDE), BUFFER],
-    )
-    received = on_chip(jnp.concatenate([r1, packed_odd[:12]], axis=0))
-    material = (packed, packed_partner, packed_odd, received[8:])
-    one = [(8, EXT1, WIDE), (10, EXT1, WIDE), (8, EXT1, WIDE), (8, EXT1, WIDE)]
-    two = [(4, EXT2, WIDE), (6, EXT2, WIDE), (4, EXT2, WIDE)]
+        [FIELD0, (NZ, EXT0, WIDE), (NZ + 2, EXT0, WIDE), (NZ, EXT0, WIDE), (NZ, EXT0, WIDE), PADDED0, (R_TILES, 8, COLS)],
+        [PADDED0, (NZ, EXT0, WIDE), (MSG_X, 8, WIDE), (2, NZ, WIDE), SUMS, BUFFER],
+    )
+    received = on_chip(call(join_kernel, (r1, packed_odd), [(R_TILES + M_TILES, 8, COLS)], place=False)[0])
+    material = (packed, packed_partner, packed_odd, received[R_TILES:])
+    one = [(8, EXT1, COLS), (10, EXT1, COLS), (8, EXT1, COLS), (8, EXT1, COLS)]
+    two = [(4, EXT2, COLS), (6, EXT2, COLS), (4, EXT2, COLS)]
     coarse = call(
         coarse_kernel, (place, *material), [*one, *two], [one[0], one[0], one[0], two[0], BUFFER]
     )
+    partner = received[:R_TILES]
+    odd = neighbours(r1, partner)
+    near = call(near_kernel, (odd, coarse[0]), [(R_TILES, 8, COLS)], place=False, far={1: pl.ANY})[0]
     r, xp, r1 = call(
         middle_kernel,
-        (place, r, g, h, d, inverse, xp, *rows_of(r1, received[:8]), *coarse),
-        [FIELD0, PADDED0, (8, 8, WIDE)],
-        [PADDED0, PADDED0, *COARSE_SCRATCH, BUFFER],
+        (place, r, g, h, d, inverse, xp, r1, partner, odd, on_chip(near), *coarse),
+        [FIELD0, PADDED0, (R_TILES, 8, COLS)],
+        [PADDED0, PADDED0, *COARSE_SCRATCH, SUMS, BUFFER],
     )
     count = count_x * count_y
     direction, image, sums = call(

time: 129 us -> 121 us (0.938)
  Pallas kernels: 27.2 us -> 21.4 us
  waiting for transfers between devices: 44.2 us -> 41.1 us
  blocking collectives: 20 us -> 22.2 us
  starting transfers between devices: 34.7 us -> 32.6 us
    ppermute x4, waiting for transfers between devices: 37 us -> 18.9 us  [across_chips(): return lax.ppermute(value, 'gx', pairs_across)]
    ppermute x2, waiting for transfers between devices: 3.11 us -> 16.7 us  [both_sides(): lax.ppermute(to_right, 'gy', forward)]
    pallas_call x9 -> x11, Pallas kernels: 27.2 us -> 21.4 us  [call(): pl.pallas_call(kernel, out_shape=[jax.ShapeDtypeStruct(shape, F32) for sh...]
    ppermute x2, starting transfers between devices: 4.63 us -> 0.74 us  [both_sides(): lax.ppermute(to_right, 'gy', forward)]
    all_to_all x1, blocking collectives: 20 us -> 22.2 us  [shards(): lax.all_to_all(sums.reshape(count, 1, COLS), ('gx', 'gy'), 0, 0)]
    ppermute x6, starting transfers between devices: 7.98 us -> 9.89 us  [on_chip(): return lax.ppermute(value, 'gx', pairs_on_chip)]
    ppermute x2, waiting for transfers between devices: 0.01 us -> 1.77 us  [both_sides(): lax.ppermute(to_left, 'gy', backward)]
  transfers between devices with their start and end apart: 14 -> 14, of which waited for: 9 -> 11; matrix products, arithmetic and copies ran while one was open for 0% -> 0% of each run, Pallas kernels for 2% -> 5%
where the time goes in v4:
time: 121 us; the launch traced here: 120 us
  waiting for transfers between devices  41.1 us (34%)
  starting transfers between devices  32.6 us (27%)
  blocking collectives  22.2 us (18%)
  Pallas kernels  21.4 us (18%)
  other arithmetic  1.25 us (1%)
    all_to_all x1, blocking collectives, shards(): lax.all_to_all(sums.reshape(count, 1, COLS), ('gx', 'gy'), 0, 0)  22.2 us
    pallas_call x11, Pallas kernels, call(): pl.pallas_call(kernel, out_shape=[jax.ShapeDtypeStruct(shape, F32) for sh...  21.4 us
    ppermute x4, waiting for transfers between devices, across_chips(): return lax.ppermute(value, 'gx', pairs_across)  18.9 us
    ppermute x2, waiting for transfers between devices, both_sides(): lax.ppermute(to_right, 'gy', forward)  16.7 us
    ppermute x4, starting transfers between devices, across_chips(): return lax.ppermute(value, 'gx', pairs_across)  12.8 us
    ppermute x6, starting transfers between devices, on_chip(): return lax.ppermute(value, 'gx', pairs_on_chip)  9.89 us
    ppermute x2, starting transfers between devices, both_sides(): lax.ppermute(to_left, 'gy', backward)  9.21 us
    ppermute x6, waiting for transfers between devices, on_chip(): return lax.ppermute(value, 'gx', pairs_on_chip)  3.74 us
  transfers between devices with their start and end apart: 14, of which 11 were waited for; matrix products, arithmetic and copies ran while one was open for 0% of the time, Pallas kernels for 5%

profile of v4, /device:TPU:1, one launch (start us, length us, event | category | flops | bytes accessed | tf_op | source)
XLA Modules:
  0.0 120.4 jit_solution(6164518595864138237)
XLA Ops:
  0.7 1.0 slice_bitcast_fusion.1
  1.7 0.1 pad_add_fusion.place
  1.8 1.1 select_select_fusion.fields.rhs
  2.9 0.0 copy-start
  2.9 0.0 copy-start.1
  2.9 1.1 shard_map.77
  4.0 8.4 %collective-permute-start.2 = (f32[56,8,128]{2,1,0:T(8,128)S(1)}, f32[56,8,128]{2,1,0:T(8,128)S(1)}, u32[]{:S(2)}, u32[]{:S(2)}) collective-permute-start(f32[56,8,128]{2,1,0:T(8,128)S(1)} %get-tuple-element.37), channel_id=1, source_target_pairs={{0,240},{16,32},{32,16},{48,64},{64,48},{80,96},{96,80},{112,128},... | collective-permute-start | bytes 688136 | tf_op jit(solution)/shard_map/ppermute | solution.py:638
  12.4 0.7 collective-permute-start
  13.1 4.6 %collective-permute-start.1 = (f32[26,16,128]{2,1,0:T(8,128)S(1)}, f32[26,16,128]{2,1,0:T(8,128)S(1)}, u32[]{:S(2)}, u32[]{:S(2)}) collective-permute-start(f32[26,16,128]{2,1,0:T(8,128)S(1)} %get-tuple-element.36), channel_id=1, source_target_pairs={{1,0},{2,1},{3,2},{4,3},{5,4},{6,5},{7,6},{8,7},{9,8},{10,9},{11,1... | collective-permute-start | bytes 638984 | tf_op jit(solution)/shard_map/ppermute | solution.py:651
  17.7 0.0 copy-done
  17.7 0.0 copy-done.1
  17.7 2.1 %collective-permute-done.2.message.from_o = f32[56,8,128]{2,1,0:T(8,128)S(1)} collective-permute-done((f32[56,8,128]{2,1,0:T(8,128)S(1)}, f32[56,8,128]{2,1,0:T(8,128)S(1)}, u32[]{:S(2)}, u32[]{:S(2)}) %collective-permute-start.2) | collective-permute-done | bytes 229408 | tf_op jit(solution)/shard_map/ppermute | solution.py:638
  19.9 0.5 shard_map.78
  20.4 9.1 %collective-permute-done.from_left = f32[26,16,128]{2,1,0:T(8,128)S(1)} collective-permute-done((f32[26,16,128]{2,1,0:T(8,128)S(1)}, f32[26,16,128]{2,1,0:T(8,128)S(1)}, u32[]{:S(2)}, u32[]{:S(2)}) %collective-permute-start) | collective-permute-done | bytes 213024 | tf_op jit(solution)/shard_map/ppermute | solution.py:651
  29.5 1.8 %collective-permute-done.1.from_right = f32[26,16,128]{2,1,0:T(8,128)S(1)} collective-permute-done((f32[26,16,128]{2,1,0:T(8,128)S(1)}, f32[26,16,128]{2,1,0:T(8,128)S(1)}, u32[]{:S(2)}, u32[]{:S(2)}) %collective-permute-start.1) | collective-permute-done | bytes 213024 | tf_op jit(solution)/shard_map/ppermute | solution.py:651
  31.2 0.0 copy-start.2
  31.2 1.1 shard_map.79
  32.4 2.6 %collective-permute-start.3 = (f32[56,8,256]{2,1,0:T(8,128)S(1)}, f32[56,8,256]{2,1,0:T(8,128)S(1)}, u32[]{:S(2)}, u32[]{:S(2)}) collective-permute-start(f32[56,8,256]{2,1,0:T(8,128)S(1)} %get-tuple-element.45), channel_id=1, source_target_pairs={{0,16},{16,0},{32,48},{48,32},{64,80},{80,64},{96,112},{112,96},{1... | collective-permute-start | bytes 1376264 | tf_op jit(solution)/shard_map/ppermute | solution.py:635
  34.9 0.0 copy-done.2
  34.9 0.9 shard_map.80
  35.9 0.1 collective-permute-start.6
  36.0 4.6 %collective-permute-start.5 = (f32[28,8,128]{2,1,0:T(8,128)S(1)}, f32[28,8,128]{2,1,0:T(8,128)S(1)}, u32[]{:S(2)}, u32[]{:S(2)}) collective-permute-start(f32[28,8,128]{2,1,0:T(8,128)S(1)} %get-tuple-element.38.after), channel_id=1, source_target_pairs={{1,0},{2,1},{3,2},{4,3},{5,4},{6,5},{7,6},{8,7},{9,8},{10,9},{11,1... | collective-permute-start | bytes 344072 | tf_op jit(solution)/shard_map/ppermute | solution.py:651
  40.6 0.0 collective-permute-start.4
  40.6 0.0 collective-permute-done.6.partner
  40.6 0.4 collective-permute-start.7
  40.9 7.7 %collective-permute-done.4.corner_left = f32[28,8,128]{2,1,0:T(8,128)S(1)} collective-permute-done((f32[28,8,128]{2,1,0:T(8,128)S(1)}, f32[28,8,128]{2,1,0:T(8,128)S(1)}, u32[]{:S(2)}, u32[]{:S(2)}) %collective-permute-start.4) | collective-permute-done | bytes 114720 | tf_op jit(solution)/shard_map/ppermute | solution.py:651
  48.6 0.0 collective-permute-done.5.corner_right
  48.6 0.0 collective-permute-done.3.from_x
  48.6 4.1 %shard_map.81 = (f32[16,2,32,256]{3,2,1,0:T(8,128)S(1)}, f32[16,32,256]{2,1,0:T(8,128)S(1)}, f32[18,32,256]{2,1,0:T(8,128)S(1)}, f32[16,32,256]{2,1,0:T(8,128)S(...) custom-call(s32[5]{0:T(128)S(1)} %pad_add_fusion.place, ...), custom_call_target="tpu_custom_call" | custom-call | flops 5000000000 | bytes 15000000 | tf_op jit(solution)/shard_map/pallas_call | solution.py:601
  52.7 2.1 %collective-permute-done.7.odd = f32[48,8,128]{2,1,0:T(8,128)S(1)} collective-permute-done((f32[48,8,128]{2,1,0:T(8,128)S(1)}, f32[48,8,128]{2,1,0:T(8,128)S(1)}, u32[]{:S(2)}, u32[]{:S(2)}) %collective-permute-start.7) | collective-permute-done | bytes 196640 | tf_op jit(solution)/shard_map/ppermute | solution.py:638
  54.9 4.7 %collective-permute-start.8 = (f32[40,8,128]{2,1,0:T(8,128)S(1)}, f32[40,8,128]{2,1,0:T(8,128)S(1)}, u32[]{:S(2)}, u32[]{:S(2)}) collective-permute-start(f32[40,8,128]{2,1,0:T(8,128)S(1)} %shard_map.82), channel_id=1, source_target_pairs={{0,16},{16,0},{32,48},{48,32},{64,80},{80,64},{96,112},{112,96},{1... | collective-permute-start | bytes 491528 | tf_op jit(solution)/shard_map/ppermute | solution.py:635
  59.5 1.0 collective-permute-done.8
  60.6 2.1 %collective-permute-start.9 = (f32[32,8,128]{2,1,0:T(8,128)S(1)}, f32[32,8,128]{2,1,0:T(8,128)S(1)}, u32[]{:S(2)}, u32[]{:S(2)}) collective-permute-start(f32[32,8,128]{2,1,0:T(8,128)S(1)} %pad_maximum_fusion.1), channel_id=1, source_target_pairs={{0,240},{16,32},{32,16},{48,64},{64,48},{80,96},{96,80},{112,128},... | collective-permute-start | bytes 393224 | tf_op jit(solution)/shard_map/ppermute | solution.py:638
  62.7 0.9 shard_map.83
  63.6 6.6 %collective-permute-done.9.odd = f32[32,8,128]{2,1,0:T(8,128)S(1)} collective-permute-done((f32[32,8,128]{2,1,0:T(8,128)S(1)}, f32[32,8,128]{2,1,0:T(8,128)S(1)}, u32[]{:S(2)}, u32[]{:S(2)}) %collective-permute-start.9) | collective-permute-done | bytes 131104 | tf_op jit(solution)/shard_map/ppermute | solution.py:638
  70.2 1.2 collective-permute-start.10
  71.4 0.9 collective-permute-done.10.far
  72.3 6.1 %shard_map.85 = (f32[16,2,32,256]{3,2,1,0:T(8,128)S(1)}, f32[18,2,32,256]{3,2,1,0:T(8,128)S(1)}, f32[16,8,128]{2,1,0:T(8,128)S(1)}) custom-call(s32[5]{0:T(128)S(1)} %pad_add_fusion.place, f32[16,2,32,256]{3,2,1,0:T(8,128)S(1)} %get-tuple-element.47.r, f32[16,32,256]{2,1,0:T(8,128)S(1)} %get-tuple-element.48.g, f32[18,32,256]{2,1,0:T(8,128)S(1)} %get-tuple-element.49.h, ...), custom_call_target="tpu_custom_call" | custom-call | flops 8999999488 | bytes 27000000 | tf_op jit(solution)/shard_map/pallas_call | solution.py:601
  78.5 0.4 collective-permute-start.11
  78.9 0.9 collective-permute-done.11.partner
  79.8 1.9 %collective-permute-start.12 = (f32[32,8,128]{2,1,0:T(8,128)S(1)}, f32[32,8,128]{2,1,0:T(8,128)S(1)}, u32[]{:S(2)}, u32[]{:S(2)}) collective-permute-start(f32[32,8,128]{2,1,0:T(8,128)S(1)} %pad_maximum_fusion.2), channel_id=1, source_target_pairs={{0,240},{16,32},{32,16},{48,64},{64,48},{80,96},{96,80},{112,128},... | collective-permute-start | bytes 393224 | tf_op jit(solution)/shard_map/ppermute | solution.py:638
  81.7 8.0 %collective-permute-done.12.odd = f32[32,8,128]{2,1,0:T(8,128)S(1)} collective-permute-done((f32[32,8,128]{2,1,0:T(8,128)S(1)}, f32[32,8,128]{2,1,0:T(8,128)S(1)}, u32[]{:S(2)}, u32[]{:S(2)}) %collective-permute-start.12) | collective-permute-done | bytes 131104 | tf_op jit(solution)/shard_map/ppermute | solution.py:638
  89.7 0.9 collective-permute-start.13
  90.7 0.9 collective-permute-done.13.far
  91.6 5.7 %shard_map.86 = (f32[2,16,16,128]{3,2,1,0:T(8,128)S(1)}, f32[2,16,16,128]{3,2,1,0:T(8,128)S(1)}, f32[256,128]{1,0:T(8,128)S(1)}) custom-call(s32[5]{0:T(128)S(1)} %pad_add_fusion.place, f32[4,16,16,128]{3,2,1,0:T(8,128)S(1)} %select_select_fusion.fields.rhs, f32[16,2,32,256]{3,2,1,0:T(8,128)S(1)} %get-tuple-element.62.r, ...), custom_call_target="tpu_custom_call" | custom-call | flops 8999999488 | bytes 27000000 | tf_op jit(solution)/shard_map/pallas_call | solution.py:601
  97.2 22.2 %all_to_all.5 = f32[256,1,128]{2,1,0:T(1,128)S(1)} all-to-all(f32[256,1,128]{2,1,0:T(1,128)S(1)} %bitcast.16), channel_id=1, replica_groups=mesh['gx'=16,'gy'=16] {'gx','gy'}, dimensions={0} | all-to-all | bytes 262144 | tf_op jit(solution)/shard_map/all_to_all | solution.py:708
  119.5 1.0 shard_map.87
  (13 shorter events, 0.1 us)
Async XLA Ops:
  2.9 14.9 %copy-start = (f32[16]{0:T(128)S(1)}, f32[16]{0:T(128)}, u32[]{:S(2)}) copy-start(f32[16]{0:T(128)} %param.11) | copy-start | bytes 196
  2.9 14.9 %copy-start.1 = (f32[16]{0:T(128)S(1)}, f32[16]{0:T(128)}, u32[]{:S(2)}) copy-start(f32[16]{0:T(128)} %param.10) | copy-start | bytes 196
  4.0 15.9 %collective-permute-start.2 = (f32[56,8,128]{2,1,0:T(8,128)S(1)}, f32[56,8,128]{2,1,0:T(8,128)S(1)}, u32[]{:S(2)}, u32[]{:S(2)}) collective-permute-start(f32[56,8,128]{2,1,0:T(8,128)S(1)} %get-tuple-element.37), channel_id=1, source_target_pairs={{0,240},{16,32},{32,16},{48,64},{64,48},{80,96},{96,80},{112,128},... | collective-permute-start | bytes 688136 | tf_op jit(solution)/shard_map/ppermute | solution.py:638
  12.4 17.1 %collective-permute-start = (f32[26,16,128]{2,1,0:T(8,128)S(1)}, f32[26,16,128]{2,1,0:T(8,128)S(1)}, u32[]{:S(2)}, u32[]{:S(2)}) collective-permute-start(f32[26,16,128]{2,1,0:T(8,128)S(1)} %get-tuple-element.35), channel_id=1, source_target_pairs={{0,1},{1,2},{2,3},{3,4},{4,5},{5,6},{6,7},{7,8},{8,9},{9,10},{10,1... | collective-permute-start | bytes 638984 | tf_op jit(solution)/shard_map/ppermute | solution.py:651
  13.1 18.1 %collective-permute-start.1 = (f32[26,16,128]{2,1,0:T(8,128)S(1)}, f32[26,16,128]{2,1,0:T(8,128)S(1)}, u32[]{:S(2)}, u32[]{:S(2)}) collective-permute-start(f32[26,16,128]{2,1,0:T(8,128)S(1)} %get-tuple-element.36), channel_id=1, source_target_pairs={{1,0},{2,1},{3,2},{4,3},{5,4},{6,5},{7,6},{8,7},{9,8},{10,9},{11,1... | collective-permute-start | bytes 638984 | tf_op jit(solution)/shard_map/ppermute | solution.py:651
  31.2 3.7 %copy-start.2 = (f32[16]{0:T(128)S(1)}, f32[16]{0:T(128)}, u32[]{:S(2)}) copy-start(f32[16]{0:T(128)} %param.9) | copy-start | bytes 196
  32.4 16.3 %collective-permute-start.3 = (f32[56,8,256]{2,1,0:T(8,128)S(1)}, f32[56,8,256]{2,1,0:T(8,128)S(1)}, u32[]{:S(2)}, u32[]{:S(2)}) collective-permute-start(f32[56,8,256]{2,1,0:T(8,128)S(1)} %get-tuple-element.45), channel_id=1, source_target_pairs={{0,16},{16,0},{32,48},{48,32},{64,80},{80,64},{96,112},{112,96},{1... | collective-permute-start | bytes 1376264 | tf_op jit(solution)/shard_map/ppermute | solution.py:635
  35.9 4.7 %collective-permute-start.6 = (f32[24,8,128]{2,1,0:T(8,128)S(1)}, f32[24,8,128]{2,1,0:T(8,128)S(1)}, u32[]{:S(2)}, u32[]{:S(2)}) collective-permute-start(f32[24,8,128]{2,1,0:T(8,128)S(1)} %get-tuple-element.54.own), channel_id=1, source_target_pairs={{0,16},{16,0},{32,48},{48,32},{64,80},{80,64},{96,112},{112,96},{1... | collective-permute-start | bytes 294920 | tf_op jit(solution)/shard_map/ppermute | solution.py:635
  36.0 12.6 %collective-permute-start.5 = (f32[28,8,128]{2,1,0:T(8,128)S(1)}, f32[28,8,128]{2,1,0:T(8,128)S(1)}, u32[]{:S(2)}, u32[]{:S(2)}) collective-permute-start(f32[28,8,128]{2,1,0:T(8,128)S(1)} %get-tuple-element.38.after), channel_id=1, source_target_pairs={{1,0},{2,1},{3,2},{4,3},{5,4},{6,5},{7,6},{8,7},{9,8},{10,9},{11,1... | collective-permute-start | bytes 344072 | tf_op jit(solution)/shard_map/ppermute | solution.py:651
  40.6 8.1 %collective-permute-start.4 = (f32[28,8,128]{2,1,0:T(8,128)S(1)}, f32[28,8,128]{2,1,0:T(8,128)S(1)}, u32[]{:S(2)}, u32[]{:S(2)}) collective-permute-start(f32[28,8,128]{2,1,0:T(8,128)S(1)} %get-tuple-element.46), channel_id=1, source_target_pairs={{0,1},{1,2},{2,3},{3,4},{4,5},{5,6},{6,7},{7,8},{8,9},{9,10},{10,1... | collective-permute-start | bytes 344072 | tf_op jit(solution)/shard_map/ppermute | solution.py:651
  40.6 14.3 %collective-permute-start.7 = (f32[48,8,128]{2,1,0:T(8,128)S(1)}, f32[48,8,128]{2,1,0:T(8,128)S(1)}, u32[]{:S(2)}, u32[]{:S(2)}) collective-permute-start(f32[48,8,128]{2,1,0:T(8,128)S(1)} %pad_maximum_fusion), channel_id=1, source_target_pairs={{0,240},{16,32},{32,16},{48,64},{64,48},{80,96},{96,80},{112,128},... | collective-permute-start | bytes 589832 | tf_op jit(solution)/shard_map/ppermute | solution.py:638
  54.9 5.7 %collective-permute-start.8 = (f32[40,8,128]{2,1,0:T(8,128)S(1)}, f32[40,8,128]{2,1,0:T(8,128)S(1)}, u32[]{:S(2)}, u32[]{:S(2)}) collective-permute-start(f32[40,8,128]{2,1,0:T(8,128)S(1)} %shard_map.82), channel_id=1, source_target_pairs={{0,16},{16,0},{32,48},{48,32},{64,80},{80,64},{96,112},{112,96},{1... | collective-permute-start | bytes 491528 | tf_op jit(solution)/shard_map/ppermute | solution.py:635
  60.6 9.7 %collective-permute-start.9 = (f32[32,8,128]{2,1,0:T(8,128)S(1)}, f32[32,8,128]{2,1,0:T(8,128)S(1)}, u32[]{:S(2)}, u32[]{:S(2)}) collective-permute-start(f32[32,8,128]{2,1,0:T(8,128)S(1)} %pad_maximum_fusion.1), channel_id=1, source_target_pairs={{0,240},{16,32},{32,16},{48,64},{64,48},{80,96},{96,80},{112,128},... | collective-permute-start | bytes 393224 | tf_op jit(solution)/shard_map/ppermute | solution.py:638
  70.2 2.1 %collective-permute-start.10 = (f32[16,8,128]{2,1,0:T(8,128)S(1)}, f32[16,8,128]{2,1,0:T(8,128)S(1)}, u32[]{:S(2)}, u32[]{:S(2)}) collective-permute-start(f32[16,8,128]{2,1,0:T(8,128)S(1)} %shard_map.84), channel_id=1, source_target_pairs={{0,16},{16,0},{32,48},{48,32},{64,80},{80,64},{96,112},{112,96},{1... | collective-permute-start | bytes 196616 | tf_op jit(solution)/shard_map/ppermute | solution.py:635
  78.5 1.3 %collective-permute-start.11 = (f32[16,8,128]{2,1,0:T(8,128)S(1)}, f32[16,8,128]{2,1,0:T(8,128)S(1)}, u32[]{:S(2)}, u32[]{:S(2)}) collective-permute-start(f32[16,8,128]{2,1,0:T(8,128)S(1)} %get-tuple-element.64.own), channel_id=1, source_target_pairs={{0,16},{16,0},{32,48},{48,32},{64,80},{80,64},{96,112},{112,96},{1... | collective-permute-start | bytes 196616 | tf_op jit(solution)/shard_map/ppermute | solution.py:635
  79.8 9.9 %collective-permute-start.12 = (f32[32,8,128]{2,1,0:T(8,128)S(1)}, f32[32,8,128]{2,1,0:T(8,128)S(1)}, u32[]{:S(2)}, u32[]{:S(2)}) collective-permute-start(f32[32,8,128]{2,1,0:T(8,128)S(1)} %pad_maximum_fusion.2), channel_id=1, source_target_pairs={{0,240},{16,32},{32,16},{48,64},{64,48},{80,96},{96,80},{112,128},... | collective-permute-start | bytes 393224 | tf_op jit(solution)/shard_map/ppermute | solution.py:638
  89.7 1.8 %collective-permute-start.13 = (f32[16,8,128]{2,1,0:T(8,128)S(1)}, f32[16,8,128]{2,1,0:T(8,128)S(1)}, u32[]{:S(2)}, u32[]{:S(2)}) collective-permute-start(f32[16,8,128]{2,1,0:T(8,128)S(1)} %slice.22), channel_id=1, source_target_pairs={{0,16},{16,0},{32,48},{48,32},{64,80},{80,64},{96,112},{112,96},{1... | collective-permute-start | bytes 196616 | tf_op jit(solution)/shard_map/ppermute | solution.py:635

commit v5 on v4

--- a/solution.py
+++ b/solution.py
@@ -145,56 +145,28 @@
     return fields
 
 
-def fill_message(message, rhs, classes, sea, start, edge):
-    def fields(z):
-        for i in range(2):
-            message[2 * z + i] = rhs(z, i)[pl.ds(start, 8), :]
-        message[32 + z] = classes.at[z][pl.ds(start, 8), :]
-        message.at[52 + z // 8][pl.ds(z % 8, 1), :] = classes.at[z][pl.ds(edge, 1), :]
-        message.at[54 + z // 8][pl.ds(z % 8, 1), :] = sea.at[z][pl.ds(edge, 1), :]
-
-    loop(NZ, fields)
-
-    def quads(j):
-        message[48 + j] = pack_sea([sea[4 * j + i, pl.ds(start, 8), :] for i in range(4)])
-
-    loop(4, quads)
-
-
 MSG_Y = 26
-MSG_X = 56
+MSG_X = 54
 R_TILES = 16
 M_TILES = 24
 
 
-def start_kernel(place, fields, to_left, to_right, message):
-    core = place[0]
-    classes, sea = fields.at[2], fields.at[3]
-
-    def convert(pair):
-        to_left[16 + pair], to_right[16 + pair] = pack_halves(classes[2 * pair], classes[2 * pair + 1])
-
-    loop(8, convert)
-    for j in range(2):
-        quads = [pack_sea([sea[8 * j + 4 * q + i] for i in range(4)]) for q in range(2)]
-        to_left[24 + j], to_right[24 + j] = pack_halves(quads[0], quads[1])
-
+def start_kernel(fields, to_left, to_right):
     def pair(z):
         to_left[z], to_right[z] = pack_halves(fields[0, z], fields[1, z])
 
     loop(NZ, pair)
-    start = pl.multiple_of(8 * core, 8)
-    fill_message(message, lambda z, i: fields.at[i, z], classes, sea, start, 8 - core)
-
-
-def corner_kernel(message, to_left, to_right):
-    def pair(p):
-        to_left[p], to_right[p] = pack_halves(message[2 * p], message[2 * p + 1])
-
-    loop(MSG_X // 2, pair)
-
-
-def rows_kernel(place, fields, from_left, from_right, after, r_out, c_out, s_out, message):
+
+    def class_pair(p):
+        to_left[16 + p], to_right[16 + p] = pack_halves(fields[2, 2 * p], fields[2, 2 * p + 1])
+
+    loop(8, class_pair)
+    for j in range(2):
+        quads = [pack_sea([fields[3, 8 * j + 4 * q + i] for i in range(4)]) for q in range(2)]
+        to_left[24 + j], to_right[24 + j] = pack_halves(quads[0], quads[1])
+
+
+def rows_kernel(place, fields, from_left, from_right, table, r_out, c_out, s_out, msg_x, msg_o, row_c, row_s):
     core = place[0]
     gy = place[2]
     left = lanes(ROWS, COLS) < HALF
@@ -222,8 +194,29 @@
             for i, field in enumerate(unpack_sea(quads[q])):
                 z = 8 * j + 4 * q + i
                 s_out[z] = jnp.concatenate([fields[3, z], field * inside], axis=1)
-    start = pl.multiple_of(8 * (1 - core), 8)
-    fill_message(message, lambda z, i: r_out.at[z, i], c_out, s_out, start, 7 + core)
+    near = pl.multiple_of(8 * (1 - core), 8)
+    far = pl.multiple_of(8 * core, 8)
+    sides = ((msg_o, far, 8 - core, 0), (msg_x, near, 7 + core, 1))
+
+    def copy(z):
+        for message, start, edge, slot in sides:
+            for i in range(2):
+                message[2 * z + i] = r_out[z, i, pl.ds(start, 8), :]
+            message[32 + z] = c_out[z, pl.ds(start, 8), :]
+            row_c[slot, pl.ds(z, 1), :] = c_out[z, pl.ds(edge, 1), :]
+            row_s[slot, pl.ds(z, 1), :] = s_out[z, pl.ds(edge, 1), :]
+
+    loop(NZ, copy)
+
+    def copy_sea(j):
+        for message, start, edge, slot in sides:
+            message[48 + j] = pack_sea([s_out[4 * j + i, pl.ds(start, 8), :] for i in range(4)])
+
+    loop(4, copy_sea)
+    for message, start, edge, slot in sides:
+        root = pick(table[0:1], row_c[slot].astype(jnp.int32)) * row_s[slot]
+        message[52] = root[0:8]
+        message[53] = root[8:16]
 
 
 def material_kernel(c_in, s_in, table, g_out, h_out, k_out, coarse, sums, buffer):
@@ -300,8 +293,8 @@
 
 
 def down_kernel(
-    place, r_own, g_own, h_own, k_own, from_x, from_o, corner_left, corner_right, table,
-    r, g, h, d, inverse, xp, r1, xa, ka, wide, edges, sums, buffer,
+    place, r_own, g_own, h_own, k_own, from_x, from_o, table,
+    r, g, h, d, inverse, xp, r1, xa, ka, edges, sums, buffer,
 ):
     core = place[0]
     gx = place[1]
@@ -324,12 +317,7 @@
 
     loop(NZ, own)
 
-    def widen(p):
-        for i, halo in enumerate(unpack_halves(corner_right[p], corner_left[p])):
-            wide[2 * p + i] = jnp.concatenate([from_o[2 * p + i], halo], axis=1)
-
-    loop(MSG_X // 2, widen)
-    for message, start, scale, slot in ((from_x, 24 * (1 - core), 1.0, 1 - core), (wide, 24 * core, open_side, core)):
+    for message, start, scale, slot in ((from_x, 24 * (1 - core), 1.0, 1 - core), (from_o, 24 * core, open_side, core)):
         start = pl.multiple_of(start, 8)
         valid = scale * ends
 
@@ -346,8 +334,7 @@
 
         loop(4, halo)
         for j in range(2):
-            index = message[52 + j].astype(jnp.int32)
-            edges[slot, 8 * j : 8 * j + 8, :] = pick(table[0:1], index) * (message[54 + j] * valid)
+            edges[slot, 8 * j : 8 * j + 8, :] = message[52 + j] * scale
 
     level = Level(NZ, 1, g, h, inverse, d)
     row = sublanes(EXT0, WIDE)
@@ -579,7 +566,6 @@
 
 COSTS = {
     "start_kernel": 3,
-    "corner_kernel": 1,
     "rows_kernel": 3,
     "material_kernel": 2,
     "down_kernel": 5,
@@ -652,20 +638,16 @@
 
     part = lax.broadcasted_iota(jnp.int32, (4, *classes.shape), 0)
     materials = jnp.where(part == 2, classes[None], sea_mask[None]).astype(F32)
-    fields = jnp.where(part == 0, right_side[0:1], jnp.where(part == 1, right_side[1:2], materials))
-    to_left, to_right, msg_o = call(
-        start_kernel, (place, fields), [(MSG_Y, ROWS, COLS), (MSG_Y, ROWS, COLS), (MSG_X, 8, COLS)]
+    twice = jnp.broadcast_to(right_side[None], (2, *right_side.shape)).reshape(part.shape)
+    fields = jnp.where(part < 2, twice, materials)
+    to_left, to_right = call(start_kernel, (fields,), [(MSG_Y, ROWS, COLS)] * 2, place=False)
+    r_own, c_own, s_own, msg_x, msg_o = call(
+        rows_kernel,
+        (place, fields, *both_sides(to_left, to_right), table),
+        [(NZ, 2, ROWS, WIDE), (NZ, ROWS, WIDE), (NZ, ROWS, WIDE), (MSG_X, 8, WIDE), (MSG_X, 8, WIDE)],
+        [(2, NZ, WIDE), (2, NZ, WIDE)],
     )
     from_o = across_chips(msg_o)
-    from_left, from_right = both_sides(to_left, to_right)
-    corner_tiles = call(corner_kernel, (from_o,), [(MSG_X // 2, 8, COLS)] * 2, place=False)
-    corners = both_sides(*corner_tiles)
-    r_own, c_own, s_own, msg_x = call(
-        rows_kernel,
-        (place, fields, from_left, from_right, corner_tiles[0]),
-        [(NZ, 2, ROWS, WIDE), (NZ, ROWS, WIDE), (NZ, ROWS, WIDE), (MSG_X, 8, WIDE)],
-        far={4: pl.ANY},
-    )
     from_x = on_chip(msg_x)
     g_own, h_own, k_own, packed = call(
         material_kernel,
@@ -678,9 +660,9 @@
     packed_odd = neighbours(packed, packed_partner)
     r, g, h, d, inverse, xp, r1 = call(
         down_kernel,
-        (place, r_own, g_own, h_own, k_own, from_x, from_o, *corners, table),
+        (place, r_own, g_own, h_own, k_own, from_x, from_o, table),
         [FIELD0, (NZ, EXT0, WIDE), (NZ + 2, EXT0, WIDE), (NZ, EXT0, WIDE), (NZ, EXT0, WIDE), PADDED0, (R_TILES, 8, COLS)],
-        [PADDED0, (NZ, EXT0, WIDE), (MSG_X, 8, WIDE), (2, NZ, WIDE), SUMS, BUFFER],
+        [PADDED0, (NZ, EXT0, WIDE), (2, NZ, WIDE), SUMS, BUFFER],
     )
     received = on_chip(call(join_kernel, (r1, packed_odd), [(R_TILES + M_TILES, 8, COLS)], place=False)[0])
     material = (packed, packed_partner, packed_odd, received[R_TILES:])

time: 121 us -> 121 us (level)
  blocking collectives: 22.2 us -> 30.7 us
  starting transfers between devices: 32.6 us -> 29.6 us
  waiting for transfers between devices: 41.1 us -> 38.9 us
  Pallas kernels: 21.4 us -> 19.6 us
    ppermute x2 -> x1, waiting for transfers between devices: 16.7 us -> 3.88 us  [both_sides(): lax.ppermute(to_right, 'gy', forward)]
    ppermute x4, waiting for transfers between devices: 18.9 us -> 28.5 us  [across_chips(): return lax.ppermute(value, 'gx', pairs_across)]
    all_to_all x1, blocking collectives: 22.2 us -> 30.7 us  [shards(): lax.all_to_all(sums.reshape(count, 1, COLS), ('gx', 'gy'), 0, 0)]
    ppermute x2 -> x1, starting transfers between devices: 9.21 us -> 4.99 us  [both_sides(): lax.ppermute(to_left, 'gy', backward)]
    ppermute x4, starting transfers between devices: 12.8 us -> 9.26 us  [across_chips(): return lax.ppermute(value, 'gx', pairs_across)]
    ppermute x6, starting transfers between devices: 9.89 us -> 12.8 us  [on_chip(): return lax.ppermute(value, 'gx', pairs_on_chip)]
    pallas_call x11 -> x10, Pallas kernels: 21.4 us -> 19.6 us  [call(): pl.pallas_call(kernel, out_shape=[jax.ShapeDtypeStruct(shape, F32) for sh...]
    ppermute x2 -> x1, starting transfers between devices: 0.74 us -> 2.54 us  [both_sides(): lax.ppermute(to_right, 'gy', forward)]
  transfers between devices with their start and end apart: 14 -> 12, of which waited for: 11 -> 11; matrix products, arithmetic and copies ran while one was open for 0% -> 0% of each run, Pallas kernels for 5% -> 4%
where the time goes in v5:
time: 121 us
  waiting for transfers between devices  38.9 us (32%)
  blocking collectives  30.7 us (25%)
  starting transfers between devices  29.6 us (24%)
  Pallas kernels  19.6 us (16%)
  other arithmetic  1.34 us (1%)
    all_to_all x1, blocking collectives, shards(): lax.all_to_all(sums.reshape(count, 1, COLS), ('gx', 'gy'), 0, 0)  30.7 us
    ppermute x4, waiting for transfers between devices, across_chips(): return lax.ppermute(value, 'gx', pairs_across)  28.5 us
    pallas_call x10, Pallas kernels, call(): pl.pallas_call(kernel, out_shape=[jax.ShapeDtypeStruct(shape, F32) for sh...  19.6 us
    ppermute x6, starting transfers between devices, on_chip(): return lax.ppermute(value, 'gx', pairs_on_chip)  12.8 us
    ppermute x4, starting transfers between devices, across_chips(): return lax.ppermute(value, 'gx', pairs_across)  9.26 us
    ppermute x1, starting transfers between devices, both_sides(): lax.ppermute(to_left, 'gy', backward)  4.99 us
    ppermute x6, waiting for transfers between devices, on_chip(): return lax.ppermute(value, 'gx', pairs_on_chip)  4.68 us
    ppermute x1, waiting for transfers between devices, both_sides(): lax.ppermute(to_right, 'gy', forward)  3.88 us
  transfers between devices with their start and end apart: 12, of which 11 were waited for; matrix products, arithmetic and copies ran while one was open for 0% of the time, Pallas kernels for 4%

profile of v5, /device:TPU:1, one launch (start us, length us, event | category | flops | bytes accessed | tf_op | source)
XLA Modules:
  0.0 120.9 jit_solution(10409346575522412889)
XLA Ops:
  0.6 1.2 bitcast_select_fusion.fields.rhs
  1.9 0.0 copy-start
  1.9 0.0 copy-start.1
  1.9 0.0 copy-start.2
  1.9 0.4 shard_map.77
  2.2 2.5 %collective-permute-start = (f32[26,16,128]{2,1,0:T(8,128)S(1)}, f32[26,16,128]{2,1,0:T(8,128)S(1)}, u32[]{:S(2)}, u32[]{:S(2)}) collective-permute-start(f32[26,16,128]{2,1,0:T(8,128)S(1)} %get-tuple-element.33), channel_id=1, source_target_pairs={{0,1},{1,2},{2,3},{3,4},{4,5},{5,6},{6,7},{7,8},{8,9},{9,10},{10,1... | collective-permute-start | bytes 638984 | tf_op jit(solution)/shard_map/ppermute | solution.py:637
  4.8 5.0 %collective-permute-start.1 = (f32[26,16,128]{2,1,0:T(8,128)S(1)}, f32[26,16,128]{2,1,0:T(8,128)S(1)}, u32[]{:S(2)}, u32[]{:S(2)}) collective-permute-start(f32[26,16,128]{2,1,0:T(8,128)S(1)} %get-tuple-element.34), channel_id=1, source_target_pairs={{1,0},{2,1},{3,2},{4,3},{5,4},{6,5},{7,6},{8,7},{9,8},{10,9},{11,1... | collective-permute-start | bytes 638984 | tf_op jit(solution)/shard_map/ppermute | solution.py:637
  9.8 0.0 copy-done
  9.8 0.0 copy-done.1
  9.8 0.1 pad_add_fusion.place
  9.9 0.0 copy-done.2
  9.9 3.9 %collective-permute-done.from_left = f32[26,16,128]{2,1,0:T(8,128)S(1)} collective-permute-done((f32[26,16,128]{2,1,0:T(8,128)S(1)}, f32[26,16,128]{2,1,0:T(8,128)S(1)}, u32[]{:S(2)}, u32[]{:S(2)}) %collective-permute-start) | collective-permute-done | bytes 213024 | tf_op jit(solution)/shard_map/ppermute | solution.py:637
  13.8 1.8 %collective-permute-done.1.from_right = f32[26,16,128]{2,1,0:T(8,128)S(1)} collective-permute-done((f32[26,16,128]{2,1,0:T(8,128)S(1)}, f32[26,16,128]{2,1,0:T(8,128)S(1)}, u32[]{:S(2)}, u32[]{:S(2)}) %collective-permute-start.1) | collective-permute-done | bytes 213024 | tf_op jit(solution)/shard_map/ppermute | solution.py:637
  15.6 1.1 shard_map.78
  16.7 2.2 %collective-permute-start.2 = (f32[54,8,256]{2,1,0:T(8,128)S(1)}, f32[54,8,256]{2,1,0:T(8,128)S(1)}, u32[]{:S(2)}, u32[]{:S(2)}) collective-permute-start(f32[54,8,256]{2,1,0:T(8,128)S(1)} %get-tuple-element.41), channel_id=1, source_target_pairs={{0,16},{16,0},{32,48},{48,32},{64,80},{80,64},{96,112},{112,96},{1... | collective-permute-start | bytes 1327112 | tf_op jit(solution)/shard_map/ppermute | solution.py:621
  18.9 5.3 %collective-permute-start.3 = (f32[54,8,256]{2,1,0:T(8,128)S(1)}, f32[54,8,256]{2,1,0:T(8,128)S(1)}, u32[]{:S(2)}, u32[]{:S(2)}) collective-permute-start(f32[54,8,256]{2,1,0:T(8,128)S(1)} %get-tuple-element.42), channel_id=1, source_target_pairs={{0,240},{16,32},{32,16},{48,64},{64,48},{80,96},{96,80},{112,128},... | collective-permute-start | bytes 1327112 | tf_op jit(solution)/shard_map/ppermute | solution.py:624
  24.2 0.9 shard_map.79
  25.2 2.9 %collective-permute-start.4 = (f32[24,8,128]{2,1,0:T(8,128)S(1)}, f32[24,8,128]{2,1,0:T(8,128)S(1)}, u32[]{:S(2)}, u32[]{:S(2)}) collective-permute-start(f32[24,8,128]{2,1,0:T(8,128)S(1)} %get-tuple-element.50.own), channel_id=1, source_target_pairs={{0,16},{16,0},{32,48},{48,32},{64,80},{80,64},{96,112},{112,96},{1... | collective-permute-start | bytes 294920 | tf_op jit(solution)/shard_map/ppermute | solution.py:621
  28.1 0.9 collective-permute-done.4.partner
  29.1 0.1 collective-permute-start.5
  29.2 0.0 collective-permute-done.2.from_x
  29.2 6.7 %collective-permute-done.3.from_o = f32[54,8,256]{2,1,0:T(8,128)S(1)} collective-permute-done((f32[54,8,256]{2,1,0:T(8,128)S(1)}, f32[54,8,256]{2,1,0:T(8,128)S(1)}, u32[]{:S(2)}, u32[]{:S(2)}) %collective-permute-start.3) | collective-permute-done | bytes 442400 | tf_op jit(solution)/shard_map/ppermute | solution.py:624
  35.9 3.5 %shard_map.80 = (f32[16,2,32,256]{3,2,1,0:T(8,128)S(1)}, f32[16,32,256]{2,1,0:T(8,128)S(1)}, f32[18,32,256]{2,1,0:T(8,128)S(1)}, f32[16,32,256]{2,1,0:T(8,128)S(...) custom-call(s32[5]{0:T(128)S(1)} %pad_add_fusion.place, ...), custom_call_target="tpu_custom_call" | custom-call | flops 5000000000 | bytes 15000000 | tf_op jit(solution)/shard_map/pallas_call | solution.py:587
  39.4 0.7 collective-permute-done.5.odd
  40.2 2.2 %collective-permute-start.6 = (f32[40,8,128]{2,1,0:T(8,128)S(1)}, f32[40,8,128]{2,1,0:T(8,128)S(1)}, u32[]{:S(2)}, u32[]{:S(2)}) collective-permute-start(f32[40,8,128]{2,1,0:T(8,128)S(1)} %shard_map.81), channel_id=1, source_target_pairs={{0,16},{16,0},{32,48},{48,32},{64,80},{80,64},{96,112},{112,96},{1... | collective-permute-start | bytes 491528 | tf_op jit(solution)/shard_map/ppermute | solution.py:621
  42.3 1.0 collective-permute-done.6
  43.4 3.8 %collective-permute-start.7 = (f32[32,8,128]{2,1,0:T(8,128)S(1)}, f32[32,8,128]{2,1,0:T(8,128)S(1)}, u32[]{:S(2)}, u32[]{:S(2)}) collective-permute-start(f32[32,8,128]{2,1,0:T(8,128)S(1)} %pad_maximum_fusion.1), channel_id=1, source_target_pairs={{0,240},{16,32},{32,16},{48,64},{64,48},{80,96},{96,80},{112,128},... | collective-permute-start | bytes 393224 | tf_op jit(solution)/shard_map/ppermute | solution.py:624
  47.1 0.9 shard_map.82
  48.1 12.8 %collective-permute-done.7.odd = f32[32,8,128]{2,1,0:T(8,128)S(1)} collective-permute-done((f32[32,8,128]{2,1,0:T(8,128)S(1)}, f32[32,8,128]{2,1,0:T(8,128)S(1)}, u32[]{:S(2)}, u32[]{:S(2)}) %collective-permute-start.7) | collective-permute-done | bytes 131104 | tf_op jit(solution)/shard_map/ppermute | solution.py:624
  60.9 2.6 %collective-permute-start.8 = (f32[16,8,128]{2,1,0:T(8,128)S(1)}, f32[16,8,128]{2,1,0:T(8,128)S(1)}, u32[]{:S(2)}, u32[]{:S(2)}) collective-permute-start(f32[16,8,128]{2,1,0:T(8,128)S(1)} %shard_map.83), channel_id=1, source_target_pairs={{0,16},{16,0},{32,48},{48,32},{64,80},{80,64},{96,112},{112,96},{1... | collective-permute-start | bytes 196616 | tf_op jit(solution)/shard_map/ppermute | solution.py:621
  63.5 0.9 collective-permute-done.8.far
  64.4 6.1 %shard_map.84 = (f32[16,2,32,256]{3,2,1,0:T(8,128)S(1)}, f32[18,2,32,256]{3,2,1,0:T(8,128)S(1)}, f32[16,8,128]{2,1,0:T(8,128)S(1)}) custom-call(s32[5]{0:T(128)S(1)} %pad_add_fusion.place, f32[16,2,32,256]{3,2,1,0:T(8,128)S(1)} %get-tuple-element.43.r, f32[16,32,256]{2,1,0:T(8,128)S(1)} %get-tuple-element.44.g, f32[18,32,256]{2,1,0:T(8,128)S(1)} %get-tuple-element.45.h, ...), custom_call_target="tpu_custom_call" | custom-call | flops 8999999488 | bytes 27000000 | tf_op jit(solution)/shard_map/pallas_call | solution.py:587
  70.5 0.4 collective-permute-start.9
  70.9 0.9 collective-permute-done.9.partner
  71.8 0.1 collective-permute-start.10
  71.9 8.3 %collective-permute-done.10.odd = f32[32,8,128]{2,1,0:T(8,128)S(1)} collective-permute-done((f32[32,8,128]{2,1,0:T(8,128)S(1)}, f32[32,8,128]{2,1,0:T(8,128)S(1)}, u32[]{:S(2)}, u32[]{:S(2)}) %collective-permute-start.10) | collective-permute-done | bytes 131104 | tf_op jit(solution)/shard_map/ppermute | solution.py:624
  80.2 2.5 %collective-permute-start.11 = (f32[16,8,128]{2,1,0:T(8,128)S(1)}, f32[16,8,128]{2,1,0:T(8,128)S(1)}, u32[]{:S(2)}, u32[]{:S(2)}) collective-permute-start(f32[16,8,128]{2,1,0:T(8,128)S(1)} %slice.14), channel_id=1, source_target_pairs={{0,16},{16,0},{32,48},{48,32},{64,80},{80,64},{96,112},{112,96},{1... | collective-permute-start | bytes 196616 | tf_op jit(solution)/shard_map/ppermute | solution.py:621
  82.7 0.9 collective-permute-done.11.far
  83.6 5.6 %shard_map.85 = (f32[2,16,16,128]{3,2,1,0:T(8,128)S(1)}, f32[2,16,16,128]{3,2,1,0:T(8,128)S(1)}, f32[256,128]{1,0:T(8,128)S(1)}) custom-call(s32[5]{0:T(128)S(1)} %pad_add_fusion.place, f32[4,16,16,128]{3,2,1,0:T(8,128)S(1)} %bitcast_select_fusion.fields.rhs, f32[16,2,32,256]{3,2,1,0:T(8,128)S(1)} %get-tuple-element.58.r, ...), custom_call_target="tpu_custom_call" | custom-call | flops 8999999488 | bytes 27000000 | tf_op jit(solution)/shard_map/pallas_call | solution.py:587
  89.2 30.7 %all_to_all.5 = f32[256,1,128]{2,1,0:T(1,128)S(1)} all-to-all(f32[256,1,128]{2,1,0:T(1,128)S(1)} %bitcast.14), channel_id=1, replica_groups=mesh['gx'=16,'gy'=16] {'gx','gy'}, dimensions={0} | all-to-all | bytes 262144 | tf_op jit(solution)/shard_map/all_to_all | solution.py:690
  120.0 1.0 shard_map.86
  (12 shorter events, 0.1 us)
Async XLA Ops:
  1.9 7.9 %copy-start = (f32[16]{0:T(128)S(1)}, f32[16]{0:T(128)}, u32[]{:S(2)}) copy-start(f32[16]{0:T(128)} %param.11) | copy-start | bytes 196
  1.9 7.9 %copy-start.1 = (f32[16]{0:T(128)S(1)}, f32[16]{0:T(128)}, u32[]{:S(2)}) copy-start(f32[16]{0:T(128)} %param.10) | copy-start | bytes 196
  1.9 8.0 %copy-start.2 = (f32[16]{0:T(128)S(1)}, f32[16]{0:T(128)}, u32[]{:S(2)}) copy-start(f32[16]{0:T(128)} %param.9) | copy-start | bytes 196
  2.2 11.5 %collective-permute-start = (f32[26,16,128]{2,1,0:T(8,128)S(1)}, f32[26,16,128]{2,1,0:T(8,128)S(1)}, u32[]{:S(2)}, u32[]{:S(2)}) collective-permute-start(f32[26,16,128]{2,1,0:T(8,128)S(1)} %get-tuple-element.33), channel_id=1, source_target_pairs={{0,1},{1,2},{2,3},{3,4},{4,5},{5,6},{6,7},{7,8},{8,9},{9,10},{10,1... | collective-permute-start | bytes 638984 | tf_op jit(solution)/shard_map/ppermute | solution.py:637
  4.8 10.8 %collective-permute-start.1 = (f32[26,16,128]{2,1,0:T(8,128)S(1)}, f32[26,16,128]{2,1,0:T(8,128)S(1)}, u32[]{:S(2)}, u32[]{:S(2)}) collective-permute-start(f32[26,16,128]{2,1,0:T(8,128)S(1)} %get-tuple-element.34), channel_id=1, source_target_pairs={{1,0},{2,1},{3,2},{4,3},{5,4},{6,5},{7,6},{8,7},{9,8},{10,9},{11,1... | collective-permute-start | bytes 638984 | tf_op jit(solution)/shard_map/ppermute | solution.py:637
  16.7 12.4 %collective-permute-start.2 = (f32[54,8,256]{2,1,0:T(8,128)S(1)}, f32[54,8,256]{2,1,0:T(8,128)S(1)}, u32[]{:S(2)}, u32[]{:S(2)}) collective-permute-start(f32[54,8,256]{2,1,0:T(8,128)S(1)} %get-tuple-element.41), channel_id=1, source_target_pairs={{0,16},{16,0},{32,48},{48,32},{64,80},{80,64},{96,112},{112,96},{1... | collective-permute-start | bytes 1327112 | tf_op jit(solution)/shard_map/ppermute | solution.py:621
  18.9 16.9 %collective-permute-start.3 = (f32[54,8,256]{2,1,0:T(8,128)S(1)}, f32[54,8,256]{2,1,0:T(8,128)S(1)}, u32[]{:S(2)}, u32[]{:S(2)}) collective-permute-start(f32[54,8,256]{2,1,0:T(8,128)S(1)} %get-tuple-element.42), channel_id=1, source_target_pairs={{0,240},{16,32},{32,16},{48,64},{64,48},{80,96},{96,80},{112,128},... | collective-permute-start | bytes 1327112 | tf_op jit(solution)/shard_map/ppermute | solution.py:624
  25.2 3.9 %collective-permute-start.4 = (f32[24,8,128]{2,1,0:T(8,128)S(1)}, f32[24,8,128]{2,1,0:T(8,128)S(1)}, u32[]{:S(2)}, u32[]{:S(2)}) collective-permute-start(f32[24,8,128]{2,1,0:T(8,128)S(1)} %get-tuple-element.50.own), channel_id=1, source_target_pairs={{0,16},{16,0},{32,48},{48,32},{64,80},{80,64},{96,112},{112,96},{1... | collective-permute-start | bytes 294920 | tf_op jit(solution)/shard_map/ppermute | solution.py:621
  29.1 11.1 %collective-permute-start.5 = (f32[48,8,128]{2,1,0:T(8,128)S(1)}, f32[48,8,128]{2,1,0:T(8,128)S(1)}, u32[]{:S(2)}, u32[]{:S(2)}) collective-permute-start(f32[48,8,128]{2,1,0:T(8,128)S(1)} %pad_maximum_fusion), channel_id=1, source_target_pairs={{0,240},{16,32},{32,16},{48,64},{64,48},{80,96},{96,80},{112,128},... | collective-permute-start | bytes 589832 | tf_op jit(solution)/shard_map/ppermute | solution.py:624
  40.2 3.2 %collective-permute-start.6 = (f32[40,8,128]{2,1,0:T(8,128)S(1)}, f32[40,8,128]{2,1,0:T(8,128)S(1)}, u32[]{:S(2)}, u32[]{:S(2)}) collective-permute-start(f32[40,8,128]{2,1,0:T(8,128)S(1)} %shard_map.81), channel_id=1, source_target_pairs={{0,16},{16,0},{32,48},{48,32},{64,80},{80,64},{96,112},{112,96},{1... | collective-permute-start | bytes 491528 | tf_op jit(solution)/shard_map/ppermute | solution.py:621
  43.4 17.5 %collective-permute-start.7 = (f32[32,8,128]{2,1,0:T(8,128)S(1)}, f32[32,8,128]{2,1,0:T(8,128)S(1)}, u32[]{:S(2)}, u32[]{:S(2)}) collective-permute-start(f32[32,8,128]{2,1,0:T(8,128)S(1)} %pad_maximum_fusion.1), channel_id=1, source_target_pairs={{0,240},{16,32},{32,16},{48,64},{64,48},{80,96},{96,80},{112,128},... | collective-permute-start | bytes 393224 | tf_op jit(solution)/shard_map/ppermute | solution.py:624
  60.9 3.5 %collective-permute-start.8 = (f32[16,8,128]{2,1,0:T(8,128)S(1)}, f32[16,8,128]{2,1,0:T(8,128)S(1)}, u32[]{:S(2)}, u32[]{:S(2)}) collective-permute-start(f32[16,8,128]{2,1,0:T(8,128)S(1)} %shard_map.83), channel_id=1, source_target_pairs={{0,16},{16,0},{32,48},{48,32},{64,80},{80,64},{96,112},{112,96},{1... | collective-permute-start | bytes 196616 | tf_op jit(solution)/shard_map/ppermute | solution.py:621
  70.5 1.3 %collective-permute-start.9 = (f32[16,8,128]{2,1,0:T(8,128)S(1)}, f32[16,8,128]{2,1,0:T(8,128)S(1)}, u32[]{:S(2)}, u32[]{:S(2)}) collective-permute-start(f32[16,8,128]{2,1,0:T(8,128)S(1)} %get-tuple-element.60.own), channel_id=1, source_target_pairs={{0,16},{16,0},{32,48},{48,32},{64,80},{80,64},{96,112},{112,96},{1... | collective-permute-start | bytes 196616 | tf_op jit(solution)/shard_map/ppermute | solution.py:621
  71.8 8.4 %collective-permute-start.10 = (f32[32,8,128]{2,1,0:T(8,128)S(1)}, f32[32,8,128]{2,1,0:T(8,128)S(1)}, u32[]{:S(2)}, u32[]{:S(2)}) collective-permute-start(f32[32,8,128]{2,1,0:T(8,128)S(1)} %pad_maximum_fusion.2), channel_id=1, source_target_pairs={{0,240},{16,32},{32,16},{48,64},{64,48},{80,96},{96,80},{112,128},... | collective-permute-start | bytes 393224 | tf_op jit(solution)/shard_map/ppermute | solution.py:624
  80.2 3.4 %collective-permute-start.11 = (f32[16,8,128]{2,1,0:T(8,128)S(1)}, f32[16,8,128]{2,1,0:T(8,128)S(1)}, u32[]{:S(2)}, u32[]{:S(2)}) collective-permute-start(f32[16,8,128]{2,1,0:T(8,128)S(1)} %slice.14), channel_id=1, source_target_pairs={{0,16},{16,0},{32,48},{48,32},{64,80},{80,64},{96,112},{112,96},{1... | collective-permute-start | bytes 196616 | tf_op jit(solution)/shard_map/ppermute | solution.py:621

commit v6 on v5

--- a/solution.py
+++ b/solution.py
@@ -357,7 +357,7 @@
 def coarse_coefficients(place, pieces, g1, h1, d1, i1, g2, h2, i2, w1, k1, u1, k2, buffer):
     core = place[0]
     clear_ends(h1, h2)
-    own, partner, odd, far = pieces
+    own, partner, near, far, second = pieces
     low = jnp.where(place[1] >= 2, 1.0, 0.0)
     high = jnp.where(place[1] < place[3] - 2, 1.0, 0.0)
     near_side = jnp.where(core == 0, low, high)
@@ -369,7 +369,7 @@
     def assemble(z):
         for i, field in enumerate((w1, u1, k1)):
             j = 8 * i + z
-            tiles = (own[j], partner[j], odd[j], odd[M_TILES + j], far[j])
+            tiles = (own[j], partner[j], near[j], far[j], second[j])
             for start, tile, scale in zip(starts, tiles, scales):
                 field[z, pl.ds(start, 8), :] = tile * scale if i < 2 else tile
 
@@ -409,7 +409,7 @@
 
 
 def coarse_solve(core, one, two, pieces, r1, xa1, xb1, r2, xa2, xb2, buffer):
-    own, partner, odd, far = pieces
+    own, partner, near, far, second = pieces
     clear_ends(xa1, xb1, xa2, xb2)
     starts = (16, 24 - 16 * core, 8 + 16 * core, 32 * core, 32 - 32 * core)
     starts = [s if isinstance(s, int) else pl.multiple_of(s, 8) for s in starts]
@@ -417,7 +417,7 @@
     def assemble(z):
         for i in range(2):
             j = 2 * z + i
-            tiles = (own[j], partner[j], odd[j], odd[R_TILES + j], far[j])
+            tiles = (own[j], partner[j], near[j], far[j], second[j])
             for start, tile in zip(starts, tiles):
                 r1[z, i, pl.ds(start, 8), :] = tile
 
@@ -464,25 +464,24 @@
     loop(NZ // 2, body)
 
 
-def join_kernel(r1, odd, message):
-    message[0:R_TILES] = r1[...]
-    message[R_TILES:] = odd[0:M_TILES]
-
-
-def near_kernel(odd, after, near):
-    near[...] = odd[0:R_TILES]
+def after_kernel(value, after, out):
+    out[...] = value[...]
+
+
+def near_kernel(value, out):
+    out[...] = value[...]
 
 
 def coarse_kernel(
-    place, own, partner, odd, far, g1, h1, d1, i1, g2, h2, i2, w1, k1, u1, k2, buffer
+    place, own, partner, near, far, second, g1, h1, d1, i1, g2, h2, i2, w1, k1, u1, k2, buffer
 ):
     coarse_coefficients(
-        place, (own, partner, odd, far), g1, h1, d1, i1, g2, h2, i2, w1, k1, u1, k2, buffer
+        place, (own, partner, near, far, second), g1, h1, d1, i1, g2, h2, i2, w1, k1, u1, k2, buffer
     )
 
 
 def middle_kernel(
-    place, r, g, h, d, inverse, xp, own, partner, odd, far, g1, h1, d1, i1, g2, h2, i2,
+    place, r, g, h, d, inverse, xp, own, partner, near, far, second, g1, h1, d1, i1, g2, h2, i2,
     z_out, xp_out, r1_out,
     xa, xb, r1, xa1, xb1, r2, xa2, xb2, wide, sums, buffer,
 ):
@@ -490,7 +489,7 @@
     zero = Level(NZ, 1, g, h, inverse, d)
     one = Level(8, 1, g1, h1, i1, d1)
     two = Level(4, 2, g2, h2, i2)
-    coarse_solve(core, one, two, (own, partner, odd, far), r1, xa1, xb1, r2, xa2, xb2, buffer)
+    coarse_solve(core, one, two, (own, partner, near, far, second), r1, xa1, xb1, r2, xa2, xb2, buffer)
     clear_ends(xa, xb, xp_out)
     fine_correct(zero, xa, xp, xa1, wide, buffer)
     zero.update(xb, xa, r, FINE[0])
@@ -507,7 +506,7 @@
 
 
 def last_kernel(
-    place, rhs, r, g, h, d, inverse, xp, own, partner, odd, far, g1, h1, d1, i1, g2, h2, i2,
+    place, rhs, r, g, h, d, inverse, xp, own, partner, near, far, second, g1, h1, d1, i1, g2, h2, i2,
     direction, image, sums,
     xa, xb, r1, xa1, xb1, r2, xa2, xb2, wide, totals, buffer,
 ):
@@ -515,7 +514,7 @@
     zero = Level(NZ, 1, g, h, inverse, d)
     one = Level(8, 1, g1, h1, i1, d1)
     two = Level(4, 2, g2, h2, i2)
-    coarse_solve(core, one, two, (own, partner, odd, far), r1, xa1, xb1, r2, xa2, xb2, buffer)
+    coarse_solve(core, one, two, (own, partner, near, far, second), r1, xa1, xb1, r2, xa2, xb2, buffer)
     clear_ends(xa, xb)
     fine_correct(zero, xa, xp, xa1, wide, buffer)
     zero.update(xb, xa, r, FINE[0])
@@ -569,8 +568,8 @@
     "rows_kernel": 3,
     "material_kernel": 2,
     "down_kernel": 5,
-    "join_kernel": 1,
-    "near_kernel": 1,
+    "after_kernel": 1,
+    "near_kernel": 30,
     "coarse_kernel": 3,
     "middle_kernel": 9,
     "last_kernel": 9,
@@ -617,18 +616,22 @@
     pairs_on_chip = [(i, i ^ 1) for i in range(count_x)]
     pairs_across = [(i, (i + 1 if i % 2 else i - 1) % count_x) for i in range(count_x)]
 
+    pairs_beyond = [(i, (i - 2 if i % 2 else i + 2) % count_x) for i in range(count_x)]
+
     def on_chip(value):
         return lax.ppermute(value, "gx", pairs_on_chip)
 
     def across_chips(value):
         return lax.ppermute(value, "gx", pairs_across)
 
-    def neighbours(own, partner):
-        return across_chips(jnp.concatenate([own, partner], axis=0))
-
-    def rows_of(own, partner):
-        odd = neighbours(own, partner)
-        return own, partner, odd, on_chip(odd[: own.shape[0]])
+    def after(value, other):
+        return call(after_kernel, (value, other), [value.shape], place=False, far={1: pl.ANY})[0]
+
+    def rows_of(own):
+        near = across_chips(own)
+        far = lax.ppermute(own, "gx", pairs_beyond)
+        near_copy = call(near_kernel, (near,), [near.shape], place=False)[0]
+        return own, on_chip(own), near, far, on_chip(near_copy)
 
     forward = [(i, (i + 1) % count_y) for i in range(count_y)]
     backward = [(target, source) for source, target in forward]
@@ -656,34 +659,30 @@
         [(M_TILES, 8, WIDE), BUFFER],
         place=False,
     )
-    packed_partner = on_chip(packed)
-    packed_odd = neighbours(packed, packed_partner)
+    material = after(packed, from_o)
     r, g, h, d, inverse, xp, r1 = call(
         down_kernel,
         (place, r_own, g_own, h_own, k_own, from_x, from_o, table),
         [FIELD0, (NZ, EXT0, WIDE), (NZ + 2, EXT0, WIDE), (NZ, EXT0, WIDE), (NZ, EXT0, WIDE), PADDED0, (R_TILES, 8, COLS)],
         [PADDED0, (NZ, EXT0, WIDE), (2, NZ, WIDE), SUMS, BUFFER],
     )
-    received = on_chip(call(join_kernel, (r1, packed_odd), [(R_TILES + M_TILES, 8, COLS)], place=False)[0])
-    material = (packed, packed_partner, packed_odd, received[R_TILES:])
+    near = lax.ppermute(material, "gx", pairs_across)
+    material = (material, on_chip(material), near, lax.ppermute(material, "gx", pairs_beyond), on_chip(after(near, r1)))
     one = [(8, EXT1, COLS), (10, EXT1, COLS), (8, EXT1, COLS), (8, EXT1, COLS)]
     two = [(4, EXT2, COLS), (6, EXT2, COLS), (4, EXT2, COLS)]
     coarse = call(
         coarse_kernel, (place, *material), [*one, *two], [one[0], one[0], one[0], two[0], BUFFER]
     )
-    partner = received[:R_TILES]
-    odd = neighbours(r1, partner)
-    near = call(near_kernel, (odd, coarse[0]), [(R_TILES, 8, COLS)], place=False, far={1: pl.ANY})[0]
     r, xp, r1 = call(
         middle_kernel,
-        (place, r, g, h, d, inverse, xp, r1, partner, odd, on_chip(near), *coarse),
+        (place, r, g, h, d, inverse, xp, *rows_of(r1), *coarse),
         [FIELD0, PADDED0, (R_TILES, 8, COLS)],
         [PADDED0, PADDED0, *COARSE_SCRATCH, SUMS, BUFFER],
     )
     count = count_x * count_y
     direction, image, sums = call(
         last_kernel,
-        (place, fields, r, g, h, d, inverse, xp, *rows_of(r1, on_chip(r1)), *coarse),
+        (place, fields, r, g, h, d, inverse, xp, *rows_of(r1), *coarse),
         [(2, NZ, ROWS, COLS)] * 2 + [(count, COLS)],
         [PADDED0, PADDED0, *COARSE_SCRATCH, (4, ROWS, COLS), BUFFER],
     )

time: 121 us -> 124 us (1.025)
  waiting for transfers between devices: 38.9 us -> 20.6 us
  starting transfers between devices: 29.6 us -> 45.2 us
  blocking collectives: 30.7 us -> 36.7 us
    ppermute x0 -> x4, starting transfers between devices: none -> 17 us  [the longest x2 9.64 us: rows_of(): far = lax.ppermute(own, 'gx', pairs_beyond)]
    ppermute x4 -> x3, waiting for transfers between devices: 28.5 us -> 13.4 us  [across_chips(): return lax.ppermute(value, 'gx', pairs_across)]
    all_to_all x1, blocking collectives: 30.7 us -> 36.7 us  [shards(): lax.all_to_all(sums.reshape(count, 1, COLS), ('gx', 'gy'), 0, 0)]
    ppermute x6 -> x7, starting transfers between devices: 12.8 us -> 7.32 us  [on_chip(): return lax.ppermute(value, 'gx', pairs_on_chip)]
    ppermute x4 -> x3, starting transfers between devices: 9.26 us -> 13.4 us  [across_chips(): return lax.ppermute(value, 'gx', pairs_across)]
    ppermute x6 -> x7, waiting for transfers between devices: 4.68 us -> 1.13 us  [on_chip(): return lax.ppermute(value, 'gx', pairs_on_chip)]
    pallas_call x10 -> x12, Pallas kernels: 19.6 us -> 19.7 us  [call(): pl.pallas_call(kernel, out_shape=[jax.ShapeDtypeStruct(shape, F32) for sh...]
  transfers between devices with their start and end apart: 12 -> 16, of which waited for: 11 -> 8; matrix products, arithmetic and copies ran while one was open for 0% -> 0% of each run, Pallas kernels for 4% -> 4%
where the time goes in v6:
time: 124 us
  starting transfers between devices  45.2 us (36%)
  blocking collectives  36.7 us (30%)
  waiting for transfers between devices  20.6 us (17%)
  Pallas kernels  19.7 us (16%)
  other arithmetic  1.31 us (1%)
    all_to_all x1, blocking collectives, shards(): lax.all_to_all(sums.reshape(count, 1, COLS), ('gx', 'gy'), 0, 0)  36.7 us
    pallas_call x12, Pallas kernels, call(): pl.pallas_call(kernel, out_shape=[jax.ShapeDtypeStruct(shape, F32) for sh...  19.7 us
    ppermute x3, waiting for transfers between devices, across_chips(): return lax.ppermute(value, 'gx', pairs_across)  13.4 us
    ppermute x3, starting transfers between devices, across_chips(): return lax.ppermute(value, 'gx', pairs_across)  13.4 us
    ppermute x2, starting transfers between devices, rows_of(): far = lax.ppermute(own, 'gx', pairs_beyond)  9.64 us
    ppermute x1, starting transfers between devices, shards(): lax.ppermute(material, 'gx', pairs_beyond)  7.34 us
    ppermute x7, starting transfers between devices, on_chip(): return lax.ppermute(value, 'gx', pairs_on_chip)  7.32 us
    ppermute x1, starting transfers between devices, both_sides(): lax.ppermute(to_left, 'gy', backward)  4.99 us
  transfers between devices with their start and end apart: 16, of which 8 were waited for; matrix products, arithmetic and copies ran while one was open for 0% of the time, Pallas kernels for 4%

profile of v6, /device:TPU:1, one launch (start us, length us, event | category | flops | bytes accessed | tf_op | source)
XLA Modules:
  0.0 124.4 jit_solution(18269419962432881432)
XLA Ops:
  0.6 1.2 bitcast_select_fusion.fields.rhs
  1.9 0.0 copy-start
  1.9 0.0 copy-start.1
  1.9 0.0 copy-start.2
  1.9 0.4 shard_map.77
  2.2 2.5 %collective-permute-start = (f32[26,16,128]{2,1,0:T(8,128)S(1)}, f32[26,16,128]{2,1,0:T(8,128)S(1)}, u32[]{:S(2)}, u32[]{:S(2)}) collective-permute-start(f32[26,16,128]{2,1,0:T(8,128)S(1)} %get-tuple-element.33), channel_id=1, source_target_pairs={{0,1},{1,2},{2,3},{3,4},{4,5},{5,6},{6,7},{7,8},{8,9},{9,10},{10,1... | collective-permute-start | bytes 638984 | tf_op jit(solution)/shard_map/ppermute | solution.py:640
  4.8 5.0 %collective-permute-start.1 = (f32[26,16,128]{2,1,0:T(8,128)S(1)}, f32[26,16,128]{2,1,0:T(8,128)S(1)}, u32[]{:S(2)}, u32[]{:S(2)}) collective-permute-start(f32[26,16,128]{2,1,0:T(8,128)S(1)} %get-tuple-element.34), channel_id=1, source_target_pairs={{1,0},{2,1},{3,2},{4,3},{5,4},{6,5},{7,6},{8,7},{9,8},{10,9},{11,1... | collective-permute-start | bytes 638984 | tf_op jit(solution)/shard_map/ppermute | solution.py:640
  9.8 0.0 copy-done
  9.8 0.0 copy-done.1
  9.8 0.1 pad_add_fusion.place
  9.9 0.0 copy-done.2
  9.9 3.9 %collective-permute-done.from_left = f32[26,16,128]{2,1,0:T(8,128)S(1)} collective-permute-done((f32[26,16,128]{2,1,0:T(8,128)S(1)}, f32[26,16,128]{2,1,0:T(8,128)S(1)}, u32[]{:S(2)}, u32[]{:S(2)}) %collective-permute-start) | collective-permute-done | bytes 213024 | tf_op jit(solution)/shard_map/ppermute | solution.py:640
  13.8 1.8 %collective-permute-done.1.from_right = f32[26,16,128]{2,1,0:T(8,128)S(1)} collective-permute-done((f32[26,16,128]{2,1,0:T(8,128)S(1)}, f32[26,16,128]{2,1,0:T(8,128)S(1)}, u32[]{:S(2)}, u32[]{:S(2)}) %collective-permute-start.1) | collective-permute-done | bytes 213024 | tf_op jit(solution)/shard_map/ppermute | solution.py:640
  15.6 1.1 shard_map.78
  16.7 7.4 %collective-permute-start.3 = (f32[54,8,256]{2,1,0:T(8,128)S(1)}, f32[54,8,256]{2,1,0:T(8,128)S(1)}, u32[]{:S(2)}, u32[]{:S(2)}) collective-permute-start(f32[54,8,256]{2,1,0:T(8,128)S(1)} %get-tuple-element.42), channel_id=1, source_target_pairs={{0,240},{16,32},{32,16},{48,64},{64,48},{80,96},{96,80},{112,128},... | collective-permute-start | bytes 1327112 | tf_op jit(solution)/shard_map/ppermute | solution.py:625
  24.1 1.0 collective-permute-start.2
  25.2 0.9 shard_map.79
  26.1 8.9 %collective-permute-done.3.from_o.after = f32[54,8,256]{2,1,0:T(8,128)S(1)} collective-permute-done((f32[54,8,256]{2,1,0:T(8,128)S(1)}, f32[54,8,256]{2,1,0:T(8,128)S(1)}, u32[]{:S(2)}, u32[]{:S(2)}) %collective-permute-start.3) | collective-permute-done | bytes 442400 | tf_op jit(solution)/shard_map/ppermute | solution.py:625
  35.0 7.3 %collective-permute-start.10 = (f32[24,8,128]{2,1,0:T(8,128)S(1)}, f32[24,8,128]{2,1,0:T(8,128)S(1)}, u32[]{:S(2)}, u32[]{:S(2)}) collective-permute-start(f32[24,8,128]{2,1,0:T(8,128)S(1)} %shard_map.82.own), channel_id=1, source_target_pairs={{0,32},{16,240},{32,64},{48,16},{64,96},{80,48},{96,128},{112,80},... | collective-permute-start | bytes 294920 | tf_op jit(solution)/shard_map/ppermute | solution.py:670
  42.4 0.0 collective-permute-start.9
  42.4 0.6 collective-permute-start.8
  43.0 0.0 collective-permute-done.2.from_x
  43.0 3.5 %shard_map.80 = (f32[16,2,32,256]{3,2,1,0:T(8,128)S(1)}, f32[16,32,256]{2,1,0:T(8,128)S(1)}, f32[18,32,256]{2,1,0:T(8,128)S(1)}, f32[16,32,256]{2,1,0:T(8,128)S(...) custom-call(s32[5]{0:T(128)S(1)} %pad_add_fusion.place, ...), custom_call_target="tpu_custom_call" | custom-call | flops 5000000000 | bytes 15000000 | tf_op jit(solution)/shard_map/pallas_call | solution.py:586
  46.5 5.4 %collective-permute-start.6 = (f32[16,8,128]{2,1,0:T(8,128)S(1)}, f32[16,8,128]{2,1,0:T(8,128)S(1)}, u32[]{:S(2)}, u32[]{:S(2)}) collective-permute-start(f32[16,8,128]{2,1,0:T(8,128)S(1)} %get-tuple-element.49.after.own), channel_id=1, source_target_pairs={{0,32},{16,240},{32,64},{48,16},{64,96},{80,48},{96,128},{112,80},... | collective-permute-start | bytes 196616 | tf_op jit(solution)/shard_map/ppermute | solution.py:632
  51.9 2.4 %collective-permute-start.5 = (f32[16,8,128]{2,1,0:T(8,128)S(1)}, f32[16,8,128]{2,1,0:T(8,128)S(1)}, u32[]{:S(2)}, u32[]{:S(2)}) collective-permute-start(f32[16,8,128]{2,1,0:T(8,128)S(1)} %get-tuple-element.49.after.own), channel_id=1, source_target_pairs={{0,240},{16,32},{32,16},{48,64},{64,48},{80,96},{96,80},{112,128},... | collective-permute-start | bytes 196616 | tf_op jit(solution)/shard_map/ppermute | solution.py:625
  54.3 0.0 collective-permute-done.9.value.near
  54.3 0.8 collective-permute-start.4
  55.1 4.4 %collective-permute-done.5.value.near = f32[16,8,128]{2,1,0:T(8,128)S(1)} collective-permute-done((f32[16,8,128]{2,1,0:T(8,128)S(1)}, f32[16,8,128]{2,1,0:T(8,128)S(1)}, u32[]{:S(2)}, u32[]{:S(2)}) %collective-permute-start.5) | collective-permute-done | bytes 65568 | tf_op jit(solution)/shard_map/ppermute | solution.py:625
  59.5 2.3 %collective-permute-start.11 = (f32[24,8,128]{2,1,0:T(8,128)S(1)}, f32[24,8,128]{2,1,0:T(8,128)S(1)}, u32[]{:S(2)}, u32[]{:S(2)}) collective-permute-start(f32[24,8,128]{2,1,0:T(8,128)S(1)} %shard_map.83), channel_id=1, source_target_pairs={{0,16},{16,0},{32,48},{48,32},{64,80},{80,64},{96,112},{112,96},{1... | collective-permute-start | bytes 294920 | tf_op jit(solution)/shard_map/ppermute | solution.py:622
  61.9 0.0 collective-permute-done.10.far
  61.9 0.3 collective-permute-start.7
  62.2 0.0 collective-permute-done.8.partner
  62.2 0.6 collective-permute-done.11.second
  62.8 0.9 shard_map.84
  63.7 0.0 collective-permute-done.6.far
  63.8 0.0 collective-permute-done.4.partner
  63.8 0.0 collective-permute-done.7.second
  63.8 6.2 %shard_map.85 = (f32[16,2,32,256]{3,2,1,0:T(8,128)S(1)}, f32[18,2,32,256]{3,2,1,0:T(8,128)S(1)}, f32[16,8,128]{2,1,0:T(8,128)S(1)}) custom-call(s32[5]{0:T(128)S(1)} %pad_add_fusion.place, f32[16,2,32,256]{3,2,1,0:T(8,128)S(1)} %get-tuple-element.43.r, f32[16,32,256]{2,1,0:T(8,128)S(1)} %get-tuple-element.44.g, f32[18,32,256]{2,1,0:T(8,128)S(1)} %get-tuple-element.45.h, ...), custom_call_target="tpu_custom_call" | custom-call | flops 8999999488 | bytes 27000000 | tf_op jit(solution)/shard_map/pallas_call | solution.py:586
  70.0 3.6 %collective-permute-start.13 = (f32[16,8,128]{2,1,0:T(8,128)S(1)}, f32[16,8,128]{2,1,0:T(8,128)S(1)}, u32[]{:S(2)}, u32[]{:S(2)}) collective-permute-start(f32[16,8,128]{2,1,0:T(8,128)S(1)} %get-tuple-element.60.own), channel_id=1, source_target_pairs={{0,240},{16,32},{32,16},{48,64},{64,48},{80,96},{96,80},{112,128},... | collective-permute-start | bytes 196616 | tf_op jit(solution)/shard_map/ppermute | solution.py:625
  73.5 4.2 %collective-permute-start.14 = (f32[16,8,128]{2,1,0:T(8,128)S(1)}, f32[16,8,128]{2,1,0:T(8,128)S(1)}, u32[]{:S(2)}, u32[]{:S(2)}) collective-permute-start(f32[16,8,128]{2,1,0:T(8,128)S(1)} %get-tuple-element.60.own), channel_id=1, source_target_pairs={{0,32},{16,240},{32,64},{48,16},{64,96},{80,48},{96,128},{112,80},... | collective-permute-start | bytes 196616 | tf_op jit(solution)/shard_map/ppermute | solution.py:632
  77.8 0.0 collective-permute-start.12
  77.8 0.1 collective-permute-done.13.value.near
  77.8 2.3 %collective-permute-start.15 = (f32[16,8,128]{2,1,0:T(8,128)S(1)}, f32[16,8,128]{2,1,0:T(8,128)S(1)}, u32[]{:S(2)}, u32[]{:S(2)}) collective-permute-start(f32[16,8,128]{2,1,0:T(8,128)S(1)} %shard_map.86), channel_id=1, source_target_pairs={{0,16},{16,0},{32,48},{48,32},{64,80},{80,64},{96,112},{112,96},{1... | collective-permute-start | bytes 196616 | tf_op jit(solution)/shard_map/ppermute | solution.py:622
  80.1 0.4 collective-permute-done.14.far
  80.5 0.0 collective-permute-done.12.partner
  80.6 0.5 collective-permute-done.15.second
  81.0 5.7 %shard_map.87 = (f32[2,16,16,128]{3,2,1,0:T(8,128)S(1)}, f32[2,16,16,128]{3,2,1,0:T(8,128)S(1)}, f32[256,128]{1,0:T(8,128)S(1)}) custom-call(s32[5]{0:T(128)S(1)} %pad_add_fusion.place, f32[4,16,16,128]{3,2,1,0:T(8,128)S(1)} %bitcast_select_fusion.fields.rhs, f32[16,2,32,256]{3,2,1,0:T(8,128)S(1)} %get-tuple-element.58.r, ...), custom_call_target="tpu_custom_call" | custom-call | flops 8999999488 | bytes 27000000 | tf_op jit(solution)/shard_map/pallas_call | solution.py:586
  86.7 36.7 %all_to_all.5 = f32[256,1,128]{2,1,0:T(1,128)S(1)} all-to-all(f32[256,1,128]{2,1,0:T(1,128)S(1)} %bitcast.14), channel_id=1, replica_groups=mesh['gx'=16,'gy'=16] {'gx','gy'}, dimensions={0} | all-to-all | bytes 262144 | tf_op jit(solution)/shard_map/all_to_all | solution.py:689
  123.4 1.0 shard_map.88
  (8 shorter events, 0.0 us)
Async XLA Ops:
  1.9 7.9 %copy-start = (f32[16]{0:T(128)S(1)}, f32[16]{0:T(128)}, u32[]{:S(2)}) copy-start(f32[16]{0:T(128)} %param.11) | copy-start | bytes 196
  1.9 7.9 %copy-start.1 = (f32[16]{0:T(128)S(1)}, f32[16]{0:T(128)}, u32[]{:S(2)}) copy-start(f32[16]{0:T(128)} %param.10) | copy-start | bytes 196
  1.9 8.0 %copy-start.2 = (f32[16]{0:T(128)S(1)}, f32[16]{0:T(128)}, u32[]{:S(2)}) copy-start(f32[16]{0:T(128)} %param.9) | copy-start | bytes 196
  2.2 11.5 %collective-permute-start = (f32[26,16,128]{2,1,0:T(8,128)S(1)}, f32[26,16,128]{2,1,0:T(8,128)S(1)}, u32[]{:S(2)}, u32[]{:S(2)}) collective-permute-start(f32[26,16,128]{2,1,0:T(8,128)S(1)} %get-tuple-element.33), channel_id=1, source_target_pairs={{0,1},{1,2},{2,3},{3,4},{4,5},{5,6},{6,7},{7,8},{8,9},{9,10},{10,1... | collective-permute-start | bytes 638984 | tf_op jit(solution)/shard_map/ppermute | solution.py:640
  4.8 10.8 %collective-permute-start.1 = (f32[26,16,128]{2,1,0:T(8,128)S(1)}, f32[26,16,128]{2,1,0:T(8,128)S(1)}, u32[]{:S(2)}, u32[]{:S(2)}) collective-permute-start(f32[26,16,128]{2,1,0:T(8,128)S(1)} %get-tuple-element.34), channel_id=1, source_target_pairs={{1,0},{2,1},{3,2},{4,3},{5,4},{6,5},{7,6},{8,7},{9,8},{10,9},{11,1... | collective-permute-start | bytes 638984 | tf_op jit(solution)/shard_map/ppermute | solution.py:640
  16.7 18.3 %collective-permute-start.3 = (f32[54,8,256]{2,1,0:T(8,128)S(1)}, f32[54,8,256]{2,1,0:T(8,128)S(1)}, u32[]{:S(2)}, u32[]{:S(2)}) collective-permute-start(f32[54,8,256]{2,1,0:T(8,128)S(1)} %get-tuple-element.42), channel_id=1, source_target_pairs={{0,240},{16,32},{32,16},{48,64},{64,48},{80,96},{96,80},{112,128},... | collective-permute-start | bytes 1327112 | tf_op jit(solution)/shard_map/ppermute | solution.py:625
  24.1 18.8 %collective-permute-start.2 = (f32[54,8,256]{2,1,0:T(8,128)S(1)}, f32[54,8,256]{2,1,0:T(8,128)S(1)}, u32[]{:S(2)}, u32[]{:S(2)}) collective-permute-start(f32[54,8,256]{2,1,0:T(8,128)S(1)} %get-tuple-element.41), channel_id=1, source_target_pairs={{0,16},{16,0},{32,48},{48,32},{64,80},{80,64},{96,112},{112,96},{1... | collective-permute-start | bytes 1327112 | tf_op jit(solution)/shard_map/ppermute | solution.py:622
  35.0 26.9 %collective-permute-start.10 = (f32[24,8,128]{2,1,0:T(8,128)S(1)}, f32[24,8,128]{2,1,0:T(8,128)S(1)}, u32[]{:S(2)}, u32[]{:S(2)}) collective-permute-start(f32[24,8,128]{2,1,0:T(8,128)S(1)} %shard_map.82.own), channel_id=1, source_target_pairs={{0,32},{16,240},{32,64},{48,16},{64,96},{80,48},{96,128},{112,80},... | collective-permute-start | bytes 294920 | tf_op jit(solution)/shard_map/ppermute | solution.py:670
  42.4 12.0 %collective-permute-start.9 = (f32[24,8,128]{2,1,0:T(8,128)S(1)}, f32[24,8,128]{2,1,0:T(8,128)S(1)}, u32[]{:S(2)}, u32[]{:S(2)}) collective-permute-start(f32[24,8,128]{2,1,0:T(8,128)S(1)} %shard_map.82.own), channel_id=1, source_target_pairs={{0,240},{16,32},{32,16},{48,64},{64,48},{80,96},{96,80},{112,128},... | collective-permute-start | bytes 294920 | tf_op jit(solution)/shard_map/ppermute | solution.py:669
  42.4 19.8 %collective-permute-start.8 = (f32[24,8,128]{2,1,0:T(8,128)S(1)}, f32[24,8,128]{2,1,0:T(8,128)S(1)}, u32[]{:S(2)}, u32[]{:S(2)}) collective-permute-start(f32[24,8,128]{2,1,0:T(8,128)S(1)} %shard_map.82.own), channel_id=1, source_target_pairs={{0,16},{16,0},{32,48},{48,32},{64,80},{80,64},{96,112},{112,96},{1... | collective-permute-start | bytes 294920 | tf_op jit(solution)/shard_map/ppermute | solution.py:622
  46.5 17.2 %collective-permute-start.6 = (f32[16,8,128]{2,1,0:T(8,128)S(1)}, f32[16,8,128]{2,1,0:T(8,128)S(1)}, u32[]{:S(2)}, u32[]{:S(2)}) collective-permute-start(f32[16,8,128]{2,1,0:T(8,128)S(1)} %get-tuple-element.49.after.own), channel_id=1, source_target_pairs={{0,32},{16,240},{32,64},{48,16},{64,96},{80,48},{96,128},{112,80},... | collective-permute-start | bytes 196616 | tf_op jit(solution)/shard_map/ppermute | solution.py:632
  51.9 7.6 %collective-permute-start.5 = (f32[16,8,128]{2,1,0:T(8,128)S(1)}, f32[16,8,128]{2,1,0:T(8,128)S(1)}, u32[]{:S(2)}, u32[]{:S(2)}) collective-permute-start(f32[16,8,128]{2,1,0:T(8,128)S(1)} %get-tuple-element.49.after.own), channel_id=1, source_target_pairs={{0,240},{16,32},{32,16},{48,64},{64,48},{80,96},{96,80},{112,128},... | collective-permute-start | bytes 196616 | tf_op jit(solution)/shard_map/ppermute | solution.py:625
  54.3 9.4 %collective-permute-start.4 = (f32[16,8,128]{2,1,0:T(8,128)S(1)}, f32[16,8,128]{2,1,0:T(8,128)S(1)}, u32[]{:S(2)}, u32[]{:S(2)}) collective-permute-start(f32[16,8,128]{2,1,0:T(8,128)S(1)} %get-tuple-element.49.after.own), channel_id=1, source_target_pairs={{0,16},{16,0},{32,48},{48,32},{64,80},{80,64},{96,112},{112,96},{1... | collective-permute-start | bytes 196616 | tf_op jit(solution)/shard_map/ppermute | solution.py:622
  59.5 3.3 %collective-permute-start.11 = (f32[24,8,128]{2,1,0:T(8,128)S(1)}, f32[24,8,128]{2,1,0:T(8,128)S(1)}, u32[]{:S(2)}, u32[]{:S(2)}) collective-permute-start(f32[24,8,128]{2,1,0:T(8,128)S(1)} %shard_map.83), channel_id=1, source_target_pairs={{0,16},{16,0},{32,48},{48,32},{64,80},{80,64},{96,112},{112,96},{1... | collective-permute-start | bytes 294920 | tf_op jit(solution)/shard_map/ppermute | solution.py:622
  61.9 1.9 %collective-permute-start.7 = (f32[16,8,128]{2,1,0:T(8,128)S(1)}, f32[16,8,128]{2,1,0:T(8,128)S(1)}, u32[]{:S(2)}, u32[]{:S(2)}) collective-permute-start(f32[16,8,128]{2,1,0:T(8,128)S(1)} %shard_map.81), channel_id=1, source_target_pairs={{0,16},{16,0},{32,48},{48,32},{64,80},{80,64},{96,112},{112,96},{1... | collective-permute-start | bytes 196616 | tf_op jit(solution)/shard_map/ppermute | solution.py:622
  70.0 7.9 %collective-permute-start.13 = (f32[16,8,128]{2,1,0:T(8,128)S(1)}, f32[16,8,128]{2,1,0:T(8,128)S(1)}, u32[]{:S(2)}, u32[]{:S(2)}) collective-permute-start(f32[16,8,128]{2,1,0:T(8,128)S(1)} %get-tuple-element.60.own), channel_id=1, source_target_pairs={{0,240},{16,32},{32,16},{48,64},{64,48},{80,96},{96,80},{112,128},... | collective-permute-start | bytes 196616 | tf_op jit(solution)/shard_map/ppermute | solution.py:625
  73.5 7.0 %collective-permute-start.14 = (f32[16,8,128]{2,1,0:T(8,128)S(1)}, f32[16,8,128]{2,1,0:T(8,128)S(1)}, u32[]{:S(2)}, u32[]{:S(2)}) collective-permute-start(f32[16,8,128]{2,1,0:T(8,128)S(1)} %get-tuple-element.60.own), channel_id=1, source_target_pairs={{0,32},{16,240},{32,64},{48,16},{64,96},{80,48},{96,128},{112,80},... | collective-permute-start | bytes 196616 | tf_op jit(solution)/shard_map/ppermute | solution.py:632
  77.8 2.8 %collective-permute-start.12 = (f32[16,8,128]{2,1,0:T(8,128)S(1)}, f32[16,8,128]{2,1,0:T(8,128)S(1)}, u32[]{:S(2)}, u32[]{:S(2)}) collective-permute-start(f32[16,8,128]{2,1,0:T(8,128)S(1)} %get-tuple-element.60.own), channel_id=1, source_target_pairs={{0,16},{16,0},{32,48},{48,32},{64,80},{80,64},{96,112},{112,96},{1... | collective-permute-start | bytes 196616 | tf_op jit(solution)/shard_map/ppermute | solution.py:622
  77.8 3.2 %collective-permute-start.15 = (f32[16,8,128]{2,1,0:T(8,128)S(1)}, f32[16,8,128]{2,1,0:T(8,128)S(1)}, u32[]{:S(2)}, u32[]{:S(2)}) collective-permute-start(f32[16,8,128]{2,1,0:T(8,128)S(1)} %shard_map.86), channel_id=1, source_target_pairs={{0,16},{16,0},{32,48},{48,32},{64,80},{80,64},{96,112},{112,96},{1... | collective-permute-start | bytes 196616 | tf_op jit(solution)/shard_map/ppermute | solution.py:622

commit v7 on v4

--- a/solution.py
+++ b/solution.py
@@ -187,14 +187,22 @@
     fill_message(message, lambda z, i: fields.at[i, z], classes, sea, start, 8 - core)
 
 
-def corner_kernel(message, to_left, to_right):
+def corner_kernel(message, after, to_left, to_right):
     def pair(p):
         to_left[p], to_right[p] = pack_halves(message[2 * p], message[2 * p + 1])
 
     loop(MSG_X // 2, pair)
 
 
-def rows_kernel(place, fields, from_left, from_right, after, r_out, c_out, s_out, message):
+def widen_kernel(message, corner_left, corner_right, wide):
+    def pair(p):
+        for i, halo in enumerate(unpack_halves(corner_right[p], corner_left[p])):
+            wide[2 * p + i] = jnp.concatenate([message[2 * p + i], halo], axis=1)
+
+    loop(MSG_X // 2, pair)
+
+
+def rows_kernel(place, fields, from_left, from_right, r_out, c_out, s_out, message):
     core = place[0]
     gy = place[2]
     left = lanes(ROWS, COLS) < HALF
@@ -300,8 +308,8 @@
 
 
 def down_kernel(
-    place, r_own, g_own, h_own, k_own, from_x, from_o, corner_left, corner_right, table,
-    r, g, h, d, inverse, xp, r1, xa, ka, wide, edges, sums, buffer,
+    place, r_own, g_own, h_own, k_own, from_x, wide, table,
+    r, g, h, d, inverse, xp, r1, xa, ka, edges, sums, buffer,
 ):
     core = place[0]
     gx = place[1]
@@ -324,11 +332,6 @@
 
     loop(NZ, own)
 
-    def widen(p):
-        for i, halo in enumerate(unpack_halves(corner_right[p], corner_left[p])):
-            wide[2 * p + i] = jnp.concatenate([from_o[2 * p + i], halo], axis=1)
-
-    loop(MSG_X // 2, widen)
     for message, start, scale, slot in ((from_x, 24 * (1 - core), 1.0, 1 - core), (wide, 24 * core, open_side, core)):
         start = pl.multiple_of(start, 8)
         valid = scale * ends
@@ -477,13 +480,12 @@
     loop(NZ // 2, body)
 
 
-def join_kernel(r1, odd, message):
-    message[0:R_TILES] = r1[...]
-    message[R_TILES:] = odd[0:M_TILES]
-
-
-def near_kernel(odd, after, near):
+def near_kernel(odd, near):
     near[...] = odd[0:R_TILES]
+
+
+def after_kernel(odd, after, near):
+    near[...] = odd[0:M_TILES]
 
 
 def coarse_kernel(
@@ -578,16 +580,17 @@
 
 
 COSTS = {
-    "start_kernel": 3,
+    "start_kernel": 1,
     "corner_kernel": 1,
-    "rows_kernel": 3,
-    "material_kernel": 2,
-    "down_kernel": 5,
-    "join_kernel": 1,
-    "near_kernel": 1,
-    "coarse_kernel": 3,
-    "middle_kernel": 9,
-    "last_kernel": 9,
+    "widen_kernel": 30,
+    "rows_kernel": 1,
+    "material_kernel": 1,
+    "down_kernel": 4,
+    "near_kernel": 30,
+    "after_kernel": 30,
+    "coarse_kernel": 1,
+    "middle_kernel": 6,
+    "last_kernel": 6,
     "scale_kernel": 1,
 }
 
@@ -637,12 +640,10 @@
     def across_chips(value):
         return lax.ppermute(value, "gx", pairs_across)
 
-    def neighbours(own, partner):
-        return across_chips(jnp.concatenate([own, partner], axis=0))
-
     def rows_of(own, partner):
-        odd = neighbours(own, partner)
-        return own, partner, odd, on_chip(odd[: own.shape[0]])
+        odd = across_chips(jnp.concatenate([own, partner], axis=0))
+        near = call(near_kernel, (odd,), [own.shape], place=False)[0]
+        return own, partner, odd, on_chip(near)
 
     forward = [(i, (i + 1) % count_y) for i in range(count_y)]
     backward = [(target, source) for source, target in forward]
@@ -652,19 +653,17 @@
 
     part = lax.broadcasted_iota(jnp.int32, (4, *classes.shape), 0)
     materials = jnp.where(part == 2, classes[None], sea_mask[None]).astype(F32)
-    fields = jnp.where(part == 0, right_side[0:1], jnp.where(part == 1, right_side[1:2], materials))
+    twice = jnp.broadcast_to(right_side[None], (2, *right_side.shape)).reshape(part.shape)
+    fields = jnp.where(part < 2, twice, materials)
     to_left, to_right, msg_o = call(
         start_kernel, (place, fields), [(MSG_Y, ROWS, COLS), (MSG_Y, ROWS, COLS), (MSG_X, 8, COLS)]
     )
     from_o = across_chips(msg_o)
     from_left, from_right = both_sides(to_left, to_right)
-    corner_tiles = call(corner_kernel, (from_o,), [(MSG_X // 2, 8, COLS)] * 2, place=False)
-    corners = both_sides(*corner_tiles)
     r_own, c_own, s_own, msg_x = call(
         rows_kernel,
-        (place, fields, from_left, from_right, corner_tiles[0]),
+        (place, fields, from_left, from_right),
         [(NZ, 2, ROWS, WIDE), (NZ, ROWS, WIDE), (NZ, ROWS, WIDE), (MSG_X, 8, WIDE)],
-        far={4: pl.ANY},
     )
     from_x = on_chip(msg_x)
     g_own, h_own, k_own, packed = call(
@@ -674,27 +673,29 @@
         [(M_TILES, 8, WIDE), BUFFER],
         place=False,
     )
+    corner_tiles = call(corner_kernel, (from_o, packed), [(MSG_X // 2, 8, COLS)] * 2, place=False, far={1: pl.ANY})
+    wide = call(widen_kernel, (from_o, *both_sides(*corner_tiles)), [(MSG_X, 8, WIDE)], place=False)[0]
     packed_partner = on_chip(packed)
-    packed_odd = neighbours(packed, packed_partner)
+    packed_odd = across_chips(jnp.concatenate([packed, packed_partner], axis=0))
     r, g, h, d, inverse, xp, r1 = call(
         down_kernel,
-        (place, r_own, g_own, h_own, k_own, from_x, from_o, *corners, table),
+        (place, r_own, g_own, h_own, k_own, from_x, wide, table),
         [FIELD0, (NZ, EXT0, WIDE), (NZ + 2, EXT0, WIDE), (NZ, EXT0, WIDE), (NZ, EXT0, WIDE), PADDED0, (R_TILES, 8, COLS)],
-        [PADDED0, (NZ, EXT0, WIDE), (MSG_X, 8, WIDE), (2, NZ, WIDE), SUMS, BUFFER],
-    )
-    received = on_chip(call(join_kernel, (r1, packed_odd), [(R_TILES + M_TILES, 8, COLS)], place=False)[0])
-    material = (packed, packed_partner, packed_odd, received[R_TILES:])
+        [PADDED0, (NZ, EXT0, WIDE), (2, NZ, WIDE), SUMS, BUFFER],
+    )
+    rows = rows_of(r1, on_chip(r1))
+    packed_near = call(
+        after_kernel, (packed_odd, rows[1]), [packed.shape], place=False, far={1: pl.ANY}
+    )[0]
+    material = (packed, packed_partner, packed_odd, on_chip(packed_near))
     one = [(8, EXT1, COLS), (10, EXT1, COLS), (8, EXT1, COLS), (8, EXT1, COLS)]
     two = [(4, EXT2, COLS), (6, EXT2, COLS), (4, EXT2, COLS)]
     coarse = call(
         coarse_kernel, (place, *material), [*one, *two], [one[0], one[0], one[0], two[0], BUFFER]
     )
-    partner = received[:R_TILES]
-    odd = neighbours(r1, partner)
-    near = call(near_kernel, (odd, coarse[0]), [(R_TILES, 8, COLS)], place=False, far={1: pl.ANY})[0]
     r, xp, r1 = call(
         middle_kernel,
-        (place, r, g, h, d, inverse, xp, r1, partner, odd, on_chip(near), *coarse),
+        (place, r, g, h, d, inverse, xp, *rows, *coarse),
         [FIELD0, PADDED0, (R_TILES, 8, COLS)],
         [PADDED0, PADDED0, *COARSE_SCRATCH, SUMS, BUFFER],
     )

time: 121 us -> 113 us (0.934)
  waiting for transfers between devices: 41.1 us -> 26.8 us
  starting transfers between devices: 32.6 us -> 42.1 us
  blocking collectives: 22.2 us -> 20.3 us
    ppermute x2, waiting for transfers between devices: 16.7 us -> 2.17 us  [both_sides(): lax.ppermute(to_right, 'gy', forward)]
    ppermute x6 -> x7, starting transfers between devices: 9.89 us -> 22.1 us  [on_chip(): return lax.ppermute(value, 'gx', pairs_on_chip)]
    ppermute x4, starting transfers between devices: 12.8 us -> 7.05 us  [across_chips(): return lax.ppermute(value, 'gx', pairs_across)]
    ppermute x4, waiting for transfers between devices: 18.9 us -> 21.9 us  [across_chips(): return lax.ppermute(value, 'gx', pairs_across)]
    all_to_all x1, blocking collectives: 22.2 us -> 20.3 us  [shards(): lax.all_to_all(sums.reshape(count, 1, COLS), ('gx', 'gy'), 0, 0)]
    ppermute x2, starting transfers between devices: 0.74 us -> 2.54 us  [both_sides(): lax.ppermute(to_right, 'gy', forward)]
    ppermute x2, waiting for transfers between devices: 1.77 us -> 0.01 us  [both_sides(): lax.ppermute(to_left, 'gy', backward)]
    ppermute x6 -> x7, waiting for transfers between devices: 3.74 us -> 2.77 us  [on_chip(): return lax.ppermute(value, 'gx', pairs_on_chip)]
  transfers between devices with their start and end apart: 14 -> 15, of which waited for: 11 -> 7; matrix products, arithmetic and copies ran while one was open for 0% -> 0% of each run, Pallas kernels for 5% -> 7%
where the time goes in v7:
time: 113 us
  starting transfers between devices  42.1 us (37%)
  waiting for transfers between devices  26.8 us (24%)
  Pallas kernels  21.4 us (19%)
  blocking collectives  20.3 us (18%)
  other arithmetic  1.34 us (1%)
    ppermute x7, starting transfers between devices, on_chip(): return lax.ppermute(value, 'gx', pairs_on_chip)  22.1 us
    ppermute x4, waiting for transfers between devices, across_chips(): return lax.ppermute(value, 'gx', pairs_across)  21.9 us
    pallas_call x13, Pallas kernels, call(): pl.pallas_call(kernel, out_shape=[jax.ShapeDtypeStruct(shape, F32) for sh...  21.4 us
    all_to_all x1, blocking collectives, shards(): lax.all_to_all(sums.reshape(count, 1, COLS), ('gx', 'gy'), 0, 0)  20.3 us
    ppermute x2, starting transfers between devices, both_sides(): lax.ppermute(to_left, 'gy', backward)  10.4 us
    ppermute x4, starting transfers between devices, across_chips(): return lax.ppermute(value, 'gx', pairs_across)  7.05 us
    ppermute x7, waiting for transfers between devices, on_chip(): return lax.ppermute(value, 'gx', pairs_on_chip)  2.77 us
    ppermute x2, starting transfers between devices, both_sides(): lax.ppermute(to_right, 'gy', forward)  2.54 us
  transfers between devices with their start and end apart: 15, of which 7 were waited for; matrix products, arithmetic and copies ran while one was open for 0% of the time, Pallas kernels for 7%

profile of v7, /device:TPU:1, one launch (start us, length us, event | category | flops | bytes accessed | tf_op | source)
XLA Modules:
  0.0 112.8 jit_solution(16868768809961412066)
XLA Ops:
  0.7 0.1 pad_add_fusion.place
  0.8 1.2 %bitcast_select_fusion.fields.rhs = f32[4,16,16,128]{3,2,1,0:T(8,128)S(1)} fusion(s32[16,16,128]{2,1,0:T(8,128)} %param.8, s32[16,16,128]{2,1,0:T(8,128)} %param.7, f32[2,16,16,128]{3,2,1,0:T(8,128)} %param.6, pred[4]{0:T(512)(128)(4,1)S(1)} %get-tuple-element.68, pred[4]{0:T(512)(128)(4,1)S(1)} %get-tuple-element.69), kind=kLoop, calls=%fused_computation | loop fusion | flops 393216 | bytes 1048584 | tf_op jit(solution)/shard_map/jit(_where)/select_n | solution.py:657
  2.0 0.0 copy-start
  2.0 0.0 copy-start.1
  2.0 0.0 copy-start.2
  2.0 1.1 shard_map.77
  3.1 2.5 %collective-permute-start = (f32[26,16,128]{2,1,0:T(8,128)S(1)}, f32[26,16,128]{2,1,0:T(8,128)S(1)}, u32[]{:S(2)}, u32[]{:S(2)}) collective-permute-start(f32[26,16,128]{2,1,0:T(8,128)S(1)} %get-tuple-element.35), channel_id=1, source_target_pairs={{0,1},{1,2},{2,3},{3,4},{4,5},{5,6},{6,7},{7,8},{8,9},{9,10},{10,1... | collective-permute-start | bytes 638984 | tf_op jit(solution)/shard_map/ppermute | solution.py:652
  5.6 5.0 %collective-permute-start.1 = (f32[26,16,128]{2,1,0:T(8,128)S(1)}, f32[26,16,128]{2,1,0:T(8,128)S(1)}, u32[]{:S(2)}, u32[]{:S(2)}) collective-permute-start(f32[26,16,128]{2,1,0:T(8,128)S(1)} %get-tuple-element.36), channel_id=1, source_target_pairs={{1,0},{2,1},{3,2},{4,3},{5,4},{6,5},{7,6},{8,7},{9,8},{10,9},{11,1... | collective-permute-start | bytes 638984 | tf_op jit(solution)/shard_map/ppermute | solution.py:652
  10.6 6.8 %collective-permute-start.3 = (f32[56,8,128]{2,1,0:T(8,128)S(1)}, f32[56,8,128]{2,1,0:T(8,128)S(1)}, u32[]{:S(2)}, u32[]{:S(2)}) collective-permute-start(f32[56,8,128]{2,1,0:T(8,128)S(1)} %get-tuple-element.44), channel_id=1, source_target_pairs={{0,240},{16,32},{32,16},{48,64},{64,48},{80,96},{96,80},{112,128},... | collective-permute-start | bytes 688136 | tf_op jit(solution)/shard_map/ppermute | solution.py:641
  17.4 0.0 copy-done
  17.4 0.0 copy-done.1
  17.4 0.0 copy-done.2
  17.4 0.0 collective-permute-done.from_left
  17.4 0.0 collective-permute-done.1.from_right
  17.5 1.1 %shard_map.78 = (f32[16,2,16,256]{3,2,1,0:T(8,128)S(1)}, f32[16,16,256]{2,1,0:T(8,128)S(1)}, f32[16,16,256]{2,1,0:T(8,128)S(1)}, f32[56,8,256]{2,1,0:T(8,128)S(1)}) custom-call(s32[5]{0:T(128)S(1)} %pad_add_fusion.place, f32[4,16,16,128]{3,2,1,0:T(8,128)S(1)} %bitcast_select_fusion.fields.rhs, f32[26,16,128]{2,1,0:T(8,128)S(1)} %collective-permute-done.from_left, ...), custom_call_target="tpu_custom_call" | custom-call | flops 1000000000 | bytes 3000000 | tf_op jit(solution)/shard_map/pallas_call | solution.py:604
  18.6 0.9 shard_map.79
  19.5 2.8 %collective-permute-start.9 = (f32[24,8,128]{2,1,0:T(8,128)S(1)}, f32[24,8,128]{2,1,0:T(8,128)S(1)}, u32[]{:S(2)}, u32[]{:S(2)}) collective-permute-start(f32[24,8,128]{2,1,0:T(8,128)S(1)} %get-tuple-element.45.after.own), channel_id=1, source_target_pairs={{0,16},{16,0},{32,48},{48,32},{64,80},{80,64},{96,112},{112,96},{1... | collective-permute-start | bytes 294920 | tf_op jit(solution)/shard_map/ppermute | solution.py:638
  22.4 0.1 collective-permute-start.2
  22.5 9.2 %collective-permute-done.3.message = f32[56,8,128]{2,1,0:T(8,128)S(1)} collective-permute-done((f32[56,8,128]{2,1,0:T(8,128)S(1)}, f32[56,8,128]{2,1,0:T(8,128)S(1)}, u32[]{:S(2)}, u32[]{:S(2)}) %collective-permute-start.3) | collective-permute-done | bytes 229408 | tf_op jit(solution)/shard_map/ppermute | solution.py:641
  31.7 0.5 shard_map.80
  32.2 0.0 collective-permute-start.4
  32.2 5.4 %collective-permute-start.5 = (f32[28,8,128]{2,1,0:T(8,128)S(1)}, f32[28,8,128]{2,1,0:T(8,128)S(1)}, u32[]{:S(2)}, u32[]{:S(2)}) collective-permute-start(f32[28,8,128]{2,1,0:T(8,128)S(1)} %get-tuple-element.47), channel_id=1, source_target_pairs={{1,0},{2,1},{3,2},{4,3},{5,4},{6,5},{7,6},{8,7},{9,8},{10,9},{11,1... | collective-permute-start | bytes 344072 | tf_op jit(solution)/shard_map/ppermute | solution.py:652
  37.6 0.0 collective-permute-done.9.partner
  37.6 0.1 collective-permute-start.10
  37.7 2.2 %collective-permute-done.4.corner_left = f32[28,8,128]{2,1,0:T(8,128)S(1)} collective-permute-done((f32[28,8,128]{2,1,0:T(8,128)S(1)}, f32[28,8,128]{2,1,0:T(8,128)S(1)}, u32[]{:S(2)}, u32[]{:S(2)}) %collective-permute-start.4) | collective-permute-done | bytes 114720 | tf_op jit(solution)/shard_map/ppermute | solution.py:652
  39.9 0.0 collective-permute-done.5.corner_right
  39.9 0.5 shard_map.81.wide
  40.5 0.0 collective-permute-done.2.from_x
  40.5 3.6 %shard_map.82 = (f32[16,2,32,256]{3,2,1,0:T(8,128)S(1)}, f32[16,32,256]{2,1,0:T(8,128)S(1)}, f32[18,32,256]{2,1,0:T(8,128)S(1)}, f32[16,32,256]{2,1,0:T(8,128)S(...) custom-call(s32[5]{0:T(128)S(1)} %pad_add_fusion.place, ...), custom_call_target="tpu_custom_call" | custom-call | flops 4000000000 | bytes 12000000 | tf_op jit(solution)/shard_map/pallas_call | solution.py:604
  44.1 6.1 %collective-permute-start.6 = (f32[16,8,128]{2,1,0:T(8,128)S(1)}, f32[16,8,128]{2,1,0:T(8,128)S(1)}, u32[]{:S(2)}, u32[]{:S(2)}) collective-permute-start(f32[16,8,128]{2,1,0:T(8,128)S(1)} %get-tuple-element.54.own), channel_id=1, source_target_pairs={{0,16},{16,0},{32,48},{48,32},{64,80},{80,64},{96,112},{112,96},{1... | collective-permute-start | bytes 196616 | tf_op jit(solution)/shard_map/ppermute | solution.py:638
  50.2 0.9 collective-permute-done.6.after.partner
  51.1 0.1 collective-permute-start.7
  51.2 0.0 collective-permute-done.10.odd
  51.3 4.2 %collective-permute-start.11 = (f32[24,8,128]{2,1,0:T(8,128)S(1)}, f32[24,8,128]{2,1,0:T(8,128)S(1)}, u32[]{:S(2)}, u32[]{:S(2)}) collective-permute-start(f32[24,8,128]{2,1,0:T(8,128)S(1)} %shard_map.84), channel_id=1, source_target_pairs={{0,16},{16,0},{32,48},{48,32},{64,80},{80,64},{96,112},{112,96},{1... | collective-permute-start | bytes 294920 | tf_op jit(solution)/shard_map/ppermute | solution.py:638
  55.4 4.2 %collective-permute-done.7.odd = f32[32,8,128]{2,1,0:T(8,128)S(1)} collective-permute-done((f32[32,8,128]{2,1,0:T(8,128)S(1)}, f32[32,8,128]{2,1,0:T(8,128)S(1)}, u32[]{:S(2)}, u32[]{:S(2)}) %collective-permute-start.7) | collective-permute-done | bytes 131104 | tf_op jit(solution)/shard_map/ppermute | solution.py:641
  59.7 5.0 %collective-permute-start.8 = (f32[16,8,128]{2,1,0:T(8,128)S(1)}, f32[16,8,128]{2,1,0:T(8,128)S(1)}, u32[]{:S(2)}, u32[]{:S(2)}) collective-permute-start(f32[16,8,128]{2,1,0:T(8,128)S(1)} %shard_map.83), channel_id=1, source_target_pairs={{0,16},{16,0},{32,48},{48,32},{64,80},{80,64},{96,112},{112,96},{1... | collective-permute-start | bytes 196616 | tf_op jit(solution)/shard_map/ppermute | solution.py:638
  64.7 0.0 collective-permute-done.11.far
  64.7 0.9 shard_map.85
  65.6 0.0 collective-permute-done.8.far
  65.6 6.1 %shard_map.86 = (f32[16,2,32,256]{3,2,1,0:T(8,128)S(1)}, f32[18,2,32,256]{3,2,1,0:T(8,128)S(1)}, f32[16,8,128]{2,1,0:T(8,128)S(1)}) custom-call(s32[5]{0:T(128)S(1)} %pad_add_fusion.place, f32[16,2,32,256]{3,2,1,0:T(8,128)S(1)} %get-tuple-element.48.r, f32[16,32,256]{2,1,0:T(8,128)S(1)} %get-tuple-element.49.g, f32[18,32,256]{2,1,0:T(8,128)S(1)} %get-tuple-element.50.h, ...), custom_call_target="tpu_custom_call" | custom-call | flops 6000000000 | bytes 18000000 | tf_op jit(solution)/shard_map/pallas_call | solution.py:604
  71.7 0.4 collective-permute-start.12
  72.1 1.0 collective-permute-done.12.partner
  73.1 0.1 collective-permute-start.13
  73.2 8.4 %collective-permute-done.13.odd = f32[32,8,128]{2,1,0:T(8,128)S(1)} collective-permute-done((f32[32,8,128]{2,1,0:T(8,128)S(1)}, f32[32,8,128]{2,1,0:T(8,128)S(1)}, u32[]{:S(2)}, u32[]{:S(2)}) %collective-permute-start.13) | collective-permute-done | bytes 131104 | tf_op jit(solution)/shard_map/ppermute | solution.py:641
  81.6 3.4 %collective-permute-start.14 = (f32[16,8,128]{2,1,0:T(8,128)S(1)}, f32[16,8,128]{2,1,0:T(8,128)S(1)}, u32[]{:S(2)}, u32[]{:S(2)}) collective-permute-start(f32[16,8,128]{2,1,0:T(8,128)S(1)} %shard_map.87), channel_id=1, source_target_pairs={{0,16},{16,0},{32,48},{48,32},{64,80},{80,64},{96,112},{112,96},{1... | collective-permute-start | bytes 196616 | tf_op jit(solution)/shard_map/ppermute | solution.py:638
  85.0 0.9 collective-permute-done.14.far
  85.9 5.6 %shard_map.88 = (f32[2,16,16,128]{3,2,1,0:T(8,128)S(1)}, f32[2,16,16,128]{3,2,1,0:T(8,128)S(1)}, f32[256,128]{1,0:T(8,128)S(1)}) custom-call(s32[5]{0:T(128)S(1)} %pad_add_fusion.place, f32[4,16,16,128]{3,2,1,0:T(8,128)S(1)} %bitcast_select_fusion.fields.rhs, f32[16,2,32,256]{3,2,1,0:T(8,128)S(1)} %get-tuple-element.62.r, ...), custom_call_target="tpu_custom_call" | custom-call | flops 6000000000 | bytes 18000000 | tf_op jit(solution)/shard_map/pallas_call | solution.py:604
  91.5 20.3 %all_to_all.5 = f32[256,1,128]{2,1,0:T(1,128)S(1)} all-to-all(f32[256,1,128]{2,1,0:T(1,128)S(1)} %bitcast.14), channel_id=1, replica_groups=mesh['gx'=16,'gy'=16] {'gx','gy'}, dimensions={0} | all-to-all | bytes 262144 | tf_op jit(solution)/shard_map/all_to_all | solution.py:709
  111.9 1.0 shard_map.89
  (10 shorter events, 0.1 us)
Async XLA Ops:
  2.0 15.4 %copy-start = (f32[16]{0:T(128)S(1)}, f32[16]{0:T(128)}, u32[]{:S(2)}) copy-start(f32[16]{0:T(128)} %param.11) | copy-start | bytes 196
  2.0 15.4 %copy-start.1 = (f32[16]{0:T(128)S(1)}, f32[16]{0:T(128)}, u32[]{:S(2)}) copy-start(f32[16]{0:T(128)} %param.10) | copy-start | bytes 196
  2.0 15.4 %copy-start.2 = (f32[16]{0:T(128)S(1)}, f32[16]{0:T(128)}, u32[]{:S(2)}) copy-start(f32[16]{0:T(128)} %param.9) | copy-start | bytes 196
  3.1 14.4 %collective-permute-start = (f32[26,16,128]{2,1,0:T(8,128)S(1)}, f32[26,16,128]{2,1,0:T(8,128)S(1)}, u32[]{:S(2)}, u32[]{:S(2)}) collective-permute-start(f32[26,16,128]{2,1,0:T(8,128)S(1)} %get-tuple-element.35), channel_id=1, source_target_pairs={{0,1},{1,2},{2,3},{3,4},{4,5},{5,6},{6,7},{7,8},{8,9},{9,10},{10,1... | collective-permute-start | bytes 638984 | tf_op jit(solution)/shard_map/ppermute | solution.py:652
  5.6 11.8 %collective-permute-start.1 = (f32[26,16,128]{2,1,0:T(8,128)S(1)}, f32[26,16,128]{2,1,0:T(8,128)S(1)}, u32[]{:S(2)}, u32[]{:S(2)}) collective-permute-start(f32[26,16,128]{2,1,0:T(8,128)S(1)} %get-tuple-element.36), channel_id=1, source_target_pairs={{1,0},{2,1},{3,2},{4,3},{5,4},{6,5},{7,6},{8,7},{9,8},{10,9},{11,1... | collective-permute-start | bytes 638984 | tf_op jit(solution)/shard_map/ppermute | solution.py:652
  10.6 21.1 %collective-permute-start.3 = (f32[56,8,128]{2,1,0:T(8,128)S(1)}, f32[56,8,128]{2,1,0:T(8,128)S(1)}, u32[]{:S(2)}, u32[]{:S(2)}) collective-permute-start(f32[56,8,128]{2,1,0:T(8,128)S(1)} %get-tuple-element.44), channel_id=1, source_target_pairs={{0,240},{16,32},{32,16},{48,64},{64,48},{80,96},{96,80},{112,128},... | collective-permute-start | bytes 688136 | tf_op jit(solution)/shard_map/ppermute | solution.py:641
  19.5 18.1 %collective-permute-start.9 = (f32[24,8,128]{2,1,0:T(8,128)S(1)}, f32[24,8,128]{2,1,0:T(8,128)S(1)}, u32[]{:S(2)}, u32[]{:S(2)}) collective-permute-start(f32[24,8,128]{2,1,0:T(8,128)S(1)} %get-tuple-element.45.after.own), channel_id=1, source_target_pairs={{0,16},{16,0},{32,48},{48,32},{64,80},{80,64},{96,112},{112,96},{1... | collective-permute-start | bytes 294920 | tf_op jit(solution)/shard_map/ppermute | solution.py:638
  22.4 18.1 %collective-permute-start.2 = (f32[56,8,256]{2,1,0:T(8,128)S(1)}, f32[56,8,256]{2,1,0:T(8,128)S(1)}, u32[]{:S(2)}, u32[]{:S(2)}) collective-permute-start(f32[56,8,256]{2,1,0:T(8,128)S(1)} %get-tuple-element.43), channel_id=1, source_target_pairs={{0,16},{16,0},{32,48},{48,32},{64,80},{80,64},{96,112},{112,96},{1... | collective-permute-start | bytes 1376264 | tf_op jit(solution)/shard_map/ppermute | solution.py:638
  32.2 7.7 %collective-permute-start.4 = (f32[28,8,128]{2,1,0:T(8,128)S(1)}, f32[28,8,128]{2,1,0:T(8,128)S(1)}, u32[]{:S(2)}, u32[]{:S(2)}) collective-permute-start(f32[28,8,128]{2,1,0:T(8,128)S(1)} %get-tuple-element.46), channel_id=1, source_target_pairs={{0,1},{1,2},{2,3},{3,4},{4,5},{5,6},{6,7},{7,8},{8,9},{9,10},{10,1... | collective-permute-start | bytes 344072 | tf_op jit(solution)/shard_map/ppermute | solution.py:652
  32.2 7.7 %collective-permute-start.5 = (f32[28,8,128]{2,1,0:T(8,128)S(1)}, f32[28,8,128]{2,1,0:T(8,128)S(1)}, u32[]{:S(2)}, u32[]{:S(2)}) collective-permute-start(f32[28,8,128]{2,1,0:T(8,128)S(1)} %get-tuple-element.47), channel_id=1, source_target_pairs={{1,0},{2,1},{3,2},{4,3},{5,4},{6,5},{7,6},{8,7},{9,8},{10,9},{11,1... | collective-permute-start | bytes 344072 | tf_op jit(solution)/shard_map/ppermute | solution.py:652
  37.6 13.6 %collective-permute-start.10 = (f32[48,8,128]{2,1,0:T(8,128)S(1)}, f32[48,8,128]{2,1,0:T(8,128)S(1)}, u32[]{:S(2)}, u32[]{:S(2)}) collective-permute-start(f32[48,8,128]{2,1,0:T(8,128)S(1)} %pad_maximum_fusion), channel_id=1, source_target_pairs={{0,240},{16,32},{32,16},{48,64},{64,48},{80,96},{96,80},{112,128},... | collective-permute-start | bytes 589832 | tf_op jit(solution)/shard_map/ppermute | solution.py:641
  44.1 7.0 %collective-permute-start.6 = (f32[16,8,128]{2,1,0:T(8,128)S(1)}, f32[16,8,128]{2,1,0:T(8,128)S(1)}, u32[]{:S(2)}, u32[]{:S(2)}) collective-permute-start(f32[16,8,128]{2,1,0:T(8,128)S(1)} %get-tuple-element.54.own), channel_id=1, source_target_pairs={{0,16},{16,0},{32,48},{48,32},{64,80},{80,64},{96,112},{112,96},{1... | collective-permute-start | bytes 196616 | tf_op jit(solution)/shard_map/ppermute | solution.py:638
  51.1 8.6 %collective-permute-start.7 = (f32[32,8,128]{2,1,0:T(8,128)S(1)}, f32[32,8,128]{2,1,0:T(8,128)S(1)}, u32[]{:S(2)}, u32[]{:S(2)}) collective-permute-start(f32[32,8,128]{2,1,0:T(8,128)S(1)} %pad_maximum_fusion.1), channel_id=1, source_target_pairs={{0,240},{16,32},{32,16},{48,64},{64,48},{80,96},{96,80},{112,128},... | collective-permute-start | bytes 393224 | tf_op jit(solution)/shard_map/ppermute | solution.py:641
  51.3 13.4 %collective-permute-start.11 = (f32[24,8,128]{2,1,0:T(8,128)S(1)}, f32[24,8,128]{2,1,0:T(8,128)S(1)}, u32[]{:S(2)}, u32[]{:S(2)}) collective-permute-start(f32[24,8,128]{2,1,0:T(8,128)S(1)} %shard_map.84), channel_id=1, source_target_pairs={{0,16},{16,0},{32,48},{48,32},{64,80},{80,64},{96,112},{112,96},{1... | collective-permute-start | bytes 294920 | tf_op jit(solution)/shard_map/ppermute | solution.py:638
  59.7 5.9 %collective-permute-start.8 = (f32[16,8,128]{2,1,0:T(8,128)S(1)}, f32[16,8,128]{2,1,0:T(8,128)S(1)}, u32[]{:S(2)}, u32[]{:S(2)}) collective-permute-start(f32[16,8,128]{2,1,0:T(8,128)S(1)} %shard_map.83), channel_id=1, source_target_pairs={{0,16},{16,0},{32,48},{48,32},{64,80},{80,64},{96,112},{112,96},{1... | collective-permute-start | bytes 196616 | tf_op jit(solution)/shard_map/ppermute | solution.py:638
  71.7 1.3 %collective-permute-start.12 = (f32[16,8,128]{2,1,0:T(8,128)S(1)}, f32[16,8,128]{2,1,0:T(8,128)S(1)}, u32[]{:S(2)}, u32[]{:S(2)}) collective-permute-start(f32[16,8,128]{2,1,0:T(8,128)S(1)} %get-tuple-element.64.own), channel_id=1, source_target_pairs={{0,16},{16,0},{32,48},{48,32},{64,80},{80,64},{96,112},{112,96},{1... | collective-permute-start | bytes 196616 | tf_op jit(solution)/shard_map/ppermute | solution.py:638
  73.1 8.5 %collective-permute-start.13 = (f32[32,8,128]{2,1,0:T(8,128)S(1)}, f32[32,8,128]{2,1,0:T(8,128)S(1)}, u32[]{:S(2)}, u32[]{:S(2)}) collective-permute-start(f32[32,8,128]{2,1,0:T(8,128)S(1)} %pad_maximum_fusion.2), channel_id=1, source_target_pairs={{0,240},{16,32},{32,16},{48,64},{64,48},{80,96},{96,80},{112,128},... | collective-permute-start | bytes 393224 | tf_op jit(solution)/shard_map/ppermute | solution.py:641
  81.6 4.3 %collective-permute-start.14 = (f32[16,8,128]{2,1,0:T(8,128)S(1)}, f32[16,8,128]{2,1,0:T(8,128)S(1)}, u32[]{:S(2)}, u32[]{:S(2)}) collective-permute-start(f32[16,8,128]{2,1,0:T(8,128)S(1)} %shard_map.87), channel_id=1, source_target_pairs={{0,16},{16,0},{32,48},{48,32},{64,80},{80,64},{96,112},{112,96},{1... | collective-permute-start | bytes 196616 | tf_op jit(solution)/shard_map/ppermute | solution.py:638

commit v8 on v7

--- a/solution.py
+++ b/solution.py
@@ -99,6 +99,13 @@
     column = lax.broadcasted_iota(jnp.int32, (COLS, WIDE), 1)
     matrix = jnp.where(column // 2 == row, 1.0, 0.0)
     return jnp.dot(value, matrix, precision=lax.Precision.HIGHEST, preferred_element_type=F32)
+
+
+def half_rows(first, second, lower):
+    row = sublanes(*first.shape)
+    low = jnp.where(row < 4, first, pltpu.roll(second, 4, 0))
+    high = jnp.where(row < 4, pltpu.roll(first, 4, 0), second)
+    return jnp.where(lower, low, high)
 
 
 def pick(table_row, index):
@@ -362,10 +369,12 @@
         beside = pltpu.roll(here, 1, 1) + pltpu.roll(here, WIDE - 1, 1)
         total = ka[z] + here * (below + above + beside) + h[z + 1] * (h[z] + h[z + 2])
         d[z] = total
-        inverse[z] = 1.0 / total
+        reciprocal = 1.0 / total
+        inverse[z] = reciprocal
+        for i in range(2):
+            xa[z + 1, i] = (FINE[0] * reciprocal) * r[z, i]
 
     loop(NZ, diagonals)
-    level.first(xa, r, FINE[0])
     level.update(xp, xa, r, FINE[1])
     fine_restrict(level, xp, r, sums, buffer, r1)
 
@@ -424,8 +433,8 @@
     loop(4, diagonals_two)
 
 
-def coarse_solve(core, one, two, pieces, r1, xa1, xb1, r2, xa2, xb2, buffer):
-    own, partner, odd, far = pieces
+def coarse_solve(core, one, two, pieces, far_tile, r1, xa1, xb1, r2, xa2, xb2, buffer):
+    own, partner, odd, second = pieces
     clear_ends(xa1, xb1, xa2, xb2)
     starts = (16, 24 - 16 * core, 8 + 16 * core, 32 * core, 32 - 32 * core)
     starts = [s if isinstance(s, int) else pl.multiple_of(s, 8) for s in starts]
@@ -433,7 +442,7 @@
     def assemble(z):
         for i in range(2):
             j = 2 * z + i
-            tiles = (own[j], partner[j], odd[j], odd[R_TILES + j], far[j])
+            tiles = (own[j], partner[j], odd[j], far_tile(z, i), second[j])
             for start, tile in zip(starts, tiles):
                 r1[z, i, pl.ds(start, 8), :] = tile
 
@@ -482,6 +491,15 @@
 
 def near_kernel(odd, near):
     near[...] = odd[0:R_TILES]
+
+
+def far_half_kernel(place, own, partner, message):
+    message[0:R_TILES] = own[...]
+
+    def pair(p):
+        message[R_TILES + p] = half_rows(partner[2 * p], partner[2 * p + 1], place[0] == 0)
+
+    loop(R_TILES // 2, pair)
 
 
 def after_kernel(odd, after, near):
@@ -505,18 +523,20 @@
     zero = Level(NZ, 1, g, h, inverse, d)
     one = Level(8, 1, g1, h1, i1, d1)
     two = Level(4, 2, g2, h2, i2)
-    coarse_solve(core, one, two, (own, partner, odd, far), r1, xa1, xb1, r2, xa2, xb2, buffer)
+    coarse_solve(core, one, two, (own, partner, odd, far), lambda z, i: odd[R_TILES + 2 * z + i], r1, xa1, xb1, r2, xa2, xb2, buffer)
     clear_ends(xa, xb, xp_out)
     fine_correct(zero, xa, xp, xa1, wide, buffer)
     zero.update(xb, xa, r, FINE[0])
 
     def last(z):
         scaled = FINE[1] * inverse[z]
-        for i in range(2):
-            z_out[z, i] = (1.0 - FINE[1]) * xb[z + 1, i] + scaled * (r[z, i] + zero.couple(xb, z, i))
+        first = FINE[0] * inverse[z]
+        for i in range(2):
+            value = (1.0 - FINE[1]) * xb[z + 1, i] + scaled * (r[z, i] + zero.couple(xb, z, i))
+            z_out[z, i] = value
+            xa[z + 1, i] = first * value
 
     loop(NZ, last)
-    zero.first(xa, z_out, FINE[0])
     zero.update(xp_out, xa, z_out, FINE[1])
     fine_restrict(zero, xp_out, z_out, sums, buffer, r1_out)
 
@@ -530,7 +550,12 @@
     zero = Level(NZ, 1, g, h, inverse, d)
     one = Level(8, 1, g1, h1, i1, d1)
     two = Level(4, 2, g2, h2, i2)
-    coarse_solve(core, one, two, (own, partner, odd, far), r1, xa1, xb1, r2, xa2, xb2, buffer)
+
+    def far_tile(z, i):
+        tile = odd[R_TILES + z]
+        return jnp.where((core == 0) == (i == 0), pltpu.roll(tile, 4, 0), tile)
+
+    coarse_solve(core, one, two, (own, partner, odd, far), far_tile, r1, xa1, xb1, r2, xa2, xb2, buffer)
     clear_ends(xa, xb)
     fine_correct(zero, xa, xp, xa1, wide, buffer)
     zero.update(xb, xa, r, FINE[0])
@@ -587,6 +612,7 @@
     "material_kernel": 1,
     "down_kernel": 4,
     "near_kernel": 30,
+    "far_half_kernel": 1,
     "after_kernel": 30,
     "coarse_kernel": 1,
     "middle_kernel": 6,
@@ -640,8 +666,8 @@
     def across_chips(value):
         return lax.ppermute(value, "gx", pairs_across)
 
-    def rows_of(own, partner):
-        odd = across_chips(jnp.concatenate([own, partner], axis=0))
+    def rows_of(own, partner, message):
+        odd = across_chips(message)
         near = call(near_kernel, (odd,), [own.shape], place=False)[0]
         return own, partner, odd, on_chip(near)
 
@@ -683,7 +709,8 @@
         [FIELD0, (NZ, EXT0, WIDE), (NZ + 2, EXT0, WIDE), (NZ, EXT0, WIDE), (NZ, EXT0, WIDE), PADDED0, (R_TILES, 8, COLS)],
         [PADDED0, (NZ, EXT0, WIDE), (2, NZ, WIDE), SUMS, BUFFER],
     )
-    rows = rows_of(r1, on_chip(r1))
+    partner = on_chip(r1)
+    rows = rows_of(r1, partner, jnp.concatenate([r1, partner], axis=0))
     packed_near = call(
         after_kernel, (packed_odd, rows[1]), [packed.shape], place=False, far={1: pl.ANY}
     )[0]
@@ -699,10 +726,12 @@
         [FIELD0, PADDED0, (R_TILES, 8, COLS)],
         [PADDED0, PADDED0, *COARSE_SCRATCH, SUMS, BUFFER],
     )
+    partner = on_chip(r1)
+    message = call(far_half_kernel, (place, r1, partner), [(R_TILES * 3 // 2, 8, COLS)])[0]
     count = count_x * count_y
     direction, image, sums = call(
         last_kernel,
-        (place, fields, r, g, h, d, inverse, xp, *rows_of(r1, on_chip(r1)), *coarse),
+        (place, fields, r, g, h, d, inverse, xp, *rows_of(r1, partner, message), *coarse),
         [(2, NZ, ROWS, COLS)] * 2 + [(count, COLS)],
         [PADDED0, PADDED0, *COARSE_SCRATCH, (4, ROWS, COLS), BUFFER],
     )

time: 113 us -> 112 us (level)
    pallas_call x13 -> x14, Pallas kernels: 21.4 us -> 21.9 us  [call(): pl.pallas_call(kernel, out_shape=[jax.ShapeDtypeStruct(shape, F32) for sh...]
where the time goes in v8:
time: 112 us
  starting transfers between devices  41.5 us (37%)
  waiting for transfers between devices  26.3 us (23%)
  Pallas kernels  21.9 us (20%)
  blocking collectives  20 us (18%)
  other arithmetic  1.33 us (1%)
    pallas_call x14, Pallas kernels, call(): pl.pallas_call(kernel, out_shape=[jax.ShapeDtypeStruct(shape, F32) for sh...  21.9 us
    ppermute x7, starting transfers between devices, on_chip(): return lax.ppermute(value, 'gx', pairs_on_chip)  21.5 us
    ppermute x4, waiting for transfers between devices, across_chips(): return lax.ppermute(value, 'gx', pairs_across)  21.4 us
    all_to_all x1, blocking collectives, shards(): lax.all_to_all(sums.reshape(count, 1, COLS), ('gx', 'gy'), 0, 0)  20 us
    ppermute x2, starting transfers between devices, both_sides(): lax.ppermute(to_left, 'gy', backward)  10.4 us
    ppermute x4, starting transfers between devices, across_chips(): return lax.ppermute(value, 'gx', pairs_across)  7.05 us
    ppermute x7, waiting for transfers between devices, on_chip(): return lax.ppermute(value, 'gx', pairs_on_chip)  2.77 us
    ppermute x2, starting transfers between devices, both_sides(): lax.ppermute(to_right, 'gy', forward)  2.54 us
  transfers between devices with their start and end apart: 15, of which 7 were waited for; matrix products, arithmetic and copies ran while one was open for 0% of the time, Pallas kernels for 7%

profile of v8, /device:TPU:1, one launch (start us, length us, event | category | flops | bytes accessed | tf_op | source)
XLA Modules:
  0.0 111.9 jit_solution(6766121671881360198)
XLA Ops:
  0.7 0.1 pad_add_fusion.place
  0.8 1.2 %bitcast_select_fusion.fields.rhs = f32[4,16,16,128]{3,2,1,0:T(8,128)S(1)} fusion(s32[16,16,128]{2,1,0:T(8,128)} %param.8, s32[16,16,128]{2,1,0:T(8,128)} %param.7, f32[2,16,16,128]{3,2,1,0:T(8,128)} %param.6, pred[4]{0:T(512)(128)(4,1)S(1)} %get-tuple-element.68, pred[4]{0:T(512)(128)(4,1)S(1)} %get-tuple-element.69), kind=kLoop, calls=%fused_computation | loop fusion | flops 393216 | bytes 1048584 | tf_op jit(solution)/shard_map/jit(_where)/select_n | solution.py:683
  2.0 0.0 copy-start
  2.0 0.0 copy-start.1
  2.0 0.0 copy-start.2
  2.0 1.1 shard_map.77
  3.1 2.5 %collective-permute-start = (f32[26,16,128]{2,1,0:T(8,128)S(1)}, f32[26,16,128]{2,1,0:T(8,128)S(1)}, u32[]{:S(2)}, u32[]{:S(2)}) collective-permute-start(f32[26,16,128]{2,1,0:T(8,128)S(1)} %get-tuple-element.35), channel_id=1, source_target_pairs={{0,1},{1,2},{2,3},{3,4},{4,5},{5,6},{6,7},{7,8},{8,9},{9,10},{10,1... | collective-permute-start | bytes 638984 | tf_op jit(solution)/shard_map/ppermute | solution.py:678
  5.6 5.0 %collective-permute-start.1 = (f32[26,16,128]{2,1,0:T(8,128)S(1)}, f32[26,16,128]{2,1,0:T(8,128)S(1)}, u32[]{:S(2)}, u32[]{:S(2)}) collective-permute-start(f32[26,16,128]{2,1,0:T(8,128)S(1)} %get-tuple-element.36), channel_id=1, source_target_pairs={{1,0},{2,1},{3,2},{4,3},{5,4},{6,5},{7,6},{8,7},{9,8},{10,9},{11,1... | collective-permute-start | bytes 638984 | tf_op jit(solution)/shard_map/ppermute | solution.py:678
  10.6 6.8 %collective-permute-start.3 = (f32[56,8,128]{2,1,0:T(8,128)S(1)}, f32[56,8,128]{2,1,0:T(8,128)S(1)}, u32[]{:S(2)}, u32[]{:S(2)}) collective-permute-start(f32[56,8,128]{2,1,0:T(8,128)S(1)} %get-tuple-element.44), channel_id=1, source_target_pairs={{0,240},{16,32},{32,16},{48,64},{64,48},{80,96},{96,80},{112,128},... | collective-permute-start | bytes 688136 | tf_op jit(solution)/shard_map/ppermute | solution.py:667
  17.4 0.0 copy-done
  17.4 0.0 copy-done.1
  17.4 0.0 copy-done.2
  17.4 0.0 collective-permute-done.from_left
  17.4 0.0 collective-permute-done.1.from_right
  17.5 1.1 %shard_map.78 = (f32[16,2,16,256]{3,2,1,0:T(8,128)S(1)}, f32[16,16,256]{2,1,0:T(8,128)S(1)}, f32[16,16,256]{2,1,0:T(8,128)S(1)}, f32[56,8,256]{2,1,0:T(8,128)S(1)}) custom-call(s32[5]{0:T(128)S(1)} %pad_add_fusion.place, f32[4,16,16,128]{3,2,1,0:T(8,128)S(1)} %bitcast_select_fusion.fields.rhs, f32[26,16,128]{2,1,0:T(8,128)S(1)} %collective-permute-done.from_left, ...), custom_call_target="tpu_custom_call" | custom-call | flops 1000000000 | bytes 3000000 | tf_op jit(solution)/shard_map/pallas_call | solution.py:630
  18.6 0.9 shard_map.79
  19.5 2.8 %collective-permute-start.9 = (f32[24,8,128]{2,1,0:T(8,128)S(1)}, f32[24,8,128]{2,1,0:T(8,128)S(1)}, u32[]{:S(2)}, u32[]{:S(2)}) collective-permute-start(f32[24,8,128]{2,1,0:T(8,128)S(1)} %get-tuple-element.45.after.own), channel_id=1, source_target_pairs={{0,16},{16,0},{32,48},{48,32},{64,80},{80,64},{96,112},{112,96},{1... | collective-permute-start | bytes 294920 | tf_op jit(solution)/shard_map/ppermute | solution.py:664
  22.4 0.1 collective-permute-start.2
  22.5 9.2 %collective-permute-done.3.message = f32[56,8,128]{2,1,0:T(8,128)S(1)} collective-permute-done((f32[56,8,128]{2,1,0:T(8,128)S(1)}, f32[56,8,128]{2,1,0:T(8,128)S(1)}, u32[]{:S(2)}, u32[]{:S(2)}) %collective-permute-start.3) | collective-permute-done | bytes 229408 | tf_op jit(solution)/shard_map/ppermute | solution.py:667
  31.7 0.5 shard_map.80
  32.2 0.0 collective-permute-start.4
  32.2 5.4 %collective-permute-start.5 = (f32[28,8,128]{2,1,0:T(8,128)S(1)}, f32[28,8,128]{2,1,0:T(8,128)S(1)}, u32[]{:S(2)}, u32[]{:S(2)}) collective-permute-start(f32[28,8,128]{2,1,0:T(8,128)S(1)} %get-tuple-element.47), channel_id=1, source_target_pairs={{1,0},{2,1},{3,2},{4,3},{5,4},{6,5},{7,6},{8,7},{9,8},{10,9},{11,1... | collective-permute-start | bytes 344072 | tf_op jit(solution)/shard_map/ppermute | solution.py:678
  37.6 0.0 collective-permute-done.9.partner
  37.6 0.1 collective-permute-start.10
  37.7 2.2 %collective-permute-done.4.corner_left = f32[28,8,128]{2,1,0:T(8,128)S(1)} collective-permute-done((f32[28,8,128]{2,1,0:T(8,128)S(1)}, f32[28,8,128]{2,1,0:T(8,128)S(1)}, u32[]{:S(2)}, u32[]{:S(2)}) %collective-permute-start.4) | collective-permute-done | bytes 114720 | tf_op jit(solution)/shard_map/ppermute | solution.py:678
  39.9 0.0 collective-permute-done.5.corner_right
  39.9 0.5 shard_map.81.wide
  40.5 0.0 collective-permute-done.2.from_x
  40.5 3.6 %shard_map.82 = (f32[16,2,32,256]{3,2,1,0:T(8,128)S(1)}, f32[16,32,256]{2,1,0:T(8,128)S(1)}, f32[18,32,256]{2,1,0:T(8,128)S(1)}, f32[16,32,256]{2,1,0:T(8,128)S(...) custom-call(s32[5]{0:T(128)S(1)} %pad_add_fusion.place, ...), custom_call_target="tpu_custom_call" | custom-call | flops 4000000000 | bytes 12000000 | tf_op jit(solution)/shard_map/pallas_call | solution.py:630
  44.0 6.1 %collective-permute-start.6 = (f32[16,8,128]{2,1,0:T(8,128)S(1)}, f32[16,8,128]{2,1,0:T(8,128)S(1)}, u32[]{:S(2)}, u32[]{:S(2)}) collective-permute-start(f32[16,8,128]{2,1,0:T(8,128)S(1)} %get-tuple-element.54.own), channel_id=1, source_target_pairs={{0,16},{16,0},{32,48},{48,32},{64,80},{80,64},{96,112},{112,96},{1... | collective-permute-start | bytes 196616 | tf_op jit(solution)/shard_map/ppermute | solution.py:664
  50.2 0.9 collective-permute-done.6.after.partner
  51.1 0.1 collective-permute-start.7
  51.2 0.0 collective-permute-done.10.odd
  51.2 4.2 %collective-permute-start.11 = (f32[24,8,128]{2,1,0:T(8,128)S(1)}, f32[24,8,128]{2,1,0:T(8,128)S(1)}, u32[]{:S(2)}, u32[]{:S(2)}) collective-permute-start(f32[24,8,128]{2,1,0:T(8,128)S(1)} %shard_map.84), channel_id=1, source_target_pairs={{0,16},{16,0},{32,48},{48,32},{64,80},{80,64},{96,112},{112,96},{1... | collective-permute-start | bytes 294920 | tf_op jit(solution)/shard_map/ppermute | solution.py:664
  55.4 4.2 %collective-permute-done.7.odd = f32[32,8,128]{2,1,0:T(8,128)S(1)} collective-permute-done((f32[32,8,128]{2,1,0:T(8,128)S(1)}, f32[32,8,128]{2,1,0:T(8,128)S(1)}, u32[]{:S(2)}, u32[]{:S(2)}) %collective-permute-start.7) | collective-permute-done | bytes 131104 | tf_op jit(solution)/shard_map/ppermute | solution.py:667
  59.6 5.0 %collective-permute-start.8 = (f32[16,8,128]{2,1,0:T(8,128)S(1)}, f32[16,8,128]{2,1,0:T(8,128)S(1)}, u32[]{:S(2)}, u32[]{:S(2)}) collective-permute-start(f32[16,8,128]{2,1,0:T(8,128)S(1)} %shard_map.83), channel_id=1, source_target_pairs={{0,16},{16,0},{32,48},{48,32},{64,80},{80,64},{96,112},{112,96},{1... | collective-permute-start | bytes 196616 | tf_op jit(solution)/shard_map/ppermute | solution.py:664
  64.7 0.0 collective-permute-done.11.far
  64.7 0.9 shard_map.85
  65.6 0.0 collective-permute-done.8.far
  65.6 6.0 %shard_map.86 = (f32[16,2,32,256]{3,2,1,0:T(8,128)S(1)}, f32[18,2,32,256]{3,2,1,0:T(8,128)S(1)}, f32[16,8,128]{2,1,0:T(8,128)S(1)}) custom-call(s32[5]{0:T(128)S(1)} %pad_add_fusion.place, f32[16,2,32,256]{3,2,1,0:T(8,128)S(1)} %get-tuple-element.48.r, f32[16,32,256]{2,1,0:T(8,128)S(1)} %get-tuple-element.49.g, f32[18,32,256]{2,1,0:T(8,128)S(1)} %get-tuple-element.50.h, ...), custom_call_target="tpu_custom_call" | custom-call | flops 6000000000 | bytes 18000000 | tf_op jit(solution)/shard_map/pallas_call | solution.py:630
  71.6 0.4 collective-permute-start.12
  72.0 1.0 collective-permute-done.12.partner
  73.0 0.6 shard_map.87
  73.6 0.1 collective-permute-start.13
  73.7 7.9 %collective-permute-done.13.odd = f32[24,8,128]{2,1,0:T(8,128)S(1)} collective-permute-done((f32[24,8,128]{2,1,0:T(8,128)S(1)}, f32[24,8,128]{2,1,0:T(8,128)S(1)}, u32[]{:S(2)}, u32[]{:S(2)}) %collective-permute-start.13) | collective-permute-done | bytes 98336 | tf_op jit(solution)/shard_map/ppermute | solution.py:667
  81.6 2.8 %collective-permute-start.14 = (f32[16,8,128]{2,1,0:T(8,128)S(1)}, f32[16,8,128]{2,1,0:T(8,128)S(1)}, u32[]{:S(2)}, u32[]{:S(2)}) collective-permute-start(f32[16,8,128]{2,1,0:T(8,128)S(1)} %shard_map.88), channel_id=1, source_target_pairs={{0,16},{16,0},{32,48},{48,32},{64,80},{80,64},{96,112},{112,96},{1... | collective-permute-start | bytes 196616 | tf_op jit(solution)/shard_map/ppermute | solution.py:664
  84.4 0.9 collective-permute-done.14.far
  85.3 5.6 %shard_map.89 = (f32[2,16,16,128]{3,2,1,0:T(8,128)S(1)}, f32[2,16,16,128]{3,2,1,0:T(8,128)S(1)}, f32[256,128]{1,0:T(8,128)S(1)}) custom-call(s32[5]{0:T(128)S(1)} %pad_add_fusion.place, f32[4,16,16,128]{3,2,1,0:T(8,128)S(1)} %bitcast_select_fusion.fields.rhs, f32[16,2,32,256]{3,2,1,0:T(8,128)S(1)} %get-tuple-element.62.r, ...), custom_call_target="tpu_custom_call" | custom-call | flops 6000000000 | bytes 18000000 | tf_op jit(solution)/shard_map/pallas_call | solution.py:630
  91.0 20.0 %all_to_all.5 = f32[256,1,128]{2,1,0:T(1,128)S(1)} all-to-all(f32[256,1,128]{2,1,0:T(1,128)S(1)} %bitcast.14), channel_id=1, replica_groups=mesh['gx'=16,'gy'=16] {'gx','gy'}, dimensions={0} | all-to-all | bytes 262144 | tf_op jit(solution)/shard_map/all_to_all | solution.py:738
  111.0 1.0 shard_map.90
  (9 shorter events, 0.1 us)
Async XLA Ops:
  2.0 15.4 %copy-start = (f32[16]{0:T(128)S(1)}, f32[16]{0:T(128)}, u32[]{:S(2)}) copy-start(f32[16]{0:T(128)} %param.11) | copy-start | bytes 196
  2.0 15.4 %copy-start.1 = (f32[16]{0:T(128)S(1)}, f32[16]{0:T(128)}, u32[]{:S(2)}) copy-start(f32[16]{0:T(128)} %param.10) | copy-start | bytes 196
  2.0 15.4 %copy-start.2 = (f32[16]{0:T(128)S(1)}, f32[16]{0:T(128)}, u32[]{:S(2)}) copy-start(f32[16]{0:T(128)} %param.9) | copy-start | bytes 196
  3.1 14.4 %collective-permute-start = (f32[26,16,128]{2,1,0:T(8,128)S(1)}, f32[26,16,128]{2,1,0:T(8,128)S(1)}, u32[]{:S(2)}, u32[]{:S(2)}) collective-permute-start(f32[26,16,128]{2,1,0:T(8,128)S(1)} %get-tuple-element.35), channel_id=1, source_target_pairs={{0,1},{1,2},{2,3},{3,4},{4,5},{5,6},{6,7},{7,8},{8,9},{9,10},{10,1... | collective-permute-start | bytes 638984 | tf_op jit(solution)/shard_map/ppermute | solution.py:678
  5.6 11.8 %collective-permute-start.1 = (f32[26,16,128]{2,1,0:T(8,128)S(1)}, f32[26,16,128]{2,1,0:T(8,128)S(1)}, u32[]{:S(2)}, u32[]{:S(2)}) collective-permute-start(f32[26,16,128]{2,1,0:T(8,128)S(1)} %get-tuple-element.36), channel_id=1, source_target_pairs={{1,0},{2,1},{3,2},{4,3},{5,4},{6,5},{7,6},{8,7},{9,8},{10,9},{11,1... | collective-permute-start | bytes 638984 | tf_op jit(solution)/shard_map/ppermute | solution.py:678
  10.6 21.1 %collective-permute-start.3 = (f32[56,8,128]{2,1,0:T(8,128)S(1)}, f32[56,8,128]{2,1,0:T(8,128)S(1)}, u32[]{:S(2)}, u32[]{:S(2)}) collective-permute-start(f32[56,8,128]{2,1,0:T(8,128)S(1)} %get-tuple-element.44), channel_id=1, source_target_pairs={{0,240},{16,32},{32,16},{48,64},{64,48},{80,96},{96,80},{112,128},... | collective-permute-start | bytes 688136 | tf_op jit(solution)/shard_map/ppermute | solution.py:667
  19.5 18.1 %collective-permute-start.9 = (f32[24,8,128]{2,1,0:T(8,128)S(1)}, f32[24,8,128]{2,1,0:T(8,128)S(1)}, u32[]{:S(2)}, u32[]{:S(2)}) collective-permute-start(f32[24,8,128]{2,1,0:T(8,128)S(1)} %get-tuple-element.45.after.own), channel_id=1, source_target_pairs={{0,16},{16,0},{32,48},{48,32},{64,80},{80,64},{96,112},{112,96},{1... | collective-permute-start | bytes 294920 | tf_op jit(solution)/shard_map/ppermute | solution.py:664
  22.4 18.1 %collective-permute-start.2 = (f32[56,8,256]{2,1,0:T(8,128)S(1)}, f32[56,8,256]{2,1,0:T(8,128)S(1)}, u32[]{:S(2)}, u32[]{:S(2)}) collective-permute-start(f32[56,8,256]{2,1,0:T(8,128)S(1)} %get-tuple-element.43), channel_id=1, source_target_pairs={{0,16},{16,0},{32,48},{48,32},{64,80},{80,64},{96,112},{112,96},{1... | collective-permute-start | bytes 1376264 | tf_op jit(solution)/shard_map/ppermute | solution.py:664
  32.2 7.7 %collective-permute-start.4 = (f32[28,8,128]{2,1,0:T(8,128)S(1)}, f32[28,8,128]{2,1,0:T(8,128)S(1)}, u32[]{:S(2)}, u32[]{:S(2)}) collective-permute-start(f32[28,8,128]{2,1,0:T(8,128)S(1)} %get-tuple-element.46), channel_id=1, source_target_pairs={{0,1},{1,2},{2,3},{3,4},{4,5},{5,6},{6,7},{7,8},{8,9},{9,10},{10,1... | collective-permute-start | bytes 344072 | tf_op jit(solution)/shard_map/ppermute | solution.py:678
  32.2 7.7 %collective-permute-start.5 = (f32[28,8,128]{2,1,0:T(8,128)S(1)}, f32[28,8,128]{2,1,0:T(8,128)S(1)}, u32[]{:S(2)}, u32[]{:S(2)}) collective-permute-start(f32[28,8,128]{2,1,0:T(8,128)S(1)} %get-tuple-element.47), channel_id=1, source_target_pairs={{1,0},{2,1},{3,2},{4,3},{5,4},{6,5},{7,6},{8,7},{9,8},{10,9},{11,1... | collective-permute-start | bytes 344072 | tf_op jit(solution)/shard_map/ppermute | solution.py:678
  37.6 13.6 %collective-permute-start.10 = (f32[48,8,128]{2,1,0:T(8,128)S(1)}, f32[48,8,128]{2,1,0:T(8,128)S(1)}, u32[]{:S(2)}, u32[]{:S(2)}) collective-permute-start(f32[48,8,128]{2,1,0:T(8,128)S(1)} %pad_maximum_fusion), channel_id=1, source_target_pairs={{0,240},{16,32},{32,16},{48,64},{64,48},{80,96},{96,80},{112,128},... | collective-permute-start | bytes 589832 | tf_op jit(solution)/shard_map/ppermute | solution.py:667
  44.0 7.0 %collective-permute-start.6 = (f32[16,8,128]{2,1,0:T(8,128)S(1)}, f32[16,8,128]{2,1,0:T(8,128)S(1)}, u32[]{:S(2)}, u32[]{:S(2)}) collective-permute-start(f32[16,8,128]{2,1,0:T(8,128)S(1)} %get-tuple-element.54.own), channel_id=1, source_target_pairs={{0,16},{16,0},{32,48},{48,32},{64,80},{80,64},{96,112},{112,96},{1... | collective-permute-start | bytes 196616 | tf_op jit(solution)/shard_map/ppermute | solution.py:664
  51.1 8.6 %collective-permute-start.7 = (f32[32,8,128]{2,1,0:T(8,128)S(1)}, f32[32,8,128]{2,1,0:T(8,128)S(1)}, u32[]{:S(2)}, u32[]{:S(2)}) collective-permute-start(f32[32,8,128]{2,1,0:T(8,128)S(1)} %pad_maximum_fusion.1), channel_id=1, source_target_pairs={{0,240},{16,32},{32,16},{48,64},{64,48},{80,96},{96,80},{112,128},... | collective-permute-start | bytes 393224 | tf_op jit(solution)/shard_map/ppermute | solution.py:667
  51.2 13.4 %collective-permute-start.11 = (f32[24,8,128]{2,1,0:T(8,128)S(1)}, f32[24,8,128]{2,1,0:T(8,128)S(1)}, u32[]{:S(2)}, u32[]{:S(2)}) collective-permute-start(f32[24,8,128]{2,1,0:T(8,128)S(1)} %shard_map.84), channel_id=1, source_target_pairs={{0,16},{16,0},{32,48},{48,32},{64,80},{80,64},{96,112},{112,96},{1... | collective-permute-start | bytes 294920 | tf_op jit(solution)/shard_map/ppermute | solution.py:664
  59.6 5.9 %collective-permute-start.8 = (f32[16,8,128]{2,1,0:T(8,128)S(1)}, f32[16,8,128]{2,1,0:T(8,128)S(1)}, u32[]{:S(2)}, u32[]{:S(2)}) collective-permute-start(f32[16,8,128]{2,1,0:T(8,128)S(1)} %shard_map.83), channel_id=1, source_target_pairs={{0,16},{16,0},{32,48},{48,32},{64,80},{80,64},{96,112},{112,96},{1... | collective-permute-start | bytes 196616 | tf_op jit(solution)/shard_map/ppermute | solution.py:664
  71.6 1.3 %collective-permute-start.12 = (f32[16,8,128]{2,1,0:T(8,128)S(1)}, f32[16,8,128]{2,1,0:T(8,128)S(1)}, u32[]{:S(2)}, u32[]{:S(2)}) collective-permute-start(f32[16,8,128]{2,1,0:T(8,128)S(1)} %get-tuple-element.64.own), channel_id=1, source_target_pairs={{0,16},{16,0},{32,48},{48,32},{64,80},{80,64},{96,112},{112,96},{1... | collective-permute-start | bytes 196616 | tf_op jit(solution)/shard_map/ppermute | solution.py:664
  73.6 8.0 %collective-permute-start.13 = (f32[24,8,128]{2,1,0:T(8,128)S(1)}, f32[24,8,128]{2,1,0:T(8,128)S(1)}, u32[]{:S(2)}, u32[]{:S(2)}) collective-permute-start(f32[24,8,128]{2,1,0:T(8,128)S(1)} %shard_map.87), channel_id=1, source_target_pairs={{0,240},{16,32},{32,16},{48,64},{64,48},{80,96},{96,80},{112,128},... | collective-permute-start | bytes 294920 | tf_op jit(solution)/shard_map/ppermute | solution.py:667
  81.6 3.7 %collective-permute-start.14 = (f32[16,8,128]{2,1,0:T(8,128)S(1)}, f32[16,8,128]{2,1,0:T(8,128)S(1)}, u32[]{:S(2)}, u32[]{:S(2)}) collective-permute-start(f32[16,8,128]{2,1,0:T(8,128)S(1)} %shard_map.88), channel_id=1, source_target_pairs={{0,16},{16,0},{32,48},{48,32},{64,80},{80,64},{96,112},{112,96},{1... | collective-permute-start | bytes 196616 | tf_op jit(solution)/shard_map/ppermute | solution.py:664

commit v9 on v8

--- a/solution.py
+++ b/solution.py
@@ -132,6 +132,43 @@
     return first, second
 
 
+SPAN = 51
+QUINTS = 6
+
+
+def pack_quint(a, b, c, d, e):
+    lane = lanes(*a.shape)
+    lows = [
+        jnp.where(lane < SPAN, x, jnp.where(lane < 2 * SPAN, pltpu.roll(y, SPAN, 1), pltpu.roll(e, shift, 1)))
+        for x, y, shift in ((a, b, 102), (c, d, 76))
+    ]
+    highs = [
+        jnp.where(
+            lane >= COLS - SPAN,
+            x,
+            jnp.where(lane >= COLS - 2 * SPAN, pltpu.roll(y, COLS - SPAN, 1), pltpu.roll(e, COLS - shift, 1)),
+        )
+        for x, y, shift in ((a, b, 102), (c, d, 76))
+    ]
+    return lows, highs
+
+
+def unpack_quint(from_right, from_left):
+    lane = lanes(*from_right[0].shape)
+    left = lane < HALF
+    fields = []
+    for right, other in zip(from_right, from_left):
+        fields.append(jnp.where(left, right, other))
+        fields.append(jnp.where(left, pltpu.roll(right, COLS - SPAN, 1), pltpu.roll(other, SPAN, 1)))
+    parts = [
+        jnp.where(left, pltpu.roll(right, COLS - shift, 1), pltpu.roll(other, shift, 1))
+        for right, other, shift in zip(from_right, from_left, (102, 76))
+    ]
+    outer = (lane < COLS - 102) | (lane >= 102)
+    fields.append(jnp.where(outer, parts[0], parts[1]))
+    return fields
+
+
 def pack_sea(fields):
     rows, width = fields[0].shape
     even_lane = lanes(rows, width) % 2 == 0
@@ -168,7 +205,8 @@
     loop(4, quads)
 
 
-MSG_Y = 26
+MSG_Y = 23
+CORNER = 25
 MSG_X = 56
 R_TILES = 16
 M_TILES = 24
@@ -179,34 +217,56 @@
     classes, sea = fields.at[2], fields.at[3]
 
     def convert(pair):
-        to_left[16 + pair], to_right[16 + pair] = pack_halves(classes[2 * pair], classes[2 * pair + 1])
+        to_left[13 + pair], to_right[13 + pair] = pack_halves(classes[2 * pair], classes[2 * pair + 1])
 
     loop(8, convert)
     for j in range(2):
         quads = [pack_sea([sea[8 * j + 4 * q + i] for i in range(4)]) for q in range(2)]
-        to_left[24 + j], to_right[24 + j] = pack_halves(quads[0], quads[1])
-
-    def pair(z):
-        to_left[z], to_right[z] = pack_halves(fields[0, z], fields[1, z])
-
-    loop(NZ, pair)
+        to_left[21 + j], to_right[21 + j] = pack_halves(quads[0], quads[1])
+
+    def quint(k):
+        group = [fields[(5 * k + t) // NZ, (5 * k + t) % NZ] for t in range(5)]
+        lows, highs = pack_quint(*group)
+        for t in range(2):
+            to_left[2 * k + t] = lows[t]
+            to_right[2 * k + t] = highs[t]
+
+    loop(QUINTS, quint)
+    to_left[12], to_right[12] = pack_halves(fields[1, 14], fields[1, 15])
     start = pl.multiple_of(8 * core, 8)
     fill_message(message, lambda z, i: fields.at[i, z], classes, sea, start, 8 - core)
 
 
 def corner_kernel(message, after, to_left, to_right):
+    def quint(k):
+        lows, highs = pack_quint(*(message[5 * k + t] for t in range(5)))
+        for t in range(2):
+            to_left[2 * k + t] = lows[t]
+            to_right[2 * k + t] = highs[t]
+
+    loop(QUINTS, quint)
+
     def pair(p):
-        to_left[p], to_right[p] = pack_halves(message[2 * p], message[2 * p + 1])
-
-    loop(MSG_X // 2, pair)
+        to_left[12 + p], to_right[12 + p] = pack_halves(message[30 + 2 * p], message[31 + 2 * p])
+
+    loop(CORNER - 12, pair)
 
 
 def widen_kernel(message, corner_left, corner_right, wide):
+    def quint(k):
+        halos = unpack_quint(
+            [corner_right[2 * k + t] for t in range(2)], [corner_left[2 * k + t] for t in range(2)]
+        )
+        for t, halo in enumerate(halos):
+            wide[5 * k + t] = jnp.concatenate([message[5 * k + t], halo], axis=1)
+
+    loop(QUINTS, quint)
+
     def pair(p):
-        for i, halo in enumerate(unpack_halves(corner_right[p], corner_left[p])):
-            wide[2 * p + i] = jnp.concatenate([message[2 * p + i], halo], axis=1)
-
-    loop(MSG_X // 2, pair)
+        for i, halo in enumerate(unpack_halves(corner_right[12 + p], corner_left[12 + p])):
+            wide[30 + 2 * p + i] = jnp.concatenate([message[30 + 2 * p + i], halo], axis=1)
+
+    loop(CORNER - 12, pair)
 
 
 def rows_kernel(place, fields, from_left, from_right, r_out, c_out, s_out, message):
@@ -219,20 +279,25 @@
         jnp.where(gy > 0, 1.0, 0.0),
     )
 
-    def rhs_step(z):
-        halo = unpack_halves(from_right[z], from_left[z])
-        for i in range(2):
-            r_out[z, i] = jnp.concatenate([fields[i, z], halo[i]], axis=1)
-
-    loop(NZ, rhs_step)
+    def rhs_step(k):
+        halos = unpack_quint(
+            [from_right[2 * k + t] for t in range(2)], [from_left[2 * k + t] for t in range(2)]
+        )
+        for t, halo in enumerate(halos):
+            i, z = (5 * k + t) // NZ, (5 * k + t) % NZ
+            r_out[z, i] = jnp.concatenate([fields[i, z], halo], axis=1)
+
+    loop(QUINTS, rhs_step)
+    for t, halo in enumerate(unpack_halves(from_right[12], from_left[12])):
+        r_out[14 + t, 1] = jnp.concatenate([fields[1, 14 + t], halo], axis=1)
 
     def class_step(pair):
-        for i, halo in enumerate(unpack_halves(from_right[16 + pair], from_left[16 + pair])):
+        for i, halo in enumerate(unpack_halves(from_right[13 + pair], from_left[13 + pair])):
             c_out[2 * pair + i] = jnp.concatenate([fields[2, 2 * pair + i], halo], axis=1)
 
     loop(8, class_step)
     for j in range(2):
-        quads = unpack_halves(from_right[24 + j], from_left[24 + j])
+        quads = unpack_halves(from_right[21 + j], from_left[21 + j])
         for q in range(2):
             for i, field in enumerate(unpack_sea(quads[q])):
                 z = 8 * j + 4 * q + i
@@ -699,7 +764,7 @@
         [(M_TILES, 8, WIDE), BUFFER],
         place=False,
     )
-    corner_tiles = call(corner_kernel, (from_o, packed), [(MSG_X // 2, 8, COLS)] * 2, place=False, far={1: pl.ANY})
+    corner_tiles = call(corner_kernel, (from_o, packed), [(CORNER, 8, COLS)] * 2, place=False, far={1: pl.ANY})
     wide = call(widen_kernel, (from_o, *both_sides(*corner_tiles)), [(MSG_X, 8, WIDE)], place=False)[0]
     packed_partner = on_chip(packed)
     packed_odd = across_chips(jnp.concatenate([packed, packed_partner], axis=0))

time: 112 us -> 110 us (0.982)
  starting transfers between devices: 41.5 us -> 33.5 us
  waiting for transfers between devices: 26.3 us -> 32.8 us
    ppermute x7, starting transfers between devices: 21.5 us -> 13.4 us  [on_chip(): return lax.ppermute(value, 'gx', pairs_on_chip)]
    ppermute x4, waiting for transfers between devices: 21.4 us -> 28.1 us  [across_chips(): return lax.ppermute(value, 'gx', pairs_across)]
where the time goes in v9:
time: 110 us
  starting transfers between devices  33.5 us (30%)
  waiting for transfers between devices  32.8 us (30%)
  Pallas kernels  21.6 us (20%)
  blocking collectives  19.9 us (18%)
  other arithmetic  1.33 us (1%)
    ppermute x4, waiting for transfers between devices, across_chips(): return lax.ppermute(value, 'gx', pairs_across)  28.1 us
    pallas_call x14, Pallas kernels, call(): pl.pallas_call(kernel, out_shape=[jax.ShapeDtypeStruct(shape, F32) for sh...  21.6 us
    all_to_all x1, blocking collectives, shards(): lax.all_to_all(sums.reshape(count, 1, COLS), ('gx', 'gy'), 0, 0)  19.9 us
    ppermute x7, starting transfers between devices, on_chip(): return lax.ppermute(value, 'gx', pairs_on_chip)  13.4 us
    ppermute x2, starting transfers between devices, both_sides(): lax.ppermute(to_left, 'gy', backward)  10.4 us
    ppermute x4, starting transfers between devices, across_chips(): return lax.ppermute(value, 'gx', pairs_across)  7.15 us
    ppermute x7, waiting for transfers between devices, on_chip(): return lax.ppermute(value, 'gx', pairs_on_chip)  2.77 us
    ppermute x2, starting transfers between devices, both_sides(): lax.ppermute(to_right, 'gy', forward)  2.54 us
  transfers between devices with their start and end apart: 15, of which 7 were waited for; matrix products, arithmetic and copies ran while one was open for 0% of the time, Pallas kernels for 7%

profile of v9, /device:TPU:1, one launch (start us, length us, event | category | flops | bytes accessed | tf_op | source)
XLA Modules:
  0.0 110.0 jit_solution(2492595465058267149)
XLA Ops:
  0.7 0.1 pad_add_fusion.place
  0.8 1.2 %bitcast_select_fusion.fields.rhs = f32[4,16,16,128]{3,2,1,0:T(8,128)S(1)} fusion(s32[16,16,128]{2,1,0:T(8,128)} %param.8, s32[16,16,128]{2,1,0:T(8,128)} %param.7, f32[2,16,16,128]{3,2,1,0:T(8,128)} %param.6, pred[4]{0:T(512)(128)(4,1)S(1)} %get-tuple-element.68, pred[4]{0:T(512)(128)(4,1)S(1)} %get-tuple-element.69), kind=kLoop, calls=%fused_computation | loop fusion | flops 393216 | bytes 1048584 | tf_op jit(solution)/shard_map/jit(_where)/select_n | solution.py:748
  2.0 0.0 copy-start
  2.0 0.0 copy-start.1
  2.0 0.0 copy-start.2
  2.0 1.0 shard_map.77
  3.0 2.5 %collective-permute-start = (f32[23,16,128]{2,1,0:T(8,128)S(1)}, f32[23,16,128]{2,1,0:T(8,128)S(1)}, u32[]{:S(2)}, u32[]{:S(2)}) collective-permute-start(f32[23,16,128]{2,1,0:T(8,128)S(1)} %get-tuple-element.35), channel_id=1, source_target_pairs={{0,1},{1,2},{2,3},{3,4},{4,5},{5,6},{6,7},{7,8},{8,9},{9,10},{10,1... | collective-permute-start | bytes 565256 | tf_op jit(solution)/shard_map/ppermute | solution.py:743
  5.5 5.0 %collective-permute-start.1 = (f32[23,16,128]{2,1,0:T(8,128)S(1)}, f32[23,16,128]{2,1,0:T(8,128)S(1)}, u32[]{:S(2)}, u32[]{:S(2)}) collective-permute-start(f32[23,16,128]{2,1,0:T(8,128)S(1)} %get-tuple-element.36), channel_id=1, source_target_pairs={{1,0},{2,1},{3,2},{4,3},{5,4},{6,5},{7,6},{8,7},{9,8},{10,9},{11,1... | collective-permute-start | bytes 565256 | tf_op jit(solution)/shard_map/ppermute | solution.py:743
  10.5 6.8 %collective-permute-start.3 = (f32[56,8,128]{2,1,0:T(8,128)S(1)}, f32[56,8,128]{2,1,0:T(8,128)S(1)}, u32[]{:S(2)}, u32[]{:S(2)}) collective-permute-start(f32[56,8,128]{2,1,0:T(8,128)S(1)} %get-tuple-element.44), channel_id=1, source_target_pairs={{0,240},{16,32},{32,16},{48,64},{64,48},{80,96},{96,80},{112,128},... | collective-permute-start | bytes 688136 | tf_op jit(solution)/shard_map/ppermute | solution.py:732
  17.3 0.0 copy-done
  17.3 0.0 copy-done.1
  17.3 0.0 copy-done.2
  17.4 0.0 collective-permute-done.from_left
  17.4 0.0 collective-permute-done.1.from_right
  17.4 1.0 shard_map.78
  18.4 0.9 shard_map.79
  19.3 1.8 %collective-permute-start.9 = (f32[24,8,128]{2,1,0:T(8,128)S(1)}, f32[24,8,128]{2,1,0:T(8,128)S(1)}, u32[]{:S(2)}, u32[]{:S(2)}) collective-permute-start(f32[24,8,128]{2,1,0:T(8,128)S(1)} %get-tuple-element.45.after.own), channel_id=1, source_target_pairs={{0,16},{16,0},{32,48},{48,32},{64,80},{80,64},{96,112},{112,96},{1... | collective-permute-start | bytes 294920 | tf_op jit(solution)/shard_map/ppermute | solution.py:729
  21.1 0.1 collective-permute-start.2
  21.2 10.1 %collective-permute-done.3.message = f32[56,8,128]{2,1,0:T(8,128)S(1)} collective-permute-done((f32[56,8,128]{2,1,0:T(8,128)S(1)}, f32[56,8,128]{2,1,0:T(8,128)S(1)}, u32[]{:S(2)}, u32[]{:S(2)}) %collective-permute-start.3) | collective-permute-done | bytes 229408 | tf_op jit(solution)/shard_map/ppermute | solution.py:732
  31.3 0.5 shard_map.80
  31.8 0.0 collective-permute-start.4
  31.8 5.4 %collective-permute-start.5 = (f32[25,8,128]{2,1,0:T(8,128)S(1)}, f32[25,8,128]{2,1,0:T(8,128)S(1)}, u32[]{:S(2)}, u32[]{:S(2)}) collective-permute-start(f32[25,8,128]{2,1,0:T(8,128)S(1)} %get-tuple-element.47), channel_id=1, source_target_pairs={{1,0},{2,1},{3,2},{4,3},{5,4},{6,5},{7,6},{8,7},{9,8},{10,9},{11,1... | collective-permute-start | bytes 307208 | tf_op jit(solution)/shard_map/ppermute | solution.py:743
  37.2 0.0 collective-permute-done.9.partner
  37.2 0.2 collective-permute-start.10
  37.4 1.9 %collective-permute-done.4.corner_left = f32[25,8,128]{2,1,0:T(8,128)S(1)} collective-permute-done((f32[25,8,128]{2,1,0:T(8,128)S(1)}, f32[25,8,128]{2,1,0:T(8,128)S(1)}, u32[]{:S(2)}, u32[]{:S(2)}) %collective-permute-start.4) | collective-permute-done | bytes 102432 | tf_op jit(solution)/shard_map/ppermute | solution.py:743
  39.3 0.0 collective-permute-done.5.corner_right
  39.3 0.5 shard_map.81.wide
  39.8 0.0 collective-permute-done.2.from_x
  39.8 3.6 %shard_map.82 = (f32[16,2,32,256]{3,2,1,0:T(8,128)S(1)}, f32[16,32,256]{2,1,0:T(8,128)S(1)}, f32[18,32,256]{2,1,0:T(8,128)S(1)}, f32[16,32,256]{2,1,0:T(8,128)S(...) custom-call(s32[5]{0:T(128)S(1)} %pad_add_fusion.place, ...), custom_call_target="tpu_custom_call" | custom-call | flops 4000000000 | bytes 12000000 | tf_op jit(solution)/shard_map/pallas_call | solution.py:695
  43.4 7.2 %collective-permute-start.6 = (f32[16,8,128]{2,1,0:T(8,128)S(1)}, f32[16,8,128]{2,1,0:T(8,128)S(1)}, u32[]{:S(2)}, u32[]{:S(2)}) collective-permute-start(f32[16,8,128]{2,1,0:T(8,128)S(1)} %get-tuple-element.54.own), channel_id=1, source_target_pairs={{0,16},{16,0},{32,48},{48,32},{64,80},{80,64},{96,112},{112,96},{1... | collective-permute-start | bytes 196616 | tf_op jit(solution)/shard_map/ppermute | solution.py:729
  50.6 0.9 collective-permute-done.6.after.partner
  51.6 0.1 collective-permute-start.7
  51.7 0.0 collective-permute-done.10.odd
  51.7 2.2 %collective-permute-start.11 = (f32[24,8,128]{2,1,0:T(8,128)S(1)}, f32[24,8,128]{2,1,0:T(8,128)S(1)}, u32[]{:S(2)}, u32[]{:S(2)}) collective-permute-start(f32[24,8,128]{2,1,0:T(8,128)S(1)} %shard_map.84), channel_id=1, source_target_pairs={{0,16},{16,0},{32,48},{48,32},{64,80},{80,64},{96,112},{112,96},{1... | collective-permute-start | bytes 294920 | tf_op jit(solution)/shard_map/ppermute | solution.py:729
  53.9 8.0 %collective-permute-done.7.odd = f32[32,8,128]{2,1,0:T(8,128)S(1)} collective-permute-done((f32[32,8,128]{2,1,0:T(8,128)S(1)}, f32[32,8,128]{2,1,0:T(8,128)S(1)}, u32[]{:S(2)}, u32[]{:S(2)}) %collective-permute-start.7) | collective-permute-done | bytes 131104 | tf_op jit(solution)/shard_map/ppermute | solution.py:732
  61.9 0.5 collective-permute-start.8
  62.4 0.0 collective-permute-done.11.far
  62.4 0.9 shard_map.85
  63.3 0.0 collective-permute-done.8.far
  63.4 6.0 %shard_map.86 = (f32[16,2,32,256]{3,2,1,0:T(8,128)S(1)}, f32[18,2,32,256]{3,2,1,0:T(8,128)S(1)}, f32[16,8,128]{2,1,0:T(8,128)S(1)}) custom-call(s32[5]{0:T(128)S(1)} %pad_add_fusion.place, f32[16,2,32,256]{3,2,1,0:T(8,128)S(1)} %get-tuple-element.48.r, f32[16,32,256]{2,1,0:T(8,128)S(1)} %get-tuple-element.49.g, f32[18,32,256]{2,1,0:T(8,128)S(1)} %get-tuple-element.50.h, ...), custom_call_target="tpu_custom_call" | custom-call | flops 6000000000 | bytes 18000000 | tf_op jit(solution)/shard_map/pallas_call | solution.py:695
  69.4 0.4 collective-permute-start.12
  69.8 1.0 collective-permute-done.12.partner
  70.7 0.6 shard_map.87
  71.3 0.1 collective-permute-start.13
  71.4 10.0 %collective-permute-done.13.odd = f32[24,8,128]{2,1,0:T(8,128)S(1)} collective-permute-done((f32[24,8,128]{2,1,0:T(8,128)S(1)}, f32[24,8,128]{2,1,0:T(8,128)S(1)}, u32[]{:S(2)}, u32[]{:S(2)}) %collective-permute-start.13) | collective-permute-done | bytes 98336 | tf_op jit(solution)/shard_map/ppermute | solution.py:732
  81.4 1.1 %collective-permute-start.14 = (f32[16,8,128]{2,1,0:T(8,128)S(1)}, f32[16,8,128]{2,1,0:T(8,128)S(1)}, u32[]{:S(2)}, u32[]{:S(2)}) collective-permute-start(f32[16,8,128]{2,1,0:T(8,128)S(1)} %shard_map.88), channel_id=1, source_target_pairs={{0,16},{16,0},{32,48},{48,32},{64,80},{80,64},{96,112},{112,96},{1... | collective-permute-start | bytes 196616 | tf_op jit(solution)/shard_map/ppermute | solution.py:729
  82.6 0.9 collective-permute-done.14.far
  83.5 5.6 %shard_map.89 = (f32[2,16,16,128]{3,2,1,0:T(8,128)S(1)}, f32[2,16,16,128]{3,2,1,0:T(8,128)S(1)}, f32[256,128]{1,0:T(8,128)S(1)}) custom-call(s32[5]{0:T(128)S(1)} %pad_add_fusion.place, f32[4,16,16,128]{3,2,1,0:T(8,128)S(1)} %bitcast_select_fusion.fields.rhs, f32[16,2,32,256]{3,2,1,0:T(8,128)S(1)} %get-tuple-element.62.r, ...), custom_call_target="tpu_custom_call" | custom-call | flops 6000000000 | bytes 18000000 | tf_op jit(solution)/shard_map/pallas_call | solution.py:695
  89.1 19.9 %all_to_all.5 = f32[256,1,128]{2,1,0:T(1,128)S(1)} all-to-all(f32[256,1,128]{2,1,0:T(1,128)S(1)} %bitcast.14), channel_id=1, replica_groups=mesh['gx'=16,'gy'=16] {'gx','gy'}, dimensions={0} | all-to-all | bytes 262144 | tf_op jit(solution)/shard_map/all_to_all | solution.py:803
  109.0 1.0 shard_map.90
  (9 shorter events, 0.1 us)
Async XLA Ops:
  2.0 15.3 %copy-start = (f32[16]{0:T(128)S(1)}, f32[16]{0:T(128)}, u32[]{:S(2)}) copy-start(f32[16]{0:T(128)} %param.11) | copy-start | bytes 196
  2.0 15.3 %copy-start.1 = (f32[16]{0:T(128)S(1)}, f32[16]{0:T(128)}, u32[]{:S(2)}) copy-start(f32[16]{0:T(128)} %param.10) | copy-start | bytes 196
  2.0 15.3 %copy-start.2 = (f32[16]{0:T(128)S(1)}, f32[16]{0:T(128)}, u32[]{:S(2)}) copy-start(f32[16]{0:T(128)} %param.9) | copy-start | bytes 196
  3.0 14.4 %collective-permute-start = (f32[23,16,128]{2,1,0:T(8,128)S(1)}, f32[23,16,128]{2,1,0:T(8,128)S(1)}, u32[]{:S(2)}, u32[]{:S(2)}) collective-permute-start(f32[23,16,128]{2,1,0:T(8,128)S(1)} %get-tuple-element.35), channel_id=1, source_target_pairs={{0,1},{1,2},{2,3},{3,4},{4,5},{5,6},{6,7},{7,8},{8,9},{9,10},{10,1... | collective-permute-start | bytes 565256 | tf_op jit(solution)/shard_map/ppermute | solution.py:743
  5.5 11.8 %collective-permute-start.1 = (f32[23,16,128]{2,1,0:T(8,128)S(1)}, f32[23,16,128]{2,1,0:T(8,128)S(1)}, u32[]{:S(2)}, u32[]{:S(2)}) collective-permute-start(f32[23,16,128]{2,1,0:T(8,128)S(1)} %get-tuple-element.36), channel_id=1, source_target_pairs={{1,0},{2,1},{3,2},{4,3},{5,4},{6,5},{7,6},{8,7},{9,8},{10,9},{11,1... | collective-permute-start | bytes 565256 | tf_op jit(solution)/shard_map/ppermute | solution.py:743
  10.5 20.8 %collective-permute-start.3 = (f32[56,8,128]{2,1,0:T(8,128)S(1)}, f32[56,8,128]{2,1,0:T(8,128)S(1)}, u32[]{:S(2)}, u32[]{:S(2)}) collective-permute-start(f32[56,8,128]{2,1,0:T(8,128)S(1)} %get-tuple-element.44), channel_id=1, source_target_pairs={{0,240},{16,32},{32,16},{48,64},{64,48},{80,96},{96,80},{112,128},... | collective-permute-start | bytes 688136 | tf_op jit(solution)/shard_map/ppermute | solution.py:732
  19.3 17.8 %collective-permute-start.9 = (f32[24,8,128]{2,1,0:T(8,128)S(1)}, f32[24,8,128]{2,1,0:T(8,128)S(1)}, u32[]{:S(2)}, u32[]{:S(2)}) collective-permute-start(f32[24,8,128]{2,1,0:T(8,128)S(1)} %get-tuple-element.45.after.own), channel_id=1, source_target_pairs={{0,16},{16,0},{32,48},{48,32},{64,80},{80,64},{96,112},{112,96},{1... | collective-permute-start | bytes 294920 | tf_op jit(solution)/shard_map/ppermute | solution.py:729
  21.1 18.7 %collective-permute-start.2 = (f32[56,8,256]{2,1,0:T(8,128)S(1)}, f32[56,8,256]{2,1,0:T(8,128)S(1)}, u32[]{:S(2)}, u32[]{:S(2)}) collective-permute-start(f32[56,8,256]{2,1,0:T(8,128)S(1)} %get-tuple-element.43), channel_id=1, source_target_pairs={{0,16},{16,0},{32,48},{48,32},{64,80},{80,64},{96,112},{112,96},{1... | collective-permute-start | bytes 1376264 | tf_op jit(solution)/shard_map/ppermute | solution.py:729
  31.8 7.5 %collective-permute-start.4 = (f32[25,8,128]{2,1,0:T(8,128)S(1)}, f32[25,8,128]{2,1,0:T(8,128)S(1)}, u32[]{:S(2)}, u32[]{:S(2)}) collective-permute-start(f32[25,8,128]{2,1,0:T(8,128)S(1)} %get-tuple-element.46), channel_id=1, source_target_pairs={{0,1},{1,2},{2,3},{3,4},{4,5},{5,6},{6,7},{7,8},{8,9},{9,10},{10,1... | collective-permute-start | bytes 307208 | tf_op jit(solution)/shard_map/ppermute | solution.py:743
  31.8 7.5 %collective-permute-start.5 = (f32[25,8,128]{2,1,0:T(8,128)S(1)}, f32[25,8,128]{2,1,0:T(8,128)S(1)}, u32[]{:S(2)}, u32[]{:S(2)}) collective-permute-start(f32[25,8,128]{2,1,0:T(8,128)S(1)} %get-tuple-element.47), channel_id=1, source_target_pairs={{1,0},{2,1},{3,2},{4,3},{5,4},{6,5},{7,6},{8,7},{9,8},{10,9},{11,1... | collective-permute-start | bytes 307208 | tf_op jit(solution)/shard_map/ppermute | solution.py:743
  37.2 14.5 %collective-permute-start.10 = (f32[48,8,128]{2,1,0:T(8,128)S(1)}, f32[48,8,128]{2,1,0:T(8,128)S(1)}, u32[]{:S(2)}, u32[]{:S(2)}) collective-permute-start(f32[48,8,128]{2,1,0:T(8,128)S(1)} %pad_maximum_fusion), channel_id=1, source_target_pairs={{0,240},{16,32},{32,16},{48,64},{64,48},{80,96},{96,80},{112,128},... | collective-permute-start | bytes 589832 | tf_op jit(solution)/shard_map/ppermute | solution.py:732
  43.4 8.1 %collective-permute-start.6 = (f32[16,8,128]{2,1,0:T(8,128)S(1)}, f32[16,8,128]{2,1,0:T(8,128)S(1)}, u32[]{:S(2)}, u32[]{:S(2)}) collective-permute-start(f32[16,8,128]{2,1,0:T(8,128)S(1)} %get-tuple-element.54.own), channel_id=1, source_target_pairs={{0,16},{16,0},{32,48},{48,32},{64,80},{80,64},{96,112},{112,96},{1... | collective-permute-start | bytes 196616 | tf_op jit(solution)/shard_map/ppermute | solution.py:729
  51.6 10.4 %collective-permute-start.7 = (f32[32,8,128]{2,1,0:T(8,128)S(1)}, f32[32,8,128]{2,1,0:T(8,128)S(1)}, u32[]{:S(2)}, u32[]{:S(2)}) collective-permute-start(f32[32,8,128]{2,1,0:T(8,128)S(1)} %pad_maximum_fusion.1), channel_id=1, source_target_pairs={{0,240},{16,32},{32,16},{48,64},{64,48},{80,96},{96,80},{112,128},... | collective-permute-start | bytes 393224 | tf_op jit(solution)/shard_map/ppermute | solution.py:732
  51.7 10.7 %collective-permute-start.11 = (f32[24,8,128]{2,1,0:T(8,128)S(1)}, f32[24,8,128]{2,1,0:T(8,128)S(1)}, u32[]{:S(2)}, u32[]{:S(2)}) collective-permute-start(f32[24,8,128]{2,1,0:T(8,128)S(1)} %shard_map.84), channel_id=1, source_target_pairs={{0,16},{16,0},{32,48},{48,32},{64,80},{80,64},{96,112},{112,96},{1... | collective-permute-start | bytes 294920 | tf_op jit(solution)/shard_map/ppermute | solution.py:729
  61.9 1.4 %collective-permute-start.8 = (f32[16,8,128]{2,1,0:T(8,128)S(1)}, f32[16,8,128]{2,1,0:T(8,128)S(1)}, u32[]{:S(2)}, u32[]{:S(2)}) collective-permute-start(f32[16,8,128]{2,1,0:T(8,128)S(1)} %shard_map.83), channel_id=1, source_target_pairs={{0,16},{16,0},{32,48},{48,32},{64,80},{80,64},{96,112},{112,96},{1... | collective-permute-start | bytes 196616 | tf_op jit(solution)/shard_map/ppermute | solution.py:729
  69.4 1.3 %collective-permute-start.12 = (f32[16,8,128]{2,1,0:T(8,128)S(1)}, f32[16,8,128]{2,1,0:T(8,128)S(1)}, u32[]{:S(2)}, u32[]{:S(2)}) collective-permute-start(f32[16,8,128]{2,1,0:T(8,128)S(1)} %get-tuple-element.64.own), channel_id=1, source_target_pairs={{0,16},{16,0},{32,48},{48,32},{64,80},{80,64},{96,112},{112,96},{1... | collective-permute-start | bytes 196616 | tf_op jit(solution)/shard_map/ppermute | solution.py:729
  71.3 10.1 %collective-permute-start.13 = (f32[24,8,128]{2,1,0:T(8,128)S(1)}, f32[24,8,128]{2,1,0:T(8,128)S(1)}, u32[]{:S(2)}, u32[]{:S(2)}) collective-permute-start(f32[24,8,128]{2,1,0:T(8,128)S(1)} %shard_map.87), channel_id=1, source_target_pairs={{0,240},{16,32},{32,16},{48,64},{64,48},{80,96},{96,80},{112,128},... | collective-permute-start | bytes 294920 | tf_op jit(solution)/shard_map/ppermute | solution.py:732
  81.4 2.1 %collective-permute-start.14 = (f32[16,8,128]{2,1,0:T(8,128)S(1)}, f32[16,8,128]{2,1,0:T(8,128)S(1)}, u32[]{:S(2)}, u32[]{:S(2)}) collective-permute-start(f32[16,8,128]{2,1,0:T(8,128)S(1)} %shard_map.88), channel_id=1, source_target_pairs={{0,16},{16,0},{32,48},{48,32},{64,80},{80,64},{96,112},{112,96},{1... | collective-permute-start | bytes 196616 | tf_op jit(solution)/shard_map/ppermute | solution.py:729

commit v10 on v9

--- a/solution.py
+++ b/solution.py
@@ -133,7 +133,7 @@
 
 
 SPAN = 51
-QUINTS = 6
+QUINTS = 9
 
 
 def pack_quint(a, b, c, d, e):
@@ -205,8 +205,8 @@
     loop(4, quads)
 
 
-MSG_Y = 23
-CORNER = 25
+MSG_Y = 22
+CORNER = 24
 MSG_X = 56
 R_TILES = 16
 M_TILES = 24
@@ -216,23 +216,18 @@
     core = place[0]
     classes, sea = fields.at[2], fields.at[3]
 
-    def convert(pair):
-        to_left[13 + pair], to_right[13 + pair] = pack_halves(classes[2 * pair], classes[2 * pair + 1])
-
-    loop(8, convert)
-    for j in range(2):
-        quads = [pack_sea([sea[8 * j + 4 * q + i] for i in range(4)]) for q in range(2)]
-        to_left[21 + j], to_right[21 + j] = pack_halves(quads[0], quads[1])
-
     def quint(k):
-        group = [fields[(5 * k + t) // NZ, (5 * k + t) % NZ] for t in range(5)]
-        lows, highs = pack_quint(*group)
+        lows, highs = pack_quint(*(fields[(5 * k + t) // NZ, (5 * k + t) % NZ] for t in range(5)))
         for t in range(2):
             to_left[2 * k + t] = lows[t]
             to_right[2 * k + t] = highs[t]
 
     loop(QUINTS, quint)
-    to_left[12], to_right[12] = pack_halves(fields[1, 14], fields[1, 15])
+    rest = [classes[13], classes[14], classes[15]]
+    rest += [pack_sea([sea[4 * q + i] for i in range(4)]) for q in range(4)]
+    rest.append(rest[-1])
+    for j in range(4):
+        to_left[18 + j], to_right[18 + j] = pack_halves(rest[2 * j], rest[2 * j + 1])
     start = pl.multiple_of(8 * core, 8)
     fill_message(message, lambda z, i: fields.at[i, z], classes, sea, start, 8 - core)
 
@@ -245,11 +240,13 @@
             to_right[2 * k + t] = highs[t]
 
     loop(QUINTS, quint)
-
-    def pair(p):
-        to_left[12 + p], to_right[12 + p] = pack_halves(message[30 + 2 * p], message[31 + 2 * p])
-
-    loop(CORNER - 12, pair)
+    for p in range(6):
+        first = 45 + 2 * p
+        to_left[18 + p], to_right[18 + p] = pack_halves(message[first], message[min(first + 1, MSG_X - 1)])
+
+
+def valid_class(halo):
+    return jnp.clip(halo, 0.0, 15.0)
 
 
 def widen_kernel(message, corner_left, corner_right, wide):
@@ -261,12 +258,13 @@
             wide[5 * k + t] = jnp.concatenate([message[5 * k + t], halo], axis=1)
 
     loop(QUINTS, quint)
-
-    def pair(p):
-        for i, halo in enumerate(unpack_halves(corner_right[12 + p], corner_left[12 + p])):
-            wide[30 + 2 * p + i] = jnp.concatenate([message[30 + 2 * p + i], halo], axis=1)
-
-    loop(CORNER - 12, pair)
+    for j in range(32, 35):
+        wide[j, :, COLS:] = valid_class(wide[j, :, COLS:])
+    for p in range(6):
+        first = 45 + 2 * p
+        for i, halo in enumerate(unpack_halves(corner_right[18 + p], corner_left[18 + p])):
+            if first + i < MSG_X:
+                wide[first + i] = jnp.concatenate([message[first + i], halo], axis=1)
 
 
 def rows_kernel(place, fields, from_left, from_right, r_out, c_out, s_out, message):
@@ -279,29 +277,38 @@
         jnp.where(gy > 0, 1.0, 0.0),
     )
 
-    def rhs_step(k):
-        halos = unpack_quint(
+    def group(k):
+        return unpack_quint(
             [from_right[2 * k + t] for t in range(2)], [from_left[2 * k + t] for t in range(2)]
         )
-        for t, halo in enumerate(halos):
-            i, z = (5 * k + t) // NZ, (5 * k + t) % NZ
-            r_out[z, i] = jnp.concatenate([fields[i, z], halo], axis=1)
-
-    loop(QUINTS, rhs_step)
-    for t, halo in enumerate(unpack_halves(from_right[12], from_left[12])):
-        r_out[14 + t, 1] = jnp.concatenate([fields[1, 14 + t], halo], axis=1)
-
-    def class_step(pair):
-        for i, halo in enumerate(unpack_halves(from_right[13 + pair], from_left[13 + pair])):
-            c_out[2 * pair + i] = jnp.concatenate([fields[2, 2 * pair + i], halo], axis=1)
-
-    loop(8, class_step)
-    for j in range(2):
-        quads = unpack_halves(from_right[21 + j], from_left[21 + j])
-        for q in range(2):
-            for i, field in enumerate(unpack_sea(quads[q])):
-                z = 8 * j + 4 * q + i
-                s_out[z] = jnp.concatenate([fields[3, z], field * inside], axis=1)
+
+    def put_rhs(f, halo):
+        r_out[f % NZ, f // NZ] = jnp.concatenate([fields[f // NZ, f % NZ], halo], axis=1)
+
+    def put_class(z, halo):
+        c_out[z] = jnp.concatenate([fields[2, z], halo], axis=1)
+
+    def rhs_step(k):
+        for t, halo in enumerate(group(k)):
+            put_rhs(5 * k + t, halo)
+
+    loop(6, rhs_step)
+    mixed = group(6)
+    for t in range(2):
+        put_rhs(30 + t, mixed[t])
+    for t in range(3):
+        put_class(t, valid_class(mixed[2 + t]))
+    for k in (7, 8):
+        for t, halo in enumerate(group(k)):
+            put_class(5 * k + t - 32, halo)
+    rest = []
+    for j in range(4):
+        rest += unpack_halves(from_right[18 + j], from_left[18 + j])
+    for t in range(3):
+        put_class(13 + t, rest[t])
+    for q in range(4):
+        for i, field in enumerate(unpack_sea(rest[3 + q])):
+            s_out[4 * q + i] = jnp.concatenate([fields[3, 4 * q + i], field * inside], axis=1)
     start = pl.multiple_of(8 * (1 - core), 8)
     fill_message(message, lambda z, i: r_out.at[z, i], c_out, s_out, start, 7 + core)
 

time: 110 us -> 109 us (level)
  waiting for transfers between devices: 32.8 us -> 30.7 us
    ppermute x4, waiting for transfers between devices: 28.1 us -> 26.1 us  [across_chips(): return lax.ppermute(value, 'gx', pairs_across)]
  transfers between devices with their start and end apart: 15 -> 15, of which waited for: 7 -> 7; matrix products, arithmetic and copies ran while one was open for 0% -> 0% of each run, Pallas kernels for 7% -> 6%
where the time goes in v10:
time: 109 us
  starting transfers between devices  34.4 us (32%)
  waiting for transfers between devices  30.7 us (28%)
  Pallas kernels  21 us (19%)
  blocking collectives  20.7 us (19%)
  other arithmetic  1.33 us (1%)
    ppermute x4, waiting for transfers between devices, across_chips(): return lax.ppermute(value, 'gx', pairs_across)  26.1 us
    pallas_call x14, Pallas kernels, call(): pl.pallas_call(kernel, out_shape=[jax.ShapeDtypeStruct(shape, F32) for sh...  21 us
    all_to_all x1, blocking collectives, shards(): lax.all_to_all(sums.reshape(count, 1, COLS), ('gx', 'gy'), 0, 0)  20.7 us
    ppermute x7, starting transfers between devices, on_chip(): return lax.ppermute(value, 'gx', pairs_on_chip)  14.3 us
    ppermute x2, starting transfers between devices, both_sides(): lax.ppermute(to_left, 'gy', backward)  10.4 us
    ppermute x4, starting transfers between devices, across_chips(): return lax.ppermute(value, 'gx', pairs_across)  7.15 us
    ppermute x7, waiting for transfers between devices, on_chip(): return lax.ppermute(value, 'gx', pairs_on_chip)  2.77 us
    ppermute x2, starting transfers between devices, both_sides(): lax.ppermute(to_right, 'gy', forward)  2.62 us
  transfers between devices with their start and end apart: 15, of which 7 were waited for; matrix products, arithmetic and copies ran while one was open for 0% of the time, Pallas kernels for 6%

profile of v10, /device:TPU:1, one launch (start us, length us, event | category | flops | bytes accessed | tf_op | source)
XLA Modules:
  0.0 109.0 jit_solution(17430980729989549969)
XLA Ops:
  0.7 0.1 pad_add_fusion.place
  0.8 1.2 %bitcast_select_fusion.fields.rhs = f32[4,16,16,128]{3,2,1,0:T(8,128)S(1)} fusion(s32[16,16,128]{2,1,0:T(8,128)} %param.8, s32[16,16,128]{2,1,0:T(8,128)} %param.7, f32[2,16,16,128]{3,2,1,0:T(8,128)} %param.6, pred[4]{0:T(512)(128)(4,1)S(1)} %get-tuple-element.68, pred[4]{0:T(512)(128)(4,1)S(1)} %get-tuple-element.69), kind=kLoop, calls=%fused_computation | loop fusion | flops 393216 | bytes 1048584 | tf_op jit(solution)/shard_map/jit(_where)/select_n | solution.py:755
  2.0 0.0 copy-start
  2.0 0.0 copy-start.1
  2.0 0.0 copy-start.2
  2.0 1.0 shard_map.77
  3.0 2.5 %collective-permute-start = (f32[22,16,128]{2,1,0:T(8,128)S(1)}, f32[22,16,128]{2,1,0:T(8,128)S(1)}, u32[]{:S(2)}, u32[]{:S(2)}) collective-permute-start(f32[22,16,128]{2,1,0:T(8,128)S(1)} %get-tuple-element.35), channel_id=1, source_target_pairs={{0,1},{1,2},{2,3},{3,4},{4,5},{5,6},{6,7},{7,8},{8,9},{9,10},{10,1... | collective-permute-start | bytes 540680 | tf_op jit(solution)/shard_map/ppermute | solution.py:750
  5.5 5.0 %collective-permute-start.1 = (f32[22,16,128]{2,1,0:T(8,128)S(1)}, f32[22,16,128]{2,1,0:T(8,128)S(1)}, u32[]{:S(2)}, u32[]{:S(2)}) collective-permute-start(f32[22,16,128]{2,1,0:T(8,128)S(1)} %get-tuple-element.36), channel_id=1, source_target_pairs={{1,0},{2,1},{3,2},{4,3},{5,4},{6,5},{7,6},{8,7},{9,8},{10,9},{11,1... | collective-permute-start | bytes 540680 | tf_op jit(solution)/shard_map/ppermute | solution.py:750
  10.5 6.8 %collective-permute-start.3 = (f32[56,8,128]{2,1,0:T(8,128)S(1)}, f32[56,8,128]{2,1,0:T(8,128)S(1)}, u32[]{:S(2)}, u32[]{:S(2)}) collective-permute-start(f32[56,8,128]{2,1,0:T(8,128)S(1)} %get-tuple-element.44), channel_id=1, source_target_pairs={{0,240},{16,32},{32,16},{48,64},{64,48},{80,96},{96,80},{112,128},... | collective-permute-start | bytes 688136 | tf_op jit(solution)/shard_map/ppermute | solution.py:739
  17.3 0.0 copy-done
  17.3 0.0 copy-done.1
  17.3 0.0 copy-done.2
  17.3 0.0 collective-permute-done.from_left
  17.3 0.0 collective-permute-done.1.from_right
  17.4 1.1 shard_map.78
  18.4 0.9 shard_map.79
  19.3 1.8 %collective-permute-start.9 = (f32[24,8,128]{2,1,0:T(8,128)S(1)}, f32[24,8,128]{2,1,0:T(8,128)S(1)}, u32[]{:S(2)}, u32[]{:S(2)}) collective-permute-start(f32[24,8,128]{2,1,0:T(8,128)S(1)} %get-tuple-element.45.after.own), channel_id=1, source_target_pairs={{0,16},{16,0},{32,48},{48,32},{64,80},{80,64},{96,112},{112,96},{1... | collective-permute-start | bytes 294920 | tf_op jit(solution)/shard_map/ppermute | solution.py:736
  21.2 0.1 collective-permute-start.2
  21.3 9.9 %collective-permute-done.3.message = f32[56,8,128]{2,1,0:T(8,128)S(1)} collective-permute-done((f32[56,8,128]{2,1,0:T(8,128)S(1)}, f32[56,8,128]{2,1,0:T(8,128)S(1)}, u32[]{:S(2)}, u32[]{:S(2)}) %collective-permute-start.3) | collective-permute-done | bytes 229408 | tf_op jit(solution)/shard_map/ppermute | solution.py:739
  31.1 0.2 shard_map.80
  31.3 0.1 collective-permute-start.4
  31.4 5.4 %collective-permute-start.5 = (f32[24,8,128]{2,1,0:T(8,128)S(1)}, f32[24,8,128]{2,1,0:T(8,128)S(1)}, u32[]{:S(2)}, u32[]{:S(2)}) collective-permute-start(f32[24,8,128]{2,1,0:T(8,128)S(1)} %get-tuple-element.47), channel_id=1, source_target_pairs={{1,0},{2,1},{3,2},{4,3},{5,4},{6,5},{7,6},{8,7},{9,8},{10,9},{11,1... | collective-permute-start | bytes 294920 | tf_op jit(solution)/shard_map/ppermute | solution.py:750
  36.7 0.0 collective-permute-done.9.partner
  36.7 0.2 collective-permute-start.10
  36.9 1.9 %collective-permute-done.4.corner_left = f32[24,8,128]{2,1,0:T(8,128)S(1)} collective-permute-done((f32[24,8,128]{2,1,0:T(8,128)S(1)}, f32[24,8,128]{2,1,0:T(8,128)S(1)}, u32[]{:S(2)}, u32[]{:S(2)}) %collective-permute-start.4) | collective-permute-done | bytes 98336 | tf_op jit(solution)/shard_map/ppermute | solution.py:750
  38.8 0.0 collective-permute-done.5.corner_right
  38.8 0.2 shard_map.81.wide
  39.0 0.0 collective-permute-done.2.from_x
  39.0 3.6 %shard_map.82 = (f32[16,2,32,256]{3,2,1,0:T(8,128)S(1)}, f32[16,32,256]{2,1,0:T(8,128)S(1)}, f32[18,32,256]{2,1,0:T(8,128)S(1)}, f32[16,32,256]{2,1,0:T(8,128)S(...) custom-call(s32[5]{0:T(128)S(1)} %pad_add_fusion.place, ...), custom_call_target="tpu_custom_call" | custom-call | flops 4000000000 | bytes 12000000 | tf_op jit(solution)/shard_map/pallas_call | solution.py:702
  42.6 7.1 %collective-permute-start.6 = (f32[16,8,128]{2,1,0:T(8,128)S(1)}, f32[16,8,128]{2,1,0:T(8,128)S(1)}, u32[]{:S(2)}, u32[]{:S(2)}) collective-permute-start(f32[16,8,128]{2,1,0:T(8,128)S(1)} %get-tuple-element.54.own), channel_id=1, source_target_pairs={{0,16},{16,0},{32,48},{48,32},{64,80},{80,64},{96,112},{112,96},{1... | collective-permute-start | bytes 196616 | tf_op jit(solution)/shard_map/ppermute | solution.py:736
  49.7 0.9 collective-permute-done.6.after.partner
  50.6 0.1 collective-permute-start.7
  50.7 0.0 collective-permute-done.10.odd
  50.7 2.3 %collective-permute-start.11 = (f32[24,8,128]{2,1,0:T(8,128)S(1)}, f32[24,8,128]{2,1,0:T(8,128)S(1)}, u32[]{:S(2)}, u32[]{:S(2)}) collective-permute-start(f32[24,8,128]{2,1,0:T(8,128)S(1)} %shard_map.84), channel_id=1, source_target_pairs={{0,16},{16,0},{32,48},{48,32},{64,80},{80,64},{96,112},{112,96},{1... | collective-permute-start | bytes 294920 | tf_op jit(solution)/shard_map/ppermute | solution.py:736
  53.0 6.9 %collective-permute-done.7.odd = f32[32,8,128]{2,1,0:T(8,128)S(1)} collective-permute-done((f32[32,8,128]{2,1,0:T(8,128)S(1)}, f32[32,8,128]{2,1,0:T(8,128)S(1)}, u32[]{:S(2)}, u32[]{:S(2)}) %collective-permute-start.7) | collective-permute-done | bytes 131104 | tf_op jit(solution)/shard_map/ppermute | solution.py:739
  59.9 1.6 %collective-permute-start.8 = (f32[16,8,128]{2,1,0:T(8,128)S(1)}, f32[16,8,128]{2,1,0:T(8,128)S(1)}, u32[]{:S(2)}, u32[]{:S(2)}) collective-permute-start(f32[16,8,128]{2,1,0:T(8,128)S(1)} %shard_map.83), channel_id=1, source_target_pairs={{0,16},{16,0},{32,48},{48,32},{64,80},{80,64},{96,112},{112,96},{1... | collective-permute-start | bytes 196616 | tf_op jit(solution)/shard_map/ppermute | solution.py:736
  61.4 0.0 collective-permute-done.11.far
  61.4 0.9 shard_map.85
  62.4 0.0 collective-permute-done.8.far
  62.4 6.0 %shard_map.86 = (f32[16,2,32,256]{3,2,1,0:T(8,128)S(1)}, f32[18,2,32,256]{3,2,1,0:T(8,128)S(1)}, f32[16,8,128]{2,1,0:T(8,128)S(1)}) custom-call(s32[5]{0:T(128)S(1)} %pad_add_fusion.place, f32[16,2,32,256]{3,2,1,0:T(8,128)S(1)} %get-tuple-element.48.r, f32[16,32,256]{2,1,0:T(8,128)S(1)} %get-tuple-element.49.g, f32[18,32,256]{2,1,0:T(8,128)S(1)} %get-tuple-element.50.h, ...), custom_call_target="tpu_custom_call" | custom-call | flops 6000000000 | bytes 18000000 | tf_op jit(solution)/shard_map/pallas_call | solution.py:702
  68.4 0.4 collective-permute-start.12
  68.8 1.0 collective-permute-done.12.partner
  69.8 0.6 shard_map.87
  70.3 0.1 collective-permute-start.13
  70.4 9.3 %collective-permute-done.13.odd = f32[24,8,128]{2,1,0:T(8,128)S(1)} collective-permute-done((f32[24,8,128]{2,1,0:T(8,128)S(1)}, f32[24,8,128]{2,1,0:T(8,128)S(1)}, u32[]{:S(2)}, u32[]{:S(2)}) %collective-permute-start.13) | collective-permute-done | bytes 98336 | tf_op jit(solution)/shard_map/ppermute | solution.py:739
  79.7 1.1 collective-permute-start.14
  80.8 0.9 collective-permute-done.14.far
  81.7 5.6 %shard_map.89 = (f32[2,16,16,128]{3,2,1,0:T(8,128)S(1)}, f32[2,16,16,128]{3,2,1,0:T(8,128)S(1)}, f32[256,128]{1,0:T(8,128)S(1)}) custom-call(s32[5]{0:T(128)S(1)} %pad_add_fusion.place, f32[4,16,16,128]{3,2,1,0:T(8,128)S(1)} %bitcast_select_fusion.fields.rhs, f32[16,2,32,256]{3,2,1,0:T(8,128)S(1)} %get-tuple-element.62.r, ...), custom_call_target="tpu_custom_call" | custom-call | flops 6000000000 | bytes 18000000 | tf_op jit(solution)/shard_map/pallas_call | solution.py:702
  87.3 20.7 %all_to_all.5 = f32[256,1,128]{2,1,0:T(1,128)S(1)} all-to-all(f32[256,1,128]{2,1,0:T(1,128)S(1)} %bitcast.14), channel_id=1, replica_groups=mesh['gx'=16,'gy'=16] {'gx','gy'}, dimensions={0} | all-to-all | bytes 262144 | tf_op jit(solution)/shard_map/all_to_all | solution.py:810
  108.0 1.0 shard_map.90
  (9 shorter events, 0.1 us)
Async XLA Ops:
  2.0 15.3 %copy-start = (f32[16]{0:T(128)S(1)}, f32[16]{0:T(128)}, u32[]{:S(2)}) copy-start(f32[16]{0:T(128)} %param.11) | copy-start | bytes 196
  2.0 15.3 %copy-start.1 = (f32[16]{0:T(128)S(1)}, f32[16]{0:T(128)}, u32[]{:S(2)}) copy-start(f32[16]{0:T(128)} %param.10) | copy-start | bytes 196
  2.0 15.3 %copy-start.2 = (f32[16]{0:T(128)S(1)}, f32[16]{0:T(128)}, u32[]{:S(2)}) copy-start(f32[16]{0:T(128)} %param.9) | copy-start | bytes 196
  3.0 14.4 %collective-permute-start = (f32[22,16,128]{2,1,0:T(8,128)S(1)}, f32[22,16,128]{2,1,0:T(8,128)S(1)}, u32[]{:S(2)}, u32[]{:S(2)}) collective-permute-start(f32[22,16,128]{2,1,0:T(8,128)S(1)} %get-tuple-element.35), channel_id=1, source_target_pairs={{0,1},{1,2},{2,3},{3,4},{4,5},{5,6},{6,7},{7,8},{8,9},{9,10},{10,1... | collective-permute-start | bytes 540680 | tf_op jit(solution)/shard_map/ppermute | solution.py:750
  5.5 11.8 %collective-permute-start.1 = (f32[22,16,128]{2,1,0:T(8,128)S(1)}, f32[22,16,128]{2,1,0:T(8,128)S(1)}, u32[]{:S(2)}, u32[]{:S(2)}) collective-permute-start(f32[22,16,128]{2,1,0:T(8,128)S(1)} %get-tuple-element.36), channel_id=1, source_target_pairs={{1,0},{2,1},{3,2},{4,3},{5,4},{6,5},{7,6},{8,7},{9,8},{10,9},{11,1... | collective-permute-start | bytes 540680 | tf_op jit(solution)/shard_map/ppermute | solution.py:750
  10.5 20.6 %collective-permute-start.3 = (f32[56,8,128]{2,1,0:T(8,128)S(1)}, f32[56,8,128]{2,1,0:T(8,128)S(1)}, u32[]{:S(2)}, u32[]{:S(2)}) collective-permute-start(f32[56,8,128]{2,1,0:T(8,128)S(1)} %get-tuple-element.44), channel_id=1, source_target_pairs={{0,240},{16,32},{32,16},{48,64},{64,48},{80,96},{96,80},{112,128},... | collective-permute-start | bytes 688136 | tf_op jit(solution)/shard_map/ppermute | solution.py:739
  19.3 17.4 %collective-permute-start.9 = (f32[24,8,128]{2,1,0:T(8,128)S(1)}, f32[24,8,128]{2,1,0:T(8,128)S(1)}, u32[]{:S(2)}, u32[]{:S(2)}) collective-permute-start(f32[24,8,128]{2,1,0:T(8,128)S(1)} %get-tuple-element.45.after.own), channel_id=1, source_target_pairs={{0,16},{16,0},{32,48},{48,32},{64,80},{80,64},{96,112},{112,96},{1... | collective-permute-start | bytes 294920 | tf_op jit(solution)/shard_map/ppermute | solution.py:736
  21.2 17.8 %collective-permute-start.2 = (f32[56,8,256]{2,1,0:T(8,128)S(1)}, f32[56,8,256]{2,1,0:T(8,128)S(1)}, u32[]{:S(2)}, u32[]{:S(2)}) collective-permute-start(f32[56,8,256]{2,1,0:T(8,128)S(1)} %get-tuple-element.43), channel_id=1, source_target_pairs={{0,16},{16,0},{32,48},{48,32},{64,80},{80,64},{96,112},{112,96},{1... | collective-permute-start | bytes 1376264 | tf_op jit(solution)/shard_map/ppermute | solution.py:736
  31.3 7.6 %collective-permute-start.4 = (f32[24,8,128]{2,1,0:T(8,128)S(1)}, f32[24,8,128]{2,1,0:T(8,128)S(1)}, u32[]{:S(2)}, u32[]{:S(2)}) collective-permute-start(f32[24,8,128]{2,1,0:T(8,128)S(1)} %get-tuple-element.46), channel_id=1, source_target_pairs={{0,1},{1,2},{2,3},{3,4},{4,5},{5,6},{6,7},{7,8},{8,9},{9,10},{10,1... | collective-permute-start | bytes 294920 | tf_op jit(solution)/shard_map/ppermute | solution.py:750
  31.4 7.5 %collective-permute-start.5 = (f32[24,8,128]{2,1,0:T(8,128)S(1)}, f32[24,8,128]{2,1,0:T(8,128)S(1)}, u32[]{:S(2)}, u32[]{:S(2)}) collective-permute-start(f32[24,8,128]{2,1,0:T(8,128)S(1)} %get-tuple-element.47), channel_id=1, source_target_pairs={{1,0},{2,1},{3,2},{4,3},{5,4},{6,5},{7,6},{8,7},{9,8},{10,9},{11,1... | collective-permute-start | bytes 294920 | tf_op jit(solution)/shard_map/ppermute | solution.py:750
  36.7 13.9 %collective-permute-start.10 = (f32[48,8,128]{2,1,0:T(8,128)S(1)}, f32[48,8,128]{2,1,0:T(8,128)S(1)}, u32[]{:S(2)}, u32[]{:S(2)}) collective-permute-start(f32[48,8,128]{2,1,0:T(8,128)S(1)} %pad_maximum_fusion), channel_id=1, source_target_pairs={{0,240},{16,32},{32,16},{48,64},{64,48},{80,96},{96,80},{112,128},... | collective-permute-start | bytes 589832 | tf_op jit(solution)/shard_map/ppermute | solution.py:739
  42.6 8.0 %collective-permute-start.6 = (f32[16,8,128]{2,1,0:T(8,128)S(1)}, f32[16,8,128]{2,1,0:T(8,128)S(1)}, u32[]{:S(2)}, u32[]{:S(2)}) collective-permute-start(f32[16,8,128]{2,1,0:T(8,128)S(1)} %get-tuple-element.54.own), channel_id=1, source_target_pairs={{0,16},{16,0},{32,48},{48,32},{64,80},{80,64},{96,112},{112,96},{1... | collective-permute-start | bytes 196616 | tf_op jit(solution)/shard_map/ppermute | solution.py:736
  50.6 9.3 %collective-permute-start.7 = (f32[32,8,128]{2,1,0:T(8,128)S(1)}, f32[32,8,128]{2,1,0:T(8,128)S(1)}, u32[]{:S(2)}, u32[]{:S(2)}) collective-permute-start(f32[32,8,128]{2,1,0:T(8,128)S(1)} %pad_maximum_fusion.1), channel_id=1, source_target_pairs={{0,240},{16,32},{32,16},{48,64},{64,48},{80,96},{96,80},{112,128},... | collective-permute-start | bytes 393224 | tf_op jit(solution)/shard_map/ppermute | solution.py:739
  50.7 10.7 %collective-permute-start.11 = (f32[24,8,128]{2,1,0:T(8,128)S(1)}, f32[24,8,128]{2,1,0:T(8,128)S(1)}, u32[]{:S(2)}, u32[]{:S(2)}) collective-permute-start(f32[24,8,128]{2,1,0:T(8,128)S(1)} %shard_map.84), channel_id=1, source_target_pairs={{0,16},{16,0},{32,48},{48,32},{64,80},{80,64},{96,112},{112,96},{1... | collective-permute-start | bytes 294920 | tf_op jit(solution)/shard_map/ppermute | solution.py:736
  59.9 2.5 %collective-permute-start.8 = (f32[16,8,128]{2,1,0:T(8,128)S(1)}, f32[16,8,128]{2,1,0:T(8,128)S(1)}, u32[]{:S(2)}, u32[]{:S(2)}) collective-permute-start(f32[16,8,128]{2,1,0:T(8,128)S(1)} %shard_map.83), channel_id=1, source_target_pairs={{0,16},{16,0},{32,48},{48,32},{64,80},{80,64},{96,112},{112,96},{1... | collective-permute-start | bytes 196616 | tf_op jit(solution)/shard_map/ppermute | solution.py:736
  68.4 1.3 %collective-permute-start.12 = (f32[16,8,128]{2,1,0:T(8,128)S(1)}, f32[16,8,128]{2,1,0:T(8,128)S(1)}, u32[]{:S(2)}, u32[]{:S(2)}) collective-permute-start(f32[16,8,128]{2,1,0:T(8,128)S(1)} %get-tuple-element.64.own), channel_id=1, source_target_pairs={{0,16},{16,0},{32,48},{48,32},{64,80},{80,64},{96,112},{112,96},{1... | collective-permute-start | bytes 196616 | tf_op jit(solution)/shard_map/ppermute | solution.py:736
  70.3 9.4 %collective-permute-start.13 = (f32[24,8,128]{2,1,0:T(8,128)S(1)}, f32[24,8,128]{2,1,0:T(8,128)S(1)}, u32[]{:S(2)}, u32[]{:S(2)}) collective-permute-start(f32[24,8,128]{2,1,0:T(8,128)S(1)} %shard_map.87), channel_id=1, source_target_pairs={{0,240},{16,32},{32,16},{48,64},{64,48},{80,96},{96,80},{112,128},... | collective-permute-start | bytes 294920 | tf_op jit(solution)/shard_map/ppermute | solution.py:739
  79.7 2.0 %collective-permute-start.14 = (f32[16,8,128]{2,1,0:T(8,128)S(1)}, f32[16,8,128]{2,1,0:T(8,128)S(1)}, u32[]{:S(2)}, u32[]{:S(2)}) collective-permute-start(f32[16,8,128]{2,1,0:T(8,128)S(1)} %shard_map.88), channel_id=1, source_target_pairs={{0,16},{16,0},{32,48},{48,32},{64,80},{80,64},{96,112},{112,96},{1... | collective-permute-start | bytes 196616 | tf_op jit(solution)/shard_map/ppermute | solution.py:736

commit v11 on v10

--- a/solution.py
+++ b/solution.py
@@ -574,6 +574,11 @@
     loop(R_TILES // 2, pair)
 
 
+def join_kernel(own, partner, after, message):
+    message[0:M_TILES] = own[...]
+    message[M_TILES:] = partner[...]
+
+
 def after_kernel(odd, after, near):
     near[...] = odd[0:M_TILES]
 
@@ -685,6 +690,7 @@
     "down_kernel": 4,
     "near_kernel": 30,
     "far_half_kernel": 1,
+    "join_kernel": 1,
     "after_kernel": 30,
     "coarse_kernel": 1,
     "middle_kernel": 6,
@@ -772,9 +778,13 @@
         place=False,
     )
     corner_tiles = call(corner_kernel, (from_o, packed), [(CORNER, 8, COLS)] * 2, place=False, far={1: pl.ANY})
-    wide = call(widen_kernel, (from_o, *both_sides(*corner_tiles)), [(MSG_X, 8, WIDE)], place=False)[0]
+    corners = both_sides(*corner_tiles)
+    wide = call(widen_kernel, (from_o, *corners), [(MSG_X, 8, WIDE)], place=False)[0]
     packed_partner = on_chip(packed)
-    packed_odd = across_chips(jnp.concatenate([packed, packed_partner], axis=0))
+    both = call(
+        join_kernel, (packed, packed_partner, corners[0]), [(2 * M_TILES, 8, COLS)], place=False, far={2: pl.ANY}
+    )[0]
+    packed_odd = across_chips(both)
     r, g, h, d, inverse, xp, r1 = call(
         down_kernel,
         (place, r_own, g_own, h_own, k_own, from_x, wide, table),

time: 109 us -> 110 us (level)
  starting transfers between devices: 34.4 us -> 39.9 us
  waiting for transfers between devices: 30.7 us -> 25.7 us
    ppermute x4, starting transfers between devices: 7.15 us -> 15.2 us  [across_chips(): return lax.ppermute(value, 'gx', pairs_across)]
    ppermute x4, waiting for transfers between devices: 26.1 us -> 22.9 us  [across_chips(): return lax.ppermute(value, 'gx', pairs_across)]
    ppermute x7, starting transfers between devices: 14.3 us -> 11.8 us  [on_chip(): return lax.ppermute(value, 'gx', pairs_on_chip)]
    ppermute x2, waiting for transfers between devices: 1.89 us -> 0.09 us  [both_sides(): lax.ppermute(to_right, 'gy', forward)]
    pallas_call x14 -> x15, Pallas kernels: 21 us -> 21 us  [call(): pl.pallas_call(kernel, out_shape=[jax.ShapeDtypeStruct(shape, F32) for sh...]
  transfers between devices with their start and end apart: 15 -> 15, of which waited for: 7 -> 8; matrix products, arithmetic and copies ran while one was open for 0% -> 0% of each run, Pallas kernels for 6% -> 6%
where the time goes in v11:
time: 110 us
  starting transfers between devices  39.9 us (36%)
  waiting for transfers between devices  25.7 us (23%)
  Pallas kernels  21 us (19%)
  blocking collectives  20.7 us (19%)
  other arithmetic  1.31 us (1%)
    ppermute x4, waiting for transfers between devices, across_chips(): return lax.ppermute(value, 'gx', pairs_across)  22.9 us
    pallas_call x15, Pallas kernels, call(): pl.pallas_call(kernel, out_shape=[jax.ShapeDtypeStruct(shape, F32) for sh...  21 us
    all_to_all x1, blocking collectives, shards(): lax.all_to_all(sums.reshape(count, 1, COLS), ('gx', 'gy'), 0, 0)  20.7 us
    ppermute x4, starting transfers between devices, across_chips(): return lax.ppermute(value, 'gx', pairs_across)  15.2 us
    ppermute x7, starting transfers between devices, on_chip(): return lax.ppermute(value, 'gx', pairs_on_chip)  11.8 us
    ppermute x2, starting transfers between devices, both_sides(): lax.ppermute(to_left, 'gy', backward)  10.4 us
    ppermute x7, waiting for transfers between devices, on_chip(): return lax.ppermute(value, 'gx', pairs_on_chip)  2.77 us
    ppermute x2, starting transfers between devices, both_sides(): lax.ppermute(to_right, 'gy', forward)  2.62 us
  transfers between devices with their start and end apart: 15, of which 8 were waited for; matrix products, arithmetic and copies ran while one was open for 0% of the time, Pallas kernels for 6%

profile of v11, /device:TPU:1, one launch (start us, length us, event | category | flops | bytes accessed | tf_op | source)
XLA Modules:
  0.0 109.5 jit_solution(5097458206038798051)
XLA Ops:
  0.7 0.1 pad_add_fusion.place
  0.8 1.2 %bitcast_select_fusion.fields.rhs = f32[4,16,16,128]{3,2,1,0:T(8,128)S(1)} fusion(s32[16,16,128]{2,1,0:T(8,128)} %param.8, s32[16,16,128]{2,1,0:T(8,128)} %param.7, f32[2,16,16,128]{3,2,1,0:T(8,128)} %param.6, pred[4]{0:T(512)(128)(4,1)S(1)} %get-tuple-element.68, pred[4]{0:T(512)(128)(4,1)S(1)} %get-tuple-element.69), kind=kLoop, calls=%fused_computation | loop fusion | flops 393216 | bytes 1048584 | tf_op jit(solution)/shard_map/jit(_where)/select_n | solution.py:761
  2.0 0.0 copy-start
  2.0 0.0 copy-start.1
  2.0 0.0 copy-start.2
  2.0 1.0 shard_map.77
  3.0 2.5 %collective-permute-start = (f32[22,16,128]{2,1,0:T(8,128)S(1)}, f32[22,16,128]{2,1,0:T(8,128)S(1)}, u32[]{:S(2)}, u32[]{:S(2)}) collective-permute-start(f32[22,16,128]{2,1,0:T(8,128)S(1)} %get-tuple-element.35), channel_id=1, source_target_pairs={{0,1},{1,2},{2,3},{3,4},{4,5},{5,6},{6,7},{7,8},{8,9},{9,10},{10,1... | collective-permute-start | bytes 540680 | tf_op jit(solution)/shard_map/ppermute | solution.py:756
  5.5 5.0 %collective-permute-start.1 = (f32[22,16,128]{2,1,0:T(8,128)S(1)}, f32[22,16,128]{2,1,0:T(8,128)S(1)}, u32[]{:S(2)}, u32[]{:S(2)}) collective-permute-start(f32[22,16,128]{2,1,0:T(8,128)S(1)} %get-tuple-element.36), channel_id=1, source_target_pairs={{1,0},{2,1},{3,2},{4,3},{5,4},{6,5},{7,6},{8,7},{9,8},{10,9},{11,1... | collective-permute-start | bytes 540680 | tf_op jit(solution)/shard_map/ppermute | solution.py:756
  10.5 6.8 %collective-permute-start.3 = (f32[56,8,128]{2,1,0:T(8,128)S(1)}, f32[56,8,128]{2,1,0:T(8,128)S(1)}, u32[]{:S(2)}, u32[]{:S(2)}) collective-permute-start(f32[56,8,128]{2,1,0:T(8,128)S(1)} %get-tuple-element.44), channel_id=1, source_target_pairs={{0,240},{16,32},{32,16},{48,64},{64,48},{80,96},{96,80},{112,128},... | collective-permute-start | bytes 688136 | tf_op jit(solution)/shard_map/ppermute | solution.py:745
  17.3 0.0 copy-done
  17.3 0.0 copy-done.1
  17.3 0.0 copy-done.2
  17.3 0.0 collective-permute-done.from_left
  17.3 0.0 collective-permute-done.1.from_right
  17.4 1.1 shard_map.78
  18.4 0.9 shard_map.79
  19.3 1.8 %collective-permute-start.9 = (f32[24,8,128]{2,1,0:T(8,128)S(1)}, f32[24,8,128]{2,1,0:T(8,128)S(1)}, u32[]{:S(2)}, u32[]{:S(2)}) collective-permute-start(f32[24,8,128]{2,1,0:T(8,128)S(1)} %get-tuple-element.45.after.own), channel_id=1, source_target_pairs={{0,16},{16,0},{32,48},{48,32},{64,80},{80,64},{96,112},{112,96},{1... | collective-permute-start | bytes 294920 | tf_op jit(solution)/shard_map/ppermute | solution.py:742
  21.2 10.0 %collective-permute-done.3.message = f32[56,8,128]{2,1,0:T(8,128)S(1)} collective-permute-done((f32[56,8,128]{2,1,0:T(8,128)S(1)}, f32[56,8,128]{2,1,0:T(8,128)S(1)}, u32[]{:S(2)}, u32[]{:S(2)}) %collective-permute-start.3) | collective-permute-done | bytes 229408 | tf_op jit(solution)/shard_map/ppermute | solution.py:745
  31.1 0.2 shard_map.80
  31.3 0.1 collective-permute-start.4
  31.4 5.4 %collective-permute-start.5 = (f32[24,8,128]{2,1,0:T(8,128)S(1)}, f32[24,8,128]{2,1,0:T(8,128)S(1)}, u32[]{:S(2)}, u32[]{:S(2)}) collective-permute-start(f32[24,8,128]{2,1,0:T(8,128)S(1)} %get-tuple-element.47), channel_id=1, source_target_pairs={{1,0},{2,1},{3,2},{4,3},{5,4},{6,5},{7,6},{8,7},{9,8},{10,9},{11,1... | collective-permute-start | bytes 294920 | tf_op jit(solution)/shard_map/ppermute | solution.py:756
  36.7 2.0 %collective-permute-start.2 = (f32[56,8,256]{2,1,0:T(8,128)S(1)}, f32[56,8,256]{2,1,0:T(8,128)S(1)}, u32[]{:S(2)}, u32[]{:S(2)}) collective-permute-start(f32[56,8,256]{2,1,0:T(8,128)S(1)} %get-tuple-element.43), channel_id=1, source_target_pairs={{0,16},{16,0},{32,48},{48,32},{64,80},{80,64},{96,112},{112,96},{1... | collective-permute-start | bytes 1376264 | tf_op jit(solution)/shard_map/ppermute | solution.py:742
  38.7 0.0 collective-permute-done.9.partner
  38.7 0.1 collective-permute-done.4.corner_left.after
  38.8 1.7 %collective-permute-start.10 = (f32[48,8,128]{2,1,0:T(8,128)S(1)}, f32[48,8,128]{2,1,0:T(8,128)S(1)}, u32[]{:S(2)}, u32[]{:S(2)}) collective-permute-start(f32[48,8,128]{2,1,0:T(8,128)S(1)} %shard_map.84), channel_id=1, source_target_pairs={{0,240},{16,32},{32,16},{48,64},{64,48},{80,96},{96,80},{112,128},... | collective-permute-start | bytes 589832 | tf_op jit(solution)/shard_map/ppermute | solution.py:745
  40.5 0.0 collective-permute-done.5.corner_right
  40.5 0.2 shard_map.81.wide
  40.7 0.0 collective-permute-done.2.from_x
  40.7 3.6 %shard_map.82 = (f32[16,2,32,256]{3,2,1,0:T(8,128)S(1)}, f32[16,32,256]{2,1,0:T(8,128)S(1)}, f32[18,32,256]{2,1,0:T(8,128)S(1)}, f32[16,32,256]{2,1,0:T(8,128)S(...) custom-call(s32[5]{0:T(128)S(1)} %pad_add_fusion.place, ...), custom_call_target="tpu_custom_call" | custom-call | flops 4000000000 | bytes 12000000 | tf_op jit(solution)/shard_map/pallas_call | solution.py:708
  44.3 1.6 %collective-permute-start.6 = (f32[16,8,128]{2,1,0:T(8,128)S(1)}, f32[16,8,128]{2,1,0:T(8,128)S(1)}, u32[]{:S(2)}, u32[]{:S(2)}) collective-permute-start(f32[16,8,128]{2,1,0:T(8,128)S(1)} %get-tuple-element.54.own), channel_id=1, source_target_pairs={{0,16},{16,0},{32,48},{48,32},{64,80},{80,64},{96,112},{112,96},{1... | collective-permute-start | bytes 196616 | tf_op jit(solution)/shard_map/ppermute | solution.py:742
  45.9 0.9 collective-permute-done.6.after.partner
  46.8 4.4 %collective-permute-start.7 = (f32[32,8,128]{2,1,0:T(8,128)S(1)}, f32[32,8,128]{2,1,0:T(8,128)S(1)}, u32[]{:S(2)}, u32[]{:S(2)}) collective-permute-start(f32[32,8,128]{2,1,0:T(8,128)S(1)} %pad_maximum_fusion), channel_id=1, source_target_pairs={{0,240},{16,32},{32,16},{48,64},{64,48},{80,96},{96,80},{112,128},... | collective-permute-start | bytes 393224 | tf_op jit(solution)/shard_map/ppermute | solution.py:745
  51.2 0.6 collective-permute-done.10.odd
  51.7 3.1 %collective-permute-start.11 = (f32[24,8,128]{2,1,0:T(8,128)S(1)}, f32[24,8,128]{2,1,0:T(8,128)S(1)}, u32[]{:S(2)}, u32[]{:S(2)}) collective-permute-start(f32[24,8,128]{2,1,0:T(8,128)S(1)} %shard_map.85), channel_id=1, source_target_pairs={{0,16},{16,0},{32,48},{48,32},{64,80},{80,64},{96,112},{112,96},{1... | collective-permute-start | bytes 294920 | tf_op jit(solution)/shard_map/ppermute | solution.py:742
  54.8 4.5 %collective-permute-done.7.odd = f32[32,8,128]{2,1,0:T(8,128)S(1)} collective-permute-done((f32[32,8,128]{2,1,0:T(8,128)S(1)}, f32[32,8,128]{2,1,0:T(8,128)S(1)}, u32[]{:S(2)}, u32[]{:S(2)}) %collective-permute-start.7) | collective-permute-done | bytes 131104 | tf_op jit(solution)/shard_map/ppermute | solution.py:745
  59.3 1.9 %collective-permute-start.8 = (f32[16,8,128]{2,1,0:T(8,128)S(1)}, f32[16,8,128]{2,1,0:T(8,128)S(1)}, u32[]{:S(2)}, u32[]{:S(2)}) collective-permute-start(f32[16,8,128]{2,1,0:T(8,128)S(1)} %shard_map.83), channel_id=1, source_target_pairs={{0,16},{16,0},{32,48},{48,32},{64,80},{80,64},{96,112},{112,96},{1... | collective-permute-start | bytes 196616 | tf_op jit(solution)/shard_map/ppermute | solution.py:742
  61.1 0.0 collective-permute-done.11.far
  61.1 0.9 shard_map.86
  62.1 0.0 collective-permute-done.8.far
  62.1 6.0 %shard_map.87 = (f32[16,2,32,256]{3,2,1,0:T(8,128)S(1)}, f32[18,2,32,256]{3,2,1,0:T(8,128)S(1)}, f32[16,8,128]{2,1,0:T(8,128)S(1)}) custom-call(s32[5]{0:T(128)S(1)} %pad_add_fusion.place, f32[16,2,32,256]{3,2,1,0:T(8,128)S(1)} %get-tuple-element.48.r, f32[16,32,256]{2,1,0:T(8,128)S(1)} %get-tuple-element.49.g, f32[18,32,256]{2,1,0:T(8,128)S(1)} %get-tuple-element.50.h, ...), custom_call_target="tpu_custom_call" | custom-call | flops 6000000000 | bytes 18000000 | tf_op jit(solution)/shard_map/pallas_call | solution.py:708
  68.1 0.4 collective-permute-start.12
  68.5 1.0 collective-permute-done.12.partner
  69.5 0.6 shard_map.88
  70.0 2.3 %collective-permute-start.13 = (f32[24,8,128]{2,1,0:T(8,128)S(1)}, f32[24,8,128]{2,1,0:T(8,128)S(1)}, u32[]{:S(2)}, u32[]{:S(2)}) collective-permute-start(f32[24,8,128]{2,1,0:T(8,128)S(1)} %shard_map.88), channel_id=1, source_target_pairs={{0,240},{16,32},{32,16},{48,64},{64,48},{80,96},{96,80},{112,128},... | collective-permute-start | bytes 294920 | tf_op jit(solution)/shard_map/ppermute | solution.py:745
  72.4 7.9 %collective-permute-done.13.odd = f32[24,8,128]{2,1,0:T(8,128)S(1)} collective-permute-done((f32[24,8,128]{2,1,0:T(8,128)S(1)}, f32[24,8,128]{2,1,0:T(8,128)S(1)}, u32[]{:S(2)}, u32[]{:S(2)}) %collective-permute-start.13) | collective-permute-done | bytes 98336 | tf_op jit(solution)/shard_map/ppermute | solution.py:745
  80.3 1.0 collective-permute-start.14
  81.3 0.9 collective-permute-done.14.far
  82.2 5.6 %shard_map.90 = (f32[2,16,16,128]{3,2,1,0:T(8,128)S(1)}, f32[2,16,16,128]{3,2,1,0:T(8,128)S(1)}, f32[256,128]{1,0:T(8,128)S(1)}) custom-call(s32[5]{0:T(128)S(1)} %pad_add_fusion.place, f32[4,16,16,128]{3,2,1,0:T(8,128)S(1)} %bitcast_select_fusion.fields.rhs, f32[16,2,32,256]{3,2,1,0:T(8,128)S(1)} %get-tuple-element.62.r, ...), custom_call_target="tpu_custom_call" | custom-call | flops 6000000000 | bytes 18000000 | tf_op jit(solution)/shard_map/pallas_call | solution.py:708
  87.9 20.7 %all_to_all.5 = f32[256,1,128]{2,1,0:T(1,128)S(1)} all-to-all(f32[256,1,128]{2,1,0:T(1,128)S(1)} %bitcast.14), channel_id=1, replica_groups=mesh['gx'=16,'gy'=16] {'gx','gy'}, dimensions={0} | all-to-all | bytes 262144 | tf_op jit(solution)/shard_map/all_to_all | solution.py:820
  108.5 1.0 shard_map.91
  (9 shorter events, 0.1 us)
Async XLA Ops:
  2.0 15.3 %copy-start = (f32[16]{0:T(128)S(1)}, f32[16]{0:T(128)}, u32[]{:S(2)}) copy-start(f32[16]{0:T(128)} %param.11) | copy-start | bytes 196
  2.0 15.3 %copy-start.1 = (f32[16]{0:T(128)S(1)}, f32[16]{0:T(128)}, u32[]{:S(2)}) copy-start(f32[16]{0:T(128)} %param.10) | copy-start | bytes 196
  2.0 15.3 %copy-start.2 = (f32[16]{0:T(128)S(1)}, f32[16]{0:T(128)}, u32[]{:S(2)}) copy-start(f32[16]{0:T(128)} %param.9) | copy-start | bytes 196
  3.0 14.4 %collective-permute-start = (f32[22,16,128]{2,1,0:T(8,128)S(1)}, f32[22,16,128]{2,1,0:T(8,128)S(1)}, u32[]{:S(2)}, u32[]{:S(2)}) collective-permute-start(f32[22,16,128]{2,1,0:T(8,128)S(1)} %get-tuple-element.35), channel_id=1, source_target_pairs={{0,1},{1,2},{2,3},{3,4},{4,5},{5,6},{6,7},{7,8},{8,9},{9,10},{10,1... | collective-permute-start | bytes 540680 | tf_op jit(solution)/shard_map/ppermute | solution.py:756
  5.5 11.8 %collective-permute-start.1 = (f32[22,16,128]{2,1,0:T(8,128)S(1)}, f32[22,16,128]{2,1,0:T(8,128)S(1)}, u32[]{:S(2)}, u32[]{:S(2)}) collective-permute-start(f32[22,16,128]{2,1,0:T(8,128)S(1)} %get-tuple-element.36), channel_id=1, source_target_pairs={{1,0},{2,1},{3,2},{4,3},{5,4},{6,5},{7,6},{8,7},{9,8},{10,9},{11,1... | collective-permute-start | bytes 540680 | tf_op jit(solution)/shard_map/ppermute | solution.py:756
  10.5 20.6 %collective-permute-start.3 = (f32[56,8,128]{2,1,0:T(8,128)S(1)}, f32[56,8,128]{2,1,0:T(8,128)S(1)}, u32[]{:S(2)}, u32[]{:S(2)}) collective-permute-start(f32[56,8,128]{2,1,0:T(8,128)S(1)} %get-tuple-element.44), channel_id=1, source_target_pairs={{0,240},{16,32},{32,16},{48,64},{64,48},{80,96},{96,80},{112,128},... | collective-permute-start | bytes 688136 | tf_op jit(solution)/shard_map/ppermute | solution.py:745
  19.3 19.4 %collective-permute-start.9 = (f32[24,8,128]{2,1,0:T(8,128)S(1)}, f32[24,8,128]{2,1,0:T(8,128)S(1)}, u32[]{:S(2)}, u32[]{:S(2)}) collective-permute-start(f32[24,8,128]{2,1,0:T(8,128)S(1)} %get-tuple-element.45.after.own), channel_id=1, source_target_pairs={{0,16},{16,0},{32,48},{48,32},{64,80},{80,64},{96,112},{112,96},{1... | collective-permute-start | bytes 294920 | tf_op jit(solution)/shard_map/ppermute | solution.py:742
  31.3 7.6 %collective-permute-start.4 = (f32[24,8,128]{2,1,0:T(8,128)S(1)}, f32[24,8,128]{2,1,0:T(8,128)S(1)}, u32[]{:S(2)}, u32[]{:S(2)}) collective-permute-start(f32[24,8,128]{2,1,0:T(8,128)S(1)} %get-tuple-element.46), channel_id=1, source_target_pairs={{0,1},{1,2},{2,3},{3,4},{4,5},{5,6},{6,7},{7,8},{8,9},{9,10},{10,1... | collective-permute-start | bytes 294920 | tf_op jit(solution)/shard_map/ppermute | solution.py:756
  31.4 9.2 %collective-permute-start.5 = (f32[24,8,128]{2,1,0:T(8,128)S(1)}, f32[24,8,128]{2,1,0:T(8,128)S(1)}, u32[]{:S(2)}, u32[]{:S(2)}) collective-permute-start(f32[24,8,128]{2,1,0:T(8,128)S(1)} %get-tuple-element.47), channel_id=1, source_target_pairs={{1,0},{2,1},{3,2},{4,3},{5,4},{6,5},{7,6},{8,7},{9,8},{10,9},{11,1... | collective-permute-start | bytes 294920 | tf_op jit(solution)/shard_map/ppermute | solution.py:756
  36.7 4.0 %collective-permute-start.2 = (f32[56,8,256]{2,1,0:T(8,128)S(1)}, f32[56,8,256]{2,1,0:T(8,128)S(1)}, u32[]{:S(2)}, u32[]{:S(2)}) collective-permute-start(f32[56,8,256]{2,1,0:T(8,128)S(1)} %get-tuple-element.43), channel_id=1, source_target_pairs={{0,16},{16,0},{32,48},{48,32},{64,80},{80,64},{96,112},{112,96},{1... | collective-permute-start | bytes 1376264 | tf_op jit(solution)/shard_map/ppermute | solution.py:742
  38.8 12.9 %collective-permute-start.10 = (f32[48,8,128]{2,1,0:T(8,128)S(1)}, f32[48,8,128]{2,1,0:T(8,128)S(1)}, u32[]{:S(2)}, u32[]{:S(2)}) collective-permute-start(f32[48,8,128]{2,1,0:T(8,128)S(1)} %shard_map.84), channel_id=1, source_target_pairs={{0,240},{16,32},{32,16},{48,64},{64,48},{80,96},{96,80},{112,128},... | collective-permute-start | bytes 589832 | tf_op jit(solution)/shard_map/ppermute | solution.py:745
  44.3 2.5 %collective-permute-start.6 = (f32[16,8,128]{2,1,0:T(8,128)S(1)}, f32[16,8,128]{2,1,0:T(8,128)S(1)}, u32[]{:S(2)}, u32[]{:S(2)}) collective-permute-start(f32[16,8,128]{2,1,0:T(8,128)S(1)} %get-tuple-element.54.own), channel_id=1, source_target_pairs={{0,16},{16,0},{32,48},{48,32},{64,80},{80,64},{96,112},{112,96},{1... | collective-permute-start | bytes 196616 | tf_op jit(solution)/shard_map/ppermute | solution.py:742
  46.8 12.5 %collective-permute-start.7 = (f32[32,8,128]{2,1,0:T(8,128)S(1)}, f32[32,8,128]{2,1,0:T(8,128)S(1)}, u32[]{:S(2)}, u32[]{:S(2)}) collective-permute-start(f32[32,8,128]{2,1,0:T(8,128)S(1)} %pad_maximum_fusion), channel_id=1, source_target_pairs={{0,240},{16,32},{32,16},{48,64},{64,48},{80,96},{96,80},{112,128},... | collective-permute-start | bytes 393224 | tf_op jit(solution)/shard_map/ppermute | solution.py:745
  51.7 9.4 %collective-permute-start.11 = (f32[24,8,128]{2,1,0:T(8,128)S(1)}, f32[24,8,128]{2,1,0:T(8,128)S(1)}, u32[]{:S(2)}, u32[]{:S(2)}) collective-permute-start(f32[24,8,128]{2,1,0:T(8,128)S(1)} %shard_map.85), channel_id=1, source_target_pairs={{0,16},{16,0},{32,48},{48,32},{64,80},{80,64},{96,112},{112,96},{1... | collective-permute-start | bytes 294920 | tf_op jit(solution)/shard_map/ppermute | solution.py:742
  59.3 2.8 %collective-permute-start.8 = (f32[16,8,128]{2,1,0:T(8,128)S(1)}, f32[16,8,128]{2,1,0:T(8,128)S(1)}, u32[]{:S(2)}, u32[]{:S(2)}) collective-permute-start(f32[16,8,128]{2,1,0:T(8,128)S(1)} %shard_map.83), channel_id=1, source_target_pairs={{0,16},{16,0},{32,48},{48,32},{64,80},{80,64},{96,112},{112,96},{1... | collective-permute-start | bytes 196616 | tf_op jit(solution)/shard_map/ppermute | solution.py:742
  68.1 1.3 %collective-permute-start.12 = (f32[16,8,128]{2,1,0:T(8,128)S(1)}, f32[16,8,128]{2,1,0:T(8,128)S(1)}, u32[]{:S(2)}, u32[]{:S(2)}) collective-permute-start(f32[16,8,128]{2,1,0:T(8,128)S(1)} %get-tuple-element.64.own), channel_id=1, source_target_pairs={{0,16},{16,0},{32,48},{48,32},{64,80},{80,64},{96,112},{112,96},{1... | collective-permute-start | bytes 196616 | tf_op jit(solution)/shard_map/ppermute | solution.py:742
  70.0 10.2 %collective-permute-start.13 = (f32[24,8,128]{2,1,0:T(8,128)S(1)}, f32[24,8,128]{2,1,0:T(8,128)S(1)}, u32[]{:S(2)}, u32[]{:S(2)}) collective-permute-start(f32[24,8,128]{2,1,0:T(8,128)S(1)} %shard_map.88), channel_id=1, source_target_pairs={{0,240},{16,32},{32,16},{48,64},{64,48},{80,96},{96,80},{112,128},... | collective-permute-start | bytes 294920 | tf_op jit(solution)/shard_map/ppermute | solution.py:745
  80.3 1.9 %collective-permute-start.14 = (f32[16,8,128]{2,1,0:T(8,128)S(1)}, f32[16,8,128]{2,1,0:T(8,128)S(1)}, u32[]{:S(2)}, u32[]{:S(2)}) collective-permute-start(f32[16,8,128]{2,1,0:T(8,128)S(1)} %shard_map.89), channel_id=1, source_target_pairs={{0,16},{16,0},{32,48},{48,32},{64,80},{80,64},{96,112},{112,96},{1... | collective-permute-start | bytes 196616 | tf_op jit(solution)/shard_map/ppermute | solution.py:742

commit v12 on v10

--- a/solution.py
+++ b/solution.py
@@ -565,11 +565,9 @@
     near[...] = odd[0:R_TILES]
 
 
-def far_half_kernel(place, own, partner, message):
-    message[0:R_TILES] = own[...]
-
+def far_half_kernel(place, partner, message):
     def pair(p):
-        message[R_TILES + p] = half_rows(partner[2 * p], partner[2 * p + 1], place[0] == 0)
+        message[p] = half_rows(partner[2 * p], partner[2 * p + 1], place[0] == 0)
 
     loop(R_TILES // 2, pair)
 
@@ -799,7 +797,8 @@
         [PADDED0, PADDED0, *COARSE_SCRATCH, SUMS, BUFFER],
     )
     partner = on_chip(r1)
-    message = call(far_half_kernel, (place, r1, partner), [(R_TILES * 3 // 2, 8, COLS)])[0]
+    halves = call(far_half_kernel, (place, partner), [(R_TILES // 2, 8, COLS)])[0]
+    message = jnp.concatenate([r1, halves], axis=0)
     count = count_x * count_y
     direction, image, sums = call(
         last_kernel,

time: 109 us -> 109 us (level)
  no operation moved by 1% of the time
where the time goes in v12:
time: 109 us
  starting transfers between devices  34.4 us (32%)
  waiting for transfers between devices  30.7 us (28%)
  Pallas kernels  21 us (19%)
  blocking collectives  20.7 us (19%)
  other arithmetic  1.34 us (1%)
    ppermute x4, waiting for transfers between devices, across_chips(): return lax.ppermute(value, 'gx', pairs_across)  26.1 us
    pallas_call x14, Pallas kernels, call(): pl.pallas_call(kernel, out_shape=[jax.ShapeDtypeStruct(shape, F32) for sh...  21 us
    all_to_all x1, blocking collectives, shards(): lax.all_to_all(sums.reshape(count, 1, COLS), ('gx', 'gy'), 0, 0)  20.7 us
    ppermute x7, starting transfers between devices, on_chip(): return lax.ppermute(value, 'gx', pairs_on_chip)  14.3 us
    ppermute x2, starting transfers between devices, both_sides(): lax.ppermute(to_left, 'gy', backward)  10.4 us
    ppermute x4, starting transfers between devices, across_chips(): return lax.ppermute(value, 'gx', pairs_across)  7.15 us
    ppermute x7, waiting for transfers between devices, on_chip(): return lax.ppermute(value, 'gx', pairs_on_chip)  2.77 us
    ppermute x2, starting transfers between devices, both_sides(): lax.ppermute(to_right, 'gy', forward)  2.62 us
  transfers between devices with their start and end apart: 15, of which 7 were waited for; matrix products, arithmetic and copies ran while one was open for 0% of the time, Pallas kernels for 6%

profile of v12, /device:TPU:1, one launch (start us, length us, event | category | flops | bytes accessed | tf_op | source)
XLA Modules:
  0.0 109.0 jit_solution(4672850220301708649)
XLA Ops:
  0.7 0.1 pad_add_fusion.place
  0.8 1.2 %bitcast_select_fusion.fields.rhs = f32[4,16,16,128]{3,2,1,0:T(8,128)S(1)} fusion(s32[16,16,128]{2,1,0:T(8,128)} %param.8, s32[16,16,128]{2,1,0:T(8,128)} %param.7, f32[2,16,16,128]{3,2,1,0:T(8,128)} %param.6, pred[4]{0:T(512)(128)(4,1)S(1)} %get-tuple-element.68, pred[4]{0:T(512)(128)(4,1)S(1)} %get-tuple-element.69), kind=kLoop, calls=%fused_computation | loop fusion | flops 393216 | bytes 1048584 | tf_op jit(solution)/shard_map/jit(_where)/select_n | solution.py:753
  2.0 0.0 copy-start
  2.0 0.0 copy-start.1
  2.0 0.0 copy-start.2
  2.0 1.0 shard_map.77
  3.0 2.5 %collective-permute-start = (f32[22,16,128]{2,1,0:T(8,128)S(1)}, f32[22,16,128]{2,1,0:T(8,128)S(1)}, u32[]{:S(2)}, u32[]{:S(2)}) collective-permute-start(f32[22,16,128]{2,1,0:T(8,128)S(1)} %get-tuple-element.35), channel_id=1, source_target_pairs={{0,1},{1,2},{2,3},{3,4},{4,5},{5,6},{6,7},{7,8},{8,9},{9,10},{10,1... | collective-permute-start | bytes 540680 | tf_op jit(solution)/shard_map/ppermute | solution.py:748
  5.5 5.0 %collective-permute-start.1 = (f32[22,16,128]{2,1,0:T(8,128)S(1)}, f32[22,16,128]{2,1,0:T(8,128)S(1)}, u32[]{:S(2)}, u32[]{:S(2)}) collective-permute-start(f32[22,16,128]{2,1,0:T(8,128)S(1)} %get-tuple-element.36), channel_id=1, source_target_pairs={{1,0},{2,1},{3,2},{4,3},{5,4},{6,5},{7,6},{8,7},{9,8},{10,9},{11,1... | collective-permute-start | bytes 540680 | tf_op jit(solution)/shard_map/ppermute | solution.py:748
  10.5 6.8 %collective-permute-start.3 = (f32[56,8,128]{2,1,0:T(8,128)S(1)}, f32[56,8,128]{2,1,0:T(8,128)S(1)}, u32[]{:S(2)}, u32[]{:S(2)}) collective-permute-start(f32[56,8,128]{2,1,0:T(8,128)S(1)} %get-tuple-element.44), channel_id=1, source_target_pairs={{0,240},{16,32},{32,16},{48,64},{64,48},{80,96},{96,80},{112,128},... | collective-permute-start | bytes 688136 | tf_op jit(solution)/shard_map/ppermute | solution.py:737
  17.3 0.0 copy-done
  17.3 0.0 copy-done.1
  17.3 0.0 copy-done.2
  17.3 0.0 collective-permute-done.from_left
  17.3 0.0 collective-permute-done.1.from_right
  17.4 1.1 shard_map.78
  18.4 0.9 shard_map.79
  19.3 1.8 %collective-permute-start.9 = (f32[24,8,128]{2,1,0:T(8,128)S(1)}, f32[24,8,128]{2,1,0:T(8,128)S(1)}, u32[]{:S(2)}, u32[]{:S(2)}) collective-permute-start(f32[24,8,128]{2,1,0:T(8,128)S(1)} %get-tuple-element.45.after.own), channel_id=1, source_target_pairs={{0,16},{16,0},{32,48},{48,32},{64,80},{80,64},{96,112},{112,96},{1... | collective-permute-start | bytes 294920 | tf_op jit(solution)/shard_map/ppermute | solution.py:734
  21.2 0.1 collective-permute-start.2
  21.3 9.9 %collective-permute-done.3.message = f32[56,8,128]{2,1,0:T(8,128)S(1)} collective-permute-done((f32[56,8,128]{2,1,0:T(8,128)S(1)}, f32[56,8,128]{2,1,0:T(8,128)S(1)}, u32[]{:S(2)}, u32[]{:S(2)}) %collective-permute-start.3) | collective-permute-done | bytes 229408 | tf_op jit(solution)/shard_map/ppermute | solution.py:737
  31.1 0.2 shard_map.80
  31.3 0.1 collective-permute-start.4
  31.4 5.4 %collective-permute-start.5 = (f32[24,8,128]{2,1,0:T(8,128)S(1)}, f32[24,8,128]{2,1,0:T(8,128)S(1)}, u32[]{:S(2)}, u32[]{:S(2)}) collective-permute-start(f32[24,8,128]{2,1,0:T(8,128)S(1)} %get-tuple-element.47), channel_id=1, source_target_pairs={{1,0},{2,1},{3,2},{4,3},{5,4},{6,5},{7,6},{8,7},{9,8},{10,9},{11,1... | collective-permute-start | bytes 294920 | tf_op jit(solution)/shard_map/ppermute | solution.py:748
  36.7 0.0 collective-permute-done.9.partner
  36.7 0.2 collective-permute-start.10
  36.9 1.9 %collective-permute-done.4.corner_left = f32[24,8,128]{2,1,0:T(8,128)S(1)} collective-permute-done((f32[24,8,128]{2,1,0:T(8,128)S(1)}, f32[24,8,128]{2,1,0:T(8,128)S(1)}, u32[]{:S(2)}, u32[]{:S(2)}) %collective-permute-start.4) | collective-permute-done | bytes 98336 | tf_op jit(solution)/shard_map/ppermute | solution.py:748
  38.8 0.0 collective-permute-done.5.corner_right
  38.8 0.2 shard_map.81.wide
  39.0 0.0 collective-permute-done.2.from_x
  39.0 3.6 %shard_map.82 = (f32[16,2,32,256]{3,2,1,0:T(8,128)S(1)}, f32[16,32,256]{2,1,0:T(8,128)S(1)}, f32[18,32,256]{2,1,0:T(8,128)S(1)}, f32[16,32,256]{2,1,0:T(8,128)S(...) custom-call(s32[5]{0:T(128)S(1)} %pad_add_fusion.place, ...), custom_call_target="tpu_custom_call" | custom-call | flops 4000000000 | bytes 12000000 | tf_op jit(solution)/shard_map/pallas_call | solution.py:700
  42.6 7.1 %collective-permute-start.6 = (f32[16,8,128]{2,1,0:T(8,128)S(1)}, f32[16,8,128]{2,1,0:T(8,128)S(1)}, u32[]{:S(2)}, u32[]{:S(2)}) collective-permute-start(f32[16,8,128]{2,1,0:T(8,128)S(1)} %get-tuple-element.54.own), channel_id=1, source_target_pairs={{0,16},{16,0},{32,48},{48,32},{64,80},{80,64},{96,112},{112,96},{1... | collective-permute-start | bytes 196616 | tf_op jit(solution)/shard_map/ppermute | solution.py:734
  49.7 0.9 collective-permute-done.6.after.partner
  50.6 0.1 collective-permute-start.7
  50.7 0.0 collective-permute-done.10.odd
  50.7 2.3 %collective-permute-start.11 = (f32[24,8,128]{2,1,0:T(8,128)S(1)}, f32[24,8,128]{2,1,0:T(8,128)S(1)}, u32[]{:S(2)}, u32[]{:S(2)}) collective-permute-start(f32[24,8,128]{2,1,0:T(8,128)S(1)} %shard_map.84), channel_id=1, source_target_pairs={{0,16},{16,0},{32,48},{48,32},{64,80},{80,64},{96,112},{112,96},{1... | collective-permute-start | bytes 294920 | tf_op jit(solution)/shard_map/ppermute | solution.py:734
  53.0 6.9 %collective-permute-done.7.odd = f32[32,8,128]{2,1,0:T(8,128)S(1)} collective-permute-done((f32[32,8,128]{2,1,0:T(8,128)S(1)}, f32[32,8,128]{2,1,0:T(8,128)S(1)}, u32[]{:S(2)}, u32[]{:S(2)}) %collective-permute-start.7) | collective-permute-done | bytes 131104 | tf_op jit(solution)/shard_map/ppermute | solution.py:737
  59.9 1.6 %collective-permute-start.8 = (f32[16,8,128]{2,1,0:T(8,128)S(1)}, f32[16,8,128]{2,1,0:T(8,128)S(1)}, u32[]{:S(2)}, u32[]{:S(2)}) collective-permute-start(f32[16,8,128]{2,1,0:T(8,128)S(1)} %shard_map.83), channel_id=1, source_target_pairs={{0,16},{16,0},{32,48},{48,32},{64,80},{80,64},{96,112},{112,96},{1... | collective-permute-start | bytes 196616 | tf_op jit(solution)/shard_map/ppermute | solution.py:734
  61.4 0.0 collective-permute-done.11.far
  61.4 0.9 shard_map.85
  62.4 0.0 collective-permute-done.8.far
  62.4 6.0 %shard_map.86 = (f32[16,2,32,256]{3,2,1,0:T(8,128)S(1)}, f32[18,2,32,256]{3,2,1,0:T(8,128)S(1)}, f32[16,8,128]{2,1,0:T(8,128)S(1)}) custom-call(s32[5]{0:T(128)S(1)} %pad_add_fusion.place, f32[16,2,32,256]{3,2,1,0:T(8,128)S(1)} %get-tuple-element.48.r, f32[16,32,256]{2,1,0:T(8,128)S(1)} %get-tuple-element.49.g, f32[18,32,256]{2,1,0:T(8,128)S(1)} %get-tuple-element.50.h, ...), custom_call_target="tpu_custom_call" | custom-call | flops 6000000000 | bytes 18000000 | tf_op jit(solution)/shard_map/pallas_call | solution.py:700
  68.4 0.4 collective-permute-start.12
  68.8 1.0 collective-permute-done.12.partner
  69.8 0.5 shard_map.87
  70.4 0.1 collective-permute-start.13
  70.5 9.3 %collective-permute-done.13.odd = f32[24,8,128]{2,1,0:T(8,128)S(1)} collective-permute-done((f32[24,8,128]{2,1,0:T(8,128)S(1)}, f32[24,8,128]{2,1,0:T(8,128)S(1)}, u32[]{:S(2)}, u32[]{:S(2)}) %collective-permute-start.13) | collective-permute-done | bytes 98336 | tf_op jit(solution)/shard_map/ppermute | solution.py:737
  79.7 1.1 collective-permute-start.14
  80.8 0.9 collective-permute-done.14.far
  81.7 5.6 %shard_map.89 = (f32[2,16,16,128]{3,2,1,0:T(8,128)S(1)}, f32[2,16,16,128]{3,2,1,0:T(8,128)S(1)}, f32[256,128]{1,0:T(8,128)S(1)}) custom-call(s32[5]{0:T(128)S(1)} %pad_add_fusion.place, f32[4,16,16,128]{3,2,1,0:T(8,128)S(1)} %bitcast_select_fusion.fields.rhs, f32[16,2,32,256]{3,2,1,0:T(8,128)S(1)} %get-tuple-element.62.r, ...), custom_call_target="tpu_custom_call" | custom-call | flops 6000000000 | bytes 18000000 | tf_op jit(solution)/shard_map/pallas_call | solution.py:700
  87.3 20.7 %all_to_all.5 = f32[256,1,128]{2,1,0:T(1,128)S(1)} all-to-all(f32[256,1,128]{2,1,0:T(1,128)S(1)} %bitcast.14), channel_id=1, replica_groups=mesh['gx'=16,'gy'=16] {'gx','gy'}, dimensions={0} | all-to-all | bytes 262144 | tf_op jit(solution)/shard_map/all_to_all | solution.py:809
  108.1 1.0 shard_map.90
  (10 shorter events, 0.1 us)
Async XLA Ops:
  2.0 15.3 %copy-start = (f32[16]{0:T(128)S(1)}, f32[16]{0:T(128)}, u32[]{:S(2)}) copy-start(f32[16]{0:T(128)} %param.11) | copy-start | bytes 196
  2.0 15.3 %copy-start.1 = (f32[16]{0:T(128)S(1)}, f32[16]{0:T(128)}, u32[]{:S(2)}) copy-start(f32[16]{0:T(128)} %param.10) | copy-start | bytes 196
  2.0 15.3 %copy-start.2 = (f32[16]{0:T(128)S(1)}, f32[16]{0:T(128)}, u32[]{:S(2)}) copy-start(f32[16]{0:T(128)} %param.9) | copy-start | bytes 196
  3.0 14.4 %collective-permute-start = (f32[22,16,128]{2,1,0:T(8,128)S(1)}, f32[22,16,128]{2,1,0:T(8,128)S(1)}, u32[]{:S(2)}, u32[]{:S(2)}) collective-permute-start(f32[22,16,128]{2,1,0:T(8,128)S(1)} %get-tuple-element.35), channel_id=1, source_target_pairs={{0,1},{1,2},{2,3},{3,4},{4,5},{5,6},{6,7},{7,8},{8,9},{9,10},{10,1... | collective-permute-start | bytes 540680 | tf_op jit(solution)/shard_map/ppermute | solution.py:748
  5.5 11.8 %collective-permute-start.1 = (f32[22,16,128]{2,1,0:T(8,128)S(1)}, f32[22,16,128]{2,1,0:T(8,128)S(1)}, u32[]{:S(2)}, u32[]{:S(2)}) collective-permute-start(f32[22,16,128]{2,1,0:T(8,128)S(1)} %get-tuple-element.36), channel_id=1, source_target_pairs={{1,0},{2,1},{3,2},{4,3},{5,4},{6,5},{7,6},{8,7},{9,8},{10,9},{11,1... | collective-permute-start | bytes 540680 | tf_op jit(solution)/shard_map/ppermute | solution.py:748
  10.5 20.6 %collective-permute-start.3 = (f32[56,8,128]{2,1,0:T(8,128)S(1)}, f32[56,8,128]{2,1,0:T(8,128)S(1)}, u32[]{:S(2)}, u32[]{:S(2)}) collective-permute-start(f32[56,8,128]{2,1,0:T(8,128)S(1)} %get-tuple-element.44), channel_id=1, source_target_pairs={{0,240},{16,32},{32,16},{48,64},{64,48},{80,96},{96,80},{112,128},... | collective-permute-start | bytes 688136 | tf_op jit(solution)/shard_map/ppermute | solution.py:737
  19.3 17.4 %collective-permute-start.9 = (f32[24,8,128]{2,1,0:T(8,128)S(1)}, f32[24,8,128]{2,1,0:T(8,128)S(1)}, u32[]{:S(2)}, u32[]{:S(2)}) collective-permute-start(f32[24,8,128]{2,1,0:T(8,128)S(1)} %get-tuple-element.45.after.own), channel_id=1, source_target_pairs={{0,16},{16,0},{32,48},{48,32},{64,80},{80,64},{96,112},{112,96},{1... | collective-permute-start | bytes 294920 | tf_op jit(solution)/shard_map/ppermute | solution.py:734
  21.2 17.8 %collective-permute-start.2 = (f32[56,8,256]{2,1,0:T(8,128)S(1)}, f32[56,8,256]{2,1,0:T(8,128)S(1)}, u32[]{:S(2)}, u32[]{:S(2)}) collective-permute-start(f32[56,8,256]{2,1,0:T(8,128)S(1)} %get-tuple-element.43), channel_id=1, source_target_pairs={{0,16},{16,0},{32,48},{48,32},{64,80},{80,64},{96,112},{112,96},{1... | collective-permute-start | bytes 1376264 | tf_op jit(solution)/shard_map/ppermute | solution.py:734
  31.3 7.6 %collective-permute-start.4 = (f32[24,8,128]{2,1,0:T(8,128)S(1)}, f32[24,8,128]{2,1,0:T(8,128)S(1)}, u32[]{:S(2)}, u32[]{:S(2)}) collective-permute-start(f32[24,8,128]{2,1,0:T(8,128)S(1)} %get-tuple-element.46), channel_id=1, source_target_pairs={{0,1},{1,2},{2,3},{3,4},{4,5},{5,6},{6,7},{7,8},{8,9},{9,10},{10,1... | collective-permute-start | bytes 294920 | tf_op jit(solution)/shard_map/ppermute | solution.py:748
  31.4 7.5 %collective-permute-start.5 = (f32[24,8,128]{2,1,0:T(8,128)S(1)}, f32[24,8,128]{2,1,0:T(8,128)S(1)}, u32[]{:S(2)}, u32[]{:S(2)}) collective-permute-start(f32[24,8,128]{2,1,0:T(8,128)S(1)} %get-tuple-element.47), channel_id=1, source_target_pairs={{1,0},{2,1},{3,2},{4,3},{5,4},{6,5},{7,6},{8,7},{9,8},{10,9},{11,1... | collective-permute-start | bytes 294920 | tf_op jit(solution)/shard_map/ppermute | solution.py:748
  36.7 13.9 %collective-permute-start.10 = (f32[48,8,128]{2,1,0:T(8,128)S(1)}, f32[48,8,128]{2,1,0:T(8,128)S(1)}, u32[]{:S(2)}, u32[]{:S(2)}) collective-permute-start(f32[48,8,128]{2,1,0:T(8,128)S(1)} %pad_maximum_fusion), channel_id=1, source_target_pairs={{0,240},{16,32},{32,16},{48,64},{64,48},{80,96},{96,80},{112,128},... | collective-permute-start | bytes 589832 | tf_op jit(solution)/shard_map/ppermute | solution.py:737
  42.6 8.0 %collective-permute-start.6 = (f32[16,8,128]{2,1,0:T(8,128)S(1)}, f32[16,8,128]{2,1,0:T(8,128)S(1)}, u32[]{:S(2)}, u32[]{:S(2)}) collective-permute-start(f32[16,8,128]{2,1,0:T(8,128)S(1)} %get-tuple-element.54.own), channel_id=1, source_target_pairs={{0,16},{16,0},{32,48},{48,32},{64,80},{80,64},{96,112},{112,96},{1... | collective-permute-start | bytes 196616 | tf_op jit(solution)/shard_map/ppermute | solution.py:734
  50.6 9.3 %collective-permute-start.7 = (f32[32,8,128]{2,1,0:T(8,128)S(1)}, f32[32,8,128]{2,1,0:T(8,128)S(1)}, u32[]{:S(2)}, u32[]{:S(2)}) collective-permute-start(f32[32,8,128]{2,1,0:T(8,128)S(1)} %pad_maximum_fusion.1), channel_id=1, source_target_pairs={{0,240},{16,32},{32,16},{48,64},{64,48},{80,96},{96,80},{112,128},... | collective-permute-start | bytes 393224 | tf_op jit(solution)/shard_map/ppermute | solution.py:737
  50.7 10.7 %collective-permute-start.11 = (f32[24,8,128]{2,1,0:T(8,128)S(1)}, f32[24,8,128]{2,1,0:T(8,128)S(1)}, u32[]{:S(2)}, u32[]{:S(2)}) collective-permute-start(f32[24,8,128]{2,1,0:T(8,128)S(1)} %shard_map.84), channel_id=1, source_target_pairs={{0,16},{16,0},{32,48},{48,32},{64,80},{80,64},{96,112},{112,96},{1... | collective-permute-start | bytes 294920 | tf_op jit(solution)/shard_map/ppermute | solution.py:734
  59.9 2.5 %collective-permute-start.8 = (f32[16,8,128]{2,1,0:T(8,128)S(1)}, f32[16,8,128]{2,1,0:T(8,128)S(1)}, u32[]{:S(2)}, u32[]{:S(2)}) collective-permute-start(f32[16,8,128]{2,1,0:T(8,128)S(1)} %shard_map.83), channel_id=1, source_target_pairs={{0,16},{16,0},{32,48},{48,32},{64,80},{80,64},{96,112},{112,96},{1... | collective-permute-start | bytes 196616 | tf_op jit(solution)/shard_map/ppermute | solution.py:734
  68.4 1.3 %collective-permute-start.12 = (f32[16,8,128]{2,1,0:T(8,128)S(1)}, f32[16,8,128]{2,1,0:T(8,128)S(1)}, u32[]{:S(2)}, u32[]{:S(2)}) collective-permute-start(f32[16,8,128]{2,1,0:T(8,128)S(1)} %get-tuple-element.64.own), channel_id=1, source_target_pairs={{0,16},{16,0},{32,48},{48,32},{64,80},{80,64},{96,112},{112,96},{1... | collective-permute-start | bytes 196616 | tf_op jit(solution)/shard_map/ppermute | solution.py:734
  70.4 9.4 %collective-permute-start.13 = (f32[24,8,128]{2,1,0:T(8,128)S(1)}, f32[24,8,128]{2,1,0:T(8,128)S(1)}, u32[]{:S(2)}, u32[]{:S(2)}) collective-permute-start(f32[24,8,128]{2,1,0:T(8,128)S(1)} %pad_maximum_fusion.2), channel_id=1, source_target_pairs={{0,240},{16,32},{32,16},{48,64},{64,48},{80,96},{96,80},{112,128},... | collective-permute-start | bytes 294920 | tf_op jit(solution)/shard_map/ppermute | solution.py:737
  79.7 2.0 %collective-permute-start.14 = (f32[16,8,128]{2,1,0:T(8,128)S(1)}, f32[16,8,128]{2,1,0:T(8,128)S(1)}, u32[]{:S(2)}, u32[]{:S(2)}) collective-permute-start(f32[16,8,128]{2,1,0:T(8,128)S(1)} %shard_map.88), channel_id=1, source_target_pairs={{0,16},{16,0},{32,48},{48,32},{64,80},{80,64},{96,112},{112,96},{1... | collective-permute-start | bytes 196616 | tf_op jit(solution)/shard_map/ppermute | solution.py:734

commit v13 on v12

--- a/solution.py
+++ b/solution.py
@@ -38,7 +38,7 @@
         body(index)
         return carry
 
-    lax.fori_loop(0, count, step, 0, unroll=min(count, UNROLL))
+    lax.fori_loop(0, count, step, 0, unroll=count if count < 2 * UNROLL else UNROLL)
 
 
 def lanes(rows, width):

time: 109 us -> 109 us (level)
  no operation moved by 1% of the time
where the time goes in v13:
time: 109 us
  starting transfers between devices  34.4 us (32%)
  waiting for transfers between devices  30.7 us (28%)
  Pallas kernels  21 us (19%)
  blocking collectives  20.7 us (19%)
  other arithmetic  1.34 us (1%)
    ppermute x4, waiting for transfers between devices, across_chips(): return lax.ppermute(value, 'gx', pairs_across)  26.1 us
    pallas_call x14, Pallas kernels, call(): pl.pallas_call(kernel, out_shape=[jax.ShapeDtypeStruct(shape, F32) for sh...  21 us
    all_to_all x1, blocking collectives, shards(): lax.all_to_all(sums.reshape(count, 1, COLS), ('gx', 'gy'), 0, 0)  20.7 us
    ppermute x7, starting transfers between devices, on_chip(): return lax.ppermute(value, 'gx', pairs_on_chip)  14.3 us
    ppermute x2, starting transfers between devices, both_sides(): lax.ppermute(to_left, 'gy', backward)  10.4 us
    ppermute x4, starting transfers between devices, across_chips(): return lax.ppermute(value, 'gx', pairs_across)  7.15 us
    ppermute x7, waiting for transfers between devices, on_chip(): return lax.ppermute(value, 'gx', pairs_on_chip)  2.77 us
    ppermute x2, starting transfers between devices, both_sides(): lax.ppermute(to_right, 'gy', forward)  2.62 us
  transfers between devices with their start and end apart: 15, of which 7 were waited for; matrix products, arithmetic and copies ran while one was open for 0% of the time, Pallas kernels for 6%

profile of v13, /device:TPU:1, one launch (start us, length us, event | category | flops | bytes accessed | tf_op | source)
XLA Modules:
  0.0 109.0 jit_solution(4672850220301708649)
XLA Ops:
  0.7 0.1 pad_add_fusion.place
  0.8 1.2 %bitcast_select_fusion.fields.rhs = f32[4,16,16,128]{3,2,1,0:T(8,128)S(1)} fusion(s32[16,16,128]{2,1,0:T(8,128)} %param.8, s32[16,16,128]{2,1,0:T(8,128)} %param.7, f32[2,16,16,128]{3,2,1,0:T(8,128)} %param.6, pred[4]{0:T(512)(128)(4,1)S(1)} %get-tuple-element.68, pred[4]{0:T(512)(128)(4,1)S(1)} %get-tuple-element.69), kind=kLoop, calls=%fused_computation | loop fusion | flops 393216 | bytes 1048584 | tf_op jit(solution)/shard_map/jit(_where)/select_n | solution.py:753
  2.0 0.0 copy-start
  2.0 0.0 copy-start.1
  2.0 0.0 copy-start.2
  2.0 1.0 shard_map.77
  3.0 2.5 %collective-permute-start = (f32[22,16,128]{2,1,0:T(8,128)S(1)}, f32[22,16,128]{2,1,0:T(8,128)S(1)}, u32[]{:S(2)}, u32[]{:S(2)}) collective-permute-start(f32[22,16,128]{2,1,0:T(8,128)S(1)} %get-tuple-element.35), channel_id=1, source_target_pairs={{0,1},{1,2},{2,3},{3,4},{4,5},{5,6},{6,7},{7,8},{8,9},{9,10},{10,1... | collective-permute-start | bytes 540680 | tf_op jit(solution)/shard_map/ppermute | solution.py:748
  5.5 5.0 %collective-permute-start.1 = (f32[22,16,128]{2,1,0:T(8,128)S(1)}, f32[22,16,128]{2,1,0:T(8,128)S(1)}, u32[]{:S(2)}, u32[]{:S(2)}) collective-permute-start(f32[22,16,128]{2,1,0:T(8,128)S(1)} %get-tuple-element.36), channel_id=1, source_target_pairs={{1,0},{2,1},{3,2},{4,3},{5,4},{6,5},{7,6},{8,7},{9,8},{10,9},{11,1... | collective-permute-start | bytes 540680 | tf_op jit(solution)/shard_map/ppermute | solution.py:748
  10.5 6.8 %collective-permute-start.3 = (f32[56,8,128]{2,1,0:T(8,128)S(1)}, f32[56,8,128]{2,1,0:T(8,128)S(1)}, u32[]{:S(2)}, u32[]{:S(2)}) collective-permute-start(f32[56,8,128]{2,1,0:T(8,128)S(1)} %get-tuple-element.44), channel_id=1, source_target_pairs={{0,240},{16,32},{32,16},{48,64},{64,48},{80,96},{96,80},{112,128},... | collective-permute-start | bytes 688136 | tf_op jit(solution)/shard_map/ppermute | solution.py:737
  17.3 0.0 copy-done
  17.3 0.0 copy-done.1
  17.3 0.0 copy-done.2
  17.3 0.0 collective-permute-done.from_left
  17.3 0.0 collective-permute-done.1.from_right
  17.4 1.1 shard_map.78
  18.4 0.9 shard_map.79
  19.3 1.8 %collective-permute-start.9 = (f32[24,8,128]{2,1,0:T(8,128)S(1)}, f32[24,8,128]{2,1,0:T(8,128)S(1)}, u32[]{:S(2)}, u32[]{:S(2)}) collective-permute-start(f32[24,8,128]{2,1,0:T(8,128)S(1)} %get-tuple-element.45.after.own), channel_id=1, source_target_pairs={{0,16},{16,0},{32,48},{48,32},{64,80},{80,64},{96,112},{112,96},{1... | collective-permute-start | bytes 294920 | tf_op jit(solution)/shard_map/ppermute | solution.py:734
  21.2 0.1 collective-permute-start.2
  21.3 9.9 %collective-permute-done.3.message = f32[56,8,128]{2,1,0:T(8,128)S(1)} collective-permute-done((f32[56,8,128]{2,1,0:T(8,128)S(1)}, f32[56,8,128]{2,1,0:T(8,128)S(1)}, u32[]{:S(2)}, u32[]{:S(2)}) %collective-permute-start.3) | collective-permute-done | bytes 229408 | tf_op jit(solution)/shard_map/ppermute | solution.py:737
  31.1 0.2 shard_map.80
  31.3 0.1 collective-permute-start.4
  31.4 5.4 %collective-permute-start.5 = (f32[24,8,128]{2,1,0:T(8,128)S(1)}, f32[24,8,128]{2,1,0:T(8,128)S(1)}, u32[]{:S(2)}, u32[]{:S(2)}) collective-permute-start(f32[24,8,128]{2,1,0:T(8,128)S(1)} %get-tuple-element.47), channel_id=1, source_target_pairs={{1,0},{2,1},{3,2},{4,3},{5,4},{6,5},{7,6},{8,7},{9,8},{10,9},{11,1... | collective-permute-start | bytes 294920 | tf_op jit(solution)/shard_map/ppermute | solution.py:748
  36.7 0.0 collective-permute-done.9.partner
  36.7 0.2 collective-permute-start.10
  36.9 1.9 %collective-permute-done.4.corner_left = f32[24,8,128]{2,1,0:T(8,128)S(1)} collective-permute-done((f32[24,8,128]{2,1,0:T(8,128)S(1)}, f32[24,8,128]{2,1,0:T(8,128)S(1)}, u32[]{:S(2)}, u32[]{:S(2)}) %collective-permute-start.4) | collective-permute-done | bytes 98336 | tf_op jit(solution)/shard_map/ppermute | solution.py:748
  38.8 0.0 collective-permute-done.5.corner_right
  38.8 0.2 shard_map.81.wide
  39.0 0.0 collective-permute-done.2.from_x
  39.0 3.6 %shard_map.82 = (f32[16,2,32,256]{3,2,1,0:T(8,128)S(1)}, f32[16,32,256]{2,1,0:T(8,128)S(1)}, f32[18,32,256]{2,1,0:T(8,128)S(1)}, f32[16,32,256]{2,1,0:T(8,128)S(...) custom-call(s32[5]{0:T(128)S(1)} %pad_add_fusion.place, ...), custom_call_target="tpu_custom_call" | custom-call | flops 4000000000 | bytes 12000000 | tf_op jit(solution)/shard_map/pallas_call | solution.py:700
  42.6 7.1 %collective-permute-start.6 = (f32[16,8,128]{2,1,0:T(8,128)S(1)}, f32[16,8,128]{2,1,0:T(8,128)S(1)}, u32[]{:S(2)}, u32[]{:S(2)}) collective-permute-start(f32[16,8,128]{2,1,0:T(8,128)S(1)} %get-tuple-element.54.own), channel_id=1, source_target_pairs={{0,16},{16,0},{32,48},{48,32},{64,80},{80,64},{96,112},{112,96},{1... | collective-permute-start | bytes 196616 | tf_op jit(solution)/shard_map/ppermute | solution.py:734
  49.7 0.9 collective-permute-done.6.after.partner
  50.6 0.1 collective-permute-start.7
  50.7 0.0 collective-permute-done.10.odd
  50.7 2.3 %collective-permute-start.11 = (f32[24,8,128]{2,1,0:T(8,128)S(1)}, f32[24,8,128]{2,1,0:T(8,128)S(1)}, u32[]{:S(2)}, u32[]{:S(2)}) collective-permute-start(f32[24,8,128]{2,1,0:T(8,128)S(1)} %shard_map.84), channel_id=1, source_target_pairs={{0,16},{16,0},{32,48},{48,32},{64,80},{80,64},{96,112},{112,96},{1... | collective-permute-start | bytes 294920 | tf_op jit(solution)/shard_map/ppermute | solution.py:734
  53.0 6.9 %collective-permute-done.7.odd = f32[32,8,128]{2,1,0:T(8,128)S(1)} collective-permute-done((f32[32,8,128]{2,1,0:T(8,128)S(1)}, f32[32,8,128]{2,1,0:T(8,128)S(1)}, u32[]{:S(2)}, u32[]{:S(2)}) %collective-permute-start.7) | collective-permute-done | bytes 131104 | tf_op jit(solution)/shard_map/ppermute | solution.py:737
  59.9 1.6 %collective-permute-start.8 = (f32[16,8,128]{2,1,0:T(8,128)S(1)}, f32[16,8,128]{2,1,0:T(8,128)S(1)}, u32[]{:S(2)}, u32[]{:S(2)}) collective-permute-start(f32[16,8,128]{2,1,0:T(8,128)S(1)} %shard_map.83), channel_id=1, source_target_pairs={{0,16},{16,0},{32,48},{48,32},{64,80},{80,64},{96,112},{112,96},{1... | collective-permute-start | bytes 196616 | tf_op jit(solution)/shard_map/ppermute | solution.py:734
  61.4 0.0 collective-permute-done.11.far
  61.4 0.9 shard_map.85
  62.4 0.0 collective-permute-done.8.far
  62.4 6.0 %shard_map.86 = (f32[16,2,32,256]{3,2,1,0:T(8,128)S(1)}, f32[18,2,32,256]{3,2,1,0:T(8,128)S(1)}, f32[16,8,128]{2,1,0:T(8,128)S(1)}) custom-call(s32[5]{0:T(128)S(1)} %pad_add_fusion.place, f32[16,2,32,256]{3,2,1,0:T(8,128)S(1)} %get-tuple-element.48.r, f32[16,32,256]{2,1,0:T(8,128)S(1)} %get-tuple-element.49.g, f32[18,32,256]{2,1,0:T(8,128)S(1)} %get-tuple-element.50.h, ...), custom_call_target="tpu_custom_call" | custom-call | flops 6000000000 | bytes 18000000 | tf_op jit(solution)/shard_map/pallas_call | solution.py:700
  68.4 0.4 collective-permute-start.12
  68.8 1.0 collective-permute-done.12.partner
  69.8 0.5 shard_map.87
  70.4 0.1 collective-permute-start.13
  70.5 9.3 %collective-permute-done.13.odd = f32[24,8,128]{2,1,0:T(8,128)S(1)} collective-permute-done((f32[24,8,128]{2,1,0:T(8,128)S(1)}, f32[24,8,128]{2,1,0:T(8,128)S(1)}, u32[]{:S(2)}, u32[]{:S(2)}) %collective-permute-start.13) | collective-permute-done | bytes 98336 | tf_op jit(solution)/shard_map/ppermute | solution.py:737
  79.7 1.1 collective-permute-start.14
  80.8 0.9 collective-permute-done.14.far
  81.7 5.6 %shard_map.89 = (f32[2,16,16,128]{3,2,1,0:T(8,128)S(1)}, f32[2,16,16,128]{3,2,1,0:T(8,128)S(1)}, f32[256,128]{1,0:T(8,128)S(1)}) custom-call(s32[5]{0:T(128)S(1)} %pad_add_fusion.place, f32[4,16,16,128]{3,2,1,0:T(8,128)S(1)} %bitcast_select_fusion.fields.rhs, f32[16,2,32,256]{3,2,1,0:T(8,128)S(1)} %get-tuple-element.62.r, ...), custom_call_target="tpu_custom_call" | custom-call | flops 6000000000 | bytes 18000000 | tf_op jit(solution)/shard_map/pallas_call | solution.py:700
  87.3 20.7 %all_to_all.5 = f32[256,1,128]{2,1,0:T(1,128)S(1)} all-to-all(f32[256,1,128]{2,1,0:T(1,128)S(1)} %bitcast.14), channel_id=1, replica_groups=mesh['gx'=16,'gy'=16] {'gx','gy'}, dimensions={0} | all-to-all | bytes 262144 | tf_op jit(solution)/shard_map/all_to_all | solution.py:809
  108.1 1.0 shard_map.90
  (10 shorter events, 0.1 us)
Async XLA Ops:
  2.0 15.3 %copy-start = (f32[16]{0:T(128)S(1)}, f32[16]{0:T(128)}, u32[]{:S(2)}) copy-start(f32[16]{0:T(128)} %param.11) | copy-start | bytes 196
  2.0 15.3 %copy-start.1 = (f32[16]{0:T(128)S(1)}, f32[16]{0:T(128)}, u32[]{:S(2)}) copy-start(f32[16]{0:T(128)} %param.10) | copy-start | bytes 196
  2.0 15.3 %copy-start.2 = (f32[16]{0:T(128)S(1)}, f32[16]{0:T(128)}, u32[]{:S(2)}) copy-start(f32[16]{0:T(128)} %param.9) | copy-start | bytes 196
  3.0 14.4 %collective-permute-start = (f32[22,16,128]{2,1,0:T(8,128)S(1)}, f32[22,16,128]{2,1,0:T(8,128)S(1)}, u32[]{:S(2)}, u32[]{:S(2)}) collective-permute-start(f32[22,16,128]{2,1,0:T(8,128)S(1)} %get-tuple-element.35), channel_id=1, source_target_pairs={{0,1},{1,2},{2,3},{3,4},{4,5},{5,6},{6,7},{7,8},{8,9},{9,10},{10,1... | collective-permute-start | bytes 540680 | tf_op jit(solution)/shard_map/ppermute | solution.py:748
  5.5 11.8 %collective-permute-start.1 = (f32[22,16,128]{2,1,0:T(8,128)S(1)}, f32[22,16,128]{2,1,0:T(8,128)S(1)}, u32[]{:S(2)}, u32[]{:S(2)}) collective-permute-start(f32[22,16,128]{2,1,0:T(8,128)S(1)} %get-tuple-element.36), channel_id=1, source_target_pairs={{1,0},{2,1},{3,2},{4,3},{5,4},{6,5},{7,6},{8,7},{9,8},{10,9},{11,1... | collective-permute-start | bytes 540680 | tf_op jit(solution)/shard_map/ppermute | solution.py:748
  10.5 20.6 %collective-permute-start.3 = (f32[56,8,128]{2,1,0:T(8,128)S(1)}, f32[56,8,128]{2,1,0:T(8,128)S(1)}, u32[]{:S(2)}, u32[]{:S(2)}) collective-permute-start(f32[56,8,128]{2,1,0:T(8,128)S(1)} %get-tuple-element.44), channel_id=1, source_target_pairs={{0,240},{16,32},{32,16},{48,64},{64,48},{80,96},{96,80},{112,128},... | collective-permute-start | bytes 688136 | tf_op jit(solution)/shard_map/ppermute | solution.py:737
  19.3 17.4 %collective-permute-start.9 = (f32[24,8,128]{2,1,0:T(8,128)S(1)}, f32[24,8,128]{2,1,0:T(8,128)S(1)}, u32[]{:S(2)}, u32[]{:S(2)}) collective-permute-start(f32[24,8,128]{2,1,0:T(8,128)S(1)} %get-tuple-element.45.after.own), channel_id=1, source_target_pairs={{0,16},{16,0},{32,48},{48,32},{64,80},{80,64},{96,112},{112,96},{1... | collective-permute-start | bytes 294920 | tf_op jit(solution)/shard_map/ppermute | solution.py:734
  21.2 17.8 %collective-permute-start.2 = (f32[56,8,256]{2,1,0:T(8,128)S(1)}, f32[56,8,256]{2,1,0:T(8,128)S(1)}, u32[]{:S(2)}, u32[]{:S(2)}) collective-permute-start(f32[56,8,256]{2,1,0:T(8,128)S(1)} %get-tuple-element.43), channel_id=1, source_target_pairs={{0,16},{16,0},{32,48},{48,32},{64,80},{80,64},{96,112},{112,96},{1... | collective-permute-start | bytes 1376264 | tf_op jit(solution)/shard_map/ppermute | solution.py:734
  31.3 7.6 %collective-permute-start.4 = (f32[24,8,128]{2,1,0:T(8,128)S(1)}, f32[24,8,128]{2,1,0:T(8,128)S(1)}, u32[]{:S(2)}, u32[]{:S(2)}) collective-permute-start(f32[24,8,128]{2,1,0:T(8,128)S(1)} %get-tuple-element.46), channel_id=1, source_target_pairs={{0,1},{1,2},{2,3},{3,4},{4,5},{5,6},{6,7},{7,8},{8,9},{9,10},{10,1... | collective-permute-start | bytes 294920 | tf_op jit(solution)/shard_map/ppermute | solution.py:748
  31.4 7.5 %collective-permute-start.5 = (f32[24,8,128]{2,1,0:T(8,128)S(1)}, f32[24,8,128]{2,1,0:T(8,128)S(1)}, u32[]{:S(2)}, u32[]{:S(2)}) collective-permute-start(f32[24,8,128]{2,1,0:T(8,128)S(1)} %get-tuple-element.47), channel_id=1, source_target_pairs={{1,0},{2,1},{3,2},{4,3},{5,4},{6,5},{7,6},{8,7},{9,8},{10,9},{11,1... | collective-permute-start | bytes 294920 | tf_op jit(solution)/shard_map/ppermute | solution.py:748
  36.7 13.9 %collective-permute-start.10 = (f32[48,8,128]{2,1,0:T(8,128)S(1)}, f32[48,8,128]{2,1,0:T(8,128)S(1)}, u32[]{:S(2)}, u32[]{:S(2)}) collective-permute-start(f32[48,8,128]{2,1,0:T(8,128)S(1)} %pad_maximum_fusion), channel_id=1, source_target_pairs={{0,240},{16,32},{32,16},{48,64},{64,48},{80,96},{96,80},{112,128},... | collective-permute-start | bytes 589832 | tf_op jit(solution)/shard_map/ppermute | solution.py:737
  42.6 8.0 %collective-permute-start.6 = (f32[16,8,128]{2,1,0:T(8,128)S(1)}, f32[16,8,128]{2,1,0:T(8,128)S(1)}, u32[]{:S(2)}, u32[]{:S(2)}) collective-permute-start(f32[16,8,128]{2,1,0:T(8,128)S(1)} %get-tuple-element.54.own), channel_id=1, source_target_pairs={{0,16},{16,0},{32,48},{48,32},{64,80},{80,64},{96,112},{112,96},{1... | collective-permute-start | bytes 196616 | tf_op jit(solution)/shard_map/ppermute | solution.py:734
  50.6 9.3 %collective-permute-start.7 = (f32[32,8,128]{2,1,0:T(8,128)S(1)}, f32[32,8,128]{2,1,0:T(8,128)S(1)}, u32[]{:S(2)}, u32[]{:S(2)}) collective-permute-start(f32[32,8,128]{2,1,0:T(8,128)S(1)} %pad_maximum_fusion.1), channel_id=1, source_target_pairs={{0,240},{16,32},{32,16},{48,64},{64,48},{80,96},{96,80},{112,128},... | collective-permute-start | bytes 393224 | tf_op jit(solution)/shard_map/ppermute | solution.py:737
  50.7 10.7 %collective-permute-start.11 = (f32[24,8,128]{2,1,0:T(8,128)S(1)}, f32[24,8,128]{2,1,0:T(8,128)S(1)}, u32[]{:S(2)}, u32[]{:S(2)}) collective-permute-start(f32[24,8,128]{2,1,0:T(8,128)S(1)} %shard_map.84), channel_id=1, source_target_pairs={{0,16},{16,0},{32,48},{48,32},{64,80},{80,64},{96,112},{112,96},{1... | collective-permute-start | bytes 294920 | tf_op jit(solution)/shard_map/ppermute | solution.py:734
  59.9 2.5 %collective-permute-start.8 = (f32[16,8,128]{2,1,0:T(8,128)S(1)}, f32[16,8,128]{2,1,0:T(8,128)S(1)}, u32[]{:S(2)}, u32[]{:S(2)}) collective-permute-start(f32[16,8,128]{2,1,0:T(8,128)S(1)} %shard_map.83), channel_id=1, source_target_pairs={{0,16},{16,0},{32,48},{48,32},{64,80},{80,64},{96,112},{112,96},{1... | collective-permute-start | bytes 196616 | tf_op jit(solution)/shard_map/ppermute | solution.py:734
  68.4 1.3 %collective-permute-start.12 = (f32[16,8,128]{2,1,0:T(8,128)S(1)}, f32[16,8,128]{2,1,0:T(8,128)S(1)}, u32[]{:S(2)}, u32[]{:S(2)}) collective-permute-start(f32[16,8,128]{2,1,0:T(8,128)S(1)} %get-tuple-element.64.own), channel_id=1, source_target_pairs={{0,16},{16,0},{32,48},{48,32},{64,80},{80,64},{96,112},{112,96},{1... | collective-permute-start | bytes 196616 | tf_op jit(solution)/shard_map/ppermute | solution.py:734
  70.4 9.4 %collective-permute-start.13 = (f32[24,8,128]{2,1,0:T(8,128)S(1)}, f32[24,8,128]{2,1,0:T(8,128)S(1)}, u32[]{:S(2)}, u32[]{:S(2)}) collective-permute-start(f32[24,8,128]{2,1,0:T(8,128)S(1)} %pad_maximum_fusion.2), channel_id=1, source_target_pairs={{0,240},{16,32},{32,16},{48,64},{64,48},{80,96},{96,80},{112,128},... | collective-permute-start | bytes 294920 | tf_op jit(solution)/shard_map/ppermute | solution.py:737
  79.7 2.0 %collective-permute-start.14 = (f32[16,8,128]{2,1,0:T(8,128)S(1)}, f32[16,8,128]{2,1,0:T(8,128)S(1)}, u32[]{:S(2)}, u32[]{:S(2)}) collective-permute-start(f32[16,8,128]{2,1,0:T(8,128)S(1)} %shard_map.88), channel_id=1, source_target_pairs={{0,16},{16,0},{32,48},{48,32},{64,80},{80,64},{96,112},{112,96},{1... | collective-permute-start | bytes 196616 | tf_op jit(solution)/shard_map/ppermute | solution.py:734
